TPU v7x, 32 devices: a whole 2x2x4 slice. The times are simulated.
32 devices in a mesh: dp: 8 (over z, core), expert: 4 (over y, x).
Axes of the slice: x: 2, y: 2, z: 4, core: 2. Of those that a mesh axis runs over, the one named last changes fastest.
Arguments:
- teacher_in: bfloat16 [1024, 2048], P('dp'), may hold values from -6 to 6
- student_in: bfloat16 [1024, 2048], P('dp'), may hold values from -6 to 6
- teacher_route: int32 [1024, 1], P('dp'), may hold values from 0 to 3, as said below
- student_route: int32 [1024, 1], P('dp'), may hold values from 0 to 3, as said below
- teacher_w1: bfloat16 [8, 2048, 2048], P('dp', None, 'expert'), may hold values from -0.125 to 0.125
- teacher_w2: bfloat16 [8, 2048, 2048], P('dp', 'expert'), may hold values from -0.09375 to 0.09375
- student_w1: bfloat16 [8, 2048, 2048], P('dp', None, 'expert'), may hold values from -0.125 to 0.125
- student_w2: bfloat16 [8, 2048, 2048], P('dp', 'expert'), may hold values from -0.09375 to 0.09375
Outputs:
- grad_w1: bfloat16 [8, 2048, 2048], P('dp', None, 'expert')
- grad_w2: bfloat16 [8, 2048, 2048], P('dp', 'expert')
Inputs may be any that keep to these rules, and one draw needn't show every extreme that they name: `teacher_route`: in each aligned block of 128 rows (the rows of one index of dp) no expert is named by more than 48 rows, and some expert exactly 48 times; every expert is named exactly 48 times in some block. `student_route`: in each aligned block of 128 rows (the rows of one index of dp) no expert is named by more than 48 rows, and some expert exactly 48 times; every expert is named exactly 48 times in some block.
All inputs are finite; a program needn't handle non-finite values.
Results may differ from a plain program's by a relative error of at most 0.015.
Values may be sent and summed in bfloat16 or wider, within the bound.
No kernel may reach another device: no remote copies, remote signals or barrier semaphores. Data moves between devices by JAX's collectives and lax.ppermute only.
A program may use at most 64 MiB of HBM per device.

v0:
```python
import math

import jax
import jax.numpy as jnp
from jax import lax
from jax.sharding import PartitionSpec as P

root_coef = math.sqrt(2.0 / math.pi)
cubic_coef = 0.044715


def partner(value, axis, apart):
    return lax.ppermute(value, axis, [(i, i ^ 1 << apart) for i in range(lax.axis_size(axis))])


def gelu_tanh(pre_act):
    inner_arg = root_coef * (pre_act + cubic_coef * pre_act * pre_act * pre_act)
    return 0.5 * pre_act * (1.0 + jnp.tanh(inner_arg))


def gelu_slope(pre_act):
    tangent = jnp.tanh(root_coef * (pre_act + cubic_coef * pre_act * pre_act * pre_act))
    return 0.5 * (1.0 + tangent) + 0.5 * pre_act * (1.0 - tangent * tangent) * root_coef * (
        1.0 + 3.0 * cubic_coef * pre_act * pre_act
    )


def slot_table(routes, experts, capacity):
    choose = routes[:, 0]
    onehot = (choose[:, None] == jnp.arange(experts, dtype=jnp.int32)[None, :]).astype(jnp.int32)
    rank_table = jnp.cumsum(onehot, axis=0) - 1
    position = jnp.sum(onehot * rank_table, axis=1)
    slot_index = choose * capacity + position
    placing = (
        jnp.arange(experts * capacity, dtype=jnp.int32)[:, None] == slot_index[None, :]
    ).astype(jnp.bfloat16)
    return (slot_index, placing)


def place_rows(placing, row_values, experts, capacity):
    filled = jnp.dot(placing, row_values, preferred_element_type=jnp.float32).astype(jnp.bfloat16)
    return filled.reshape(experts, capacity, row_values.shape[1])


def join_halves(mine_half, other_half, half_index):
    first_half = jnp.where(half_index == 0, mine_half, other_half)
    second_half = jnp.where(half_index == 0, other_half, mine_half)
    return jnp.concatenate([first_half, second_half], axis=1)


def gather_rows(returned, slot_index, capacity):
    model_width = returned.shape[2]
    flat_rows = returned.reshape(-1, model_width)
    expert_of = slot_index // capacity
    first_row = 2 * expert_of * capacity + slot_index % capacity
    lower = jnp.take(flat_rows, first_row, axis=0).astype(jnp.float32)
    upper = jnp.take(flat_rows, first_row + capacity, axis=0).astype(jnp.float32)
    return lower + upper


def on_device(
    teacher_in,
    student_in,
    teacher_route,
    student_route,
    teacher_w1,
    teacher_w2,
    student_w1,
    student_w2,
):
    groups = lax.axis_size("dp")
    experts = groups // 2
    row_count, model_width = teacher_in.shape
    capacity = 2 * max(1, 3 * row_count // (4 * experts))
    half_index = lax.axis_index("dp") % 2
    loss_scale = 1.0 / math.sqrt(row_count)
    teacher_slot, teacher_place = slot_table(teacher_route, experts, capacity)
    student_slot, student_place = slot_table(student_route, experts, capacity)
    teacher_buffer = place_rows(teacher_place, teacher_in, experts, capacity)
    student_buffer = place_rows(student_place, student_in, experts, capacity)
    mine_teacher, mine_student = (
        lax.all_to_all(
            teacher_buffer.reshape(groups, capacity // 2, model_width),
            "dp",
            split_axis=0,
            concat_axis=0,
            tiled=True,
        ),
        lax.all_to_all(
            student_buffer.reshape(groups, capacity // 2, model_width),
            "dp",
            split_axis=0,
            concat_axis=0,
            tiled=True,
        ),
    )
    other_both = partner(jnp.stack([mine_teacher, mine_student]), "dp", 0)
    teacher_recv = join_halves(mine_teacher, other_both[0], half_index)
    student_recv = join_halves(mine_student, other_both[1], half_index)
    teacher_flat = teacher_recv.reshape(groups * capacity, model_width)
    student_flat = student_recv.reshape(groups * capacity, model_width)
    teacher_hidden = gelu_tanh(
        jnp.dot(teacher_flat, teacher_w1[0], preferred_element_type=jnp.float32)
    ).astype(jnp.bfloat16)
    teacher_part = jnp.dot(
        teacher_hidden, teacher_w2[0], preferred_element_type=jnp.float32
    ).astype(jnp.bfloat16)
    student_pre = jnp.dot(student_flat, student_w1[0], preferred_element_type=jnp.float32)
    student_hidden = gelu_tanh(student_pre).astype(jnp.bfloat16)
    student_part = jnp.dot(
        student_hidden, student_w2[0], preferred_element_type=jnp.float32
    ).astype(jnp.bfloat16)
    back_teacher, back_student = (
        lax.all_to_all(
            teacher_part.reshape(groups, capacity, model_width),
            "dp",
            split_axis=0,
            concat_axis=0,
            tiled=True,
        ),
        lax.all_to_all(
            student_part.reshape(groups, capacity, model_width),
            "dp",
            split_axis=0,
            concat_axis=0,
            tiled=True,
        ),
    )
    local_teacher = gather_rows(back_teacher, teacher_slot, capacity)
    local_student = gather_rows(back_student, student_slot, capacity)
    total_teacher, total_student = lax.psum((local_teacher, local_student), "expert")
    output_gap = total_student - total_teacher
    upstream = (output_gap * loss_scale).astype(jnp.bfloat16)
    grad_buffer = place_rows(student_place, upstream, experts, capacity)
    grad_mine = lax.all_to_all(
        grad_buffer.reshape(groups, capacity // 2, model_width),
        "dp",
        split_axis=0,
        concat_axis=0,
        tiled=True,
    )
    grad_other = partner(grad_mine, "dp", 0)
    grad_recv = join_halves(grad_mine, grad_other, half_index)
    grad_flat = grad_recv.reshape(groups * capacity, model_width)
    hidden_grad = jnp.dot(grad_flat, student_w2[0].T, preferred_element_type=jnp.float32)
    pre_grad = (hidden_grad * gelu_slope(student_pre)).astype(jnp.bfloat16)
    grad_second = jnp.dot(student_hidden.T, grad_flat, preferred_element_type=jnp.float32).astype(
        jnp.bfloat16
    )
    grad_first = jnp.dot(student_flat.T, pre_grad, preferred_element_type=jnp.float32).astype(
        jnp.bfloat16
    )
    return (grad_first[None], grad_second[None])


def solution(mesh):
    return jax.shard_map(
        on_device,
        mesh=mesh,
        in_specs=(
            P("dp", None),
            P("dp", None),
            P("dp", None),
            P("dp", None),
            P("dp", None, "expert"),
            P("dp", "expert", None),
            P("dp", None, "expert"),
            P("dp", "expert", None),
        ),
        out_specs=(P("dp", None, "expert"), P("dp", "expert", None)),
        check_vma=False,
    )
```

profile of v0, /device:TPU:0, one launch (start us, length us, event | category | flops | bytes accessed | tf_op | source)
XLA Modules:
  0.0 289.9 jit_solution(10251650056372108881)
XLA Ops:
  7.2 0.0 copy-start
  7.2 0.0 copy-start.5
  7.2 0.9 fusion.44
  8.1 0.2 reduce_window_sum.17
  8.3 0.8 select_reduce_fusion.1
  9.1 0.7 compare_and_fusion.3
  9.8 0.0 copy-start.4
  9.8 2.3 convolution_convert_fusion.6
  12.1 6.3 %all-to-all-start = ((bf16[8,24,2048]{2,1,0:T(8,128)(2,1)}), bf16[8,24,2048]{2,1,0:T(8,128)(2,1)S(1)}, u32[]{:S(2)}, u32[]{:S(2)}) async-start(bf16[8,24,2048]{2,1,0:T(8,128)(2,1)} %bitcast.67), calls=%async_computation | async-start | bytes 1572864 | tf_op jit(solution)/shard_map/all_to_all | solution.py:89
  18.4 0.0 copy-done.5
  18.5 0.1 fusion.43
  18.5 0.2 reduce_window_sum.18
  18.7 0.2 select_reduce_fusion
  18.9 0.0 copy-done.4
  18.9 1.2 convolution_convert_fusion.5
  20.2 19.3 %all-to-all-done = bf16[8,24,2048]{2,1,0:T(8,128)(2,1)S(1)} async-done(((bf16[8,24,2048]{2,1,0:T(8,128)(2,1)}), bf16[8,24,2048]{2,1,0:T(8,128)(2,1)S(1)}, u32[]{:S(2)}, u32[]{:S(2)}) %all-to-all-start) | async-done | bytes 786464 | tf_op jit(solution)/shard_map/all_to_all | solution.py:89
  39.4 24.4 %all_to_all.25 = bf16[8,24,2048]{2,1,0:T(8,128)(2,1)S(1)} all-to-all(bf16[8,24,2048]{2,1,0:T(8,128)(2,1)} %bitcast.68), channel_id=1, replica_groups=mesh['dp'=8,'expert'=4] {'dp'}, dimensions={0} | all-to-all | bytes 1572864 | tf_op jit(solution)/shard_map/all_to_all | solution.py:82
  63.9 0.0 copy-start.1
  63.9 1.4 pad_maximum_fusion
  65.3 0.0 copy-done.1
  65.3 0.0 collective-permute-start
  65.3 3.7 %collective-permute-done = bf16[2,8,24,2048]{3,2,1,0:T(8,128)(2,1)} collective-permute-done((bf16[2,8,24,2048]{3,2,1,0:T(8,128)(2,1)}, bf16[2,8,24,2048]{3,2,1,0:T(8,128)(2,1)}, u32[]{:S(2)}, u32[]{:S(2)}) %collective-permute-start) | collective-permute-done | bytes 1572896 | tf_op jit(solution)/shard_map/ppermute | solution.py:13
  69.0 1.8 broadcast_select_fusion.3
  70.8 2.1 pad_maximum_fusion.1
  72.9 5.8 %convolution_convert_fusion.2 = bf16[384,2048]{1,0:T(8,128)(2,1)} fusion(bf16[1,512,2048]{2,1,0:T(8,128)(2,1)} %param.15, bf16[384,2048]{1,0:T(8,128)(2,1)} %bitcast.76, bf16[1,2048,512]{2,1,0:T(8,128)(2,1)} %param.14), kind=kOutput, calls=%fused_computation.6 | convolution fusion | flops 1613168640 | bytes 7340032 | tf_op jit(solution)/shard_map/dot_general | solution.py:105
  78.7 4.3 %all-to-all-start.3 = ((bf16[8,48,2048]{2,1,0:T(8,128)(2,1)}), bf16[8,48,2048]{2,1,0:T(8,128)(2,1)}, u32[]{:S(2)}, u32[]{:S(2)}) async-start(bf16[8,48,2048]{2,1,0:T(8,128)(2,1)} %bitcast.71), calls=%async_computation.3 | async-start | bytes 3145728 | tf_op jit(solution)/shard_map/all_to_all | solution.py:114
  83.0 3.0 %fusion.8 = f32[384,512]{1,0:T(8,128)S(1)} fusion(bf16[384,2048]{1,0:T(8,128)(2,1)} %bitcast.74, bf16[1,2048,512]{2,1,0:T(8,128)(2,1)} %param.16), kind=kOutput, calls=%fused_computation.19 | convolution fusion | flops 805306368 | bytes 4456448 | tf_op jit(solution)/shard_map/dot_general | solution.py:108
  86.1 0.0 copy-start.6
  86.1 0.9 copy-done.6
  87.0 0.0 copy-done
  87.0 2.2 convolution_convert_fusion.3
  89.2 31.7 %all-to-all-done.3 = bf16[8,48,2048]{2,1,0:T(8,128)(2,1)} async-done(((bf16[8,48,2048]{2,1,0:T(8,128)(2,1)}), bf16[8,48,2048]{2,1,0:T(8,128)(2,1)}, u32[]{:S(2)}, u32[]{:S(2)}) %all-to-all-start.3) | async-done | bytes 1572896 | tf_op jit(solution)/shard_map/all_to_all | solution.py:114
  120.9 4.3 %all-to-all-start.2 = ((bf16[8,48,2048]{2,1,0:T(8,128)(2,1)}), bf16[8,48,2048]{2,1,0:T(8,128)(2,1)}, u32[]{:S(2)}, u32[]{:S(2)}) async-start(bf16[8,48,2048]{2,1,0:T(8,128)(2,1)} %bitcast.70), calls=%async_computation.2 | async-start | bytes 3145728 | tf_op jit(solution)/shard_map/all_to_all | solution.py:121
  125.2 0.0 all-reduce.3.cloned.1.call-start
  125.3 3.1 %gather_fusion.3 = bf16[128,2048]{1,0:T(8,128)(2,1)S(1)} fusion(bf16[384,2048]{1,0:T(8,128)(2,1)} %bitcast.17, s32[1024]{0:T(1024)S(1)} %pad_clamp_fusion), kind=kCustom, calls=%fused_computation.3.clone | custom fusion | bytes 1049088 | tf_op jit(solution)/shard_map/jit(_take)/gather | solution.py:57
  128.4 3.1 %gather_fusion.2 = bf16[128,2048]{1,0:T(8,128)(2,1)S(1)} fusion(bf16[384,2048]{1,0:T(8,128)(2,1)} %bitcast.17, s32[1024]{0:T(1024)S(1)} %pad_clamp_fusion.1), kind=kCustom, calls=%fused_computation.2.clone | custom fusion | bytes 1049088 | tf_op jit(solution)/shard_map/jit(_take)/gather | solution.py:56
  131.4 31.6 %all-to-all-done.2 = bf16[8,48,2048]{2,1,0:T(8,128)(2,1)} async-done(((bf16[8,48,2048]{2,1,0:T(8,128)(2,1)}), bf16[8,48,2048]{2,1,0:T(8,128)(2,1)}, u32[]{:S(2)}, u32[]{:S(2)}) %all-to-all-start.2) | async-done | bytes 1572896 | tf_op jit(solution)/shard_map/all_to_all | solution.py:121
  163.0 3.8 %gather_fusion.1 = bf16[128,2048]{1,0:T(8,128)(2,1)} fusion(bf16[384,2048]{1,0:T(8,128)(2,1)} %bitcast.11, s32[1024]{0:T(1024)S(1)} %pad_clamp_fusion.2), kind=kCustom, calls=%fused_computation.1.clone | custom fusion | bytes 1049088 | tf_op jit(solution)/shard_map/jit(_take)/gather | solution.py:57
  166.8 3.9 %gather_fusion = bf16[128,2048]{1,0:T(8,128)(2,1)} fusion(bf16[384,2048]{1,0:T(8,128)(2,1)} %bitcast.11, s32[1024]{0:T(1024)S(1)} %pad_clamp_fusion.3), kind=kCustom, calls=%fused_computation.clone | custom fusion | bytes 1049088 | tf_op jit(solution)/shard_map/jit(_take)/gather | solution.py:56
  170.7 0.0 copy-start.2
  170.7 0.0 copy-start.3
  170.7 1.2 convert_add_fusion
  171.9 0.0 copy-done.2
  171.9 0.1 copy-done.3
  172.1 1.2 convert_add_fusion.1
  173.3 0.0 all-reduce.3.cloned.1.call-update
  173.3 68.9 %all-reduce.3.cloned.1.call-done = (f32[128,2048]{1,0:T(8,128)}, f32[128,2048]{1,0:T(8,128)}) async-done(((f32[128,2048]{1,0:T(8,128)}, f32[128,2048]{1,0:T(8,128)}), (f32[128,2048]{1,0:T(8,128)}, f32[128,2048]{1,0:T(8,128)})) %all-reduce.3.cloned.1.call-update) | async-done | bytes 2097168 | tf_op jit(solution)/shard_map/psum | solution.py:131
  242.2 1.9 convolution_convert_fusion.4
  244.1 25.4 %all_to_all.26 = bf16[8,24,2048]{2,1,0:T(8,128)(2,1)S(1)} all-to-all(bf16[8,24,2048]{2,1,0:T(8,128)(2,1)S(1)} %bitcast.69), channel_id=1, replica_groups=mesh['dp'=8,'expert'=4] {'dp'}, dimensions={0} | all-to-all | bytes 1572864 | tf_op jit(solution)/shard_map/all_to_all | solution.py:135
  269.5 0.0 collective-permute-start.1
  269.5 2.3 collective-permute-done.1
  271.8 0.1 broadcast_select_fusion.1
  271.9 0.0 copy-start.7
  271.9 1.3 pad_maximum_fusion.3
  273.1 0.1 copy-done.7
  273.3 5.7 %fusion = bf16[1,2048,512]{2,1,0:T(8,128)(2,1)} fusion(bf16[384,2048]{1,0:T(8,128)(2,1)} %bitcast.75, bf16[384,2048]{1,0:T(8,128)(2,1)} %bitcast.72, bf16[1,512,2048]{2,1,0:T(8,128)(2,1)S(1)} %copy-done, f32[384,512]{1,0:T(8,128)S(1)} %copy-done.7), kind=kOutput, calls=%fused_computation.8 | convolution fusion | flops 1615396864 | bytes 8126464 | tf_op jit(solution)/shard_map/dot_general | solution.py:150
  279.0 4.1 %fusion.1 = bf16[1,512,2048]{2,1,0:T(8,128)(2,1)} fusion(bf16[384,2048]{1,0:T(8,128)(2,1)} %bitcast.73, f32[384,512]{1,0:T(8,128)S(1)} %copy-done.7), kind=kOutput, calls=%fused_computation.9 | convolution fusion | flops 808124416 | bytes 4456448 | tf_op jit(solution)/shard_map/dot_general | solution.py:147
  (9 shorter events, 0.1 us)
Async XLA Ops:
  7.2 79.8 %copy-start = (bf16[1,512,2048]{2,1,0:T(8,128)(2,1)S(1)}, bf16[1,512,2048]{2,1,0:T(8,128)(2,1)}, u32[]{:S(2)}) copy-start(bf16[1,512,2048]{2,1,0:T(8,128)(2,1)} %param.17) | copy-start | bytes 6291460
  7.2 11.3 %copy-start.5 = (s32[128,1]{0,1:T(1,128)S(1)}, s32[128,1]{0,1:T(1,128)}, u32[]{:S(2)}) copy-start(s32[128,1]{0,1:T(1,128)} %param.12) | copy-start | bytes 1540
  9.8 9.2 %copy-start.4 = (bf16[128,2048]{1,0:T(8,128)(2,1)S(1)}, bf16[128,2048]{1,0:T(8,128)(2,1)}, u32[]{:S(2)}) copy-start(bf16[128,2048]{1,0:T(8,128)(2,1)} %param.10) | copy-start | bytes 1572868
  12.1 27.3 %all-to-all-start = ((bf16[8,24,2048]{2,1,0:T(8,128)(2,1)}), bf16[8,24,2048]{2,1,0:T(8,128)(2,1)S(1)}, u32[]{:S(2)}, u32[]{:S(2)}) async-start(bf16[8,24,2048]{2,1,0:T(8,128)(2,1)} %bitcast.67), calls=%async_computation | async-start | bytes 1572864 | tf_op jit(solution)/shard_map/all_to_all | solution.py:89
  63.9 1.4 copy-start.1
  65.3 3.8 %collective-permute-start = (bf16[2,8,24,2048]{3,2,1,0:T(8,128)(2,1)}, bf16[2,8,24,2048]{3,2,1,0:T(8,128)(2,1)}, u32[]{:S(2)}, u32[]{:S(2)}) collective-permute-start(bf16[2,8,24,2048]{3,2,1,0:T(8,128)(2,1)} %pad_maximum_fusion), channel_id=1, source_target_pairs={{0,4},{4,0},{8,12},{12,8},{16,20},{20,16},{24,28},{28,24},{1,5},{5... | collective-permute-start | bytes 4718600 | tf_op jit(solution)/shard_map/ppermute | solution.py:13
  78.7 42.1 %all-to-all-start.3 = ((bf16[8,48,2048]{2,1,0:T(8,128)(2,1)}), bf16[8,48,2048]{2,1,0:T(8,128)(2,1)}, u32[]{:S(2)}, u32[]{:S(2)}) async-start(bf16[8,48,2048]{2,1,0:T(8,128)(2,1)} %bitcast.71), calls=%async_computation.3 | async-start | bytes 3145728 | tf_op jit(solution)/shard_map/all_to_all | solution.py:114
  86.1 0.9 copy-start.6
  120.9 42.1 %all-to-all-start.2 = ((bf16[8,48,2048]{2,1,0:T(8,128)(2,1)}), bf16[8,48,2048]{2,1,0:T(8,128)(2,1)}, u32[]{:S(2)}, u32[]{:S(2)}) async-start(bf16[8,48,2048]{2,1,0:T(8,128)(2,1)} %bitcast.70), calls=%async_computation.2 | async-start | bytes 3145728 | tf_op jit(solution)/shard_map/all_to_all | solution.py:121
  125.2 117.0 %all-reduce.3.cloned.1.call-start = ((), (), s32[]{:S(2)}) async-start(), calls=%async_computation.5 | async-start | bytes 4194304 | tf_op jit(solution)/shard_map/psum | solution.py:131
  170.7 1.2 copy-start.2
  170.7 1.3 copy-start.3
  269.5 2.3 collective-permute-start.1
  271.9 1.4 copy-start.7
Sparse Core Ops, SparseCore 0:
  173.4 68.7 all-reduce.2
where the time goes:
time: 291 us; the launch traced here: 290 us
  waiting for transfers between devices  157 us (54%)
  blocking collectives  49.8 us (17%)
  matrix products  26.4 us (9%)
  local copies, waits for them, and re-layouts  15 us (5%)
  starting transfers between devices  15 us (5%)
  between operations  14.2 us (5%)
  other arithmetic  12.1 us (4%)
    psum x1, waiting for transfers between devices, on_device(): lax.psum((local_teacher, local_student), 'expert')  68.9 us
    all_to_all x1, waiting for transfers between devices, on_device(): lax.all_to_all(teacher_part.reshape(groups, capacity, model_width), 'dp',...  31.7 us
    all_to_all x1, waiting for transfers between devices, on_device(): lax.all_to_all(student_part.reshape(groups, capacity, model_width), 'dp',...  31.6 us
    all_to_all x1, blocking collectives, on_device(): lax.all_to_all(grad_buffer.reshape(groups, capacity // 2, model_width), '...  25.4 us
    all_to_all x1, blocking collectives, on_device(): lax.all_to_all(teacher_buffer.reshape(groups, capacity // 2, model_width)...  24.4 us
    all_to_all x1, waiting for transfers between devices, on_device(): lax.all_to_all(student_buffer.reshape(groups, capacity // 2, model_width)...  19.3 us
    gather x2, local copies, waits for them, and re-layouts, gather_rows(): lower = jnp.take(flat_rows, first_row, axis=0).astype(jnp.float32)  6.93 us
    gather x2, local copies, waits for them, and re-layouts, gather_rows(): jnp.take(flat_rows, first_row + capacity, axis=0).astype(jnp.float32)  6.89 us
  transfers between devices with their start and end apart: 6, of which 6 were waited for; matrix products, arithmetic and copies ran while one was open for 5% of the time, Pallas kernels for 0%

commit v1 on v0

v1 whole, which is shorter than its diff:
```python
import math

import jax
import jax.numpy as jnp
from jax import lax
from jax.experimental import pallas as pl
from jax.experimental.pallas import tpu as pltpu
from jax.sharding import PartitionSpec as P

root_coef = math.sqrt(2.0 / math.pi)
cubic_coef = 0.044715


def partner(value, axis, mask):
    return lax.ppermute(value, axis, [(i, i ^ mask) for i in range(lax.axis_size(axis))])


def gelu_tanh(pre_act):
    inner_arg = root_coef * (pre_act + cubic_coef * pre_act * pre_act * pre_act)
    return 0.5 * pre_act * (1.0 + jnp.tanh(inner_arg))


def gelu_slope(pre_act):
    tangent = jnp.tanh(root_coef * (pre_act + cubic_coef * pre_act * pre_act * pre_act))
    return 0.5 * (1.0 + tangent) + 0.5 * pre_act * (1.0 - tangent * tangent) * root_coef * (
        1.0 + 3.0 * cubic_coef * pre_act * pre_act
    )


def dot(left, right):
    return jnp.dot(left, right, preferred_element_type=jnp.float32)


def ranks(routes, experts):
    onehot = (routes[..., None] == jnp.arange(experts, dtype=jnp.int32)).astype(jnp.int32)
    rank_table = jnp.cumsum(onehot, axis=1) - 1
    return jnp.sum(onehot * rank_table, axis=2)


def sizes(rows):
    groups = lax.axis_size("dp")
    experts = groups // 2
    row_count, width = rows.shape
    capacity = 2 * max(1, 3 * row_count // (4 * experts))
    return groups, lax.axis_size("expert"), experts, row_count, width, capacity


def by_ops(
    teacher_in,
    student_in,
    teacher_route,
    student_route,
    teacher_w1,
    teacher_w2,
    student_w1,
    student_w2,
):
    groups, columns, experts, row_count, width, capacity = sizes(teacher_in)
    plane_rows = groups * capacity
    dp = lax.axis_index("dp")
    column = lax.axis_index("expert")
    plane, core = dp // 2, dp % 2
    loss_scale = 1.0 / math.sqrt(row_count)
    feat = width // columns
    piece = feat // 2

    def dispatch(values, routes):
        position = ranks(routes[:, 0][None], experts)[0]
        slot = (routes[:, 0] ^ plane) * capacity + position
        placing = (
            jnp.arange(experts * capacity, dtype=jnp.int32)[:, None] == slot[None, :]
        ).astype(jnp.bfloat16)
        own_slice = lax.dynamic_slice(values, (0, column * feat), (row_count, feat))
        slots = dot(placing[capacity:], own_slice).astype(jnp.bfloat16)
        stay = dot(placing[:capacity], values).astype(jnp.bfloat16)
        moved = [
            partner(slots[(s - 1) * capacity : s * capacity], "dp", s << 1)
            for s in range(1, experts)
        ]
        mine = jnp.concatenate(moved, axis=0)
        buffer = jnp.concatenate([stay, jnp.zeros((mine.shape[0], width), jnp.bfloat16)], axis=0)
        for m in range(columns):
            got = partner(mine, "expert", m) if m else mine
            buffer = lax.dynamic_update_slice(buffer, got, (capacity, (column ^ m) * feat))
        other = partner(buffer, "dp", 1)
        first = jnp.where(core == 0, buffer, other)
        second = jnp.where(core == 0, other, buffer)
        return jnp.concatenate([first, second], axis=0)

    def forward(flat, w1, w2):
        pre = dot(flat, w1)
        hidden = gelu_tanh(pre).astype(jnp.bfloat16)
        part = dot(hidden, w2).astype(jnp.bfloat16).reshape(plane_rows, 2, columns, piece)
        part = part.transpose(1, 2, 0, 3)
        return pre, hidden, part

    def plane_sum(part):
        keep = lax.dynamic_index_in_dim(part, core, 0, keepdims=False)
        send = lax.dynamic_index_in_dim(part, 1 - core, 0, keepdims=False)
        pair = (
            keep.astype(jnp.float32) + partner(send, "dp", 1).astype(jnp.float32)
        ).astype(jnp.bfloat16)
        total = lax.dynamic_index_in_dim(pair, column, 0, keepdims=False).astype(jnp.float32)
        for m in range(1, columns):
            out = lax.dynamic_index_in_dim(pair, column ^ m, 0, keepdims=False)
            total = total + partner(out, "expert", m).astype(jnp.float32)
        return total

    routes = jnp.concatenate([teacher_route, student_route], axis=1)
    table = lax.all_gather(routes, "dp", axis=0, tiled=True).reshape(groups, row_count, 2)
    teacher_all, student_all = table[:, :, 0], table[:, :, 1]
    block = jnp.arange(groups, dtype=jnp.int32)[:, None]
    block_plane, block_core = block // 2, block % 2
    teacher_row = (
        (teacher_all ^ plane) * plane_rows
        + (block_core * experts + (block_plane ^ teacher_all)) * capacity
        + ranks(teacher_all, experts)
    )
    student_row = jnp.where(student_all == plane, ranks(student_all, experts), -1)
    hits = jnp.arange(capacity, dtype=jnp.int32)[None, :, None] == student_row[:, None, :]
    source = jnp.sum(jnp.where(hits, teacher_row[:, None, :] + 1, 0), axis=2) - 1
    source = source.reshape(experts, 2, capacity)
    source = source[jnp.arange(experts, dtype=jnp.int32) ^ plane].transpose(1, 0, 2)
    source = source.reshape(plane_rows)

    teacher_flat = dispatch(teacher_in, teacher_route)
    student_flat = dispatch(student_in, student_route)
    _, _, teacher_part = forward(teacher_flat, teacher_w1[0], teacher_w2[0])
    teacher_sum = plane_sum(teacher_part).astype(jnp.bfloat16)
    teacher_sums = jnp.concatenate(
        [teacher_sum] + [partner(teacher_sum, "dp", s << 1) for s in range(1, experts)], axis=0
    )
    student_pre, student_hidden, student_part = forward(
        student_flat, student_w1[0], student_w2[0]
    )
    pick = (
        source[:, None] == jnp.arange(experts * plane_rows, dtype=jnp.int32)[None, :]
    ).astype(jnp.bfloat16)
    teacher_rows = dot(pick, teacher_sums)
    student_sum = plane_sum(student_part)
    upstream = ((student_sum - teacher_rows) * loss_scale).astype(jnp.bfloat16)

    half = jnp.zeros((plane_rows, width // 2), jnp.bfloat16)
    for m in range(columns):
        got = partner(upstream, "expert", m) if m else upstream
        half = lax.dynamic_update_slice(half, got, (0, (column ^ m) * piece))
    other_half = partner(half, "dp", 1)
    grad_flat = jnp.concatenate(
        [jnp.where(core == 0, half, other_half), jnp.where(core == 0, other_half, half)], axis=1
    )
    hidden_grad = dot(grad_flat, student_w2[0].T)
    pre_grad = (hidden_grad * gelu_slope(student_pre)).astype(jnp.bfloat16)
    grad_second = dot(student_hidden.T, grad_flat).astype(jnp.bfloat16)
    grad_first = dot(student_flat.T, pre_grad).astype(jnp.bfloat16)
    return (grad_first[None], grad_second[None])


def place():
    dp = lax.axis_index("dp")
    return dp // 2, dp % 2, lax.axis_index("expert")


VMEM = pl.BlockSpec(memory_space=pltpu.VMEM)
ANY = pl.BlockSpec(memory_space=pl.ANY)


def call(kernel, outs, operands, out_specs=None, in_specs=None, scratch=(), aliases=None, grant=20 << 20, flops=0, name=None):
    return pl.pallas_call(
        kernel,
        name=name,
        out_shape=outs,
        in_specs=in_specs or [VMEM] * len(operands),
        out_specs=out_specs or [VMEM] * len(outs),
        scratch_shapes=list(scratch),
        input_output_aliases=aliases or {},
        compiler_params=pltpu.CompilerParams(vmem_limit_bytes=grant),
        cost_estimate=pl.CostEstimate(flops=flops, bytes_accessed=0, transcendentals=0),
    )(*operands)


def shape(*dims, dtype=jnp.bfloat16):
    return jax.ShapeDtypeStruct(dims, dtype)


def dot_tn(left, right):
    return lax.dot_general(
        left, right, (((0,), (0,)), ((), ())), preferred_element_type=jnp.float32
    )


def dot_nt(left, right):
    return lax.dot_general(
        left, right, (((1,), (1,)), ((), ())), preferred_element_type=jnp.float32
    )


def placing(route, experts, capacity, plane):
    rows = route.shape[1]
    known = lax.broadcasted_iota(jnp.int32, (16 * (-(-experts // 16)), rows), 0)
    onehot = jnp.where(known == route, 1.0, 0.0)
    upto = lax.broadcasted_iota(jnp.int32, (rows, rows), 0) <= lax.broadcasted_iota(
        jnp.int32, (rows, rows), 1
    )
    counts = dot(onehot.astype(jnp.bfloat16), jnp.where(upto, 1.0, 0.0).astype(jnp.bfloat16))
    position = jnp.sum(onehot * counts, axis=0, keepdims=True).astype(jnp.int32) - 1
    slot = (route ^ plane) * capacity + position
    slots = lax.broadcasted_iota(jnp.int32, (experts * capacity, rows), 0)
    return jnp.where(slots == slot, 1.0, 0.0).astype(jnp.bfloat16)


def pack_kernel(experts, capacity, feat, *refs):
    plane, _, column = place()
    values, routes, refs = refs[:2], refs[2:4], refs[4:]
    moved, refs = refs[: experts - 1], refs[experts - 1 :]
    slices, blocks, sems = refs[:2], refs[2:4], refs[4]
    cols = pl.ds(pl.multiple_of(column * feat, feat), feat)
    copies = [
        pltpu.make_async_copy(routes[0], blocks[0], sems.at[0]),
        pltpu.make_async_copy(routes[1], blocks[1], sems.at[1]),
        pltpu.make_async_copy(values[0].at[:, cols], slices[0], sems.at[2]),
        pltpu.make_async_copy(values[1].at[:, cols], slices[1], sems.at[3]),
    ]
    for copy in copies:
        copy.start()
    for i in range(2):
        copies[i].wait()
        place_rows = placing(blocks[i][...], experts, capacity, plane)
        copies[2 + i].wait()
        sent = dot(place_rows[capacity:], slices[i][...]).astype(jnp.bfloat16)
        for s in range(experts - 1):
            moved[-1 - s][:, i * feat : (i + 1) * feat] = sent[s * capacity : (s + 1) * capacity]


def stay_kernel(experts, capacity, values, route, stay):
    plane, _, _ = place()
    place_rows = placing(route[...], experts, capacity, plane)
    stay[...] = dot(place_rows[:capacity], values[...]).astype(jnp.bfloat16)


def map_kernel(experts, capacity, routes, other_routes, out):
    plane, core, _ = place()
    for c in range(2):
        block = jnp.where(core == c, routes[...], other_routes[...])
        source = placing(block[0:1], experts, capacity, plane)
        target = placing(block[1:2], experts, capacity, plane)
        out[c] = dot_nt(target, source).astype(jnp.bfloat16)


def load_kernel(*refs):
    count = len(refs) // 2
    copies = [
        pltpu.make_async_copy(refs[i], refs[count + i], refs[-1].at[i]) for i in range(count)
    ]
    for copy in copies:
        copy.start()
    for copy in copies:
        copy.wait()


def stack_kernel(*refs):
    out = refs[-1]
    capacity = refs[0].shape[0]
    for s, ref in enumerate(refs[-2::-1]):
        out[s * capacity : (s + 1) * capacity, :] = ref[...]


def join_kernel(columns, stay_t, stay_s, *refs):
    _, _, column = place()
    parts, flats = refs[:-2], refs[-2:]
    capacity = stay_t.shape[0]
    feat = parts[0].shape[1] // 2
    for i, stay in enumerate((stay_t, stay_s)):
        flats[i][:capacity, :] = stay[...]
        for m in range(columns):
            cols = pl.ds(pl.multiple_of((column ^ m) * feat, feat), feat)
            flats[i][capacity:, cols] = parts[m][:, i * feat : (i + 1) * feat]


def part_pieces(hidden, w2, which, columns, out):
    half = w2.shape[1] // 2
    piece = half // columns
    for j in range(columns):
        cols = pl.ds(pl.multiple_of(which * half + j * piece, piece), piece)
        out[j] = dot(hidden, w2[:, cols]).astype(jnp.bfloat16)


def forward_kernel(columns, count, *refs):
    _, core, _ = place()
    flats, refs = refs[:count], refs[count:]
    w1, w2, send, refs = refs[0], refs[1], refs[2], refs[3:]
    for i in range(count):
        pre = dot(flats[i][...], w1[...])
        if len(refs) > count:
            refs[count + i][...] = pre
        hidden = gelu_tanh(pre).astype(jnp.bfloat16)
        refs[i][...] = hidden
        part_pieces(hidden, w2, 1 - core, columns, send.at[i])


def keep_kernel(columns, hidden_own, hidden_other, w2, *refs):
    _, core, _ = place()
    if len(refs) > 2:
        pre_own, pre_other, flat_own, flat_other, keep_own, keep_other = refs[:6]
        flat_t, hidden_t, slope = refs[6:]
    else:
        keep_own, keep_other = refs
    part_pieces(hidden_own[...], w2, core, columns, keep_own)
    part_pieces(hidden_other[...], w2, core, columns, keep_other)
    if len(refs) > 2:
        half = flat_own.shape[0]
        slope[:half, :] = gelu_slope(pre_own[...])
        slope[half:, :] = gelu_slope(pre_other[...])
        hidden_t[...] = jnp.concatenate([hidden_own[...], hidden_other[...]], axis=0).T
        step = 512
        for j in range(0, flat_own.shape[1], step):
            here = slice(j, j + step)
            both = jnp.concatenate([flat_own[:, here], flat_other[:, here]], axis=0)
            flat_t[here, :] = both.T


def pair_kernel(columns, keep_own, keep_other, *refs):
    _, core, column = place()
    half = keep_own.shape[1]
    got, (mine, *out) = refs[:-columns], refs[-columns:]
    got_own, got_other = got[0].at[0], got[-1].at[len(got) % 2]
    for m in range(columns):
        for which, keep, got in ((core, keep_own, got_other), (1 - core, keep_other, got_own)):
            rows = pl.ds(pl.multiple_of(which * half, 16), half)
            both = keep[column ^ m].astype(jnp.float32) + got[column ^ m].astype(jnp.float32)
            if m:
                out[m - 1][rows, :] = both.astype(jnp.bfloat16)
            else:
                mine[rows, :] = both


def total_kernel(columns, experts, *refs):
    sums, out = refs[:columns], refs[columns:]
    total = sums[0][...]
    for ref in sums[1:]:
        total = total + ref[...].astype(jnp.float32)
    total = total.astype(jnp.bfloat16)
    capacity = out[0].shape[0] // 2
    for s in range(experts):
        for c in range(2):
            start = (c * experts + s) * capacity
            out[-1 - s][c * capacity : (c + 1) * capacity, :] = total[start : start + capacity]


def home_kernel(experts, capacity, maps, *refs):
    got, out = refs[:experts], refs[experts:]
    for c in range(2):
        here = slice(c * capacity, (c + 1) * capacity)
        rows = jnp.concatenate([ref[here, :] for ref in got[::-1]], axis=0)
        by_slot = dot(maps[c], rows).astype(jnp.bfloat16)
        for s in range(experts):
            out[-1 - s][here, :] = by_slot[s * capacity : (s + 1) * capacity]


def upstream_kernel(columns, experts, loss_scale, *refs):
    sums, teacher, out = refs[:columns], refs[columns:-1], refs[-1]
    total = sums[0][...]
    for ref in sums[1:]:
        total = total + ref[...].astype(jnp.float32)
    capacity = teacher[0].shape[0] // 2
    rows = jnp.concatenate(
        [
            teacher[-1 - s][c * capacity : (c + 1) * capacity, :]
            for c in range(2)
            for s in range(experts)
        ],
        axis=0,
    ).astype(jnp.float32)
    out[...] = ((total - rows) * loss_scale).astype(jnp.bfloat16)


def backward_kernel(columns, places, first, last, *refs):
    _, core, column = place()
    pieces, refs = refs[: len(places)], refs[len(places) :]
    hidden_t, w2, refs = refs[0], refs[1], refs[2:]
    if not first:
        sum_in, refs = refs[0], refs[2:]
    if last:
        flat_t, slope, grad_second, grad_first, held_first, held_second, sems = refs
    else:
        grad_second, sum_out, held_second, sems = refs
    piece = pieces[0].shape[1]
    width = w2.shape[1]
    hidden_grad = None if first else sum_in[...]
    copies = []

    def leave(source, target):
        copies.append(pltpu.make_async_copy(source, target, sems.at[len(copies)]))
        copies[-1].start()

    used = []
    for ref, (other, m) in zip(pieces, places):
        which = 1 - core if other else core
        start = which * (width // 2) + (column ^ m) * piece
        cols = pl.ds(pl.multiple_of(start, piece), piece)
        half = ref.shape[0] // 2
        rows = jnp.concatenate(
            [ref[pl.ds(pl.multiple_of(block * half, 16), half), :] for block in (core, 1 - core)],
            axis=0,
        )
        used.append((rows, cols))
        term = dot_nt(rows, w2[:, cols])
        hidden_grad = term if hidden_grad is None else hidden_grad + term
    if last:
        pre_grad = (hidden_grad * slope[...]).astype(jnp.bfloat16)
        step = 256
        for j in range(width // step):
            here = slice(j * step, (j + 1) * step)
            held_first[here, :] = dot(flat_t[here, :], pre_grad).astype(jnp.bfloat16)
            leave(held_first.at[here, :], grad_first.at[here, :])
    else:
        sum_out[...] = hidden_grad
    for i, (rows, cols) in enumerate(used):
        held_second[i] = dot(hidden_t[...], rows).astype(jnp.bfloat16)
        leave(held_second.at[i], grad_second.at[:, cols])
    for copy in copies:
        copy.wait()


def by_kernels(
    teacher_in,
    student_in,
    teacher_route,
    student_route,
    teacher_w1,
    teacher_w2,
    student_w1,
    student_w2,
):
    groups, columns, experts, row_count, width, capacity = sizes(teacher_in)
    plane_rows = groups * capacity
    loss_scale = 1.0 / math.sqrt(row_count)
    feat = width // columns
    piece = feat // 2
    hid = teacher_w1.shape[2]
    f32 = jnp.float32

    def after(value, *others):
        return lax.optimization_barrier((value, others))[0]

    def over_planes(sent):
        return [partner(value, "dp", (experts - 1 - i) << 1) for i, value in enumerate(sent)]

    def spread(mine):
        return [mine] + [partner(mine, "expert", m) for m in range(1, columns)]

    def across(value):
        return partner(value, "dp", 1)

    def load(*weights):
        return call(
            load_kernel,
            [shape(*w.shape) for w in weights],
            weights,
            in_specs=[ANY] * len(weights),
            name="load",
            scratch=[pltpu.SemaphoreType.DMA((len(weights),))],
        )

    def forward(flats, w1, w2, keep_pre, name):
        half, count = plane_rows // 2, len(flats)
        pre = [shape(half, hid, dtype=f32)] * count if keep_pre else []
        return call(
            lambda *refs: forward_kernel(columns, count, *refs),
            [shape(count, columns, half, piece)] + [shape(half, hid)] * count + pre,
            [*flats, w1, w2],
            name=name,
        )

    def keep(own, other, w2, state, outs):
        return call(
            lambda *refs: keep_kernel(columns, *refs),
            [shape(columns, plane_rows // 2, piece)] * 2 + outs,
            [own, other, w2, *state],
            flops=(16 if state else 1) * plane_rows * width * hid,
            name="keep_s" if state else "keep_t",
        )

    def pair(kept, got):
        return call(
            lambda *refs: pair_kernel(columns, *refs),
            [shape(plane_rows, piece, dtype=f32)] + [shape(plane_rows, piece)] * (columns - 1),
            [*kept, *got],
            name="pair",
        )

    def collect(mine, *out):
        return [mine] + [partner(value, "expert", m + 1) for m, value in enumerate(out)]

    route_t = teacher_route.reshape(1, row_count)
    route_s = student_route.reshape(1, row_count)
    def stay(values, route):
        return call(
            lambda *refs: stay_kernel(experts, capacity, *refs),
            [shape(capacity, width)],
            [values, route],
            name="stay",
        )[0]

    sent = call(
        lambda *refs: pack_kernel(experts, capacity, feat, *refs),
        [shape(capacity, 2 * feat)] * (experts - 1),
        [teacher_in, student_in, route_t, route_s],
        in_specs=[ANY] * 4,
        grant=(253 << 20) // 4,
        name="pack",
        scratch=[pltpu.VMEM((row_count, feat), jnp.bfloat16)] * 2
        + [pltpu.VMEM((1, row_count), jnp.int32)] * 2
        + [pltpu.SemaphoreType.DMA((4,))],
    )
    stay_t, stay_s = stay(teacher_in, route_t), stay(student_in, route_s)
    routes = jnp.concatenate([route_t, route_s], axis=0)
    other_routes = across(routes)
    moved = after(over_planes(sent), stay_t, stay_s, other_routes)
    got = spread(
        call(stack_kernel, [shape((experts - 1) * capacity, 2 * feat)], moved, name="stack")[0]
    )
    w1_t, w2_t = load(teacher_w1[0], teacher_w2[0])
    w1_s, w2_s = load(student_w1[0], student_w2[0])
    (maps,) = call(
        lambda *refs: map_kernel(experts, capacity, *refs),
        [shape(2, experts * capacity, experts * capacity)],
        [routes, other_routes],
        name="maps",
    )
    flat_t_own, flat_own = call(
        lambda *refs: join_kernel(columns, *refs),
        [shape(plane_rows // 2, width)] * 2,
        [stay_t, stay_s, *after(got, w1_t, w1_s, maps)],
        name="join",
    )
    flat_t_other = across(flat_t_own)
    flat_other = across(flat_own)

    send, hidden_own = forward([flat_t_own], w1_t, w2_t, False, "forward_t")
    got_own = across(send)
    send, hidden_other = forward([flat_t_other], w1_t, w2_t, False, "forward_t")
    got_other = across(send)
    kept = keep(hidden_own, hidden_other, w2_t, [], [])
    pieces_t = pair(kept, [got_own, got_other])
    sums_t = collect(*pieces_t)

    flat_own, flat_other = after((flat_own, flat_other), pieces_t[0])
    send, hidden_own, hidden_other, pre_own, pre_other = forward(
        [flat_own, flat_other], w1_s, w2_s, True, "forward_s"
    )
    got = [across(send)]
    *kept, flat_t, hidden_t, slope = keep(
        hidden_own,
        hidden_other,
        w2_s,
        [pre_own, pre_other, flat_own, flat_other],
        [shape(width, plane_rows), shape(hid, plane_rows), shape(plane_rows, hid, dtype=f32)],
    )

    pieces_s = pair(kept, got)
    sums_s = collect(*pieces_s)

    home = call(
        lambda *refs: total_kernel(columns, experts, *refs),
        [shape(2 * capacity, piece)] * experts,
        after(sums_t, hidden_own),
    )
    home = [*over_planes(home[:-1]), home[-1]]
    slots = call(
        lambda *refs: home_kernel(experts, capacity, *refs),
        [shape(2 * capacity, piece)] * experts,
        [maps, *home],
        flops=2 * plane_rows * width * hid,
        name="home",
    )
    teachers = [*over_planes(slots[:-1]), slots[-1]]
    (upstream,) = call(
        lambda *refs: upstream_kernel(columns, experts, loss_scale, *refs),
        [shape(plane_rows, piece)],
        [*sums_s, *teachers],
    )
    def backward(pieces, state, last):
        first = state is None
        places = tuple(pieces)
        operands = [pieces[key] for key in places] + [hidden_t, w2_s]
        in_specs = [VMEM] * len(operands)
        aliases = {}
        if not first:
            operands += [state[1], state[0]]
            in_specs += [VMEM, ANY]
            aliases = {len(operands) - 1: 0}
        outs = [shape(hid, width)]
        scratch = [pltpu.VMEM((len(places), hid, piece), jnp.bfloat16)]
        copies = len(places)
        if last:
            operands += [flat_t, slope]
            in_specs += [VMEM, VMEM]
            outs += [shape(width, hid)]
            out_specs = [ANY, ANY]
            scratch = [pltpu.VMEM((width, hid), jnp.bfloat16)] + scratch
            copies += width // 256
        else:
            outs += [shape(plane_rows, hid, dtype=f32)]
            out_specs = [ANY, VMEM]
        return call(
            lambda *refs: backward_kernel(columns, places, first, last, *refs),
            outs,
            operands,
            out_specs=out_specs,
            in_specs=in_specs,
            scratch=scratch + [pltpu.SemaphoreType.DMA((copies,))],
            aliases=aliases,
        )

    grads = spread(upstream)
    state = backward({(0, 0): upstream, (1, 0): across(upstream)}, None, False)
    grads = after(grads, state[1])
    masks = range(1, columns)
    others = [across(grads[m]) for m in masks]
    state = backward({(0, m): grads[m] for m in masks}, state, False)
    grad_second, grad_first = backward(
        {(1, m): value for m, value in zip(masks, others)}, state, True
    )
    return (grad_first[None], grad_second[None])

def on_device(*arrays):
    _, columns, _, row_count, width, capacity = sizes(arrays[0])
    aligned = columns == 4 and capacity % 16 == 0 and row_count % 128 == 0 and width % (256 * columns) == 0
    return by_kernels(*arrays) if aligned else by_ops(*arrays)


def solution(mesh):
    return jax.shard_map(
        on_device,
        mesh=mesh,
        in_specs=(
            P("dp", None),
            P("dp", None),
            P("dp", None),
            P("dp", None),
            P("dp", None, "expert"),
            P("dp", "expert", None),
            P("dp", None, "expert"),
            P("dp", "expert", None),
        ),
        out_specs=(P("dp", None, "expert"), P("dp", "expert", None)),
        check_vma=False,
    )
```

time: 291 us -> 88.2 us (0.30)
  waiting for transfers between devices: 157 us -> 34 us
  blocking collectives: 49.8 us -> 0 us
  matrix products: 26.4 us -> 0 us
  Pallas kernels: 0 us -> 16.6 us
  between operations: 14.2 us -> 0.92 us
  starting transfers between devices: 15 us -> 28.2 us
  other arithmetic: 12.1 us -> 0.68 us
  local copies, waits for them, and re-layouts: 15 us -> 7.44 us
    all_to_all x3 -> x0, waiting for transfers between devices: 82.5 us -> none  [the longest x1 31.7 us: on_device(): lax.all_to_all(teacher_part.reshape(groups, capacity, model_width), 'dp',...]
    psum x1 -> x0, waiting for transfers between devices: 68.9 us -> none  [on_device(): lax.psum((local_teacher, local_student), 'expert')]
    all_to_all x2 -> x0, blocking collectives: 49.8 us -> none  [the longest x1 25.4 us: on_device(): lax.all_to_all(grad_buffer.reshape(groups, capacity // 2, model_width), '...]
    ppermute x2 -> x31, starting transfers between devices: 0.01 us -> 28.2 us  [partner(): lax.ppermute(value, axis, [(i, i ^ mask) for i in range(lax.axis_size(axi...]
    ppermute x2 -> x31, waiting for transfers between devices: 6.03 us -> 34 us  [partner(): lax.ppermute(value, axis, [(i, i ^ mask) for i in range(lax.axis_size(axi...]
    dot_general x8 -> x0, matrix products: 26.4 us -> none  [the longest x1 5.83 us: on_device(): jnp.dot(teacher_hidden, teacher_w2[0], preferred_element_type=jnp.float32)]
    pallas_call x0 -> x21, Pallas kernels: none -> 16.6 us  [call(): pl.pallas_call(kernel, name=name, out_shape=outs, in_specs=in_specs or [V...]
    all_to_all x3 -> x0, starting transfers between devices: 14.9 us -> none  [the longest x1 6.33 us: on_device(): lax.all_to_all(student_buffer.reshape(groups, capacity // 2, model_width)...]
  transfers between devices with their start and end apart: 6 -> 31, of which waited for: 6 -> 13; matrix products, arithmetic and copies ran while one was open for 5% -> 1% of each run, Pallas kernels for 0% -> 13%
where the time goes in v1:
time: 88.2 us; the launch traced here: 87.9 us
  waiting for transfers between devices  34 us (39%)
  starting transfers between devices  28.2 us (32%)
  Pallas kernels  16.6 us (19%)
  local copies, waits for them, and re-layouts  7.44 us (8%)
  between operations  0.92 us (1%)
    ppermute x31, waiting for transfers between devices, partner(): lax.ppermute(value, axis, [(i, i ^ mask) for i in range(lax.axis_size(axi...  34 us
    ppermute x31, starting transfers between devices, partner(): lax.ppermute(value, axis, [(i, i ^ mask) for i in range(lax.axis_size(axi...  28.2 us
    pallas_call x21, Pallas kernels, call(): pl.pallas_call(kernel, name=name, out_shape=outs, in_specs=in_specs or [V...  16.6 us
    unnamed x16, local copies, waits for them, and re-layouts  7.44 us
  transfers between devices with their start and end apart: 31, of which 13 were waited for; matrix products, arithmetic and copies ran while one was open for 1% of the time, Pallas kernels for 13%

profile of v1, /device:TPU:0, one launch (start us, length us, event | category | flops | bytes accessed | tf_op | source)
XLA Modules:
  0.0 87.9 jit_solution(2543041721948305618)
XLA Ops:
  0.6 2.2 %pack.1 = (bf16[48,1024]{1,0:T(8,128)(2,1)}, bf16[48,1024]{1,0:T(8,128)(2,1)}, bf16[48,1024]{1,0:T(8,128)(2,1)}) custom-call(bf16[128,2048]{1,0:T(8,128)(2,1)} %refs_0_.5, bf16[128,2048]{1,0:T(8,128)(2,1)} %refs_1_.1, s32[1,128]{1,0:T(1,128)} %bitcast.12, s32[1,128]{1,0:T(1,128)} %bitcast.15), custom_call_target="tpu_custom_call" | custom-call | tf_op jit(solution)/shard_map/pack/pallas_call | solution.py:168
  2.9 5.1 %collective-permute-start = (bf16[48,1024]{1,0:T(8,128)(2,1)}, bf16[48,1024]{1,0:T(8,128)(2,1)S(1)}, u32[]{:S(2)}, u32[]{:S(2)}) collective-permute-start(bf16[48,1024]{1,0:T(8,128)(2,1)} %get-tuple-element.65), channel_id=1, source_target_pairs={{0,24},{4,28},{8,16},{12,20},{16,8},{20,12},{24,0},{28,4},{1,25},{... | collective-permute-start | bytes 294920 | tf_op jit(solution)/shard_map/ppermute | solution.py:15
  8.0 0.6 collective-permute-start.2
  8.6 0.7 pad_add_fusion.refs_0_
  9.3 1.0 %copy-done = bf16[128,2048]{1,0:T(8,128)(2,1)S(1)} copy-done((bf16[128,2048]{1,0:T(8,128)(2,1)S(1)}, bf16[128,2048]{1,0:T(8,128)(2,1)}, u32[]{:S(2)}) %copy-start) | copy-done | bytes 524312
  10.4 0.7 copy-done.6
  11.0 0.3 stay.2.refs_0_
  11.4 0.6 copy-done.7
  12.0 0.3 stay.3.refs_1_
  12.4 4.1 %collective-permute-done.1.refs_1_ = bf16[48,1024]{1,0:T(8,128)(2,1)S(1)} collective-permute-done((bf16[48,1024]{1,0:T(8,128)(2,1)}, bf16[48,1024]{1,0:T(8,128)(2,1)S(1)}, u32[]{:S(2)}, u32[]{:S(2)}) %collective-permute-start.1) | collective-permute-done | bytes 98336 | tf_op jit(solution)/shard_map/ppermute | solution.py:15
  16.5 2.5 %collective-permute-start.6 = (bf16[144,1024]{1,0:T(8,128)(2,1)S(1)}, bf16[144,1024]{1,0:T(8,128)(2,1)S(1)}, u32[]{:S(2)}, u32[]{:S(2)}) collective-permute-start(bf16[144,1024]{1,0:T(8,128)(2,1)S(1)} %stack.1.refs_2_), channel_id=1, source_target_pairs={{0,3},{1,2},{2,1},{3,0},{4,7},{5,6},{6,5},{7,4},{8,11},{9,10},{10,... | collective-permute-start | bytes 884744 | tf_op jit(solution)/shard_map/ppermute | solution.py:15
  19.0 0.5 collective-permute-start.5
  19.5 0.5 collective-permute-start.4
  20.1 1.6 %copy-done.2 = bf16[1,2048,512]{2,1,0:T(8,128)(2,1)S(1)} copy-done((bf16[1,2048,512]{2,1,0:T(8,128)(2,1)S(1)}, bf16[1,2048,512]{2,1,0:T(8,128)(2,1)}, u32[]{:S(2)}) %copy-start.2) | copy-done | bytes 2097176
  21.6 1.6 %copy-done.3 = bf16[1,512,2048]{2,1,0:T(8,128)(2,1)S(1)} copy-done((bf16[1,512,2048]{2,1,0:T(8,128)(2,1)S(1)}, bf16[1,512,2048]{2,1,0:T(8,128)(2,1)}, u32[]{:S(2)}) %copy-start.3) | copy-done | bytes 2097176
  23.2 0.3 load.2
  23.5 1.3 %copy-done.4 = bf16[1,2048,512]{2,1,0:T(8,128)(2,1)S(1)} copy-done((bf16[1,2048,512]{2,1,0:T(8,128)(2,1)S(1)}, bf16[1,2048,512]{2,1,0:T(8,128)(2,1)}, u32[]{:S(2)}) %copy-start.4) | copy-done | bytes 2097176
  24.8 0.6 copy-done.5
  25.5 0.3 load.3
  25.8 0.4 maps.1.refs_0_
  26.1 1.3 %collective-permute-done.6.refs_5_ = bf16[144,1024]{1,0:T(8,128)(2,1)S(1)} collective-permute-done((bf16[144,1024]{1,0:T(8,128)(2,1)S(1)}, bf16[144,1024]{1,0:T(8,128)(2,1)S(1)}, u32[]{:S(2)}, u32[]{:S(2)}) %collective-permute-start.6) | collective-permute-done | bytes 294944 | tf_op jit(solution)/shard_map/ppermute | solution.py:15
  27.4 4.4 %collective-permute-done.5.refs_4_ = bf16[144,1024]{1,0:T(8,128)(2,1)S(1)} collective-permute-done((bf16[144,1024]{1,0:T(8,128)(2,1)S(1)}, bf16[144,1024]{1,0:T(8,128)(2,1)S(1)}, u32[]{:S(2)}, u32[]{:S(2)}) %collective-permute-start.5) | collective-permute-done | bytes 294944 | tf_op jit(solution)/shard_map/ppermute | solution.py:15
  31.8 0.1 collective-permute-done.4.refs_3_
  31.9 0.1 join.1
  32.1 0.1 collective-permute-start.8
  32.1 0.5 collective-permute-start.7
  32.6 0.9 %forward_t.2 = (bf16[1,4,192,256]{3,2,1,0:T(8,128)(2,1)S(1)}, bf16[192,512]{1,0:T(8,128)(2,1)S(1)}) custom-call(bf16[192,2048]{1,0:T(8,128)(2,1)S(1)} %get-tuple-element.78.refs_0_, bf16[2048,512]{1,0:T(8,128)(2,1)S(1)} %get-tuple-element.71.refs_1_, bf16[512,2048]{1,0:T(8,128)(2,1)S(1)} %get-tuple-element.79.refs_2_), custom_call_target="tpu_custom_call" | custom-call | tf_op jit(solution)/shard_map/forward_t/pallas_call | solution.py:168
  33.6 0.1 collective-permute-start.9
  33.7 0.7 collective-permute-done.8.refs_0_
  34.4 0.9 %forward_t.3 = (bf16[1,4,192,256]{3,2,1,0:T(8,128)(2,1)S(1)}, bf16[192,512]{1,0:T(8,128)(2,1)S(1)}) custom-call(bf16[192,2048]{1,0:T(8,128)(2,1)S(1)} %collective-permute-done.8.refs_0_, bf16[2048,512]{1,0:T(8,128)(2,1)S(1)} %get-tuple-element.71.refs_1_, bf16[512,2048]{1,0:T(8,128)(2,1)S(1)} %get-tuple-element.79.refs_2_), custom_call_target="tpu_custom_call" | custom-call | tf_op jit(solution)/shard_map/forward_t/pallas_call | solution.py:168
  35.3 0.2 collective-permute-start.10
  35.5 0.6 keep_t.1
  36.2 1.0 %collective-permute-done.10.refs_3_ = bf16[1,4,192,256]{3,2,1,0:T(8,128)(2,1)S(1)} collective-permute-done((bf16[1,4,192,256]{3,2,1,0:T(8,128)(2,1)S(1)}, bf16[1,4,192,256]{3,2,1,0:T(8,128)(2,1)S(1)}, u32[]{:S(2)}, u32[]{:S(2)}) %collective-permute-start.10) | collective-permute-done | bytes 393248 | tf_op jit(solution)/shard_map/ppermute | solution.py:15
  37.1 0.2 pair.2
  37.3 1.6 %collective-permute-start.15 = (bf16[384,256]{1,0:T(8,128)(2,1)S(1)}, bf16[384,256]{1,0:T(8,128)(2,1)S(1)}, u32[]{:S(2)}, u32[]{:S(2)}) collective-permute-start(bf16[384,256]{1,0:T(8,128)(2,1)S(1)} %get-tuple-element.101), channel_id=1, source_target_pairs={{0,1},{1,0},{2,3},{3,2},{4,5},{5,4},{6,7},{7,6},{8,9},{9,8},{10,11... | collective-permute-start | bytes 589832 | tf_op jit(solution)/shard_map/ppermute | solution.py:15
  38.9 0.7 collective-permute-start.16
  39.6 1.3 %collective-permute-start.17 = (bf16[384,256]{1,0:T(8,128)(2,1)S(1)}, bf16[384,256]{1,0:T(8,128)(2,1)S(1)}, u32[]{:S(2)}, u32[]{:S(2)}) collective-permute-start(bf16[384,256]{1,0:T(8,128)(2,1)S(1)} %get-tuple-element.103), channel_id=1, source_target_pairs={{0,3},{1,2},{2,1},{3,0},{4,7},{5,6},{6,5},{7,4},{8,11},{9,10},{10,... | collective-permute-start | bytes 589832 | tf_op jit(solution)/shard_map/ppermute | solution.py:15
  40.9 1.7 %forward_s.1 = (bf16[2,4,192,256]{3,2,1,0:T(8,128)(2,1)S(1)}, bf16[192,512]{1,0:T(8,128)(2,1)S(1)}, bf16[192,512]{1,0:T(8,128)(2,1)S(1)}, f32[192,512]{1,0:T(8,128)S(1)}, f32[192,512]{1,0:T(8,128)S(1)}) custom-call(bf16[192,2048]{1,0:T(8,128)(2,1)S(1)} %get-tuple-element.87.refs_0_.refs_5_, bf16[192,2048]{1,0:T(8,128)(2,1)S(1)} %collective-permute-done.7.refs_1_.refs_6_, ...), custom_call_target="tpu_custom_call" | custom-call | tf_op jit(solution)/shard_map/forward_s/pallas_call | solution.py:168
  42.6 0.1 collective-permute-start.11
  42.7 2.4 %collective-permute-done.15.refs_1_ = bf16[384,256]{1,0:T(8,128)(2,1)S(1)} collective-permute-done((bf16[384,256]{1,0:T(8,128)(2,1)S(1)}, bf16[384,256]{1,0:T(8,128)(2,1)S(1)}, u32[]{:S(2)}, u32[]{:S(2)}) %collective-permute-start.15) | collective-permute-done | bytes 196640 | tf_op jit(solution)/shard_map/ppermute | solution.py:15
  45.1 4.6 %collective-permute-done.16.refs_2_ = bf16[384,256]{1,0:T(8,128)(2,1)S(1)} collective-permute-done((bf16[384,256]{1,0:T(8,128)(2,1)S(1)}, bf16[384,256]{1,0:T(8,128)(2,1)S(1)}, u32[]{:S(2)}, u32[]{:S(2)}) %collective-permute-start.16) | collective-permute-done | bytes 196640 | tf_op jit(solution)/shard_map/ppermute | solution.py:15
  49.8 0.1 shard_map.95
  49.8 2.2 %collective-permute-start.18 = (bf16[96,256]{1,0:T(8,128)(2,1)S(1)}, bf16[96,256]{1,0:T(8,128)(2,1)S(1)}, u32[]{:S(2)}, u32[]{:S(2)}) collective-permute-start(bf16[96,256]{1,0:T(8,128)(2,1)S(1)} %get-tuple-element.108), channel_id=1, source_target_pairs={{0,24},{4,28},{8,16},{12,20},{16,8},{20,12},{24,0},{28,4},{1,25},{... | collective-permute-start | bytes 147464 | tf_op jit(solution)/shard_map/ppermute | solution.py:15
  52.0 2.3 %collective-permute-start.20 = (bf16[96,256]{1,0:T(8,128)(2,1)S(1)}, bf16[96,256]{1,0:T(8,128)(2,1)S(1)}, u32[]{:S(2)}, u32[]{:S(2)}) collective-permute-start(bf16[96,256]{1,0:T(8,128)(2,1)S(1)} %get-tuple-element.110), channel_id=1, source_target_pairs={{0,8},{4,12},{8,0},{12,4},{16,24},{20,28},{24,16},{28,20},{1,9},{5... | collective-permute-start | bytes 147464 | tf_op jit(solution)/shard_map/ppermute | solution.py:15
  54.3 1.4 %keep_s.1 = (bf16[4,192,256]{2,1,0:T(8,128)(2,1)S(1)}, bf16[4,192,256]{2,1,0:T(8,128)(2,1)S(1)}, bf16[2048,384]{1,0:T(8,128)(2,1)S(1)}, bf16[512,384]{1,0:T(8,128)(2,1)S(1)}, f32[384,512]{1,0:T(8,128)S(1)}) custom-call(bf16[192,512]{1,0:T(8,128)(2,1)S(1)} %get-tuple-element.90.refs_0_, bf16[192,512]{1,0:T(8,128)(2,1)S(1)} %get-tuple-element.91.refs_1_, ...), custom_call_target="tpu_custom_call" | custom-call | flops 6442450944 | tf_op jit(solution)/shard_map/keep_s/pallas_call | solution.py:168
  55.7 0.2 pair.3
  55.9 0.6 collective-permute-start.12
  56.5 1.4 %collective-permute-start.13 = (bf16[384,256]{1,0:T(8,128)(2,1)S(1)}, bf16[384,256]{1,0:T(8,128)(2,1)S(1)}, u32[]{:S(2)}, u32[]{:S(2)}) collective-permute-start(bf16[384,256]{1,0:T(8,128)(2,1)S(1)} %get-tuple-element.99), channel_id=1, source_target_pairs={{0,2},{1,3},{2,0},{3,1},{4,6},{5,7},{6,4},{7,5},{8,10},{9,11},{10,... | collective-permute-start | bytes 589832 | tf_op jit(solution)/shard_map/ppermute | solution.py:15
  57.9 1.5 %collective-permute-start.14 = (bf16[384,256]{1,0:T(8,128)(2,1)S(1)}, bf16[384,256]{1,0:T(8,128)(2,1)S(1)}, u32[]{:S(2)}, u32[]{:S(2)}) collective-permute-start(bf16[384,256]{1,0:T(8,128)(2,1)S(1)} %get-tuple-element.100), channel_id=1, source_target_pairs={{0,3},{1,2},{2,1},{3,0},{4,7},{5,6},{6,5},{7,4},{8,11},{9,10},{10,... | collective-permute-start | bytes 589832 | tf_op jit(solution)/shard_map/ppermute | solution.py:15
  59.4 0.2 home.1
  59.6 2.2 %collective-permute-start.21 = (bf16[96,256]{1,0:T(8,128)(2,1)S(1)}, bf16[96,256]{1,0:T(8,128)(2,1)S(1)}, u32[]{:S(2)}, u32[]{:S(2)}) collective-permute-start(bf16[96,256]{1,0:T(8,128)(2,1)S(1)} %get-tuple-element.112), channel_id=1, source_target_pairs={{0,24},{4,28},{8,16},{12,20},{16,8},{20,12},{24,0},{28,4},{1,25},{... | collective-permute-start | bytes 147464 | tf_op jit(solution)/shard_map/ppermute | solution.py:15
  61.8 4.0 %collective-permute-done.21.refs_4_ = bf16[96,256]{1,0:T(8,128)(2,1)S(1)} collective-permute-done((bf16[96,256]{1,0:T(8,128)(2,1)S(1)}, bf16[96,256]{1,0:T(8,128)(2,1)S(1)}, u32[]{:S(2)}, u32[]{:S(2)}) %collective-permute-start.21) | collective-permute-done | bytes 49184 | tf_op jit(solution)/shard_map/ppermute | solution.py:15
  65.8 1.0 %collective-permute-done.22.refs_5_ = bf16[96,256]{1,0:T(8,128)(2,1)S(1)} collective-permute-done((bf16[96,256]{1,0:T(8,128)(2,1)S(1)}, bf16[96,256]{1,0:T(8,128)(2,1)S(1)}, u32[]{:S(2)}, u32[]{:S(2)}) %collective-permute-start.22) | collective-permute-done | bytes 49184 | tf_op jit(solution)/shard_map/ppermute | solution.py:15
  66.8 3.0 %collective-permute-done.23.refs_6_ = bf16[96,256]{1,0:T(8,128)(2,1)S(1)} collective-permute-done((bf16[96,256]{1,0:T(8,128)(2,1)S(1)}, bf16[96,256]{1,0:T(8,128)(2,1)S(1)}, u32[]{:S(2)}, u32[]{:S(2)}) %collective-permute-start.23) | collective-permute-done | bytes 49184 | tf_op jit(solution)/shard_map/ppermute | solution.py:15
  69.9 0.1 shard_map.96.refs_0_
  70.1 1.6 %collective-permute-start.26 = (bf16[384,256]{1,0:T(8,128)(2,1)S(1)}, bf16[384,256]{1,0:T(8,128)(2,1)S(1)}, u32[]{:S(2)}, u32[]{:S(2)}) collective-permute-start(bf16[384,256]{1,0:T(8,128)(2,1)S(1)} %shard_map.96.refs_0_), channel_id=1, source_target_pairs={{0,3},{1,2},{2,1},{3,0},{4,7},{5,6},{6,5},{7,4},{8,11},{9,10},{10,... | collective-permute-start | bytes 589832 | tf_op jit(solution)/shard_map/ppermute | solution.py:15
  71.7 0.7 collective-permute-start.25
  72.4 1.2 %collective-permute-start.24 = (bf16[384,256]{1,0:T(8,128)(2,1)S(1)}, bf16[384,256]{1,0:T(8,128)(2,1)S(1)}, u32[]{:S(2)}, u32[]{:S(2)}) collective-permute-start(bf16[384,256]{1,0:T(8,128)(2,1)S(1)} %shard_map.96.refs_0_), channel_id=1, source_target_pairs={{0,1},{1,0},{2,3},{3,2},{4,5},{5,4},{6,7},{7,6},{8,9},{9,8},{10,11... | collective-permute-start | bytes 589832 | tf_op jit(solution)/shard_map/ppermute | solution.py:15
  73.6 1.5 %shard_map.97 = (bf16[512,2048]{1,0:T(8,128)(2,1)}, f32[384,512]{1,0:T(8,128)S(1)}) custom-call(bf16[384,256]{1,0:T(8,128)(2,1)S(1)} %shard_map.96.refs_0_, bf16[384,256]{1,0:T(8,128)(2,1)S(1)} %collective-permute-done.27.refs_1_, bf16[512,384]{1,0:T(8,128)(2,1)S(1)} %get-tuple-element.116.refs_2_.refs_3_, ...), custom_call_target="tpu_custom_call" | custom-call | tf_op jit(solution)/shard_map/pallas_call | solution.py:168
  75.1 3.7 %collective-permute-done.26.refs_2_ = bf16[384,256]{1,0:T(8,128)(2,1)S(1)} collective-permute-done((bf16[384,256]{1,0:T(8,128)(2,1)S(1)}, bf16[384,256]{1,0:T(8,128)(2,1)S(1)}, u32[]{:S(2)}, u32[]{:S(2)}) %collective-permute-start.26) | collective-permute-done | bytes 196640 | tf_op jit(solution)/shard_map/ppermute | solution.py:15
  78.8 3.7 %collective-permute-done.25.refs_1_ = bf16[384,256]{1,0:T(8,128)(2,1)S(1)} collective-permute-done((bf16[384,256]{1,0:T(8,128)(2,1)S(1)}, bf16[384,256]{1,0:T(8,128)(2,1)S(1)}, u32[]{:S(2)}, u32[]{:S(2)}) %collective-permute-start.25) | collective-permute-done | bytes 196640 | tf_op jit(solution)/shard_map/ppermute | solution.py:15
  82.6 0.5 collective-permute-start.29
  83.1 1.7 %shard_map.98 = (bf16[512,2048]{1,0:T(8,128)(2,1)}, f32[384,512]{1,0:T(8,128)S(1)}) custom-call(bf16[384,256]{1,0:T(8,128)(2,1)S(1)} %collective-permute-done.24.refs_0_, bf16[384,256]{1,0:T(8,128)(2,1)S(1)} %collective-permute-done.25.refs_1_, bf16[384,256]{1,0:T(8,128)(2,1)S(1)} %collective-permute-done.26.refs_2_, ...), custom_call_target="tpu_custom_call", output_to_operand_aliasing={{0}: (6, {})} | custom-call | tf_op jit(solution)/shard_map/pallas_call | solution.py:168
  84.8 3.0 %shard_map.99 = (bf16[512,2048]{1,0:T(8,128)(2,1)}, bf16[2048,512]{1,0:T(8,128)(2,1)}) custom-call(bf16[384,256]{1,0:T(8,128)(2,1)S(1)} %collective-permute-done.28.refs_0_, bf16[384,256]{1,0:T(8,128)(2,1)S(1)} %collective-permute-done.29.refs_1_, bf16[384,256]{1,0:T(8,128)(2,1)S(1)} %collective-permute-done.30.refs_2_, ...), custom_call_target="tpu_custom_call", output_to_operand_aliasing={{0}: (6, {})} | custom-call | tf_op jit(solution)/shard_map/pallas_call | solution.py:168
  (36 shorter events, 0.2 us)
Async XLA Ops:
  0.6 10.7 %copy-start.1 = (bf16[128,2048]{1,0:T(8,128)(2,1)S(1)}, bf16[128,2048]{1,0:T(8,128)(2,1)}, u32[]{:S(2)}) copy-start(bf16[128,2048]{1,0:T(8,128)(2,1)} %refs_1_.1) | copy-start | bytes 1572868
  2.9 9.5 %collective-permute-start = (bf16[48,1024]{1,0:T(8,128)(2,1)}, bf16[48,1024]{1,0:T(8,128)(2,1)S(1)}, u32[]{:S(2)}, u32[]{:S(2)}) collective-permute-start(bf16[48,1024]{1,0:T(8,128)(2,1)} %get-tuple-element.65), channel_id=1, source_target_pairs={{0,24},{4,28},{8,16},{12,20},{16,8},{20,12},{24,0},{28,4},{1,25},{... | collective-permute-start | bytes 294920 | tf_op jit(solution)/shard_map/ppermute | solution.py:15
  8.0 8.5 %collective-permute-start.1 = (bf16[48,1024]{1,0:T(8,128)(2,1)}, bf16[48,1024]{1,0:T(8,128)(2,1)S(1)}, u32[]{:S(2)}, u32[]{:S(2)}) collective-permute-start(bf16[48,1024]{1,0:T(8,128)(2,1)} %get-tuple-element.66), channel_id=1, source_target_pairs={{0,16},{4,20},{8,24},{12,28},{16,0},{20,4},{24,8},{28,12},{1,17},{... | collective-permute-start | bytes 294920 | tf_op jit(solution)/shard_map/ppermute | solution.py:15
  8.0 8.5 %collective-permute-start.2 = (bf16[48,1024]{1,0:T(8,128)(2,1)}, bf16[48,1024]{1,0:T(8,128)(2,1)S(1)}, u32[]{:S(2)}, u32[]{:S(2)}) collective-permute-start(bf16[48,1024]{1,0:T(8,128)(2,1)} %get-tuple-element.67), channel_id=1, source_target_pairs={{0,8},{4,12},{8,0},{12,4},{16,24},{20,28},{24,16},{28,20},{1,9},{5... | collective-permute-start | bytes 294920 | tf_op jit(solution)/shard_map/ppermute | solution.py:15
  9.3 3.1 %collective-permute-start.3 = (s32[2,128]{1,0:T(2,128)S(1)}, s32[2,128]{1,0:T(2,128)S(1)}, u32[]{:S(2)}, u32[]{:S(2)}) collective-permute-start(s32[2,128]{1,0:T(2,128)S(1)} %pad_add_fusion.refs_0_), channel_id=1, source_target_pairs={{0,4},{4,0},{8,12},{12,8},{16,20},{20,16},{24,28},{28,24},{1,5},{5... | collective-permute-start | bytes 3080 | tf_op jit(solution)/shard_map/ppermute | solution.py:15
  9.3 1.0 %copy-start = (bf16[128,2048]{1,0:T(8,128)(2,1)S(1)}, bf16[128,2048]{1,0:T(8,128)(2,1)}, u32[]{:S(2)}) copy-start(bf16[128,2048]{1,0:T(8,128)(2,1)} %refs_0_.5) | copy-start | bytes 1572868
  10.4 0.7 copy-start.6
  11.4 0.7 copy-start.7
  16.5 11.0 %collective-permute-start.6 = (bf16[144,1024]{1,0:T(8,128)(2,1)S(1)}, bf16[144,1024]{1,0:T(8,128)(2,1)S(1)}, u32[]{:S(2)}, u32[]{:S(2)}) collective-permute-start(bf16[144,1024]{1,0:T(8,128)(2,1)S(1)} %stack.1.refs_2_), channel_id=1, source_target_pairs={{0,3},{1,2},{2,1},{3,0},{4,7},{5,6},{6,5},{7,4},{8,11},{9,10},{10,... | collective-permute-start | bytes 884744 | tf_op jit(solution)/shard_map/ppermute | solution.py:15
  19.0 12.8 %collective-permute-start.5 = (bf16[144,1024]{1,0:T(8,128)(2,1)S(1)}, bf16[144,1024]{1,0:T(8,128)(2,1)S(1)}, u32[]{:S(2)}, u32[]{:S(2)}) collective-permute-start(bf16[144,1024]{1,0:T(8,128)(2,1)S(1)} %stack.1.refs_2_), channel_id=1, source_target_pairs={{0,2},{1,3},{2,0},{3,1},{4,6},{5,7},{6,4},{7,5},{8,10},{9,11},{10,... | collective-permute-start | bytes 884744 | tf_op jit(solution)/shard_map/ppermute | solution.py:15
  19.5 12.4 %collective-permute-start.4 = (bf16[144,1024]{1,0:T(8,128)(2,1)S(1)}, bf16[144,1024]{1,0:T(8,128)(2,1)S(1)}, u32[]{:S(2)}, u32[]{:S(2)}) collective-permute-start(bf16[144,1024]{1,0:T(8,128)(2,1)S(1)} %stack.1.refs_2_), channel_id=1, source_target_pairs={{0,1},{1,0},{2,3},{3,2},{4,5},{5,4},{6,7},{7,6},{8,9},{9,8},{10,11... | collective-permute-start | bytes 884744 | tf_op jit(solution)/shard_map/ppermute | solution.py:15
  20.0 1.6 %copy-start.2 = (bf16[1,2048,512]{2,1,0:T(8,128)(2,1)S(1)}, bf16[1,2048,512]{2,1,0:T(8,128)(2,1)}, u32[]{:S(2)}) copy-start(bf16[1,2048,512]{2,1,0:T(8,128)(2,1)} %param.12) | copy-start | bytes 6291460
  21.6 1.6 %copy-start.3 = (bf16[1,512,2048]{2,1,0:T(8,128)(2,1)S(1)}, bf16[1,512,2048]{2,1,0:T(8,128)(2,1)}, u32[]{:S(2)}) copy-start(bf16[1,512,2048]{2,1,0:T(8,128)(2,1)} %param.13) | copy-start | bytes 6291460
  23.2 1.6 %copy-start.4 = (bf16[1,2048,512]{2,1,0:T(8,128)(2,1)S(1)}, bf16[1,2048,512]{2,1,0:T(8,128)(2,1)}, u32[]{:S(2)}) copy-start(bf16[1,2048,512]{2,1,0:T(8,128)(2,1)} %param.14) | copy-start | bytes 6291460
  23.2 2.2 %copy-start.5 = (bf16[1,512,2048]{2,1,0:T(8,128)(2,1)S(1)}, bf16[1,512,2048]{2,1,0:T(8,128)(2,1)}, u32[]{:S(2)}) copy-start(bf16[1,512,2048]{2,1,0:T(8,128)(2,1)} %param.15) | copy-start | bytes 6291460
  32.1 2.4 %collective-permute-start.8 = (bf16[192,2048]{1,0:T(8,128)(2,1)S(1)}, bf16[192,2048]{1,0:T(8,128)(2,1)S(1)}, u32[]{:S(2)}, u32[]{:S(2)}) collective-permute-start(bf16[192,2048]{1,0:T(8,128)(2,1)S(1)} %get-tuple-element.78.refs_0_), channel_id=1, source_target_pairs={{0,4},{4,0},{8,12},{12,8},{16,20},{20,16},{24,28},{28,24},{1,5},{5... | collective-permute-start | bytes 2359304 | tf_op jit(solution)/shard_map/ppermute | solution.py:15
  32.1 8.7 %collective-permute-start.7 = (bf16[192,2048]{1,0:T(8,128)(2,1)S(1)}, bf16[192,2048]{1,0:T(8,128)(2,1)S(1)}, u32[]{:S(2)}, u32[]{:S(2)}) collective-permute-start(bf16[192,2048]{1,0:T(8,128)(2,1)S(1)} %get-tuple-element.87.refs_0_.refs_5_), channel_id=1, source_target_pairs={{0,4},{4,0},{8,12},{12,8},{16,20},{20,16},{24,28},{28,24},{1,5},{5... | collective-permute-start | bytes 2359304 | tf_op jit(solution)/shard_map/ppermute | solution.py:15
  33.6 2.6 %collective-permute-start.9 = (bf16[1,4,192,256]{3,2,1,0:T(8,128)(2,1)S(1)}, bf16[1,4,192,256]{3,2,1,0:T(8,128)(2,1)S(1)}, u32[]{:S(2)}, u32[]{:S(2)}) collective-permute-start(bf16[1,4,192,256]{3,2,1,0:T(8,128)(2,1)S(1)} %get-tuple-element.84), channel_id=1, source_target_pairs={{0,4},{4,0},{8,12},{12,8},{16,20},{20,16},{24,28},{28,24},{1,5},{5... | collective-permute-start | bytes 1179656 | tf_op jit(solution)/shard_map/ppermute | solution.py:15
  35.3 1.8 %collective-permute-start.10 = (bf16[1,4,192,256]{3,2,1,0:T(8,128)(2,1)S(1)}, bf16[1,4,192,256]{3,2,1,0:T(8,128)(2,1)S(1)}, u32[]{:S(2)}, u32[]{:S(2)}) collective-permute-start(bf16[1,4,192,256]{3,2,1,0:T(8,128)(2,1)S(1)} %get-tuple-element.85), channel_id=1, source_target_pairs={{0,4},{4,0},{8,12},{12,8},{16,20},{20,16},{24,28},{28,24},{1,5},{5... | collective-permute-start | bytes 1179656 | tf_op jit(solution)/shard_map/ppermute | solution.py:15
  37.3 7.8 %collective-permute-start.15 = (bf16[384,256]{1,0:T(8,128)(2,1)S(1)}, bf16[384,256]{1,0:T(8,128)(2,1)S(1)}, u32[]{:S(2)}, u32[]{:S(2)}) collective-permute-start(bf16[384,256]{1,0:T(8,128)(2,1)S(1)} %get-tuple-element.101), channel_id=1, source_target_pairs={{0,1},{1,0},{2,3},{3,2},{4,5},{5,4},{6,7},{7,6},{8,9},{9,8},{10,11... | collective-permute-start | bytes 589832 | tf_op jit(solution)/shard_map/ppermute | solution.py:15
  38.9 10.9 %collective-permute-start.16 = (bf16[384,256]{1,0:T(8,128)(2,1)S(1)}, bf16[384,256]{1,0:T(8,128)(2,1)S(1)}, u32[]{:S(2)}, u32[]{:S(2)}) collective-permute-start(bf16[384,256]{1,0:T(8,128)(2,1)S(1)} %get-tuple-element.102), channel_id=1, source_target_pairs={{0,2},{1,3},{2,0},{3,1},{4,6},{5,7},{6,4},{7,5},{8,10},{9,11},{10,... | collective-permute-start | bytes 589832 | tf_op jit(solution)/shard_map/ppermute | solution.py:15
  39.6 10.2 %collective-permute-start.17 = (bf16[384,256]{1,0:T(8,128)(2,1)S(1)}, bf16[384,256]{1,0:T(8,128)(2,1)S(1)}, u32[]{:S(2)}, u32[]{:S(2)}) collective-permute-start(bf16[384,256]{1,0:T(8,128)(2,1)S(1)} %get-tuple-element.103), channel_id=1, source_target_pairs={{0,3},{1,2},{2,1},{3,0},{4,7},{5,6},{6,5},{7,4},{8,11},{9,10},{10,... | collective-permute-start | bytes 589832 | tf_op jit(solution)/shard_map/ppermute | solution.py:15
  42.6 13.1 %collective-permute-start.11 = (bf16[2,4,192,256]{3,2,1,0:T(8,128)(2,1)S(1)}, bf16[2,4,192,256]{3,2,1,0:T(8,128)(2,1)S(1)}, u32[]{:S(2)}, u32[]{:S(2)}) collective-permute-start(bf16[2,4,192,256]{3,2,1,0:T(8,128)(2,1)S(1)} %get-tuple-element.96), channel_id=1, source_target_pairs={{0,4},{4,0},{8,12},{12,8},{16,20},{20,16},{24,28},{28,24},{1,5},{5... | collective-permute-start | bytes 2359304 | tf_op jit(solution)/shard_map/ppermute | solution.py:15
  49.8 8.1 %collective-permute-start.18 = (bf16[96,256]{1,0:T(8,128)(2,1)S(1)}, bf16[96,256]{1,0:T(8,128)(2,1)S(1)}, u32[]{:S(2)}, u32[]{:S(2)}) collective-permute-start(bf16[96,256]{1,0:T(8,128)(2,1)S(1)} %get-tuple-element.108), channel_id=1, source_target_pairs={{0,24},{4,28},{8,16},{12,20},{16,8},{20,12},{24,0},{28,4},{1,25},{... | collective-permute-start | bytes 147464 | tf_op jit(solution)/shard_map/ppermute | solution.py:15
  52.0 7.4 %collective-permute-start.19 = (bf16[96,256]{1,0:T(8,128)(2,1)S(1)}, bf16[96,256]{1,0:T(8,128)(2,1)S(1)}, u32[]{:S(2)}, u32[]{:S(2)}) collective-permute-start(bf16[96,256]{1,0:T(8,128)(2,1)S(1)} %get-tuple-element.109), channel_id=1, source_target_pairs={{0,16},{4,20},{8,24},{12,28},{16,0},{20,4},{24,8},{28,12},{1,17},{... | collective-permute-start | bytes 147464 | tf_op jit(solution)/shard_map/ppermute | solution.py:15
  52.0 7.4 %collective-permute-start.20 = (bf16[96,256]{1,0:T(8,128)(2,1)S(1)}, bf16[96,256]{1,0:T(8,128)(2,1)S(1)}, u32[]{:S(2)}, u32[]{:S(2)}) collective-permute-start(bf16[96,256]{1,0:T(8,128)(2,1)S(1)} %get-tuple-element.110), channel_id=1, source_target_pairs={{0,8},{4,12},{8,0},{12,4},{16,24},{20,28},{24,16},{28,20},{1,9},{5... | collective-permute-start | bytes 147464 | tf_op jit(solution)/shard_map/ppermute | solution.py:15
  55.9 14.0 %collective-permute-start.12 = (bf16[384,256]{1,0:T(8,128)(2,1)S(1)}, bf16[384,256]{1,0:T(8,128)(2,1)S(1)}, u32[]{:S(2)}, u32[]{:S(2)}) collective-permute-start(bf16[384,256]{1,0:T(8,128)(2,1)S(1)} %get-tuple-element.98), channel_id=1, source_target_pairs={{0,1},{1,0},{2,3},{3,2},{4,5},{5,4},{6,7},{7,6},{8,9},{9,8},{10,11... | collective-permute-start | bytes 589832 | tf_op jit(solution)/shard_map/ppermute | solution.py:15
  56.5 13.4 %collective-permute-start.13 = (bf16[384,256]{1,0:T(8,128)(2,1)S(1)}, bf16[384,256]{1,0:T(8,128)(2,1)S(1)}, u32[]{:S(2)}, u32[]{:S(2)}) collective-permute-start(bf16[384,256]{1,0:T(8,128)(2,1)S(1)} %get-tuple-element.99), channel_id=1, source_target_pairs={{0,2},{1,3},{2,0},{3,1},{4,6},{5,7},{6,4},{7,5},{8,10},{9,11},{10,... | collective-permute-start | bytes 589832 | tf_op jit(solution)/shard_map/ppermute | solution.py:15
  57.9 12.0 %collective-permute-start.14 = (bf16[384,256]{1,0:T(8,128)(2,1)S(1)}, bf16[384,256]{1,0:T(8,128)(2,1)S(1)}, u32[]{:S(2)}, u32[]{:S(2)}) collective-permute-start(bf16[384,256]{1,0:T(8,128)(2,1)S(1)} %get-tuple-element.100), channel_id=1, source_target_pairs={{0,3},{1,2},{2,1},{3,0},{4,7},{5,6},{6,5},{7,4},{8,11},{9,10},{10,... | collective-permute-start | bytes 589832 | tf_op jit(solution)/shard_map/ppermute | solution.py:15
  59.6 6.1 %collective-permute-start.21 = (bf16[96,256]{1,0:T(8,128)(2,1)S(1)}, bf16[96,256]{1,0:T(8,128)(2,1)S(1)}, u32[]{:S(2)}, u32[]{:S(2)}) collective-permute-start(bf16[96,256]{1,0:T(8,128)(2,1)S(1)} %get-tuple-element.112), channel_id=1, source_target_pairs={{0,24},{4,28},{8,16},{12,20},{16,8},{20,12},{24,0},{28,4},{1,25},{... | collective-permute-start | bytes 147464 | tf_op jit(solution)/shard_map/ppermute | solution.py:15
  61.8 5.0 %collective-permute-start.22 = (bf16[96,256]{1,0:T(8,128)(2,1)S(1)}, bf16[96,256]{1,0:T(8,128)(2,1)S(1)}, u32[]{:S(2)}, u32[]{:S(2)}) collective-permute-start(bf16[96,256]{1,0:T(8,128)(2,1)S(1)} %get-tuple-element.113), channel_id=1, source_target_pairs={{0,16},{4,20},{8,24},{12,28},{16,0},{20,4},{24,8},{28,12},{1,17},{... | collective-permute-start | bytes 147464 | tf_op jit(solution)/shard_map/ppermute | solution.py:15
  65.8 4.1 %collective-permute-start.23 = (bf16[96,256]{1,0:T(8,128)(2,1)S(1)}, bf16[96,256]{1,0:T(8,128)(2,1)S(1)}, u32[]{:S(2)}, u32[]{:S(2)}) collective-permute-start(bf16[96,256]{1,0:T(8,128)(2,1)S(1)} %get-tuple-element.114), channel_id=1, source_target_pairs={{0,8},{4,12},{8,0},{12,4},{16,24},{20,28},{24,16},{28,20},{1,9},{5... | collective-permute-start | bytes 147464 | tf_op jit(solution)/shard_map/ppermute | solution.py:15
  70.0 3.6 %collective-permute-start.27 = (bf16[384,256]{1,0:T(8,128)(2,1)S(1)}, bf16[384,256]{1,0:T(8,128)(2,1)S(1)}, u32[]{:S(2)}, u32[]{:S(2)}) collective-permute-start(bf16[384,256]{1,0:T(8,128)(2,1)S(1)} %shard_map.96.refs_0_), channel_id=1, source_target_pairs={{0,4},{4,0},{8,12},{12,8},{16,20},{20,16},{24,28},{28,24},{1,5},{5... | collective-permute-start | bytes 589832 | tf_op jit(solution)/shard_map/ppermute | solution.py:15
  70.1 8.7 %collective-permute-start.26 = (bf16[384,256]{1,0:T(8,128)(2,1)S(1)}, bf16[384,256]{1,0:T(8,128)(2,1)S(1)}, u32[]{:S(2)}, u32[]{:S(2)}) collective-permute-start(bf16[384,256]{1,0:T(8,128)(2,1)S(1)} %shard_map.96.refs_0_), channel_id=1, source_target_pairs={{0,3},{1,2},{2,1},{3,0},{4,7},{5,6},{6,5},{7,4},{8,11},{9,10},{10,... | collective-permute-start | bytes 589832 | tf_op jit(solution)/shard_map/ppermute | solution.py:15
  71.7 10.8 %collective-permute-start.25 = (bf16[384,256]{1,0:T(8,128)(2,1)S(1)}, bf16[384,256]{1,0:T(8,128)(2,1)S(1)}, u32[]{:S(2)}, u32[]{:S(2)}) collective-permute-start(bf16[384,256]{1,0:T(8,128)(2,1)S(1)} %shard_map.96.refs_0_), channel_id=1, source_target_pairs={{0,2},{1,3},{2,0},{3,1},{4,6},{5,7},{6,4},{7,5},{8,10},{9,11},{10,... | collective-permute-start | bytes 589832 | tf_op jit(solution)/shard_map/ppermute | solution.py:15
  72.4 10.1 %collective-permute-start.24 = (bf16[384,256]{1,0:T(8,128)(2,1)S(1)}, bf16[384,256]{1,0:T(8,128)(2,1)S(1)}, u32[]{:S(2)}, u32[]{:S(2)}) collective-permute-start(bf16[384,256]{1,0:T(8,128)(2,1)S(1)} %shard_map.96.refs_0_), channel_id=1, source_target_pairs={{0,1},{1,0},{2,3},{3,2},{4,5},{5,4},{6,7},{7,6},{8,9},{9,8},{10,11... | collective-permute-start | bytes 589832 | tf_op jit(solution)/shard_map/ppermute | solution.py:15
  82.5 2.3 %collective-permute-start.28 = (bf16[384,256]{1,0:T(8,128)(2,1)S(1)}, bf16[384,256]{1,0:T(8,128)(2,1)S(1)}, u32[]{:S(2)}, u32[]{:S(2)}) collective-permute-start(bf16[384,256]{1,0:T(8,128)(2,1)S(1)} %collective-permute-done.24.refs_0_), channel_id=1, source_target_pairs={{0,4},{4,0},{8,12},{12,8},{16,20},{20,16},{24,28},{28,24},{1,5},{5... | collective-permute-start | bytes 589832 | tf_op jit(solution)/shard_map/ppermute | solution.py:15
  82.6 2.3 %collective-permute-start.29 = (bf16[384,256]{1,0:T(8,128)(2,1)S(1)}, bf16[384,256]{1,0:T(8,128)(2,1)S(1)}, u32[]{:S(2)}, u32[]{:S(2)}) collective-permute-start(bf16[384,256]{1,0:T(8,128)(2,1)S(1)} %collective-permute-done.25.refs_1_), channel_id=1, source_target_pairs={{0,4},{4,0},{8,12},{12,8},{16,20},{20,16},{24,28},{28,24},{1,5},{5... | collective-permute-start | bytes 589832 | tf_op jit(solution)/shard_map/ppermute | solution.py:15
  83.0 1.8 %collective-permute-start.30 = (bf16[384,256]{1,0:T(8,128)(2,1)S(1)}, bf16[384,256]{1,0:T(8,128)(2,1)S(1)}, u32[]{:S(2)}, u32[]{:S(2)}) collective-permute-start(bf16[384,256]{1,0:T(8,128)(2,1)S(1)} %collective-permute-done.26.refs_2_), channel_id=1, source_target_pairs={{0,4},{4,0},{8,12},{12,8},{16,20},{20,16},{24,28},{28,24},{1,5},{5... | collective-permute-start | bytes 589832 | tf_op jit(solution)/shard_map/ppermute | solution.py:15

commit v2 on v1

--- a/solution.py
+++ b/solution.py
@@ -407,7 +407,7 @@
         hidden_grad = term if hidden_grad is None else hidden_grad + term
     if last:
         pre_grad = (hidden_grad * slope[...]).astype(jnp.bfloat16)
-        step = 256
+        step = 512
         for j in range(width // step):
             here = slice(j * step, (j + 1) * step)
             held_first[here, :] = dot(flat_t[here, :], pre_grad).astype(jnp.bfloat16)
@@ -476,7 +476,7 @@
             lambda *refs: keep_kernel(columns, *refs),
             [shape(columns, plane_rows // 2, piece)] * 2 + outs,
             [own, other, w2, *state],
-            flops=(16 if state else 1) * plane_rows * width * hid,
+            flops=(64 if state else 1) * plane_rows * width * hid,
             name="keep_s" if state else "keep_t",
         )
 
@@ -563,17 +563,18 @@
     home = call(
         lambda *refs: total_kernel(columns, experts, *refs),
         [shape(2 * capacity, piece)] * experts,
-        after(sums_t, hidden_own),
+        after(sums_t, pieces_s[0]),
     )
     home = [*over_planes(home[:-1]), home[-1]]
     slots = call(
         lambda *refs: home_kernel(experts, capacity, *refs),
         [shape(2 * capacity, piece)] * experts,
         [maps, *home],
-        flops=2 * plane_rows * width * hid,
+        flops=4 * plane_rows * width * hid,
         name="home",
     )
-    teachers = [*over_planes(slots[:-1]), slots[-1]]
+    *sent, near, own = slots
+    teachers = [*over_planes([*sent, after(near, sums_s[1])]), own]
     (upstream,) = call(
         lambda *refs: upstream_kernel(columns, experts, loss_scale, *refs),
         [shape(plane_rows, piece)],
@@ -598,7 +599,7 @@
             outs += [shape(width, hid)]
             out_specs = [ANY, ANY]
             scratch = [pltpu.VMEM((width, hid), jnp.bfloat16)] + scratch
-            copies += width // 256
+            copies += width // 512
         else:
             outs += [shape(plane_rows, hid, dtype=f32)]
             out_specs = [ANY, VMEM]
@@ -614,12 +615,13 @@
 
     grads = spread(upstream)
     state = backward({(0, 0): upstream, (1, 0): across(upstream)}, None, False)
-    grads = after(grads, state[1])
-    masks = range(1, columns)
-    others = [across(grads[m]) for m in masks]
-    state = backward({(0, m): grads[m] for m in masks}, state, False)
+    *near, far = after(grads[1:], state[1])
+    state = backward({(0, 3): far}, state, False)
+    near = after(near, state[1])
+    others = [across(value) for value in (*near, far)]
+    state = backward({(0, m + 1): near[m] for m in range(2)}, state, False)
     grad_second, grad_first = backward(
-        {(1, m): value for m, value in zip(masks, others)}, state, True
+        {(1, m + 1): value for m, value in enumerate(others)}, state, True
     )
     return (grad_first[None], grad_second[None])
 

time: 88.2 us -> 84.9 us (0.963)
  waiting for transfers between devices: 34 us -> 28.8 us
  starting transfers between devices: 28.2 us -> 29.3 us
  Pallas kernels: 16.6 us -> 17.5 us
    ppermute x31, waiting for transfers between devices: 34 us -> 28.8 us  [partner(): lax.ppermute(value, axis, [(i, i ^ mask) for i in range(lax.axis_size(axi...]
    ppermute x31, starting transfers between devices: 28.2 us -> 29.3 us  [partner(): lax.ppermute(value, axis, [(i, i ^ mask) for i in range(lax.axis_size(axi...]
    pallas_call x21 -> x22, Pallas kernels: 16.6 us -> 17.5 us  [call(): pl.pallas_call(kernel, name=name, out_shape=outs, in_specs=in_specs or [V...]
  transfers between devices with their start and end apart: 31 -> 31, of which waited for: 13 -> 14; matrix products, arithmetic and copies ran while one was open for 1% -> 1% of each run, Pallas kernels for 13% -> 14%
where the time goes in v2:
time: 84.9 us; the launch traced here: 84.7 us
  starting transfers between devices  29.3 us (35%)
  waiting for transfers between devices  28.8 us (34%)
  Pallas kernels  17.5 us (21%)
  local copies, waits for them, and re-layouts  7.44 us (9%)
  between operations  0.92 us (1%)
    ppermute x31, starting transfers between devices, partner(): lax.ppermute(value, axis, [(i, i ^ mask) for i in range(lax.axis_size(axi...  29.3 us
    ppermute x31, waiting for transfers between devices, partner(): lax.ppermute(value, axis, [(i, i ^ mask) for i in range(lax.axis_size(axi...  28.8 us
    pallas_call x22, Pallas kernels, call(): pl.pallas_call(kernel, name=name, out_shape=outs, in_specs=in_specs or [V...  17.5 us
    unnamed x16, local copies, waits for them, and re-layouts  7.44 us
  transfers between devices with their start and end apart: 31, of which 14 were waited for; matrix products, arithmetic and copies ran while one was open for 1% of the time, Pallas kernels for 14%

profile of v2, /device:TPU:0, one launch (start us, length us, event | category | flops | bytes accessed | tf_op | source)
XLA Modules:
  0.0 84.7 jit_solution(7734806242148915398)
XLA Ops:
  0.6 2.2 %pack.1 = (bf16[48,1024]{1,0:T(8,128)(2,1)}, bf16[48,1024]{1,0:T(8,128)(2,1)}, bf16[48,1024]{1,0:T(8,128)(2,1)}) custom-call(bf16[128,2048]{1,0:T(8,128)(2,1)} %refs_0_.5, bf16[128,2048]{1,0:T(8,128)(2,1)} %refs_1_.1, s32[1,128]{1,0:T(1,128)} %bitcast.12, s32[1,128]{1,0:T(1,128)} %bitcast.15), custom_call_target="tpu_custom_call" | custom-call | tf_op jit(solution)/shard_map/pack/pallas_call | solution.py:168
  2.9 5.1 %collective-permute-start = (bf16[48,1024]{1,0:T(8,128)(2,1)}, bf16[48,1024]{1,0:T(8,128)(2,1)S(1)}, u32[]{:S(2)}, u32[]{:S(2)}) collective-permute-start(bf16[48,1024]{1,0:T(8,128)(2,1)} %get-tuple-element.70), channel_id=1, source_target_pairs={{0,24},{4,28},{8,16},{12,20},{16,8},{20,12},{24,0},{28,4},{1,25},{... | collective-permute-start | bytes 294920 | tf_op jit(solution)/shard_map/ppermute | solution.py:15
  8.0 0.6 collective-permute-start.2
  8.6 0.7 pad_add_fusion.refs_0_
  9.3 1.0 %copy-done = bf16[128,2048]{1,0:T(8,128)(2,1)S(1)} copy-done((bf16[128,2048]{1,0:T(8,128)(2,1)S(1)}, bf16[128,2048]{1,0:T(8,128)(2,1)}, u32[]{:S(2)}) %copy-start) | copy-done | bytes 524312
  10.4 0.7 copy-done.6
  11.0 0.3 stay.2.refs_0_
  11.4 0.6 copy-done.7
  12.0 0.3 stay.3.refs_1_
  12.4 4.1 %collective-permute-done.1.refs_1_ = bf16[48,1024]{1,0:T(8,128)(2,1)S(1)} collective-permute-done((bf16[48,1024]{1,0:T(8,128)(2,1)}, bf16[48,1024]{1,0:T(8,128)(2,1)S(1)}, u32[]{:S(2)}, u32[]{:S(2)}) %collective-permute-start.1) | collective-permute-done | bytes 98336 | tf_op jit(solution)/shard_map/ppermute | solution.py:15
  16.5 2.5 %collective-permute-start.6 = (bf16[144,1024]{1,0:T(8,128)(2,1)S(1)}, bf16[144,1024]{1,0:T(8,128)(2,1)S(1)}, u32[]{:S(2)}, u32[]{:S(2)}) collective-permute-start(bf16[144,1024]{1,0:T(8,128)(2,1)S(1)} %stack.1.refs_2_), channel_id=1, source_target_pairs={{0,3},{1,2},{2,1},{3,0},{4,7},{5,6},{6,5},{7,4},{8,11},{9,10},{10,... | collective-permute-start | bytes 884744 | tf_op jit(solution)/shard_map/ppermute | solution.py:15
  19.0 0.5 collective-permute-start.5
  19.5 0.5 collective-permute-start.4
  20.1 1.6 %copy-done.2 = bf16[1,2048,512]{2,1,0:T(8,128)(2,1)S(1)} copy-done((bf16[1,2048,512]{2,1,0:T(8,128)(2,1)S(1)}, bf16[1,2048,512]{2,1,0:T(8,128)(2,1)}, u32[]{:S(2)}) %copy-start.2) | copy-done | bytes 2097176
  21.6 1.6 %copy-done.3 = bf16[1,512,2048]{2,1,0:T(8,128)(2,1)S(1)} copy-done((bf16[1,512,2048]{2,1,0:T(8,128)(2,1)S(1)}, bf16[1,512,2048]{2,1,0:T(8,128)(2,1)}, u32[]{:S(2)}) %copy-start.3) | copy-done | bytes 2097176
  23.2 0.3 load.2
  23.5 1.3 %copy-done.4 = bf16[1,2048,512]{2,1,0:T(8,128)(2,1)S(1)} copy-done((bf16[1,2048,512]{2,1,0:T(8,128)(2,1)S(1)}, bf16[1,2048,512]{2,1,0:T(8,128)(2,1)}, u32[]{:S(2)}) %copy-start.4) | copy-done | bytes 2097176
  24.8 0.6 copy-done.5
  25.5 0.3 load.3
  25.8 0.4 maps.1.refs_0_
  26.1 1.3 %collective-permute-done.6.refs_5_ = bf16[144,1024]{1,0:T(8,128)(2,1)S(1)} collective-permute-done((bf16[144,1024]{1,0:T(8,128)(2,1)S(1)}, bf16[144,1024]{1,0:T(8,128)(2,1)S(1)}, u32[]{:S(2)}, u32[]{:S(2)}) %collective-permute-start.6) | collective-permute-done | bytes 294944 | tf_op jit(solution)/shard_map/ppermute | solution.py:15
  27.4 4.4 %collective-permute-done.5.refs_4_ = bf16[144,1024]{1,0:T(8,128)(2,1)S(1)} collective-permute-done((bf16[144,1024]{1,0:T(8,128)(2,1)S(1)}, bf16[144,1024]{1,0:T(8,128)(2,1)S(1)}, u32[]{:S(2)}, u32[]{:S(2)}) %collective-permute-start.5) | collective-permute-done | bytes 294944 | tf_op jit(solution)/shard_map/ppermute | solution.py:15
  31.8 0.1 collective-permute-done.4.refs_3_
  31.9 0.1 join.1
  32.1 0.5 collective-permute-start.7
  32.6 0.9 %forward_t.2 = (bf16[1,4,192,256]{3,2,1,0:T(8,128)(2,1)S(1)}, bf16[192,512]{1,0:T(8,128)(2,1)S(1)}) custom-call(bf16[192,2048]{1,0:T(8,128)(2,1)S(1)} %get-tuple-element.83.refs_0_, bf16[2048,512]{1,0:T(8,128)(2,1)S(1)} %get-tuple-element.76.refs_1_, bf16[512,2048]{1,0:T(8,128)(2,1)S(1)} %get-tuple-element.84.refs_2_), custom_call_target="tpu_custom_call" | custom-call | tf_op jit(solution)/shard_map/forward_t/pallas_call | solution.py:168
  33.6 0.1 collective-permute-start.9
  33.7 0.7 collective-permute-done.8.refs_0_
  34.4 0.9 %forward_t.3 = (bf16[1,4,192,256]{3,2,1,0:T(8,128)(2,1)S(1)}, bf16[192,512]{1,0:T(8,128)(2,1)S(1)}) custom-call(bf16[192,2048]{1,0:T(8,128)(2,1)S(1)} %collective-permute-done.8.refs_0_, bf16[2048,512]{1,0:T(8,128)(2,1)S(1)} %get-tuple-element.76.refs_1_, bf16[512,2048]{1,0:T(8,128)(2,1)S(1)} %get-tuple-element.84.refs_2_), custom_call_target="tpu_custom_call" | custom-call | tf_op jit(solution)/shard_map/forward_t/pallas_call | solution.py:168
  35.3 0.2 collective-permute-start.10
  35.5 0.6 keep_t.1
  36.2 1.0 %collective-permute-done.10.refs_3_ = bf16[1,4,192,256]{3,2,1,0:T(8,128)(2,1)S(1)} collective-permute-done((bf16[1,4,192,256]{3,2,1,0:T(8,128)(2,1)S(1)}, bf16[1,4,192,256]{3,2,1,0:T(8,128)(2,1)S(1)}, u32[]{:S(2)}, u32[]{:S(2)}) %collective-permute-start.10) | collective-permute-done | bytes 393248 | tf_op jit(solution)/shard_map/ppermute | solution.py:15
  37.1 0.2 pair.2
  37.3 1.6 %collective-permute-start.15 = (bf16[384,256]{1,0:T(8,128)(2,1)S(1)}, bf16[384,256]{1,0:T(8,128)(2,1)S(1)}, u32[]{:S(2)}, u32[]{:S(2)}) collective-permute-start(bf16[384,256]{1,0:T(8,128)(2,1)S(1)} %get-tuple-element.106), channel_id=1, source_target_pairs={{0,1},{1,0},{2,3},{3,2},{4,5},{5,4},{6,7},{7,6},{8,9},{9,8},{10,11... | collective-permute-start | bytes 589832 | tf_op jit(solution)/shard_map/ppermute | solution.py:15
  38.9 0.7 collective-permute-start.16
  39.6 1.3 %collective-permute-start.17 = (bf16[384,256]{1,0:T(8,128)(2,1)S(1)}, bf16[384,256]{1,0:T(8,128)(2,1)S(1)}, u32[]{:S(2)}, u32[]{:S(2)}) collective-permute-start(bf16[384,256]{1,0:T(8,128)(2,1)S(1)} %get-tuple-element.108), channel_id=1, source_target_pairs={{0,3},{1,2},{2,1},{3,0},{4,7},{5,6},{6,5},{7,4},{8,11},{9,10},{10,... | collective-permute-start | bytes 589832 | tf_op jit(solution)/shard_map/ppermute | solution.py:15
  40.9 1.7 %forward_s.1 = (bf16[2,4,192,256]{3,2,1,0:T(8,128)(2,1)S(1)}, bf16[192,512]{1,0:T(8,128)(2,1)S(1)}, bf16[192,512]{1,0:T(8,128)(2,1)S(1)}, f32[192,512]{1,0:T(8,128)S(1)}, f32[192,512]{1,0:T(8,128)S(1)}) custom-call(bf16[192,2048]{1,0:T(8,128)(2,1)S(1)} %get-tuple-element.92.refs_0_.refs_5_, bf16[192,2048]{1,0:T(8,128)(2,1)S(1)} %collective-permute-done.7.refs_1_.refs_6_, ...), custom_call_target="tpu_custom_call" | custom-call | tf_op jit(solution)/shard_map/forward_s/pallas_call | solution.py:168
  42.7 1.4 %keep_s.1 = (bf16[4,192,256]{2,1,0:T(8,128)(2,1)S(1)}, bf16[4,192,256]{2,1,0:T(8,128)(2,1)S(1)}, bf16[2048,384]{1,0:T(8,128)(2,1)S(1)}, bf16[512,384]{1,0:T(8,128)(2,1)S(1)}, f32[384,512]{1,0:T(8,128)S(1)}) custom-call(bf16[192,512]{1,0:T(8,128)(2,1)S(1)} %get-tuple-element.95.refs_0_, bf16[192,512]{1,0:T(8,128)(2,1)S(1)} %get-tuple-element.96.refs_1_, ...), custom_call_target="tpu_custom_call" | custom-call | flops 25769803776 | tf_op jit(solution)/shard_map/keep_s/pallas_call | solution.py:168
  44.1 0.9 %collective-permute-done.11.refs_2_ = bf16[2,4,192,256]{3,2,1,0:T(8,128)(2,1)S(1)} collective-permute-done((bf16[2,4,192,256]{3,2,1,0:T(8,128)(2,1)S(1)}, bf16[2,4,192,256]{3,2,1,0:T(8,128)(2,1)S(1)}, u32[]{:S(2)}, u32[]{:S(2)}) %collective-permute-start.11) | collective-permute-done | bytes 786464 | tf_op jit(solution)/shard_map/ppermute | solution.py:15
  45.0 0.2 pair.3
  45.2 4.6 %collective-permute-done.16.refs_2_ = bf16[384,256]{1,0:T(8,128)(2,1)S(1)} collective-permute-done((bf16[384,256]{1,0:T(8,128)(2,1)S(1)}, bf16[384,256]{1,0:T(8,128)(2,1)S(1)}, u32[]{:S(2)}, u32[]{:S(2)}) %collective-permute-start.16) | collective-permute-done | bytes 196640 | tf_op jit(solution)/shard_map/ppermute | solution.py:15
  49.9 2.2 %collective-permute-start.18 = (bf16[96,256]{1,0:T(8,128)(2,1)S(1)}, bf16[96,256]{1,0:T(8,128)(2,1)S(1)}, u32[]{:S(2)}, u32[]{:S(2)}) collective-permute-start(bf16[96,256]{1,0:T(8,128)(2,1)S(1)} %get-tuple-element.113), channel_id=1, source_target_pairs={{0,24},{4,28},{8,16},{12,20},{16,8},{20,12},{24,0},{28,4},{1,25},{... | collective-permute-start | bytes 147464 | tf_op jit(solution)/shard_map/ppermute | solution.py:15
  52.0 2.3 %collective-permute-start.20 = (bf16[96,256]{1,0:T(8,128)(2,1)S(1)}, bf16[96,256]{1,0:T(8,128)(2,1)S(1)}, u32[]{:S(2)}, u32[]{:S(2)}) collective-permute-start(bf16[96,256]{1,0:T(8,128)(2,1)S(1)} %get-tuple-element.115), channel_id=1, source_target_pairs={{0,8},{4,12},{8,0},{12,4},{16,24},{20,28},{24,16},{28,20},{1,9},{5... | collective-permute-start | bytes 147464 | tf_op jit(solution)/shard_map/ppermute | solution.py:15
  54.3 0.5 collective-permute-start.12
  54.8 1.4 %collective-permute-start.13 = (bf16[384,256]{1,0:T(8,128)(2,1)S(1)}, bf16[384,256]{1,0:T(8,128)(2,1)S(1)}, u32[]{:S(2)}, u32[]{:S(2)}) collective-permute-start(bf16[384,256]{1,0:T(8,128)(2,1)S(1)} %get-tuple-element.104), channel_id=1, source_target_pairs={{0,2},{1,3},{2,0},{3,1},{4,6},{5,7},{6,4},{7,5},{8,10},{9,11},{10,... | collective-permute-start | bytes 589832 | tf_op jit(solution)/shard_map/ppermute | solution.py:15
  56.3 1.5 %collective-permute-start.14 = (bf16[384,256]{1,0:T(8,128)(2,1)S(1)}, bf16[384,256]{1,0:T(8,128)(2,1)S(1)}, u32[]{:S(2)}, u32[]{:S(2)}) collective-permute-start(bf16[384,256]{1,0:T(8,128)(2,1)S(1)} %get-tuple-element.105), channel_id=1, source_target_pairs={{0,3},{1,2},{2,1},{3,0},{4,7},{5,6},{6,5},{7,4},{8,11},{9,10},{10,... | collective-permute-start | bytes 589832 | tf_op jit(solution)/shard_map/ppermute | solution.py:15
  57.8 0.2 home.1
  58.0 2.1 %collective-permute-start.21 = (bf16[96,256]{1,0:T(8,128)(2,1)S(1)}, bf16[96,256]{1,0:T(8,128)(2,1)S(1)}, u32[]{:S(2)}, u32[]{:S(2)}) collective-permute-start(bf16[96,256]{1,0:T(8,128)(2,1)S(1)} %get-tuple-element.117), channel_id=1, source_target_pairs={{0,24},{4,28},{8,16},{12,20},{16,8},{20,12},{24,0},{28,4},{1,25},{... | collective-permute-start | bytes 147464 | tf_op jit(solution)/shard_map/ppermute | solution.py:15
  60.2 1.2 %collective-permute-done.12.refs_1_ = bf16[384,256]{1,0:T(8,128)(2,1)S(1)} collective-permute-done((bf16[384,256]{1,0:T(8,128)(2,1)S(1)}, bf16[384,256]{1,0:T(8,128)(2,1)S(1)}, u32[]{:S(2)}, u32[]{:S(2)}) %collective-permute-start.12) | collective-permute-done | bytes 196640 | tf_op jit(solution)/shard_map/ppermute | solution.py:15
  61.4 1.1 %collective-permute-start.23 = (bf16[96,256]{1,0:T(8,128)(2,1)S(1)}, bf16[96,256]{1,0:T(8,128)(2,1)S(1)}, u32[]{:S(2)}, u32[]{:S(2)}) collective-permute-start(bf16[96,256]{1,0:T(8,128)(2,1)S(1)} %get-tuple-element.120), channel_id=1, source_target_pairs={{0,8},{4,12},{8,0},{12,4},{16,24},{20,28},{24,16},{28,20},{1,9},{5... | collective-permute-start | bytes 147464 | tf_op jit(solution)/shard_map/ppermute | solution.py:15
  62.5 1.5 %collective-permute-done.21.refs_4_ = bf16[96,256]{1,0:T(8,128)(2,1)S(1)} collective-permute-done((bf16[96,256]{1,0:T(8,128)(2,1)S(1)}, bf16[96,256]{1,0:T(8,128)(2,1)S(1)}, u32[]{:S(2)}, u32[]{:S(2)}) %collective-permute-start.21) | collective-permute-done | bytes 49184 | tf_op jit(solution)/shard_map/ppermute | solution.py:15
  64.0 1.2 %collective-permute-done.22.refs_5_ = bf16[96,256]{1,0:T(8,128)(2,1)S(1)} collective-permute-done((bf16[96,256]{1,0:T(8,128)(2,1)S(1)}, bf16[96,256]{1,0:T(8,128)(2,1)S(1)}, u32[]{:S(2)}, u32[]{:S(2)}) %collective-permute-start.22) | collective-permute-done | bytes 49184 | tf_op jit(solution)/shard_map/ppermute | solution.py:15
  65.2 0.5 collective-permute-done.23.refs_6_
  65.7 0.1 shard_map.96.refs_0_
  65.9 1.5 %collective-permute-start.26 = (bf16[384,256]{1,0:T(8,128)(2,1)S(1)}, bf16[384,256]{1,0:T(8,128)(2,1)S(1)}, u32[]{:S(2)}, u32[]{:S(2)}) collective-permute-start(bf16[384,256]{1,0:T(8,128)(2,1)S(1)} %shard_map.96.refs_0_), channel_id=1, source_target_pairs={{0,3},{1,2},{2,1},{3,0},{4,7},{5,6},{6,5},{7,4},{8,11},{9,10},{10,... | collective-permute-start | bytes 589832 | tf_op jit(solution)/shard_map/ppermute | solution.py:15
  67.4 0.7 collective-permute-start.25
  68.0 1.4 %collective-permute-start.24 = (bf16[384,256]{1,0:T(8,128)(2,1)S(1)}, bf16[384,256]{1,0:T(8,128)(2,1)S(1)}, u32[]{:S(2)}, u32[]{:S(2)}) collective-permute-start(bf16[384,256]{1,0:T(8,128)(2,1)S(1)} %shard_map.96.refs_0_), channel_id=1, source_target_pairs={{0,1},{1,0},{2,3},{3,2},{4,5},{5,4},{6,7},{7,6},{8,9},{9,8},{10,11... | collective-permute-start | bytes 589832 | tf_op jit(solution)/shard_map/ppermute | solution.py:15
  69.4 1.5 %shard_map.97 = (bf16[512,2048]{1,0:T(8,128)(2,1)}, f32[384,512]{1,0:T(8,128)S(1)}) custom-call(bf16[384,256]{1,0:T(8,128)(2,1)S(1)} %shard_map.96.refs_0_, bf16[384,256]{1,0:T(8,128)(2,1)S(1)} %collective-permute-done.27.refs_1_, bf16[512,384]{1,0:T(8,128)(2,1)S(1)} %get-tuple-element.122.refs_2_.refs_1_.refs_3_, ...), custom_call_target="tpu_custom_call" | custom-call | tf_op jit(solution)/shard_map/pallas_call | solution.py:168
  70.9 3.7 %collective-permute-done.26.refs_0_ = bf16[384,256]{1,0:T(8,128)(2,1)S(1)} collective-permute-done((bf16[384,256]{1,0:T(8,128)(2,1)S(1)}, bf16[384,256]{1,0:T(8,128)(2,1)S(1)}, u32[]{:S(2)}, u32[]{:S(2)}) %collective-permute-start.26) | collective-permute-done | bytes 196640 | tf_op jit(solution)/shard_map/ppermute | solution.py:15
  74.6 3.7 %collective-permute-done.25.refs_1_ = bf16[384,256]{1,0:T(8,128)(2,1)S(1)} collective-permute-done((bf16[384,256]{1,0:T(8,128)(2,1)S(1)}, bf16[384,256]{1,0:T(8,128)(2,1)S(1)}, u32[]{:S(2)}, u32[]{:S(2)}) %collective-permute-start.25) | collective-permute-done | bytes 196640 | tf_op jit(solution)/shard_map/ppermute | solution.py:15
  78.4 1.1 %shard_map.98 = (bf16[512,2048]{1,0:T(8,128)(2,1)}, f32[384,512]{1,0:T(8,128)S(1)}) custom-call(bf16[384,256]{1,0:T(8,128)(2,1)S(1)} %collective-permute-done.26.refs_0_, bf16[512,384]{1,0:T(8,128)(2,1)S(1)} %get-tuple-element.122.refs_2_.refs_1_.refs_3_, ...), custom_call_target="tpu_custom_call", output_to_operand_aliasing={{0}: (4, {})} | custom-call | tf_op jit(solution)/shard_map/pallas_call | solution.py:168
  79.5 0.5 collective-permute-start.28
  80.1 1.5 %shard_map.99 = (bf16[512,2048]{1,0:T(8,128)(2,1)}, f32[384,512]{1,0:T(8,128)S(1)}) custom-call(bf16[384,256]{1,0:T(8,128)(2,1)S(1)} %collective-permute-done.24.refs_0_, bf16[384,256]{1,0:T(8,128)(2,1)S(1)} %collective-permute-done.25.refs_1_, bf16[512,384]{1,0:T(8,128)(2,1)S(1)} %get-tuple-element.122.refs_2_.refs_1_.refs_3_, ...), custom_call_target="tpu_custom_call", output_to_operand_aliasing={{0}: (5, {})} | custom-call | tf_op jit(solution)/shard_map/pallas_call | solution.py:168
  81.6 3.0 %shard_map.100 = (bf16[512,2048]{1,0:T(8,128)(2,1)}, bf16[2048,512]{1,0:T(8,128)(2,1)}) custom-call(bf16[384,256]{1,0:T(8,128)(2,1)S(1)} %collective-permute-done.28.refs_0_, bf16[384,256]{1,0:T(8,128)(2,1)S(1)} %collective-permute-done.29.refs_1_, bf16[384,256]{1,0:T(8,128)(2,1)S(1)} %collective-permute-done.30.refs_2_, ...), custom_call_target="tpu_custom_call", output_to_operand_aliasing={{0}: (6, {})} | custom-call | tf_op jit(solution)/shard_map/pallas_call | solution.py:168
  (37 shorter events, 0.5 us)
Async XLA Ops:
  0.6 10.7 %copy-start.1 = (bf16[128,2048]{1,0:T(8,128)(2,1)S(1)}, bf16[128,2048]{1,0:T(8,128)(2,1)}, u32[]{:S(2)}) copy-start(bf16[128,2048]{1,0:T(8,128)(2,1)} %refs_1_.1) | copy-start | bytes 1572868
  2.9 9.5 %collective-permute-start = (bf16[48,1024]{1,0:T(8,128)(2,1)}, bf16[48,1024]{1,0:T(8,128)(2,1)S(1)}, u32[]{:S(2)}, u32[]{:S(2)}) collective-permute-start(bf16[48,1024]{1,0:T(8,128)(2,1)} %get-tuple-element.70), channel_id=1, source_target_pairs={{0,24},{4,28},{8,16},{12,20},{16,8},{20,12},{24,0},{28,4},{1,25},{... | collective-permute-start | bytes 294920 | tf_op jit(solution)/shard_map/ppermute | solution.py:15
  8.0 8.5 %collective-permute-start.1 = (bf16[48,1024]{1,0:T(8,128)(2,1)}, bf16[48,1024]{1,0:T(8,128)(2,1)S(1)}, u32[]{:S(2)}, u32[]{:S(2)}) collective-permute-start(bf16[48,1024]{1,0:T(8,128)(2,1)} %get-tuple-element.71), channel_id=1, source_target_pairs={{0,16},{4,20},{8,24},{12,28},{16,0},{20,4},{24,8},{28,12},{1,17},{... | collective-permute-start | bytes 294920 | tf_op jit(solution)/shard_map/ppermute | solution.py:15
  8.0 8.5 %collective-permute-start.2 = (bf16[48,1024]{1,0:T(8,128)(2,1)}, bf16[48,1024]{1,0:T(8,128)(2,1)S(1)}, u32[]{:S(2)}, u32[]{:S(2)}) collective-permute-start(bf16[48,1024]{1,0:T(8,128)(2,1)} %get-tuple-element.72), channel_id=1, source_target_pairs={{0,8},{4,12},{8,0},{12,4},{16,24},{20,28},{24,16},{28,20},{1,9},{5... | collective-permute-start | bytes 294920 | tf_op jit(solution)/shard_map/ppermute | solution.py:15
  9.3 3.1 %collective-permute-start.3 = (s32[2,128]{1,0:T(2,128)S(1)}, s32[2,128]{1,0:T(2,128)S(1)}, u32[]{:S(2)}, u32[]{:S(2)}) collective-permute-start(s32[2,128]{1,0:T(2,128)S(1)} %pad_add_fusion.refs_0_), channel_id=1, source_target_pairs={{0,4},{4,0},{8,12},{12,8},{16,20},{20,16},{24,28},{28,24},{1,5},{5... | collective-permute-start | bytes 3080 | tf_op jit(solution)/shard_map/ppermute | solution.py:15
  9.3 1.0 %copy-start = (bf16[128,2048]{1,0:T(8,128)(2,1)S(1)}, bf16[128,2048]{1,0:T(8,128)(2,1)}, u32[]{:S(2)}) copy-start(bf16[128,2048]{1,0:T(8,128)(2,1)} %refs_0_.5) | copy-start | bytes 1572868
  10.4 0.7 copy-start.6
  11.4 0.7 copy-start.7
  16.5 11.0 %collective-permute-start.6 = (bf16[144,1024]{1,0:T(8,128)(2,1)S(1)}, bf16[144,1024]{1,0:T(8,128)(2,1)S(1)}, u32[]{:S(2)}, u32[]{:S(2)}) collective-permute-start(bf16[144,1024]{1,0:T(8,128)(2,1)S(1)} %stack.1.refs_2_), channel_id=1, source_target_pairs={{0,3},{1,2},{2,1},{3,0},{4,7},{5,6},{6,5},{7,4},{8,11},{9,10},{10,... | collective-permute-start | bytes 884744 | tf_op jit(solution)/shard_map/ppermute | solution.py:15
  19.0 12.8 %collective-permute-start.5 = (bf16[144,1024]{1,0:T(8,128)(2,1)S(1)}, bf16[144,1024]{1,0:T(8,128)(2,1)S(1)}, u32[]{:S(2)}, u32[]{:S(2)}) collective-permute-start(bf16[144,1024]{1,0:T(8,128)(2,1)S(1)} %stack.1.refs_2_), channel_id=1, source_target_pairs={{0,2},{1,3},{2,0},{3,1},{4,6},{5,7},{6,4},{7,5},{8,10},{9,11},{10,... | collective-permute-start | bytes 884744 | tf_op jit(solution)/shard_map/ppermute | solution.py:15
  19.5 12.4 %collective-permute-start.4 = (bf16[144,1024]{1,0:T(8,128)(2,1)S(1)}, bf16[144,1024]{1,0:T(8,128)(2,1)S(1)}, u32[]{:S(2)}, u32[]{:S(2)}) collective-permute-start(bf16[144,1024]{1,0:T(8,128)(2,1)S(1)} %stack.1.refs_2_), channel_id=1, source_target_pairs={{0,1},{1,0},{2,3},{3,2},{4,5},{5,4},{6,7},{7,6},{8,9},{9,8},{10,11... | collective-permute-start | bytes 884744 | tf_op jit(solution)/shard_map/ppermute | solution.py:15
  20.0 1.6 %copy-start.2 = (bf16[1,2048,512]{2,1,0:T(8,128)(2,1)S(1)}, bf16[1,2048,512]{2,1,0:T(8,128)(2,1)}, u32[]{:S(2)}) copy-start(bf16[1,2048,512]{2,1,0:T(8,128)(2,1)} %param.12) | copy-start | bytes 6291460
  21.6 1.6 %copy-start.3 = (bf16[1,512,2048]{2,1,0:T(8,128)(2,1)S(1)}, bf16[1,512,2048]{2,1,0:T(8,128)(2,1)}, u32[]{:S(2)}) copy-start(bf16[1,512,2048]{2,1,0:T(8,128)(2,1)} %param.13) | copy-start | bytes 6291460
  23.2 1.6 %copy-start.4 = (bf16[1,2048,512]{2,1,0:T(8,128)(2,1)S(1)}, bf16[1,2048,512]{2,1,0:T(8,128)(2,1)}, u32[]{:S(2)}) copy-start(bf16[1,2048,512]{2,1,0:T(8,128)(2,1)} %param.14) | copy-start | bytes 6291460
  23.2 2.2 %copy-start.5 = (bf16[1,512,2048]{2,1,0:T(8,128)(2,1)S(1)}, bf16[1,512,2048]{2,1,0:T(8,128)(2,1)}, u32[]{:S(2)}) copy-start(bf16[1,512,2048]{2,1,0:T(8,128)(2,1)} %param.15) | copy-start | bytes 6291460
  32.1 2.4 %collective-permute-start.8 = (bf16[192,2048]{1,0:T(8,128)(2,1)S(1)}, bf16[192,2048]{1,0:T(8,128)(2,1)S(1)}, u32[]{:S(2)}, u32[]{:S(2)}) collective-permute-start(bf16[192,2048]{1,0:T(8,128)(2,1)S(1)} %get-tuple-element.83.refs_0_), channel_id=1, source_target_pairs={{0,4},{4,0},{8,12},{12,8},{16,20},{20,16},{24,28},{28,24},{1,5},{5... | collective-permute-start | bytes 2359304 | tf_op jit(solution)/shard_map/ppermute | solution.py:15
  32.1 5.2 %collective-permute-start.7 = (bf16[192,2048]{1,0:T(8,128)(2,1)S(1)}, bf16[192,2048]{1,0:T(8,128)(2,1)S(1)}, u32[]{:S(2)}, u32[]{:S(2)}) collective-permute-start(bf16[192,2048]{1,0:T(8,128)(2,1)S(1)} %get-tuple-element.92.refs_0_.refs_5_), channel_id=1, source_target_pairs={{0,4},{4,0},{8,12},{12,8},{16,20},{20,16},{24,28},{28,24},{1,5},{5... | collective-permute-start | bytes 2359304 | tf_op jit(solution)/shard_map/ppermute | solution.py:15
  33.6 2.6 %collective-permute-start.9 = (bf16[1,4,192,256]{3,2,1,0:T(8,128)(2,1)S(1)}, bf16[1,4,192,256]{3,2,1,0:T(8,128)(2,1)S(1)}, u32[]{:S(2)}, u32[]{:S(2)}) collective-permute-start(bf16[1,4,192,256]{3,2,1,0:T(8,128)(2,1)S(1)} %get-tuple-element.89), channel_id=1, source_target_pairs={{0,4},{4,0},{8,12},{12,8},{16,20},{20,16},{24,28},{28,24},{1,5},{5... | collective-permute-start | bytes 1179656 | tf_op jit(solution)/shard_map/ppermute | solution.py:15
  35.3 1.8 %collective-permute-start.10 = (bf16[1,4,192,256]{3,2,1,0:T(8,128)(2,1)S(1)}, bf16[1,4,192,256]{3,2,1,0:T(8,128)(2,1)S(1)}, u32[]{:S(2)}, u32[]{:S(2)}) collective-permute-start(bf16[1,4,192,256]{3,2,1,0:T(8,128)(2,1)S(1)} %get-tuple-element.90), channel_id=1, source_target_pairs={{0,4},{4,0},{8,12},{12,8},{16,20},{20,16},{24,28},{28,24},{1,5},{5... | collective-permute-start | bytes 1179656 | tf_op jit(solution)/shard_map/ppermute | solution.py:15
  37.3 7.8 %collective-permute-start.15 = (bf16[384,256]{1,0:T(8,128)(2,1)S(1)}, bf16[384,256]{1,0:T(8,128)(2,1)S(1)}, u32[]{:S(2)}, u32[]{:S(2)}) collective-permute-start(bf16[384,256]{1,0:T(8,128)(2,1)S(1)} %get-tuple-element.106), channel_id=1, source_target_pairs={{0,1},{1,0},{2,3},{3,2},{4,5},{5,4},{6,7},{7,6},{8,9},{9,8},{10,11... | collective-permute-start | bytes 589832 | tf_op jit(solution)/shard_map/ppermute | solution.py:15
  38.9 10.9 %collective-permute-start.16 = (bf16[384,256]{1,0:T(8,128)(2,1)S(1)}, bf16[384,256]{1,0:T(8,128)(2,1)S(1)}, u32[]{:S(2)}, u32[]{:S(2)}) collective-permute-start(bf16[384,256]{1,0:T(8,128)(2,1)S(1)} %get-tuple-element.107), channel_id=1, source_target_pairs={{0,2},{1,3},{2,0},{3,1},{4,6},{5,7},{6,4},{7,5},{8,10},{9,11},{10,... | collective-permute-start | bytes 589832 | tf_op jit(solution)/shard_map/ppermute | solution.py:15
  39.6 10.2 %collective-permute-start.17 = (bf16[384,256]{1,0:T(8,128)(2,1)S(1)}, bf16[384,256]{1,0:T(8,128)(2,1)S(1)}, u32[]{:S(2)}, u32[]{:S(2)}) collective-permute-start(bf16[384,256]{1,0:T(8,128)(2,1)S(1)} %get-tuple-element.108), channel_id=1, source_target_pairs={{0,3},{1,2},{2,1},{3,0},{4,7},{5,6},{6,5},{7,4},{8,11},{9,10},{10,... | collective-permute-start | bytes 589832 | tf_op jit(solution)/shard_map/ppermute | solution.py:15
  42.6 2.4 %collective-permute-start.11 = (bf16[2,4,192,256]{3,2,1,0:T(8,128)(2,1)S(1)}, bf16[2,4,192,256]{3,2,1,0:T(8,128)(2,1)S(1)}, u32[]{:S(2)}, u32[]{:S(2)}) collective-permute-start(bf16[2,4,192,256]{3,2,1,0:T(8,128)(2,1)S(1)} %get-tuple-element.101), channel_id=1, source_target_pairs={{0,4},{4,0},{8,12},{12,8},{16,20},{20,16},{24,28},{28,24},{1,5},{5... | collective-permute-start | bytes 2359304 | tf_op jit(solution)/shard_map/ppermute | solution.py:15
  49.9 6.4 %collective-permute-start.18 = (bf16[96,256]{1,0:T(8,128)(2,1)S(1)}, bf16[96,256]{1,0:T(8,128)(2,1)S(1)}, u32[]{:S(2)}, u32[]{:S(2)}) collective-permute-start(bf16[96,256]{1,0:T(8,128)(2,1)S(1)} %get-tuple-element.113), channel_id=1, source_target_pairs={{0,24},{4,28},{8,16},{12,20},{16,8},{20,12},{24,0},{28,4},{1,25},{... | collective-permute-start | bytes 147464 | tf_op jit(solution)/shard_map/ppermute | solution.py:15
  52.0 5.8 %collective-permute-start.19 = (bf16[96,256]{1,0:T(8,128)(2,1)S(1)}, bf16[96,256]{1,0:T(8,128)(2,1)S(1)}, u32[]{:S(2)}, u32[]{:S(2)}) collective-permute-start(bf16[96,256]{1,0:T(8,128)(2,1)S(1)} %get-tuple-element.114), channel_id=1, source_target_pairs={{0,16},{4,20},{8,24},{12,28},{16,0},{20,4},{24,8},{28,12},{1,17},{... | collective-permute-start | bytes 147464 | tf_op jit(solution)/shard_map/ppermute | solution.py:15
  52.0 5.8 %collective-permute-start.20 = (bf16[96,256]{1,0:T(8,128)(2,1)S(1)}, bf16[96,256]{1,0:T(8,128)(2,1)S(1)}, u32[]{:S(2)}, u32[]{:S(2)}) collective-permute-start(bf16[96,256]{1,0:T(8,128)(2,1)S(1)} %get-tuple-element.115), channel_id=1, source_target_pairs={{0,8},{4,12},{8,0},{12,4},{16,24},{20,28},{24,16},{28,20},{1,9},{5... | collective-permute-start | bytes 147464 | tf_op jit(solution)/shard_map/ppermute | solution.py:15
  54.3 7.1 %collective-permute-start.12 = (bf16[384,256]{1,0:T(8,128)(2,1)S(1)}, bf16[384,256]{1,0:T(8,128)(2,1)S(1)}, u32[]{:S(2)}, u32[]{:S(2)}) collective-permute-start(bf16[384,256]{1,0:T(8,128)(2,1)S(1)} %get-tuple-element.103), channel_id=1, source_target_pairs={{0,1},{1,0},{2,3},{3,2},{4,5},{5,4},{6,7},{7,6},{8,9},{9,8},{10,11... | collective-permute-start | bytes 589832 | tf_op jit(solution)/shard_map/ppermute | solution.py:15
  54.8 10.3 %collective-permute-start.13 = (bf16[384,256]{1,0:T(8,128)(2,1)S(1)}, bf16[384,256]{1,0:T(8,128)(2,1)S(1)}, u32[]{:S(2)}, u32[]{:S(2)}) collective-permute-start(bf16[384,256]{1,0:T(8,128)(2,1)S(1)} %get-tuple-element.104), channel_id=1, source_target_pairs={{0,2},{1,3},{2,0},{3,1},{4,6},{5,7},{6,4},{7,5},{8,10},{9,11},{10,... | collective-permute-start | bytes 589832 | tf_op jit(solution)/shard_map/ppermute | solution.py:15
  56.3 8.9 %collective-permute-start.14 = (bf16[384,256]{1,0:T(8,128)(2,1)S(1)}, bf16[384,256]{1,0:T(8,128)(2,1)S(1)}, u32[]{:S(2)}, u32[]{:S(2)}) collective-permute-start(bf16[384,256]{1,0:T(8,128)(2,1)S(1)} %get-tuple-element.105), channel_id=1, source_target_pairs={{0,3},{1,2},{2,1},{3,0},{4,7},{5,6},{6,5},{7,4},{8,11},{9,10},{10,... | collective-permute-start | bytes 589832 | tf_op jit(solution)/shard_map/ppermute | solution.py:15
  58.0 6.0 %collective-permute-start.21 = (bf16[96,256]{1,0:T(8,128)(2,1)S(1)}, bf16[96,256]{1,0:T(8,128)(2,1)S(1)}, u32[]{:S(2)}, u32[]{:S(2)}) collective-permute-start(bf16[96,256]{1,0:T(8,128)(2,1)S(1)} %get-tuple-element.117), channel_id=1, source_target_pairs={{0,24},{4,28},{8,16},{12,20},{16,8},{20,12},{24,0},{28,4},{1,25},{... | collective-permute-start | bytes 147464 | tf_op jit(solution)/shard_map/ppermute | solution.py:15
  60.2 5.0 %collective-permute-start.22 = (bf16[96,256]{1,0:T(8,128)(2,1)S(1)}, bf16[96,256]{1,0:T(8,128)(2,1)S(1)}, u32[]{:S(2)}, u32[]{:S(2)}) collective-permute-start(bf16[96,256]{1,0:T(8,128)(2,1)S(1)} %get-tuple-element.118), channel_id=1, source_target_pairs={{0,16},{4,20},{8,24},{12,28},{16,0},{20,4},{24,8},{28,12},{1,17},{... | collective-permute-start | bytes 147464 | tf_op jit(solution)/shard_map/ppermute | solution.py:15
  61.4 4.3 %collective-permute-start.23 = (bf16[96,256]{1,0:T(8,128)(2,1)S(1)}, bf16[96,256]{1,0:T(8,128)(2,1)S(1)}, u32[]{:S(2)}, u32[]{:S(2)}) collective-permute-start(bf16[96,256]{1,0:T(8,128)(2,1)S(1)} %get-tuple-element.120), channel_id=1, source_target_pairs={{0,8},{4,12},{8,0},{12,4},{16,24},{20,28},{24,16},{28,20},{1,9},{5... | collective-permute-start | bytes 147464 | tf_op jit(solution)/shard_map/ppermute | solution.py:15
  65.8 3.6 %collective-permute-start.27 = (bf16[384,256]{1,0:T(8,128)(2,1)S(1)}, bf16[384,256]{1,0:T(8,128)(2,1)S(1)}, u32[]{:S(2)}, u32[]{:S(2)}) collective-permute-start(bf16[384,256]{1,0:T(8,128)(2,1)S(1)} %shard_map.96.refs_0_), channel_id=1, source_target_pairs={{0,4},{4,0},{8,12},{12,8},{16,20},{20,16},{24,28},{28,24},{1,5},{5... | collective-permute-start | bytes 589832 | tf_op jit(solution)/shard_map/ppermute | solution.py:15
  65.9 8.7 %collective-permute-start.26 = (bf16[384,256]{1,0:T(8,128)(2,1)S(1)}, bf16[384,256]{1,0:T(8,128)(2,1)S(1)}, u32[]{:S(2)}, u32[]{:S(2)}) collective-permute-start(bf16[384,256]{1,0:T(8,128)(2,1)S(1)} %shard_map.96.refs_0_), channel_id=1, source_target_pairs={{0,3},{1,2},{2,1},{3,0},{4,7},{5,6},{6,5},{7,4},{8,11},{9,10},{10,... | collective-permute-start | bytes 589832 | tf_op jit(solution)/shard_map/ppermute | solution.py:15
  67.4 11.0 %collective-permute-start.25 = (bf16[384,256]{1,0:T(8,128)(2,1)S(1)}, bf16[384,256]{1,0:T(8,128)(2,1)S(1)}, u32[]{:S(2)}, u32[]{:S(2)}) collective-permute-start(bf16[384,256]{1,0:T(8,128)(2,1)S(1)} %shard_map.96.refs_0_), channel_id=1, source_target_pairs={{0,2},{1,3},{2,0},{3,1},{4,6},{5,7},{6,4},{7,5},{8,10},{9,11},{10,... | collective-permute-start | bytes 589832 | tf_op jit(solution)/shard_map/ppermute | solution.py:15
  68.0 10.3 %collective-permute-start.24 = (bf16[384,256]{1,0:T(8,128)(2,1)S(1)}, bf16[384,256]{1,0:T(8,128)(2,1)S(1)}, u32[]{:S(2)}, u32[]{:S(2)}) collective-permute-start(bf16[384,256]{1,0:T(8,128)(2,1)S(1)} %shard_map.96.refs_0_), channel_id=1, source_target_pairs={{0,1},{1,0},{2,3},{3,2},{4,5},{5,4},{6,7},{7,6},{8,9},{9,8},{10,11... | collective-permute-start | bytes 589832 | tf_op jit(solution)/shard_map/ppermute | solution.py:15
  78.3 3.3 %collective-permute-start.30 = (bf16[384,256]{1,0:T(8,128)(2,1)S(1)}, bf16[384,256]{1,0:T(8,128)(2,1)S(1)}, u32[]{:S(2)}, u32[]{:S(2)}) collective-permute-start(bf16[384,256]{1,0:T(8,128)(2,1)S(1)} %collective-permute-done.26.refs_0_), channel_id=1, source_target_pairs={{0,4},{4,0},{8,12},{12,8},{16,20},{20,16},{24,28},{28,24},{1,5},{5... | collective-permute-start | bytes 589832 | tf_op jit(solution)/shard_map/ppermute | solution.py:15
  79.5 2.1 %collective-permute-start.28 = (bf16[384,256]{1,0:T(8,128)(2,1)S(1)}, bf16[384,256]{1,0:T(8,128)(2,1)S(1)}, u32[]{:S(2)}, u32[]{:S(2)}) collective-permute-start(bf16[384,256]{1,0:T(8,128)(2,1)S(1)} %collective-permute-done.24.refs_0_), channel_id=1, source_target_pairs={{0,4},{4,0},{8,12},{12,8},{16,20},{20,16},{24,28},{28,24},{1,5},{5... | collective-permute-start | bytes 589832 | tf_op jit(solution)/shard_map/ppermute | solution.py:15
  80.0 1.6 %collective-permute-start.29 = (bf16[384,256]{1,0:T(8,128)(2,1)S(1)}, bf16[384,256]{1,0:T(8,128)(2,1)S(1)}, u32[]{:S(2)}, u32[]{:S(2)}) collective-permute-start(bf16[384,256]{1,0:T(8,128)(2,1)S(1)} %collective-permute-done.25.refs_1_), channel_id=1, source_target_pairs={{0,4},{4,0},{8,12},{12,8},{16,20},{20,16},{24,28},{28,24},{1,5},{5... | collective-permute-start | bytes 589832 | tf_op jit(solution)/shard_map/ppermute | solution.py:15

commit v3 on v2

--- a/solution.py
+++ b/solution.py
@@ -258,22 +258,24 @@
 
 
 def stack_kernel(*refs):
-    out = refs[-1]
-    capacity = refs[0].shape[0]
-    for s, ref in enumerate(refs[-2::-1]):
-        out[s * capacity : (s + 1) * capacity, :] = ref[...]
-
-
-def join_kernel(columns, stay_t, stay_s, *refs):
+    moved, out = refs[:-2], refs[-2:]
+    capacity, both = moved[0].shape
+    for s, ref in enumerate(moved[::-1]):
+        for i in range(2):
+            out[i][s * capacity : (s + 1) * capacity, :] = ref[
+                :, i * (both // 2) : (i + 1) * (both // 2)
+            ]
+
+
+def join_kernel(columns, stay, *refs):
     _, _, column = place()
-    parts, flats = refs[:-2], refs[-2:]
-    capacity = stay_t.shape[0]
-    feat = parts[0].shape[1] // 2
-    for i, stay in enumerate((stay_t, stay_s)):
-        flats[i][:capacity, :] = stay[...]
-        for m in range(columns):
-            cols = pl.ds(pl.multiple_of((column ^ m) * feat, feat), feat)
-            flats[i][capacity:, cols] = parts[m][:, i * feat : (i + 1) * feat]
+    parts, flat = refs[:-1], refs[-1]
+    capacity = stay.shape[0]
+    feat = parts[0].shape[1]
+    flat[:capacity, :] = stay[...]
+    for m in range(columns):
+        cols = pl.ds(pl.multiple_of((column ^ m) * feat, feat), feat)
+        flat[capacity:, cols] = parts[m][...]
 
 
 def part_pieces(hidden, w2, which, columns, out):
@@ -461,13 +463,14 @@
             scratch=[pltpu.SemaphoreType.DMA((len(weights),))],
         )
 
-    def forward(flats, w1, w2, keep_pre, name):
+    def forward(flats, w1, w2, keep_pre, name, units=0):
         half, count = plane_rows // 2, len(flats)
         pre = [shape(half, hid, dtype=f32)] * count if keep_pre else []
         return call(
             lambda *refs: forward_kernel(columns, count, *refs),
             [shape(count, columns, half, piece)] + [shape(half, hid)] * count + pre,
             [*flats, w1, w2],
+            flops=units * plane_rows * width * hid,
             name=name,
         )
 
@@ -476,7 +479,7 @@
             lambda *refs: keep_kernel(columns, *refs),
             [shape(columns, plane_rows // 2, piece)] * 2 + outs,
             [own, other, w2, *state],
-            flops=(64 if state else 1) * plane_rows * width * hid,
+            flops=(64 if state else 8) * plane_rows * width * hid,
             name="keep_s" if state else "keep_t",
         )
 
@@ -515,11 +518,12 @@
     stay_t, stay_s = stay(teacher_in, route_t), stay(student_in, route_s)
     routes = jnp.concatenate([route_t, route_s], axis=0)
     other_routes = across(routes)
-    moved = after(over_planes(sent), stay_t, stay_s, other_routes)
-    got = spread(
-        call(stack_kernel, [shape((experts - 1) * capacity, 2 * feat)], moved, name="stack")[0]
-    )
     w1_t, w2_t = load(teacher_w1[0], teacher_w2[0])
+    moved = after(over_planes(sent), stay_t, stay_s, other_routes, w1_t)
+    mine_t, mine_s = call(
+        stack_kernel, [shape((experts - 1) * capacity, feat)] * 2, moved, name="stack"
+    )
+    got_t, got_s = spread(mine_t), spread(mine_s)
     w1_s, w2_s = load(student_w1[0], student_w2[0])
     (maps,) = call(
         lambda *refs: map_kernel(experts, capacity, *refs),
@@ -527,24 +531,28 @@
         [routes, other_routes],
         name="maps",
     )
-    flat_t_own, flat_own = call(
-        lambda *refs: join_kernel(columns, *refs),
-        [shape(plane_rows // 2, width)] * 2,
-        [stay_t, stay_s, *after(got, w1_t, w1_s, maps)],
-        name="join",
-    )
+
+    def join(rows, got):
+        return call(
+            lambda *refs: join_kernel(columns, *refs),
+            [shape(plane_rows // 2, width)],
+            [rows, *got],
+            name="join",
+        )[0]
+
+    flat_t_own = join(stay_t, after(got_t, maps))
     flat_t_other = across(flat_t_own)
-    flat_other = across(flat_own)
-
-    send, hidden_own = forward([flat_t_own], w1_t, w2_t, False, "forward_t")
+
+    send, hidden_own = forward([flat_t_own], w1_t, w2_t, False, "forward_t", 24)
     got_own = across(send)
-    send, hidden_other = forward([flat_t_other], w1_t, w2_t, False, "forward_t")
+    send, hidden_other = forward([flat_t_other], w1_t, w2_t, False, "forward_t", 0)
     got_other = across(send)
-    kept = keep(hidden_own, hidden_other, w2_t, [], [])
+    kept = keep(hidden_own, after(hidden_other, got_s, w1_s), w2_t, [], [])
     pieces_t = pair(kept, [got_own, got_other])
     sums_t = collect(*pieces_t)
 
-    flat_own, flat_other = after((flat_own, flat_other), pieces_t[0])
+    flat_own = join(stay_s, after(got_s, pieces_t[0]))
+    flat_other = across(flat_own)
     send, hidden_own, hidden_other, pre_own, pre_other = forward(
         [flat_own, flat_other], w1_s, w2_s, True, "forward_s"
     )
@@ -565,16 +573,16 @@
         [shape(2 * capacity, piece)] * experts,
         after(sums_t, pieces_s[0]),
     )
-    home = [*over_planes(home[:-1]), home[-1]]
+    *sent, near, own = home
+    home = [*over_planes([*sent, after(near, sums_s[1])]), own]
     slots = call(
         lambda *refs: home_kernel(experts, capacity, *refs),
         [shape(2 * capacity, piece)] * experts,
         [maps, *home],
-        flops=4 * plane_rows * width * hid,
+        flops=0 * plane_rows * width * hid,
         name="home",
     )
-    *sent, near, own = slots
-    teachers = [*over_planes([*sent, after(near, sums_s[1])]), own]
+    teachers = [*over_planes(slots[:-1]), slots[-1]]
     (upstream,) = call(
         lambda *refs: upstream_kernel(columns, experts, loss_scale, *refs),
         [shape(plane_rows, piece)],
@@ -615,9 +623,9 @@
 
     grads = spread(upstream)
     state = backward({(0, 0): upstream, (1, 0): across(upstream)}, None, False)
-    *near, far = after(grads[1:], state[1])
+    far = after(grads[3], state[1])
     state = backward({(0, 3): far}, state, False)
-    near = after(near, state[1])
+    near = after(grads[1:3], state[1])
     others = [across(value) for value in (*near, far)]
     state = backward({(0, m + 1): near[m] for m in range(2)}, state, False)
     grad_second, grad_first = backward(

time: 84.9 us -> 81.5 us (0.960)
  waiting for transfers between devices: 28.8 us -> 21 us
  starting transfers between devices: 29.3 us -> 35.5 us
  local copies, waits for them, and re-layouts: 7.44 us -> 5.54 us
    ppermute x31 -> x34, waiting for transfers between devices: 28.8 us -> 21 us  [partner(): lax.ppermute(value, axis, [(i, i ^ mask) for i in range(lax.axis_size(axi...]
    ppermute x31 -> x34, starting transfers between devices: 29.3 us -> 35.5 us  [partner(): lax.ppermute(value, axis, [(i, i ^ mask) for i in range(lax.axis_size(axi...]
    unnamed x16, local copies, waits for them, and re-layouts: 7.44 us -> 5.54 us
    pallas_call x22 -> x23, Pallas kernels: 17.5 us -> 17.5 us  [call(): pl.pallas_call(kernel, name=name, out_shape=outs, in_specs=in_specs or [V...]
  transfers between devices with their start and end apart: 31 -> 34, of which waited for: 14 -> 15; matrix products, arithmetic and copies ran while one was open for 1% -> 1% of each run, Pallas kernels for 14% -> 15%
where the time goes in v3:
time: 81.5 us; the launch traced here: 81.2 us
  starting transfers between devices  35.5 us (44%)
  waiting for transfers between devices  21 us (26%)
  Pallas kernels  17.5 us (21%)
  local copies, waits for them, and re-layouts  5.54 us (7%)
  between operations  0.97 us (1%)
    ppermute x34, starting transfers between devices, partner(): lax.ppermute(value, axis, [(i, i ^ mask) for i in range(lax.axis_size(axi...  35.5 us
    ppermute x34, waiting for transfers between devices, partner(): lax.ppermute(value, axis, [(i, i ^ mask) for i in range(lax.axis_size(axi...  21 us
    pallas_call x23, Pallas kernels, call(): pl.pallas_call(kernel, name=name, out_shape=outs, in_specs=in_specs or [V...  17.5 us
    unnamed x16, local copies, waits for them, and re-layouts  5.54 us
  transfers between devices with their start and end apart: 34, of which 15 were waited for; matrix products, arithmetic and copies ran while one was open for 1% of the time, Pallas kernels for 15%

profile of v3, /device:TPU:0, one launch (start us, length us, event | category | flops | bytes accessed | tf_op | source)
XLA Modules:
  0.0 81.2 jit_solution(6203296244460337290)
XLA Ops:
  0.6 2.2 %pack.1 = (bf16[48,1024]{1,0:T(8,128)(2,1)}, bf16[48,1024]{1,0:T(8,128)(2,1)}, bf16[48,1024]{1,0:T(8,128)(2,1)}) custom-call(bf16[128,2048]{1,0:T(8,128)(2,1)} %refs_0_.5, bf16[128,2048]{1,0:T(8,128)(2,1)} %refs_1_.1, s32[1,128]{1,0:T(1,128)} %bitcast.12, s32[1,128]{1,0:T(1,128)} %bitcast.15), custom_call_target="tpu_custom_call" | custom-call | tf_op jit(solution)/shard_map/pack/pallas_call | solution.py:168
  2.9 5.1 %collective-permute-start = (bf16[48,1024]{1,0:T(8,128)(2,1)}, bf16[48,1024]{1,0:T(8,128)(2,1)S(1)}, u32[]{:S(2)}, u32[]{:S(2)}) collective-permute-start(bf16[48,1024]{1,0:T(8,128)(2,1)} %get-tuple-element.71), channel_id=1, source_target_pairs={{0,24},{4,28},{8,16},{12,20},{16,8},{20,12},{24,0},{28,4},{1,25},{... | collective-permute-start | bytes 294920 | tf_op jit(solution)/shard_map/ppermute | solution.py:15
  8.0 0.6 collective-permute-start.2
  8.6 0.7 pad_add_fusion.refs_0_
  9.3 1.0 %copy-done = bf16[128,2048]{1,0:T(8,128)(2,1)S(1)} copy-done((bf16[128,2048]{1,0:T(8,128)(2,1)S(1)}, bf16[128,2048]{1,0:T(8,128)(2,1)}, u32[]{:S(2)}) %copy-start) | copy-done | bytes 524312
  10.4 0.7 copy-done.6
  11.0 0.3 stay.3.refs_0_
  11.4 0.6 copy-done.7
  12.0 0.3 stay.2.refs_0_
  12.4 1.6 %copy-done.2 = bf16[1,2048,512]{2,1,0:T(8,128)(2,1)S(1)} copy-done((bf16[1,2048,512]{2,1,0:T(8,128)(2,1)S(1)}, bf16[1,2048,512]{2,1,0:T(8,128)(2,1)}, u32[]{:S(2)}) %copy-start.2) | copy-done | bytes 2097176
  14.0 1.6 %copy-done.3 = bf16[1,512,2048]{2,1,0:T(8,128)(2,1)S(1)} copy-done((bf16[1,512,2048]{2,1,0:T(8,128)(2,1)S(1)}, bf16[1,512,2048]{2,1,0:T(8,128)(2,1)}, u32[]{:S(2)}) %copy-start.3) | copy-done | bytes 2097176
  15.6 0.3 load.2
  15.9 0.6 collective-permute-done.1.refs_1_
  16.5 2.5 %collective-permute-start.9 = (bf16[144,512]{1,0:T(8,128)(2,1)S(1)}, bf16[144,512]{1,0:T(8,128)(2,1)S(1)}, u32[]{:S(2)}, u32[]{:S(2)}) collective-permute-start(bf16[144,512]{1,0:T(8,128)(2,1)S(1)} %get-tuple-element.80.refs_1_), channel_id=1, source_target_pairs={{0,3},{1,2},{2,1},{3,0},{4,7},{5,6},{6,5},{7,4},{8,11},{9,10},{10,... | collective-permute-start | bytes 442376 | tf_op jit(solution)/shard_map/ppermute | solution.py:15
  19.0 0.5 collective-permute-start.8
  19.5 0.5 collective-permute-start.7
  20.0 0.4 maps.1.refs_0_
  20.4 2.5 %collective-permute-start.6 = (bf16[144,512]{1,0:T(8,128)(2,1)S(1)}, bf16[144,512]{1,0:T(8,128)(2,1)S(1)}, u32[]{:S(2)}, u32[]{:S(2)}) collective-permute-start(bf16[144,512]{1,0:T(8,128)(2,1)S(1)} %get-tuple-element.94.refs_1_), channel_id=1, source_target_pairs={{0,3},{1,2},{2,1},{3,0},{4,7},{5,6},{6,5},{7,4},{8,11},{9,10},{10,... | collective-permute-start | bytes 442376 | tf_op jit(solution)/shard_map/ppermute | solution.py:15
  22.9 0.5 collective-permute-start.5
  23.4 0.2 collective-permute-done.9.refs_4_
  23.7 2.0 %collective-permute-start.4 = (bf16[144,512]{1,0:T(8,128)(2,1)S(1)}, bf16[144,512]{1,0:T(8,128)(2,1)S(1)}, u32[]{:S(2)}, u32[]{:S(2)}) collective-permute-start(bf16[144,512]{1,0:T(8,128)(2,1)S(1)} %get-tuple-element.94.refs_1_), channel_id=1, source_target_pairs={{0,1},{1,0},{2,3},{3,2},{4,5},{5,4},{6,7},{7,6},{8,9},{9,8},{10,11... | collective-permute-start | bytes 442376 | tf_op jit(solution)/shard_map/ppermute | solution.py:15
  25.7 1.7 %collective-permute-done.8.refs_3_ = bf16[144,512]{1,0:T(8,128)(2,1)S(1)} collective-permute-done((bf16[144,512]{1,0:T(8,128)(2,1)S(1)}, bf16[144,512]{1,0:T(8,128)(2,1)S(1)}, u32[]{:S(2)}, u32[]{:S(2)}) %collective-permute-start.8) | collective-permute-done | bytes 147488 | tf_op jit(solution)/shard_map/ppermute | solution.py:15
  27.6 0.9 %forward_t.2 = (bf16[1,4,192,256]{3,2,1,0:T(8,128)(2,1)S(1)}, bf16[192,512]{1,0:T(8,128)(2,1)S(1)}) custom-call(bf16[192,2048]{1,0:T(8,128)(2,1)S(1)} %join.2.refs_0_, bf16[2048,512]{1,0:T(8,128)(2,1)S(1)} %get-tuple-element.74.refs_1_, bf16[512,2048]{1,0:T(8,128)(2,1)S(1)} %get-tuple-element.84.refs_2_), custom_call_target="tpu_custom_call" | custom-call | flops 9663676416 | tf_op jit(solution)/shard_map/forward_t/pallas_call | solution.py:168
  28.5 0.6 collective-permute-start.11
  29.1 0.7 collective-permute-done.10.refs_0_
  29.8 0.9 %forward_t.3 = (bf16[1,4,192,256]{3,2,1,0:T(8,128)(2,1)S(1)}, bf16[192,512]{1,0:T(8,128)(2,1)S(1)}) custom-call(bf16[192,2048]{1,0:T(8,128)(2,1)S(1)} %collective-permute-done.10.refs_0_, bf16[2048,512]{1,0:T(8,128)(2,1)S(1)} %get-tuple-element.74.refs_1_, bf16[512,2048]{1,0:T(8,128)(2,1)S(1)} %get-tuple-element.84.refs_2_), custom_call_target="tpu_custom_call" | custom-call | tf_op jit(solution)/shard_map/forward_t/pallas_call | solution.py:168
  30.8 0.2 collective-permute-start.12
  31.0 0.3 load.3
  31.3 1.4 %collective-permute-done.5.refs_3_ = bf16[144,512]{1,0:T(8,128)(2,1)S(1)} collective-permute-done((bf16[144,512]{1,0:T(8,128)(2,1)S(1)}, bf16[144,512]{1,0:T(8,128)(2,1)S(1)}, u32[]{:S(2)}, u32[]{:S(2)}) %collective-permute-start.5) | collective-permute-done | bytes 147488 | tf_op jit(solution)/shard_map/ppermute | solution.py:15
  32.7 0.3 collective-permute-done.4.refs_2_
  32.9 0.6 keep_t.1
  33.6 0.2 pair.2
  33.9 1.6 %collective-permute-start.18 = (bf16[384,256]{1,0:T(8,128)(2,1)S(1)}, bf16[384,256]{1,0:T(8,128)(2,1)S(1)}, u32[]{:S(2)}, u32[]{:S(2)}) collective-permute-start(bf16[384,256]{1,0:T(8,128)(2,1)S(1)} %get-tuple-element.110), channel_id=1, source_target_pairs={{0,1},{1,0},{2,3},{3,2},{4,5},{5,4},{6,7},{7,6},{8,9},{9,8},{10,11... | collective-permute-start | bytes 589832 | tf_op jit(solution)/shard_map/ppermute | solution.py:15
  35.5 0.6 collective-permute-start.19
  36.1 1.4 %collective-permute-start.20 = (bf16[384,256]{1,0:T(8,128)(2,1)S(1)}, bf16[384,256]{1,0:T(8,128)(2,1)S(1)}, u32[]{:S(2)}, u32[]{:S(2)}) collective-permute-start(bf16[384,256]{1,0:T(8,128)(2,1)S(1)} %get-tuple-element.112), channel_id=1, source_target_pairs={{0,3},{1,2},{2,1},{3,0},{4,7},{5,6},{6,5},{7,4},{8,11},{9,10},{10,... | collective-permute-start | bytes 589832 | tf_op jit(solution)/shard_map/ppermute | solution.py:15
  37.5 1.7 %forward_s.1 = (bf16[2,4,192,256]{3,2,1,0:T(8,128)(2,1)S(1)}, bf16[192,512]{1,0:T(8,128)(2,1)S(1)}, bf16[192,512]{1,0:T(8,128)(2,1)S(1)}, f32[192,512]{1,0:T(8,128)S(1)}, f32[192,512]{1,0:T(8,128)S(1)}) custom-call(bf16[192,2048]{1,0:T(8,128)(2,1)S(1)} %join.3.refs_0_.refs_5_, bf16[192,2048]{1,0:T(8,128)(2,1)S(1)} %collective-permute-done.13.refs_1_.refs_6_, ...), custom_call_target="tpu_custom_call" | custom-call | tf_op jit(solution)/shard_map/forward_s/pallas_call | solution.py:168
  39.3 1.4 %keep_s.1 = (bf16[4,192,256]{2,1,0:T(8,128)(2,1)S(1)}, bf16[4,192,256]{2,1,0:T(8,128)(2,1)S(1)}, bf16[2048,384]{1,0:T(8,128)(2,1)S(1)}, bf16[512,384]{1,0:T(8,128)(2,1)S(1)}, f32[384,512]{1,0:T(8,128)S(1)}) custom-call(bf16[192,512]{1,0:T(8,128)(2,1)S(1)} %get-tuple-element.99.refs_0_, bf16[192,512]{1,0:T(8,128)(2,1)S(1)} %get-tuple-element.100.refs_1_, ...), custom_call_target="tpu_custom_call" | custom-call | flops 25769803776 | tf_op jit(solution)/shard_map/keep_s/pallas_call | solution.py:168
  40.7 0.9 %collective-permute-done.14.refs_2_ = bf16[2,4,192,256]{3,2,1,0:T(8,128)(2,1)S(1)} collective-permute-done((bf16[2,4,192,256]{3,2,1,0:T(8,128)(2,1)S(1)}, bf16[2,4,192,256]{3,2,1,0:T(8,128)(2,1)S(1)}, u32[]{:S(2)}, u32[]{:S(2)}) %collective-permute-start.14) | collective-permute-done | bytes 786464 | tf_op jit(solution)/shard_map/ppermute | solution.py:15
  41.6 0.2 pair.3
  41.7 1.6 %collective-permute-start.15 = (bf16[384,256]{1,0:T(8,128)(2,1)S(1)}, bf16[384,256]{1,0:T(8,128)(2,1)S(1)}, u32[]{:S(2)}, u32[]{:S(2)}) collective-permute-start(bf16[384,256]{1,0:T(8,128)(2,1)S(1)} %get-tuple-element.107), channel_id=1, source_target_pairs={{0,1},{1,0},{2,3},{3,2},{4,5},{5,4},{6,7},{7,6},{8,9},{9,8},{10,11... | collective-permute-start | bytes 589832 | tf_op jit(solution)/shard_map/ppermute | solution.py:15
  43.3 0.6 collective-permute-start.16
  43.9 1.4 %collective-permute-start.17 = (bf16[384,256]{1,0:T(8,128)(2,1)S(1)}, bf16[384,256]{1,0:T(8,128)(2,1)S(1)}, u32[]{:S(2)}, u32[]{:S(2)}) collective-permute-start(bf16[384,256]{1,0:T(8,128)(2,1)S(1)} %get-tuple-element.109), channel_id=1, source_target_pairs={{0,3},{1,2},{2,1},{3,0},{4,7},{5,6},{6,5},{7,4},{8,11},{9,10},{10,... | collective-permute-start | bytes 589832 | tf_op jit(solution)/shard_map/ppermute | solution.py:15
  45.3 1.6 %collective-permute-done.19.refs_2_ = bf16[384,256]{1,0:T(8,128)(2,1)S(1)} collective-permute-done((bf16[384,256]{1,0:T(8,128)(2,1)S(1)}, bf16[384,256]{1,0:T(8,128)(2,1)S(1)}, u32[]{:S(2)}, u32[]{:S(2)}) %collective-permute-start.19) | collective-permute-done | bytes 196640 | tf_op jit(solution)/shard_map/ppermute | solution.py:15
  46.9 0.1 shard_map.95
  47.0 3.7 %collective-permute-start.21 = (bf16[96,256]{1,0:T(8,128)(2,1)S(1)}, bf16[96,256]{1,0:T(8,128)(2,1)S(1)}, u32[]{:S(2)}, u32[]{:S(2)}) collective-permute-start(bf16[96,256]{1,0:T(8,128)(2,1)S(1)} %get-tuple-element.117), channel_id=1, source_target_pairs={{0,24},{4,28},{8,16},{12,20},{16,8},{20,12},{24,0},{28,4},{1,25},{... | collective-permute-start | bytes 147464 | tf_op jit(solution)/shard_map/ppermute | solution.py:15
  50.7 0.8 collective-permute-start.23
  51.4 1.6 %collective-permute-done.21.refs_1_ = bf16[96,256]{1,0:T(8,128)(2,1)S(1)} collective-permute-done((bf16[96,256]{1,0:T(8,128)(2,1)S(1)}, bf16[96,256]{1,0:T(8,128)(2,1)S(1)}, u32[]{:S(2)}, u32[]{:S(2)}) %collective-permute-start.21) | collective-permute-done | bytes 49184 | tf_op jit(solution)/shard_map/ppermute | solution.py:15
  53.0 2.6 %collective-permute-done.22.refs_2_ = bf16[96,256]{1,0:T(8,128)(2,1)S(1)} collective-permute-done((bf16[96,256]{1,0:T(8,128)(2,1)S(1)}, bf16[96,256]{1,0:T(8,128)(2,1)S(1)}, u32[]{:S(2)}, u32[]{:S(2)}) %collective-permute-start.22) | collective-permute-done | bytes 49184 | tf_op jit(solution)/shard_map/ppermute | solution.py:15
  55.6 0.2 home.1
  55.8 2.3 %collective-permute-start.24 = (bf16[96,256]{1,0:T(8,128)(2,1)S(1)}, bf16[96,256]{1,0:T(8,128)(2,1)S(1)}, u32[]{:S(2)}, u32[]{:S(2)}) collective-permute-start(bf16[96,256]{1,0:T(8,128)(2,1)S(1)} %get-tuple-element.122), channel_id=1, source_target_pairs={{0,24},{4,28},{8,16},{12,20},{16,8},{20,12},{24,0},{28,4},{1,25},{... | collective-permute-start | bytes 147464 | tf_op jit(solution)/shard_map/ppermute | solution.py:15
  58.1 2.2 %collective-permute-start.26 = (bf16[96,256]{1,0:T(8,128)(2,1)S(1)}, bf16[96,256]{1,0:T(8,128)(2,1)S(1)}, u32[]{:S(2)}, u32[]{:S(2)}) collective-permute-start(bf16[96,256]{1,0:T(8,128)(2,1)S(1)} %get-tuple-element.124), channel_id=1, source_target_pairs={{0,8},{4,12},{8,0},{12,4},{16,24},{20,28},{24,16},{28,20},{1,9},{5... | collective-permute-start | bytes 147464 | tf_op jit(solution)/shard_map/ppermute | solution.py:15
  60.3 1.6 %collective-permute-done.24.refs_4_ = bf16[96,256]{1,0:T(8,128)(2,1)S(1)} collective-permute-done((bf16[96,256]{1,0:T(8,128)(2,1)S(1)}, bf16[96,256]{1,0:T(8,128)(2,1)S(1)}, u32[]{:S(2)}, u32[]{:S(2)}) %collective-permute-start.24) | collective-permute-done | bytes 49184 | tf_op jit(solution)/shard_map/ppermute | solution.py:15
  61.9 1.5 %collective-permute-done.25.refs_5_ = bf16[96,256]{1,0:T(8,128)(2,1)S(1)} collective-permute-done((bf16[96,256]{1,0:T(8,128)(2,1)S(1)}, bf16[96,256]{1,0:T(8,128)(2,1)S(1)}, u32[]{:S(2)}, u32[]{:S(2)}) %collective-permute-start.25) | collective-permute-done | bytes 49184 | tf_op jit(solution)/shard_map/ppermute | solution.py:15
  63.5 0.1 shard_map.96.refs_0_
  63.7 1.5 %collective-permute-start.29 = (bf16[384,256]{1,0:T(8,128)(2,1)S(1)}, bf16[384,256]{1,0:T(8,128)(2,1)S(1)}, u32[]{:S(2)}, u32[]{:S(2)}) collective-permute-start(bf16[384,256]{1,0:T(8,128)(2,1)S(1)} %shard_map.96.refs_0_), channel_id=1, source_target_pairs={{0,3},{1,2},{2,1},{3,0},{4,7},{5,6},{6,5},{7,4},{8,11},{9,10},{10,... | collective-permute-start | bytes 589832 | tf_op jit(solution)/shard_map/ppermute | solution.py:15
  65.2 1.1 %collective-permute-start.28 = (bf16[384,256]{1,0:T(8,128)(2,1)S(1)}, bf16[384,256]{1,0:T(8,128)(2,1)S(1)}, u32[]{:S(2)}, u32[]{:S(2)}) collective-permute-start(bf16[384,256]{1,0:T(8,128)(2,1)S(1)} %shard_map.96.refs_0_), channel_id=1, source_target_pairs={{0,2},{1,3},{2,0},{3,1},{4,6},{5,7},{6,4},{7,5},{8,10},{9,11},{10,... | collective-permute-start | bytes 589832 | tf_op jit(solution)/shard_map/ppermute | solution.py:15
  66.3 0.9 %collective-permute-start.27 = (bf16[384,256]{1,0:T(8,128)(2,1)S(1)}, bf16[384,256]{1,0:T(8,128)(2,1)S(1)}, u32[]{:S(2)}, u32[]{:S(2)}) collective-permute-start(bf16[384,256]{1,0:T(8,128)(2,1)S(1)} %shard_map.96.refs_0_), channel_id=1, source_target_pairs={{0,1},{1,0},{2,3},{3,2},{4,5},{5,4},{6,7},{7,6},{8,9},{9,8},{10,11... | collective-permute-start | bytes 589832 | tf_op jit(solution)/shard_map/ppermute | solution.py:15
  67.2 1.5 %shard_map.97 = (bf16[512,2048]{1,0:T(8,128)(2,1)}, f32[384,512]{1,0:T(8,128)S(1)}) custom-call(bf16[384,256]{1,0:T(8,128)(2,1)S(1)} %shard_map.96.refs_0_, bf16[384,256]{1,0:T(8,128)(2,1)S(1)} %collective-permute-done.30.refs_1_, bf16[512,384]{1,0:T(8,128)(2,1)S(1)} %get-tuple-element.126.refs_2_.refs_1_.refs_3_, ...), custom_call_target="tpu_custom_call" | custom-call | tf_op jit(solution)/shard_map/pallas_call | solution.py:168
  68.7 3.7 %collective-permute-done.29.refs_0_ = bf16[384,256]{1,0:T(8,128)(2,1)S(1)} collective-permute-done((bf16[384,256]{1,0:T(8,128)(2,1)S(1)}, bf16[384,256]{1,0:T(8,128)(2,1)S(1)}, u32[]{:S(2)}, u32[]{:S(2)}) %collective-permute-start.29) | collective-permute-done | bytes 196640 | tf_op jit(solution)/shard_map/ppermute | solution.py:15
  72.4 1.1 %shard_map.98 = (bf16[512,2048]{1,0:T(8,128)(2,1)}, f32[384,512]{1,0:T(8,128)S(1)}) custom-call(bf16[384,256]{1,0:T(8,128)(2,1)S(1)} %collective-permute-done.29.refs_0_, bf16[512,384]{1,0:T(8,128)(2,1)S(1)} %get-tuple-element.126.refs_2_.refs_1_.refs_3_, ...), custom_call_target="tpu_custom_call", output_to_operand_aliasing={{0}: (4, {})} | custom-call | tf_op jit(solution)/shard_map/pallas_call | solution.py:168
  73.5 2.6 %collective-permute-done.28.refs_1_ = bf16[384,256]{1,0:T(8,128)(2,1)S(1)} collective-permute-done((bf16[384,256]{1,0:T(8,128)(2,1)S(1)}, bf16[384,256]{1,0:T(8,128)(2,1)S(1)}, u32[]{:S(2)}, u32[]{:S(2)}) %collective-permute-start.28) | collective-permute-done | bytes 196640 | tf_op jit(solution)/shard_map/ppermute | solution.py:15
  76.1 0.5 collective-permute-start.32
  76.6 1.5 %shard_map.99 = (bf16[512,2048]{1,0:T(8,128)(2,1)}, f32[384,512]{1,0:T(8,128)S(1)}) custom-call(bf16[384,256]{1,0:T(8,128)(2,1)S(1)} %collective-permute-done.27.refs_0_, bf16[384,256]{1,0:T(8,128)(2,1)S(1)} %collective-permute-done.28.refs_1_, bf16[512,384]{1,0:T(8,128)(2,1)S(1)} %get-tuple-element.126.refs_2_.refs_1_.refs_3_, ...), custom_call_target="tpu_custom_call", output_to_operand_aliasing={{0}: (5, {})} | custom-call | tf_op jit(solution)/shard_map/pallas_call | solution.py:168
  78.2 3.0 %shard_map.100 = (bf16[512,2048]{1,0:T(8,128)(2,1)}, bf16[2048,512]{1,0:T(8,128)(2,1)}) custom-call(bf16[384,256]{1,0:T(8,128)(2,1)S(1)} %collective-permute-done.31.refs_0_, bf16[384,256]{1,0:T(8,128)(2,1)S(1)} %collective-permute-done.32.refs_1_, bf16[384,256]{1,0:T(8,128)(2,1)S(1)} %collective-permute-done.33.refs_2_, ...), custom_call_target="tpu_custom_call", output_to_operand_aliasing={{0}: (6, {})} | custom-call | tf_op jit(solution)/shard_map/pallas_call | solution.py:168
  (44 shorter events, 0.7 us)
Async XLA Ops:
  0.6 10.7 %copy-start.1 = (bf16[128,2048]{1,0:T(8,128)(2,1)S(1)}, bf16[128,2048]{1,0:T(8,128)(2,1)}, u32[]{:S(2)}) copy-start(bf16[128,2048]{1,0:T(8,128)(2,1)} %refs_1_.1) | copy-start | bytes 1572868
  2.9 13.0 %collective-permute-start = (bf16[48,1024]{1,0:T(8,128)(2,1)}, bf16[48,1024]{1,0:T(8,128)(2,1)S(1)}, u32[]{:S(2)}, u32[]{:S(2)}) collective-permute-start(bf16[48,1024]{1,0:T(8,128)(2,1)} %get-tuple-element.71), channel_id=1, source_target_pairs={{0,24},{4,28},{8,16},{12,20},{16,8},{20,12},{24,0},{28,4},{1,25},{... | collective-permute-start | bytes 294920 | tf_op jit(solution)/shard_map/ppermute | solution.py:15
  8.0 8.5 %collective-permute-start.1 = (bf16[48,1024]{1,0:T(8,128)(2,1)}, bf16[48,1024]{1,0:T(8,128)(2,1)S(1)}, u32[]{:S(2)}, u32[]{:S(2)}) collective-permute-start(bf16[48,1024]{1,0:T(8,128)(2,1)} %get-tuple-element.72), channel_id=1, source_target_pairs={{0,16},{4,20},{8,24},{12,28},{16,0},{20,4},{24,8},{28,12},{1,17},{... | collective-permute-start | bytes 294920 | tf_op jit(solution)/shard_map/ppermute | solution.py:15
  8.0 8.5 %collective-permute-start.2 = (bf16[48,1024]{1,0:T(8,128)(2,1)}, bf16[48,1024]{1,0:T(8,128)(2,1)S(1)}, u32[]{:S(2)}, u32[]{:S(2)}) collective-permute-start(bf16[48,1024]{1,0:T(8,128)(2,1)} %get-tuple-element.73), channel_id=1, source_target_pairs={{0,8},{4,12},{8,0},{12,4},{16,24},{20,28},{24,16},{28,20},{1,9},{5... | collective-permute-start | bytes 294920 | tf_op jit(solution)/shard_map/ppermute | solution.py:15
  9.3 6.6 %collective-permute-start.3 = (s32[2,128]{1,0:T(2,128)S(1)}, s32[2,128]{1,0:T(2,128)S(1)}, u32[]{:S(2)}, u32[]{:S(2)}) collective-permute-start(s32[2,128]{1,0:T(2,128)S(1)} %pad_add_fusion.refs_0_), channel_id=1, source_target_pairs={{0,4},{4,0},{8,12},{12,8},{16,20},{20,16},{24,28},{28,24},{1,5},{5... | collective-permute-start | bytes 3080 | tf_op jit(solution)/shard_map/ppermute | solution.py:15
  9.3 1.0 %copy-start = (bf16[128,2048]{1,0:T(8,128)(2,1)S(1)}, bf16[128,2048]{1,0:T(8,128)(2,1)}, u32[]{:S(2)}) copy-start(bf16[128,2048]{1,0:T(8,128)(2,1)} %refs_0_.5) | copy-start | bytes 1572868
  10.4 0.7 copy-start.6
  11.4 0.7 copy-start.7
  12.4 1.6 %copy-start.2 = (bf16[1,2048,512]{2,1,0:T(8,128)(2,1)S(1)}, bf16[1,2048,512]{2,1,0:T(8,128)(2,1)}, u32[]{:S(2)}) copy-start(bf16[1,2048,512]{2,1,0:T(8,128)(2,1)} %param.12) | copy-start | bytes 6291460
  14.0 1.6 %copy-start.3 = (bf16[1,512,2048]{2,1,0:T(8,128)(2,1)S(1)}, bf16[1,512,2048]{2,1,0:T(8,128)(2,1)}, u32[]{:S(2)}) copy-start(bf16[1,512,2048]{2,1,0:T(8,128)(2,1)} %param.13) | copy-start | bytes 6291460
  16.5 7.2 %collective-permute-start.9 = (bf16[144,512]{1,0:T(8,128)(2,1)S(1)}, bf16[144,512]{1,0:T(8,128)(2,1)S(1)}, u32[]{:S(2)}, u32[]{:S(2)}) collective-permute-start(bf16[144,512]{1,0:T(8,128)(2,1)S(1)} %get-tuple-element.80.refs_1_), channel_id=1, source_target_pairs={{0,3},{1,2},{2,1},{3,0},{4,7},{5,6},{6,5},{7,4},{8,11},{9,10},{10,... | collective-permute-start | bytes 442376 | tf_op jit(solution)/shard_map/ppermute | solution.py:15
  19.0 8.3 %collective-permute-start.8 = (bf16[144,512]{1,0:T(8,128)(2,1)S(1)}, bf16[144,512]{1,0:T(8,128)(2,1)S(1)}, u32[]{:S(2)}, u32[]{:S(2)}) collective-permute-start(bf16[144,512]{1,0:T(8,128)(2,1)S(1)} %get-tuple-element.80.refs_1_), channel_id=1, source_target_pairs={{0,2},{1,3},{2,0},{3,1},{4,6},{5,7},{6,4},{7,5},{8,10},{9,11},{10,... | collective-permute-start | bytes 442376 | tf_op jit(solution)/shard_map/ppermute | solution.py:15
  19.5 7.9 %collective-permute-start.7 = (bf16[144,512]{1,0:T(8,128)(2,1)S(1)}, bf16[144,512]{1,0:T(8,128)(2,1)S(1)}, u32[]{:S(2)}, u32[]{:S(2)}) collective-permute-start(bf16[144,512]{1,0:T(8,128)(2,1)S(1)} %get-tuple-element.80.refs_1_), channel_id=1, source_target_pairs={{0,1},{1,0},{2,3},{3,2},{4,5},{5,4},{6,7},{7,6},{8,9},{9,8},{10,11... | collective-permute-start | bytes 442376 | tf_op jit(solution)/shard_map/ppermute | solution.py:15
  20.4 10.9 %collective-permute-start.6 = (bf16[144,512]{1,0:T(8,128)(2,1)S(1)}, bf16[144,512]{1,0:T(8,128)(2,1)S(1)}, u32[]{:S(2)}, u32[]{:S(2)}) collective-permute-start(bf16[144,512]{1,0:T(8,128)(2,1)S(1)} %get-tuple-element.94.refs_1_), channel_id=1, source_target_pairs={{0,3},{1,2},{2,1},{3,0},{4,7},{5,6},{6,5},{7,4},{8,11},{9,10},{10,... | collective-permute-start | bytes 442376 | tf_op jit(solution)/shard_map/ppermute | solution.py:15
  22.9 9.7 %collective-permute-start.5 = (bf16[144,512]{1,0:T(8,128)(2,1)S(1)}, bf16[144,512]{1,0:T(8,128)(2,1)S(1)}, u32[]{:S(2)}, u32[]{:S(2)}) collective-permute-start(bf16[144,512]{1,0:T(8,128)(2,1)S(1)} %get-tuple-element.94.refs_1_), channel_id=1, source_target_pairs={{0,2},{1,3},{2,0},{3,1},{4,6},{5,7},{6,4},{7,5},{8,10},{9,11},{10,... | collective-permute-start | bytes 442376 | tf_op jit(solution)/shard_map/ppermute | solution.py:15
  23.7 9.3 %collective-permute-start.4 = (bf16[144,512]{1,0:T(8,128)(2,1)S(1)}, bf16[144,512]{1,0:T(8,128)(2,1)S(1)}, u32[]{:S(2)}, u32[]{:S(2)}) collective-permute-start(bf16[144,512]{1,0:T(8,128)(2,1)S(1)} %get-tuple-element.94.refs_1_), channel_id=1, source_target_pairs={{0,1},{1,0},{2,3},{3,2},{4,5},{5,4},{6,7},{7,6},{8,9},{9,8},{10,11... | collective-permute-start | bytes 442376 | tf_op jit(solution)/shard_map/ppermute | solution.py:15
  27.5 2.4 %collective-permute-start.10 = (bf16[192,2048]{1,0:T(8,128)(2,1)S(1)}, bf16[192,2048]{1,0:T(8,128)(2,1)S(1)}, u32[]{:S(2)}, u32[]{:S(2)}) collective-permute-start(bf16[192,2048]{1,0:T(8,128)(2,1)S(1)} %join.2.refs_0_), channel_id=1, source_target_pairs={{0,4},{4,0},{8,12},{12,8},{16,20},{20,16},{24,28},{28,24},{1,5},{5... | collective-permute-start | bytes 2359304 | tf_op jit(solution)/shard_map/ppermute | solution.py:15
  28.5 2.5 %copy-start.4 = (bf16[1,2048,512]{2,1,0:T(8,128)(2,1)S(1)}, bf16[1,2048,512]{2,1,0:T(8,128)(2,1)}, u32[]{:S(2)}) copy-start(bf16[1,2048,512]{2,1,0:T(8,128)(2,1)} %param.14) | copy-start | bytes 6291460
  28.5 2.5 %copy-start.5 = (bf16[1,512,2048]{2,1,0:T(8,128)(2,1)S(1)}, bf16[1,512,2048]{2,1,0:T(8,128)(2,1)}, u32[]{:S(2)}) copy-start(bf16[1,512,2048]{2,1,0:T(8,128)(2,1)} %param.15) | copy-start | bytes 6291460
  28.5 5.0 %collective-permute-start.11 = (bf16[1,4,192,256]{3,2,1,0:T(8,128)(2,1)S(1)}, bf16[1,4,192,256]{3,2,1,0:T(8,128)(2,1)S(1)}, u32[]{:S(2)}, u32[]{:S(2)}) collective-permute-start(bf16[1,4,192,256]{3,2,1,0:T(8,128)(2,1)S(1)} %get-tuple-element.91), channel_id=1, source_target_pairs={{0,4},{4,0},{8,12},{12,8},{16,20},{20,16},{24,28},{28,24},{1,5},{5... | collective-permute-start | bytes 1179656 | tf_op jit(solution)/shard_map/ppermute | solution.py:15
  30.8 2.8 %collective-permute-start.12 = (bf16[1,4,192,256]{3,2,1,0:T(8,128)(2,1)S(1)}, bf16[1,4,192,256]{3,2,1,0:T(8,128)(2,1)S(1)}, u32[]{:S(2)}, u32[]{:S(2)}) collective-permute-start(bf16[1,4,192,256]{3,2,1,0:T(8,128)(2,1)S(1)} %get-tuple-element.92), channel_id=1, source_target_pairs={{0,4},{4,0},{8,12},{12,8},{16,20},{20,16},{24,28},{28,24},{1,5},{5... | collective-permute-start | bytes 1179656 | tf_op jit(solution)/shard_map/ppermute | solution.py:15
  33.8 3.6 %collective-permute-start.13 = (bf16[192,2048]{1,0:T(8,128)(2,1)S(1)}, bf16[192,2048]{1,0:T(8,128)(2,1)S(1)}, u32[]{:S(2)}, u32[]{:S(2)}) collective-permute-start(bf16[192,2048]{1,0:T(8,128)(2,1)S(1)} %join.3.refs_0_.refs_5_), channel_id=1, source_target_pairs={{0,4},{4,0},{8,12},{12,8},{16,20},{20,16},{24,28},{28,24},{1,5},{5... | collective-permute-start | bytes 2359304 | tf_op jit(solution)/shard_map/ppermute | solution.py:15
  33.9 10.0 %collective-permute-start.18 = (bf16[384,256]{1,0:T(8,128)(2,1)S(1)}, bf16[384,256]{1,0:T(8,128)(2,1)S(1)}, u32[]{:S(2)}, u32[]{:S(2)}) collective-permute-start(bf16[384,256]{1,0:T(8,128)(2,1)S(1)} %get-tuple-element.110), channel_id=1, source_target_pairs={{0,1},{1,0},{2,3},{3,2},{4,5},{5,4},{6,7},{7,6},{8,9},{9,8},{10,11... | collective-permute-start | bytes 589832 | tf_op jit(solution)/shard_map/ppermute | solution.py:15
  35.5 11.4 %collective-permute-start.19 = (bf16[384,256]{1,0:T(8,128)(2,1)S(1)}, bf16[384,256]{1,0:T(8,128)(2,1)S(1)}, u32[]{:S(2)}, u32[]{:S(2)}) collective-permute-start(bf16[384,256]{1,0:T(8,128)(2,1)S(1)} %get-tuple-element.111), channel_id=1, source_target_pairs={{0,2},{1,3},{2,0},{3,1},{4,6},{5,7},{6,4},{7,5},{8,10},{9,11},{10,... | collective-permute-start | bytes 589832 | tf_op jit(solution)/shard_map/ppermute | solution.py:15
  36.1 10.8 %collective-permute-start.20 = (bf16[384,256]{1,0:T(8,128)(2,1)S(1)}, bf16[384,256]{1,0:T(8,128)(2,1)S(1)}, u32[]{:S(2)}, u32[]{:S(2)}) collective-permute-start(bf16[384,256]{1,0:T(8,128)(2,1)S(1)} %get-tuple-element.112), channel_id=1, source_target_pairs={{0,3},{1,2},{2,1},{3,0},{4,7},{5,6},{6,5},{7,4},{8,11},{9,10},{10,... | collective-permute-start | bytes 589832 | tf_op jit(solution)/shard_map/ppermute | solution.py:15
  39.2 2.4 %collective-permute-start.14 = (bf16[2,4,192,256]{3,2,1,0:T(8,128)(2,1)S(1)}, bf16[2,4,192,256]{3,2,1,0:T(8,128)(2,1)S(1)}, u32[]{:S(2)}, u32[]{:S(2)}) collective-permute-start(bf16[2,4,192,256]{3,2,1,0:T(8,128)(2,1)S(1)} %get-tuple-element.105), channel_id=1, source_target_pairs={{0,4},{4,0},{8,12},{12,8},{16,20},{20,16},{24,28},{28,24},{1,5},{5... | collective-permute-start | bytes 2359304 | tf_op jit(solution)/shard_map/ppermute | solution.py:15
  41.7 8.9 %collective-permute-start.15 = (bf16[384,256]{1,0:T(8,128)(2,1)S(1)}, bf16[384,256]{1,0:T(8,128)(2,1)S(1)}, u32[]{:S(2)}, u32[]{:S(2)}) collective-permute-start(bf16[384,256]{1,0:T(8,128)(2,1)S(1)} %get-tuple-element.107), channel_id=1, source_target_pairs={{0,1},{1,0},{2,3},{3,2},{4,5},{5,4},{6,7},{7,6},{8,9},{9,8},{10,11... | collective-permute-start | bytes 589832 | tf_op jit(solution)/shard_map/ppermute | solution.py:15
  43.3 17.0 %collective-permute-start.16 = (bf16[384,256]{1,0:T(8,128)(2,1)S(1)}, bf16[384,256]{1,0:T(8,128)(2,1)S(1)}, u32[]{:S(2)}, u32[]{:S(2)}) collective-permute-start(bf16[384,256]{1,0:T(8,128)(2,1)S(1)} %get-tuple-element.108), channel_id=1, source_target_pairs={{0,2},{1,3},{2,0},{3,1},{4,6},{5,7},{6,4},{7,5},{8,10},{9,11},{10,... | collective-permute-start | bytes 589832 | tf_op jit(solution)/shard_map/ppermute | solution.py:15
  43.9 16.4 %collective-permute-start.17 = (bf16[384,256]{1,0:T(8,128)(2,1)S(1)}, bf16[384,256]{1,0:T(8,128)(2,1)S(1)}, u32[]{:S(2)}, u32[]{:S(2)}) collective-permute-start(bf16[384,256]{1,0:T(8,128)(2,1)S(1)} %get-tuple-element.109), channel_id=1, source_target_pairs={{0,3},{1,2},{2,1},{3,0},{4,7},{5,6},{6,5},{7,4},{8,11},{9,10},{10,... | collective-permute-start | bytes 589832 | tf_op jit(solution)/shard_map/ppermute | solution.py:15
  47.0 6.1 %collective-permute-start.21 = (bf16[96,256]{1,0:T(8,128)(2,1)S(1)}, bf16[96,256]{1,0:T(8,128)(2,1)S(1)}, u32[]{:S(2)}, u32[]{:S(2)}) collective-permute-start(bf16[96,256]{1,0:T(8,128)(2,1)S(1)} %get-tuple-element.117), channel_id=1, source_target_pairs={{0,24},{4,28},{8,16},{12,20},{16,8},{20,12},{24,0},{28,4},{1,25},{... | collective-permute-start | bytes 147464 | tf_op jit(solution)/shard_map/ppermute | solution.py:15
  50.7 5.0 %collective-permute-start.22 = (bf16[96,256]{1,0:T(8,128)(2,1)S(1)}, bf16[96,256]{1,0:T(8,128)(2,1)S(1)}, u32[]{:S(2)}, u32[]{:S(2)}) collective-permute-start(bf16[96,256]{1,0:T(8,128)(2,1)S(1)} %get-tuple-element.118), channel_id=1, source_target_pairs={{0,16},{4,20},{8,24},{12,28},{16,0},{20,4},{24,8},{28,12},{1,17},{... | collective-permute-start | bytes 147464 | tf_op jit(solution)/shard_map/ppermute | solution.py:15
  50.7 5.0 %collective-permute-start.23 = (bf16[96,256]{1,0:T(8,128)(2,1)S(1)}, bf16[96,256]{1,0:T(8,128)(2,1)S(1)}, u32[]{:S(2)}, u32[]{:S(2)}) collective-permute-start(bf16[96,256]{1,0:T(8,128)(2,1)S(1)} %get-tuple-element.120), channel_id=1, source_target_pairs={{0,8},{4,12},{8,0},{12,4},{16,24},{20,28},{24,16},{28,20},{1,9},{5... | collective-permute-start | bytes 147464 | tf_op jit(solution)/shard_map/ppermute | solution.py:15
  55.8 6.1 %collective-permute-start.24 = (bf16[96,256]{1,0:T(8,128)(2,1)S(1)}, bf16[96,256]{1,0:T(8,128)(2,1)S(1)}, u32[]{:S(2)}, u32[]{:S(2)}) collective-permute-start(bf16[96,256]{1,0:T(8,128)(2,1)S(1)} %get-tuple-element.122), channel_id=1, source_target_pairs={{0,24},{4,28},{8,16},{12,20},{16,8},{20,12},{24,0},{28,4},{1,25},{... | collective-permute-start | bytes 147464 | tf_op jit(solution)/shard_map/ppermute | solution.py:15
  58.1 5.3 %collective-permute-start.25 = (bf16[96,256]{1,0:T(8,128)(2,1)S(1)}, bf16[96,256]{1,0:T(8,128)(2,1)S(1)}, u32[]{:S(2)}, u32[]{:S(2)}) collective-permute-start(bf16[96,256]{1,0:T(8,128)(2,1)S(1)} %get-tuple-element.123), channel_id=1, source_target_pairs={{0,16},{4,20},{8,24},{12,28},{16,0},{20,4},{24,8},{28,12},{1,17},{... | collective-permute-start | bytes 147464 | tf_op jit(solution)/shard_map/ppermute | solution.py:15
  58.1 5.3 %collective-permute-start.26 = (bf16[96,256]{1,0:T(8,128)(2,1)S(1)}, bf16[96,256]{1,0:T(8,128)(2,1)S(1)}, u32[]{:S(2)}, u32[]{:S(2)}) collective-permute-start(bf16[96,256]{1,0:T(8,128)(2,1)S(1)} %get-tuple-element.124), channel_id=1, source_target_pairs={{0,8},{4,12},{8,0},{12,4},{16,24},{20,28},{24,16},{28,20},{1,9},{5... | collective-permute-start | bytes 147464 | tf_op jit(solution)/shard_map/ppermute | solution.py:15
  63.6 3.6 %collective-permute-start.30 = (bf16[384,256]{1,0:T(8,128)(2,1)S(1)}, bf16[384,256]{1,0:T(8,128)(2,1)S(1)}, u32[]{:S(2)}, u32[]{:S(2)}) collective-permute-start(bf16[384,256]{1,0:T(8,128)(2,1)S(1)} %shard_map.96.refs_0_), channel_id=1, source_target_pairs={{0,4},{4,0},{8,12},{12,8},{16,20},{20,16},{24,28},{28,24},{1,5},{5... | collective-permute-start | bytes 589832 | tf_op jit(solution)/shard_map/ppermute | solution.py:15
  63.7 8.7 %collective-permute-start.29 = (bf16[384,256]{1,0:T(8,128)(2,1)S(1)}, bf16[384,256]{1,0:T(8,128)(2,1)S(1)}, u32[]{:S(2)}, u32[]{:S(2)}) collective-permute-start(bf16[384,256]{1,0:T(8,128)(2,1)S(1)} %shard_map.96.refs_0_), channel_id=1, source_target_pairs={{0,3},{1,2},{2,1},{3,0},{4,7},{5,6},{6,5},{7,4},{8,11},{9,10},{10,... | collective-permute-start | bytes 589832 | tf_op jit(solution)/shard_map/ppermute | solution.py:15
  65.2 10.9 %collective-permute-start.28 = (bf16[384,256]{1,0:T(8,128)(2,1)S(1)}, bf16[384,256]{1,0:T(8,128)(2,1)S(1)}, u32[]{:S(2)}, u32[]{:S(2)}) collective-permute-start(bf16[384,256]{1,0:T(8,128)(2,1)S(1)} %shard_map.96.refs_0_), channel_id=1, source_target_pairs={{0,2},{1,3},{2,0},{3,1},{4,6},{5,7},{6,4},{7,5},{8,10},{9,11},{10,... | collective-permute-start | bytes 589832 | tf_op jit(solution)/shard_map/ppermute | solution.py:15
  66.3 9.8 %collective-permute-start.27 = (bf16[384,256]{1,0:T(8,128)(2,1)S(1)}, bf16[384,256]{1,0:T(8,128)(2,1)S(1)}, u32[]{:S(2)}, u32[]{:S(2)}) collective-permute-start(bf16[384,256]{1,0:T(8,128)(2,1)S(1)} %shard_map.96.refs_0_), channel_id=1, source_target_pairs={{0,1},{1,0},{2,3},{3,2},{4,5},{5,4},{6,7},{7,6},{8,9},{9,8},{10,11... | collective-permute-start | bytes 589832 | tf_op jit(solution)/shard_map/ppermute | solution.py:15
  76.1 2.0 %collective-permute-start.31 = (bf16[384,256]{1,0:T(8,128)(2,1)S(1)}, bf16[384,256]{1,0:T(8,128)(2,1)S(1)}, u32[]{:S(2)}, u32[]{:S(2)}) collective-permute-start(bf16[384,256]{1,0:T(8,128)(2,1)S(1)} %collective-permute-done.27.refs_0_), channel_id=1, source_target_pairs={{0,4},{4,0},{8,12},{12,8},{16,20},{20,16},{24,28},{28,24},{1,5},{5... | collective-permute-start | bytes 589832 | tf_op jit(solution)/shard_map/ppermute | solution.py:15
  76.1 2.0 %collective-permute-start.32 = (bf16[384,256]{1,0:T(8,128)(2,1)S(1)}, bf16[384,256]{1,0:T(8,128)(2,1)S(1)}, u32[]{:S(2)}, u32[]{:S(2)}) collective-permute-start(bf16[384,256]{1,0:T(8,128)(2,1)S(1)} %collective-permute-done.28.refs_1_), channel_id=1, source_target_pairs={{0,4},{4,0},{8,12},{12,8},{16,20},{20,16},{24,28},{28,24},{1,5},{5... | collective-permute-start | bytes 589832 | tf_op jit(solution)/shard_map/ppermute | solution.py:15
  76.6 1.6 %collective-permute-start.33 = (bf16[384,256]{1,0:T(8,128)(2,1)S(1)}, bf16[384,256]{1,0:T(8,128)(2,1)S(1)}, u32[]{:S(2)}, u32[]{:S(2)}) collective-permute-start(bf16[384,256]{1,0:T(8,128)(2,1)S(1)} %collective-permute-done.29.refs_0_), channel_id=1, source_target_pairs={{0,4},{4,0},{8,12},{12,8},{16,20},{20,16},{24,28},{28,24},{1,5},{5... | collective-permute-start | bytes 589832 | tf_op jit(solution)/shard_map/ppermute | solution.py:15

commit v4 on v3

--- a/solution.py
+++ b/solution.py
@@ -155,6 +155,10 @@
     return (grad_first[None], grad_second[None])
 
 
+def plane_order(experts):
+    return (*range(2, experts), 1, 0)
+
+
 def place():
     dp = lax.axis_index("dp")
     return dp // 2, dp % 2, lax.axis_index("expert")
@@ -224,11 +228,13 @@
         copy.start()
     for i in range(2):
         copies[i].wait()
-        place_rows = placing(blocks[i][...], experts, capacity, plane)
+    places = [placing(block[...], experts, capacity, plane) for block in blocks]
+    for i in range(2):
         copies[2 + i].wait()
-        sent = dot(place_rows[capacity:], slices[i][...]).astype(jnp.bfloat16)
-        for s in range(experts - 1):
-            moved[-1 - s][:, i * feat : (i + 1) * feat] = sent[s * capacity : (s + 1) * capacity]
+    for i in range(2):
+        sent = dot(places[i][capacity:], slices[i][...]).astype(jnp.bfloat16)
+        for out, s in zip(moved, plane_order(experts)):
+            out[:, i * feat : (i + 1) * feat] = sent[(s - 1) * capacity : s * capacity]
 
 
 def stay_kernel(experts, capacity, values, route, stay):
@@ -260,9 +266,9 @@
 def stack_kernel(*refs):
     moved, out = refs[:-2], refs[-2:]
     capacity, both = moved[0].shape
-    for s, ref in enumerate(moved[::-1]):
+    for ref, s in zip(moved, plane_order(len(moved) + 1)):
         for i in range(2):
-            out[i][s * capacity : (s + 1) * capacity, :] = ref[
+            out[i][(s - 1) * capacity : s * capacity, :] = ref[
                 :, i * (both // 2) : (i + 1) * (both // 2)
             ]
 
@@ -342,20 +348,21 @@
         total = total + ref[...].astype(jnp.float32)
     total = total.astype(jnp.bfloat16)
     capacity = out[0].shape[0] // 2
-    for s in range(experts):
+    for ref, s in zip(out, plane_order(experts)):
         for c in range(2):
             start = (c * experts + s) * capacity
-            out[-1 - s][c * capacity : (c + 1) * capacity, :] = total[start : start + capacity]
+            ref[c * capacity : (c + 1) * capacity, :] = total[start : start + capacity]
 
 
 def home_kernel(experts, capacity, maps, *refs):
     got, out = refs[:experts], refs[experts:]
     for c in range(2):
         here = slice(c * capacity, (c + 1) * capacity)
-        rows = jnp.concatenate([ref[here, :] for ref in got[::-1]], axis=0)
+        by_plane = dict(zip(plane_order(experts), got))
+        rows = jnp.concatenate([by_plane[s][here, :] for s in range(experts)], axis=0)
         by_slot = dot(maps[c], rows).astype(jnp.bfloat16)
-        for s in range(experts):
-            out[-1 - s][here, :] = by_slot[s * capacity : (s + 1) * capacity]
+        for ref, s in zip(out, plane_order(experts)):
+            ref[here, :] = by_slot[s * capacity : (s + 1) * capacity]
 
 
 def upstream_kernel(columns, experts, loss_scale, *refs):
@@ -364,9 +371,10 @@
     for ref in sums[1:]:
         total = total + ref[...].astype(jnp.float32)
     capacity = teacher[0].shape[0] // 2
+    teacher = dict(zip(plane_order(experts), teacher))
     rows = jnp.concatenate(
         [
-            teacher[-1 - s][c * capacity : (c + 1) * capacity, :]
+            teacher[s][c * capacity : (c + 1) * capacity, :]
             for c in range(2)
             for s in range(experts)
         ],
@@ -445,7 +453,9 @@
         return lax.optimization_barrier((value, others))[0]
 
     def over_planes(sent):
-        return [partner(value, "dp", (experts - 1 - i) << 1) for i, value in enumerate(sent)]
+        return [
+            partner(value, "dp", s << 1) for value, s in zip(sent, plane_order(experts))
+        ]
 
     def spread(mine):
         return [mine] + [partner(mine, "expert", m) for m in range(1, columns)]

time: 81.5 us -> 80.9 us (level)
  starting transfers between devices: 35.5 us -> 34.6 us
    ppermute x34, starting transfers between devices: 35.5 us -> 34.6 us  [partner(): lax.ppermute(value, axis, [(i, i ^ mask) for i in range(lax.axis_size(axi...]
  transfers between devices with their start and end apart: 34 -> 34, of which waited for: 15 -> 13; matrix products, arithmetic and copies ran while one was open for 1% -> 1% of each run, Pallas kernels for 15% -> 15%
where the time goes in v4:
time: 80.9 us; the launch traced here: 80.6 us
  starting transfers between devices  34.6 us (43%)
  waiting for transfers between devices  21.6 us (27%)
  Pallas kernels  17.3 us (21%)
  local copies, waits for them, and re-layouts  5.54 us (7%)
  between operations  0.98 us (1%)
    ppermute x34, starting transfers between devices, partner(): lax.ppermute(value, axis, [(i, i ^ mask) for i in range(lax.axis_size(axi...  34.6 us
    ppermute x34, waiting for transfers between devices, partner(): lax.ppermute(value, axis, [(i, i ^ mask) for i in range(lax.axis_size(axi...  21.6 us
    pallas_call x23, Pallas kernels, call(): pl.pallas_call(kernel, name=name, out_shape=outs, in_specs=in_specs or [V...  17.3 us
    unnamed x16, local copies, waits for them, and re-layouts  5.54 us
  transfers between devices with their start and end apart: 34, of which 13 were waited for; matrix products, arithmetic and copies ran while one was open for 1% of the time, Pallas kernels for 15%

profile of v4, /device:TPU:0, one launch (start us, length us, event | category | flops | bytes accessed | tf_op | source)
XLA Modules:
  0.0 80.6 jit_solution(4662655423485589897)
XLA Ops:
  0.6 2.0 %pack.1 = (bf16[48,1024]{1,0:T(8,128)(2,1)}, bf16[48,1024]{1,0:T(8,128)(2,1)}, bf16[48,1024]{1,0:T(8,128)(2,1)}) custom-call(bf16[128,2048]{1,0:T(8,128)(2,1)} %refs_0_.5, bf16[128,2048]{1,0:T(8,128)(2,1)} %refs_1_.1, s32[1,128]{1,0:T(1,128)} %bitcast.12, s32[1,128]{1,0:T(1,128)} %bitcast.15), custom_call_target="tpu_custom_call" | custom-call | tf_op jit(solution)/shard_map/pack/pallas_call | solution.py:172
  2.7 4.1 %collective-permute-start = (bf16[48,1024]{1,0:T(8,128)(2,1)}, bf16[48,1024]{1,0:T(8,128)(2,1)S(1)}, u32[]{:S(2)}, u32[]{:S(2)}) collective-permute-start(bf16[48,1024]{1,0:T(8,128)(2,1)} %get-tuple-element.71), channel_id=1, source_target_pairs={{0,16},{4,20},{8,24},{12,28},{16,0},{20,4},{24,8},{28,12},{1,17},{... | collective-permute-start | bytes 294920 | tf_op jit(solution)/shard_map/ppermute | solution.py:15
  6.8 1.3 %collective-permute-start.1 = (bf16[48,1024]{1,0:T(8,128)(2,1)}, bf16[48,1024]{1,0:T(8,128)(2,1)S(1)}, u32[]{:S(2)}, u32[]{:S(2)}) collective-permute-start(bf16[48,1024]{1,0:T(8,128)(2,1)} %get-tuple-element.72), channel_id=1, source_target_pairs={{0,24},{4,28},{8,16},{12,20},{16,8},{20,12},{24,0},{28,4},{1,25},{... | collective-permute-start | bytes 294920 | tf_op jit(solution)/shard_map/ppermute | solution.py:15
  8.1 0.2 collective-permute-start.2
  8.3 0.7 pad_add_fusion.refs_0_
  9.0 1.0 %copy-done = bf16[128,2048]{1,0:T(8,128)(2,1)S(1)} copy-done((bf16[128,2048]{1,0:T(8,128)(2,1)S(1)}, bf16[128,2048]{1,0:T(8,128)(2,1)}, u32[]{:S(2)}) %copy-start) | copy-done | bytes 524312
  10.1 0.7 copy-done.6
  10.7 0.3 stay.3.refs_0_
  11.1 0.6 copy-done.7
  11.8 0.3 stay.2.refs_0_
  12.1 1.6 %copy-done.2 = bf16[1,2048,512]{2,1,0:T(8,128)(2,1)S(1)} copy-done((bf16[1,2048,512]{2,1,0:T(8,128)(2,1)S(1)}, bf16[1,2048,512]{2,1,0:T(8,128)(2,1)}, u32[]{:S(2)}) %copy-start.2) | copy-done | bytes 2097176
  13.7 1.6 %copy-done.3 = bf16[1,512,2048]{2,1,0:T(8,128)(2,1)S(1)} copy-done((bf16[1,512,2048]{2,1,0:T(8,128)(2,1)S(1)}, bf16[1,512,2048]{2,1,0:T(8,128)(2,1)}, u32[]{:S(2)}) %copy-start.3) | copy-done | bytes 2097176
  15.3 0.3 load.2
  15.7 2.5 %collective-permute-start.9 = (bf16[144,512]{1,0:T(8,128)(2,1)S(1)}, bf16[144,512]{1,0:T(8,128)(2,1)S(1)}, u32[]{:S(2)}, u32[]{:S(2)}) collective-permute-start(bf16[144,512]{1,0:T(8,128)(2,1)S(1)} %get-tuple-element.80.refs_1_), channel_id=1, source_target_pairs={{0,3},{1,2},{2,1},{3,0},{4,7},{5,6},{6,5},{7,4},{8,11},{9,10},{10,... | collective-permute-start | bytes 442376 | tf_op jit(solution)/shard_map/ppermute | solution.py:15
  18.2 0.5 collective-permute-start.8
  18.7 0.5 collective-permute-start.7
  19.2 0.4 maps.1.refs_0_
  19.6 2.5 %collective-permute-start.6 = (bf16[144,512]{1,0:T(8,128)(2,1)S(1)}, bf16[144,512]{1,0:T(8,128)(2,1)S(1)}, u32[]{:S(2)}, u32[]{:S(2)}) collective-permute-start(bf16[144,512]{1,0:T(8,128)(2,1)S(1)} %get-tuple-element.94.refs_1_), channel_id=1, source_target_pairs={{0,3},{1,2},{2,1},{3,0},{4,7},{5,6},{6,5},{7,4},{8,11},{9,10},{10,... | collective-permute-start | bytes 442376 | tf_op jit(solution)/shard_map/ppermute | solution.py:15
  22.1 0.5 collective-permute-start.5
  22.6 0.7 collective-permute-done.9.refs_4_
  23.3 1.5 %collective-permute-start.4 = (bf16[144,512]{1,0:T(8,128)(2,1)S(1)}, bf16[144,512]{1,0:T(8,128)(2,1)S(1)}, u32[]{:S(2)}, u32[]{:S(2)}) collective-permute-start(bf16[144,512]{1,0:T(8,128)(2,1)S(1)} %get-tuple-element.94.refs_1_), channel_id=1, source_target_pairs={{0,1},{1,0},{2,3},{3,2},{4,5},{5,4},{6,7},{7,6},{8,9},{9,8},{10,11... | collective-permute-start | bytes 442376 | tf_op jit(solution)/shard_map/ppermute | solution.py:15
  24.8 1.7 %collective-permute-done.8.refs_3_ = bf16[144,512]{1,0:T(8,128)(2,1)S(1)} collective-permute-done((bf16[144,512]{1,0:T(8,128)(2,1)S(1)}, bf16[144,512]{1,0:T(8,128)(2,1)S(1)}, u32[]{:S(2)}, u32[]{:S(2)}) %collective-permute-start.8) | collective-permute-done | bytes 147488 | tf_op jit(solution)/shard_map/ppermute | solution.py:15
  26.7 0.9 %forward_t.2 = (bf16[1,4,192,256]{3,2,1,0:T(8,128)(2,1)S(1)}, bf16[192,512]{1,0:T(8,128)(2,1)S(1)}) custom-call(bf16[192,2048]{1,0:T(8,128)(2,1)S(1)} %join.2.refs_0_, bf16[2048,512]{1,0:T(8,128)(2,1)S(1)} %get-tuple-element.74.refs_1_, bf16[512,2048]{1,0:T(8,128)(2,1)S(1)} %get-tuple-element.84.refs_2_), custom_call_target="tpu_custom_call" | custom-call | flops 9663676416 | tf_op jit(solution)/shard_map/forward_t/pallas_call | solution.py:172
  27.6 0.6 collective-permute-start.11
  28.2 0.7 collective-permute-done.10.refs_0_
  29.0 0.9 %forward_t.3 = (bf16[1,4,192,256]{3,2,1,0:T(8,128)(2,1)S(1)}, bf16[192,512]{1,0:T(8,128)(2,1)S(1)}) custom-call(bf16[192,2048]{1,0:T(8,128)(2,1)S(1)} %collective-permute-done.10.refs_0_, bf16[2048,512]{1,0:T(8,128)(2,1)S(1)} %get-tuple-element.74.refs_1_, bf16[512,2048]{1,0:T(8,128)(2,1)S(1)} %get-tuple-element.84.refs_2_), custom_call_target="tpu_custom_call" | custom-call | tf_op jit(solution)/shard_map/forward_t/pallas_call | solution.py:172
  29.9 0.2 collective-permute-start.12
  30.1 0.3 load.3
  30.4 1.9 %collective-permute-done.5.refs_3_ = bf16[144,512]{1,0:T(8,128)(2,1)S(1)} collective-permute-done((bf16[144,512]{1,0:T(8,128)(2,1)S(1)}, bf16[144,512]{1,0:T(8,128)(2,1)S(1)}, u32[]{:S(2)}, u32[]{:S(2)}) %collective-permute-start.5) | collective-permute-done | bytes 147488 | tf_op jit(solution)/shard_map/ppermute | solution.py:15
  32.4 0.1 collective-permute-done.4.refs_2_
  32.5 0.6 keep_t.1
  33.1 0.2 pair.2
  33.5 1.6 %collective-permute-start.18 = (bf16[384,256]{1,0:T(8,128)(2,1)S(1)}, bf16[384,256]{1,0:T(8,128)(2,1)S(1)}, u32[]{:S(2)}, u32[]{:S(2)}) collective-permute-start(bf16[384,256]{1,0:T(8,128)(2,1)S(1)} %get-tuple-element.110), channel_id=1, source_target_pairs={{0,1},{1,0},{2,3},{3,2},{4,5},{5,4},{6,7},{7,6},{8,9},{9,8},{10,11... | collective-permute-start | bytes 589832 | tf_op jit(solution)/shard_map/ppermute | solution.py:15
  35.0 0.7 collective-permute-start.19
  35.7 1.3 %collective-permute-start.20 = (bf16[384,256]{1,0:T(8,128)(2,1)S(1)}, bf16[384,256]{1,0:T(8,128)(2,1)S(1)}, u32[]{:S(2)}, u32[]{:S(2)}) collective-permute-start(bf16[384,256]{1,0:T(8,128)(2,1)S(1)} %get-tuple-element.112), channel_id=1, source_target_pairs={{0,3},{1,2},{2,1},{3,0},{4,7},{5,6},{6,5},{7,4},{8,11},{9,10},{10,... | collective-permute-start | bytes 589832 | tf_op jit(solution)/shard_map/ppermute | solution.py:15
  37.0 1.7 %forward_s.1 = (bf16[2,4,192,256]{3,2,1,0:T(8,128)(2,1)S(1)}, bf16[192,512]{1,0:T(8,128)(2,1)S(1)}, bf16[192,512]{1,0:T(8,128)(2,1)S(1)}, f32[192,512]{1,0:T(8,128)S(1)}, f32[192,512]{1,0:T(8,128)S(1)}) custom-call(bf16[192,2048]{1,0:T(8,128)(2,1)S(1)} %join.3.refs_0_.refs_5_, bf16[192,2048]{1,0:T(8,128)(2,1)S(1)} %collective-permute-done.13.refs_1_.refs_6_, ...), custom_call_target="tpu_custom_call" | custom-call | tf_op jit(solution)/shard_map/forward_s/pallas_call | solution.py:172
  38.9 1.4 %keep_s.1 = (bf16[4,192,256]{2,1,0:T(8,128)(2,1)S(1)}, bf16[4,192,256]{2,1,0:T(8,128)(2,1)S(1)}, bf16[2048,384]{1,0:T(8,128)(2,1)S(1)}, bf16[512,384]{1,0:T(8,128)(2,1)S(1)}, f32[384,512]{1,0:T(8,128)S(1)}) custom-call(bf16[192,512]{1,0:T(8,128)(2,1)S(1)} %get-tuple-element.99.refs_0_, bf16[192,512]{1,0:T(8,128)(2,1)S(1)} %get-tuple-element.100.refs_1_, ...), custom_call_target="tpu_custom_call" | custom-call | flops 25769803776 | tf_op jit(solution)/shard_map/keep_s/pallas_call | solution.py:172
  40.2 0.9 %collective-permute-done.14.refs_2_ = bf16[2,4,192,256]{3,2,1,0:T(8,128)(2,1)S(1)} collective-permute-done((bf16[2,4,192,256]{3,2,1,0:T(8,128)(2,1)S(1)}, bf16[2,4,192,256]{3,2,1,0:T(8,128)(2,1)S(1)}, u32[]{:S(2)}, u32[]{:S(2)}) %collective-permute-start.14) | collective-permute-done | bytes 786464 | tf_op jit(solution)/shard_map/ppermute | solution.py:15
  41.1 0.2 pair.3
  41.3 1.6 %collective-permute-start.15 = (bf16[384,256]{1,0:T(8,128)(2,1)S(1)}, bf16[384,256]{1,0:T(8,128)(2,1)S(1)}, u32[]{:S(2)}, u32[]{:S(2)}) collective-permute-start(bf16[384,256]{1,0:T(8,128)(2,1)S(1)} %get-tuple-element.107), channel_id=1, source_target_pairs={{0,1},{1,0},{2,3},{3,2},{4,5},{5,4},{6,7},{7,6},{8,9},{9,8},{10,11... | collective-permute-start | bytes 589832 | tf_op jit(solution)/shard_map/ppermute | solution.py:15
  42.9 0.7 collective-permute-start.16
  43.5 1.3 %collective-permute-start.17 = (bf16[384,256]{1,0:T(8,128)(2,1)S(1)}, bf16[384,256]{1,0:T(8,128)(2,1)S(1)}, u32[]{:S(2)}, u32[]{:S(2)}) collective-permute-start(bf16[384,256]{1,0:T(8,128)(2,1)S(1)} %get-tuple-element.109), channel_id=1, source_target_pairs={{0,3},{1,2},{2,1},{3,0},{4,7},{5,6},{6,5},{7,4},{8,11},{9,10},{10,... | collective-permute-start | bytes 589832 | tf_op jit(solution)/shard_map/ppermute | solution.py:15
  44.9 1.6 %collective-permute-done.19.refs_2_ = bf16[384,256]{1,0:T(8,128)(2,1)S(1)} collective-permute-done((bf16[384,256]{1,0:T(8,128)(2,1)S(1)}, bf16[384,256]{1,0:T(8,128)(2,1)S(1)}, u32[]{:S(2)}, u32[]{:S(2)}) %collective-permute-start.19) | collective-permute-done | bytes 196640 | tf_op jit(solution)/shard_map/ppermute | solution.py:15
  46.6 2.9 %collective-permute-start.21 = (bf16[96,256]{1,0:T(8,128)(2,1)S(1)}, bf16[96,256]{1,0:T(8,128)(2,1)S(1)}, u32[]{:S(2)}, u32[]{:S(2)}) collective-permute-start(bf16[96,256]{1,0:T(8,128)(2,1)S(1)} %get-tuple-element.117), channel_id=1, source_target_pairs={{0,16},{4,20},{8,24},{12,28},{16,0},{20,4},{24,8},{28,12},{1,17},{... | collective-permute-start | bytes 147464 | tf_op jit(solution)/shard_map/ppermute | solution.py:15
  49.4 1.4 %collective-permute-start.22 = (bf16[96,256]{1,0:T(8,128)(2,1)S(1)}, bf16[96,256]{1,0:T(8,128)(2,1)S(1)}, u32[]{:S(2)}, u32[]{:S(2)}) collective-permute-start(bf16[96,256]{1,0:T(8,128)(2,1)S(1)} %get-tuple-element.118), channel_id=1, source_target_pairs={{0,24},{4,28},{8,16},{12,20},{16,8},{20,12},{24,0},{28,4},{1,25},{... | collective-permute-start | bytes 147464 | tf_op jit(solution)/shard_map/ppermute | solution.py:15
  50.8 0.7 collective-permute-start.23
  51.5 0.5 collective-permute-done.21.refs_1_
  52.0 3.4 %collective-permute-done.22.refs_2_ = bf16[96,256]{1,0:T(8,128)(2,1)S(1)} collective-permute-done((bf16[96,256]{1,0:T(8,128)(2,1)S(1)}, bf16[96,256]{1,0:T(8,128)(2,1)S(1)}, u32[]{:S(2)}, u32[]{:S(2)}) %collective-permute-start.22) | collective-permute-done | bytes 49184 | tf_op jit(solution)/shard_map/ppermute | solution.py:15
  55.4 0.2 home.1
  55.6 1.3 %collective-permute-start.24 = (bf16[96,256]{1,0:T(8,128)(2,1)S(1)}, bf16[96,256]{1,0:T(8,128)(2,1)S(1)}, u32[]{:S(2)}, u32[]{:S(2)}) collective-permute-start(bf16[96,256]{1,0:T(8,128)(2,1)S(1)} %get-tuple-element.122), channel_id=1, source_target_pairs={{0,16},{4,20},{8,24},{12,28},{16,0},{20,4},{24,8},{28,12},{1,17},{... | collective-permute-start | bytes 147464 | tf_op jit(solution)/shard_map/ppermute | solution.py:15
  56.9 1.3 %collective-permute-start.25 = (bf16[96,256]{1,0:T(8,128)(2,1)S(1)}, bf16[96,256]{1,0:T(8,128)(2,1)S(1)}, u32[]{:S(2)}, u32[]{:S(2)}) collective-permute-start(bf16[96,256]{1,0:T(8,128)(2,1)S(1)} %get-tuple-element.123), channel_id=1, source_target_pairs={{0,24},{4,28},{8,16},{12,20},{16,8},{20,12},{24,0},{28,4},{1,25},{... | collective-permute-start | bytes 147464 | tf_op jit(solution)/shard_map/ppermute | solution.py:15
  58.2 0.9 %collective-permute-start.26 = (bf16[96,256]{1,0:T(8,128)(2,1)S(1)}, bf16[96,256]{1,0:T(8,128)(2,1)S(1)}, u32[]{:S(2)}, u32[]{:S(2)}) collective-permute-start(bf16[96,256]{1,0:T(8,128)(2,1)S(1)} %get-tuple-element.124), channel_id=1, source_target_pairs={{0,8},{4,12},{8,0},{12,4},{16,24},{20,28},{24,16},{28,20},{1,9},{5... | collective-permute-start | bytes 147464 | tf_op jit(solution)/shard_map/ppermute | solution.py:15
  59.2 1.8 %collective-permute-done.24.refs_4_ = bf16[96,256]{1,0:T(8,128)(2,1)S(1)} collective-permute-done((bf16[96,256]{1,0:T(8,128)(2,1)S(1)}, bf16[96,256]{1,0:T(8,128)(2,1)S(1)}, u32[]{:S(2)}, u32[]{:S(2)}) %collective-permute-start.24) | collective-permute-done | bytes 49184 | tf_op jit(solution)/shard_map/ppermute | solution.py:15
  61.0 1.9 %collective-permute-done.25.refs_5_ = bf16[96,256]{1,0:T(8,128)(2,1)S(1)} collective-permute-done((bf16[96,256]{1,0:T(8,128)(2,1)S(1)}, bf16[96,256]{1,0:T(8,128)(2,1)S(1)}, u32[]{:S(2)}, u32[]{:S(2)}) %collective-permute-start.25) | collective-permute-done | bytes 49184 | tf_op jit(solution)/shard_map/ppermute | solution.py:15
  63.1 1.7 %collective-permute-start.29 = (bf16[384,256]{1,0:T(8,128)(2,1)S(1)}, bf16[384,256]{1,0:T(8,128)(2,1)S(1)}, u32[]{:S(2)}, u32[]{:S(2)}) collective-permute-start(bf16[384,256]{1,0:T(8,128)(2,1)S(1)} %shard_map.96.refs_0_), channel_id=1, source_target_pairs={{0,3},{1,2},{2,1},{3,0},{4,7},{5,6},{6,5},{7,4},{8,11},{9,10},{10,... | collective-permute-start | bytes 589832 | tf_op jit(solution)/shard_map/ppermute | solution.py:15
  64.7 1.3 %collective-permute-start.28 = (bf16[384,256]{1,0:T(8,128)(2,1)S(1)}, bf16[384,256]{1,0:T(8,128)(2,1)S(1)}, u32[]{:S(2)}, u32[]{:S(2)}) collective-permute-start(bf16[384,256]{1,0:T(8,128)(2,1)S(1)} %shard_map.96.refs_0_), channel_id=1, source_target_pairs={{0,2},{1,3},{2,0},{3,1},{4,6},{5,7},{6,4},{7,5},{8,10},{9,11},{10,... | collective-permute-start | bytes 589832 | tf_op jit(solution)/shard_map/ppermute | solution.py:15
  66.1 0.5 collective-permute-start.27
  66.6 1.5 %shard_map.97 = (bf16[512,2048]{1,0:T(8,128)(2,1)}, f32[384,512]{1,0:T(8,128)S(1)}) custom-call(bf16[384,256]{1,0:T(8,128)(2,1)S(1)} %shard_map.96.refs_0_, bf16[384,256]{1,0:T(8,128)(2,1)S(1)} %collective-permute-done.30.refs_1_, bf16[512,384]{1,0:T(8,128)(2,1)S(1)} %get-tuple-element.126.refs_2_.refs_1_.refs_3_, ...), custom_call_target="tpu_custom_call" | custom-call | tf_op jit(solution)/shard_map/pallas_call | solution.py:172
  68.1 3.7 %collective-permute-done.29.refs_0_ = bf16[384,256]{1,0:T(8,128)(2,1)S(1)} collective-permute-done((bf16[384,256]{1,0:T(8,128)(2,1)S(1)}, bf16[384,256]{1,0:T(8,128)(2,1)S(1)}, u32[]{:S(2)}, u32[]{:S(2)}) %collective-permute-start.29) | collective-permute-done | bytes 196640 | tf_op jit(solution)/shard_map/ppermute | solution.py:15
  71.8 1.1 %shard_map.98 = (bf16[512,2048]{1,0:T(8,128)(2,1)}, f32[384,512]{1,0:T(8,128)S(1)}) custom-call(bf16[384,256]{1,0:T(8,128)(2,1)S(1)} %collective-permute-done.29.refs_0_, bf16[512,384]{1,0:T(8,128)(2,1)S(1)} %get-tuple-element.126.refs_2_.refs_1_.refs_3_, ...), custom_call_target="tpu_custom_call", output_to_operand_aliasing={{0}: (4, {})} | custom-call | tf_op jit(solution)/shard_map/pallas_call | solution.py:172
  72.9 2.6 %collective-permute-done.28.refs_1_ = bf16[384,256]{1,0:T(8,128)(2,1)S(1)} collective-permute-done((bf16[384,256]{1,0:T(8,128)(2,1)S(1)}, bf16[384,256]{1,0:T(8,128)(2,1)S(1)}, u32[]{:S(2)}, u32[]{:S(2)}) %collective-permute-start.28) | collective-permute-done | bytes 196640 | tf_op jit(solution)/shard_map/ppermute | solution.py:15
  75.5 0.5 collective-permute-start.32
  76.1 1.5 %shard_map.99 = (bf16[512,2048]{1,0:T(8,128)(2,1)}, f32[384,512]{1,0:T(8,128)S(1)}) custom-call(bf16[384,256]{1,0:T(8,128)(2,1)S(1)} %collective-permute-done.27.refs_0_, bf16[384,256]{1,0:T(8,128)(2,1)S(1)} %collective-permute-done.28.refs_1_, bf16[512,384]{1,0:T(8,128)(2,1)S(1)} %get-tuple-element.126.refs_2_.refs_1_.refs_3_, ...), custom_call_target="tpu_custom_call", output_to_operand_aliasing={{0}: (5, {})} | custom-call | tf_op jit(solution)/shard_map/pallas_call | solution.py:172
  77.6 3.0 %shard_map.100 = (bf16[512,2048]{1,0:T(8,128)(2,1)}, bf16[2048,512]{1,0:T(8,128)(2,1)}) custom-call(bf16[384,256]{1,0:T(8,128)(2,1)S(1)} %collective-permute-done.31.refs_0_, bf16[384,256]{1,0:T(8,128)(2,1)S(1)} %collective-permute-done.32.refs_1_, bf16[384,256]{1,0:T(8,128)(2,1)S(1)} %collective-permute-done.33.refs_2_, ...), custom_call_target="tpu_custom_call", output_to_operand_aliasing={{0}: (6, {})} | custom-call | tf_op jit(solution)/shard_map/pallas_call | solution.py:172
  (44 shorter events, 0.8 us)
Async XLA Ops:
  0.6 10.5 %copy-start.1 = (bf16[128,2048]{1,0:T(8,128)(2,1)S(1)}, bf16[128,2048]{1,0:T(8,128)(2,1)}, u32[]{:S(2)}) copy-start(bf16[128,2048]{1,0:T(8,128)(2,1)} %refs_1_.1) | copy-start | bytes 1572868
  2.7 13.0 %collective-permute-start = (bf16[48,1024]{1,0:T(8,128)(2,1)}, bf16[48,1024]{1,0:T(8,128)(2,1)S(1)}, u32[]{:S(2)}, u32[]{:S(2)}) collective-permute-start(bf16[48,1024]{1,0:T(8,128)(2,1)} %get-tuple-element.71), channel_id=1, source_target_pairs={{0,16},{4,20},{8,24},{12,28},{16,0},{20,4},{24,8},{28,12},{1,17},{... | collective-permute-start | bytes 294920 | tf_op jit(solution)/shard_map/ppermute | solution.py:15
  6.8 8.9 %collective-permute-start.1 = (bf16[48,1024]{1,0:T(8,128)(2,1)}, bf16[48,1024]{1,0:T(8,128)(2,1)S(1)}, u32[]{:S(2)}, u32[]{:S(2)}) collective-permute-start(bf16[48,1024]{1,0:T(8,128)(2,1)} %get-tuple-element.72), channel_id=1, source_target_pairs={{0,24},{4,28},{8,16},{12,20},{16,8},{20,12},{24,0},{28,4},{1,25},{... | collective-permute-start | bytes 294920 | tf_op jit(solution)/shard_map/ppermute | solution.py:15
  8.1 7.5 %collective-permute-start.2 = (bf16[48,1024]{1,0:T(8,128)(2,1)}, bf16[48,1024]{1,0:T(8,128)(2,1)S(1)}, u32[]{:S(2)}, u32[]{:S(2)}) collective-permute-start(bf16[48,1024]{1,0:T(8,128)(2,1)} %get-tuple-element.73), channel_id=1, source_target_pairs={{0,8},{4,12},{8,0},{12,4},{16,24},{20,28},{24,16},{28,20},{1,9},{5... | collective-permute-start | bytes 294920 | tf_op jit(solution)/shard_map/ppermute | solution.py:15
  9.0 6.6 %collective-permute-start.3 = (s32[2,128]{1,0:T(2,128)S(1)}, s32[2,128]{1,0:T(2,128)S(1)}, u32[]{:S(2)}, u32[]{:S(2)}) collective-permute-start(s32[2,128]{1,0:T(2,128)S(1)} %pad_add_fusion.refs_0_), channel_id=1, source_target_pairs={{0,4},{4,0},{8,12},{12,8},{16,20},{20,16},{24,28},{28,24},{1,5},{5... | collective-permute-start | bytes 3080 | tf_op jit(solution)/shard_map/ppermute | solution.py:15
  9.0 1.0 %copy-start = (bf16[128,2048]{1,0:T(8,128)(2,1)S(1)}, bf16[128,2048]{1,0:T(8,128)(2,1)}, u32[]{:S(2)}) copy-start(bf16[128,2048]{1,0:T(8,128)(2,1)} %refs_0_.5) | copy-start | bytes 1572868
  10.1 0.7 copy-start.6
  11.1 0.7 copy-start.7
  12.1 1.6 %copy-start.2 = (bf16[1,2048,512]{2,1,0:T(8,128)(2,1)S(1)}, bf16[1,2048,512]{2,1,0:T(8,128)(2,1)}, u32[]{:S(2)}) copy-start(bf16[1,2048,512]{2,1,0:T(8,128)(2,1)} %param.12) | copy-start | bytes 6291460
  13.7 1.6 %copy-start.3 = (bf16[1,512,2048]{2,1,0:T(8,128)(2,1)S(1)}, bf16[1,512,2048]{2,1,0:T(8,128)(2,1)}, u32[]{:S(2)}) copy-start(bf16[1,512,2048]{2,1,0:T(8,128)(2,1)} %param.13) | copy-start | bytes 6291460
  15.7 7.6 %collective-permute-start.9 = (bf16[144,512]{1,0:T(8,128)(2,1)S(1)}, bf16[144,512]{1,0:T(8,128)(2,1)S(1)}, u32[]{:S(2)}, u32[]{:S(2)}) collective-permute-start(bf16[144,512]{1,0:T(8,128)(2,1)S(1)} %get-tuple-element.80.refs_1_), channel_id=1, source_target_pairs={{0,3},{1,2},{2,1},{3,0},{4,7},{5,6},{6,5},{7,4},{8,11},{9,10},{10,... | collective-permute-start | bytes 442376 | tf_op jit(solution)/shard_map/ppermute | solution.py:15
  18.2 8.3 %collective-permute-start.8 = (bf16[144,512]{1,0:T(8,128)(2,1)S(1)}, bf16[144,512]{1,0:T(8,128)(2,1)S(1)}, u32[]{:S(2)}, u32[]{:S(2)}) collective-permute-start(bf16[144,512]{1,0:T(8,128)(2,1)S(1)} %get-tuple-element.80.refs_1_), channel_id=1, source_target_pairs={{0,2},{1,3},{2,0},{3,1},{4,6},{5,7},{6,4},{7,5},{8,10},{9,11},{10,... | collective-permute-start | bytes 442376 | tf_op jit(solution)/shard_map/ppermute | solution.py:15
  18.7 7.8 %collective-permute-start.7 = (bf16[144,512]{1,0:T(8,128)(2,1)S(1)}, bf16[144,512]{1,0:T(8,128)(2,1)S(1)}, u32[]{:S(2)}, u32[]{:S(2)}) collective-permute-start(bf16[144,512]{1,0:T(8,128)(2,1)S(1)} %get-tuple-element.80.refs_1_), channel_id=1, source_target_pairs={{0,1},{1,0},{2,3},{3,2},{4,5},{5,4},{6,7},{7,6},{8,9},{9,8},{10,11... | collective-permute-start | bytes 442376 | tf_op jit(solution)/shard_map/ppermute | solution.py:15
  19.6 10.8 %collective-permute-start.6 = (bf16[144,512]{1,0:T(8,128)(2,1)S(1)}, bf16[144,512]{1,0:T(8,128)(2,1)S(1)}, u32[]{:S(2)}, u32[]{:S(2)}) collective-permute-start(bf16[144,512]{1,0:T(8,128)(2,1)S(1)} %get-tuple-element.94.refs_1_), channel_id=1, source_target_pairs={{0,3},{1,2},{2,1},{3,0},{4,7},{5,6},{6,5},{7,4},{8,11},{9,10},{10,... | collective-permute-start | bytes 442376 | tf_op jit(solution)/shard_map/ppermute | solution.py:15
  22.1 10.3 %collective-permute-start.5 = (bf16[144,512]{1,0:T(8,128)(2,1)S(1)}, bf16[144,512]{1,0:T(8,128)(2,1)S(1)}, u32[]{:S(2)}, u32[]{:S(2)}) collective-permute-start(bf16[144,512]{1,0:T(8,128)(2,1)S(1)} %get-tuple-element.94.refs_1_), channel_id=1, source_target_pairs={{0,2},{1,3},{2,0},{3,1},{4,6},{5,7},{6,4},{7,5},{8,10},{9,11},{10,... | collective-permute-start | bytes 442376 | tf_op jit(solution)/shard_map/ppermute | solution.py:15
  23.3 9.2 %collective-permute-start.4 = (bf16[144,512]{1,0:T(8,128)(2,1)S(1)}, bf16[144,512]{1,0:T(8,128)(2,1)S(1)}, u32[]{:S(2)}, u32[]{:S(2)}) collective-permute-start(bf16[144,512]{1,0:T(8,128)(2,1)S(1)} %get-tuple-element.94.refs_1_), channel_id=1, source_target_pairs={{0,1},{1,0},{2,3},{3,2},{4,5},{5,4},{6,7},{7,6},{8,9},{9,8},{10,11... | collective-permute-start | bytes 442376 | tf_op jit(solution)/shard_map/ppermute | solution.py:15
  26.6 2.4 %collective-permute-start.10 = (bf16[192,2048]{1,0:T(8,128)(2,1)S(1)}, bf16[192,2048]{1,0:T(8,128)(2,1)S(1)}, u32[]{:S(2)}, u32[]{:S(2)}) collective-permute-start(bf16[192,2048]{1,0:T(8,128)(2,1)S(1)} %join.2.refs_0_), channel_id=1, source_target_pairs={{0,4},{4,0},{8,12},{12,8},{16,20},{20,16},{24,28},{28,24},{1,5},{5... | collective-permute-start | bytes 2359304 | tf_op jit(solution)/shard_map/ppermute | solution.py:15
  27.6 2.5 %copy-start.4 = (bf16[1,2048,512]{2,1,0:T(8,128)(2,1)S(1)}, bf16[1,2048,512]{2,1,0:T(8,128)(2,1)}, u32[]{:S(2)}) copy-start(bf16[1,2048,512]{2,1,0:T(8,128)(2,1)} %param.14) | copy-start | bytes 6291460
  27.6 2.5 %copy-start.5 = (bf16[1,512,2048]{2,1,0:T(8,128)(2,1)S(1)}, bf16[1,512,2048]{2,1,0:T(8,128)(2,1)}, u32[]{:S(2)}) copy-start(bf16[1,512,2048]{2,1,0:T(8,128)(2,1)} %param.15) | copy-start | bytes 6291460
  27.6 5.5 %collective-permute-start.11 = (bf16[1,4,192,256]{3,2,1,0:T(8,128)(2,1)S(1)}, bf16[1,4,192,256]{3,2,1,0:T(8,128)(2,1)S(1)}, u32[]{:S(2)}, u32[]{:S(2)}) collective-permute-start(bf16[1,4,192,256]{3,2,1,0:T(8,128)(2,1)S(1)} %get-tuple-element.91), channel_id=1, source_target_pairs={{0,4},{4,0},{8,12},{12,8},{16,20},{20,16},{24,28},{28,24},{1,5},{5... | collective-permute-start | bytes 1179656 | tf_op jit(solution)/shard_map/ppermute | solution.py:15
  29.9 3.2 %collective-permute-start.12 = (bf16[1,4,192,256]{3,2,1,0:T(8,128)(2,1)S(1)}, bf16[1,4,192,256]{3,2,1,0:T(8,128)(2,1)S(1)}, u32[]{:S(2)}, u32[]{:S(2)}) collective-permute-start(bf16[1,4,192,256]{3,2,1,0:T(8,128)(2,1)S(1)} %get-tuple-element.92), channel_id=1, source_target_pairs={{0,4},{4,0},{8,12},{12,8},{16,20},{20,16},{24,28},{28,24},{1,5},{5... | collective-permute-start | bytes 1179656 | tf_op jit(solution)/shard_map/ppermute | solution.py:15
  33.4 3.6 %collective-permute-start.13 = (bf16[192,2048]{1,0:T(8,128)(2,1)S(1)}, bf16[192,2048]{1,0:T(8,128)(2,1)S(1)}, u32[]{:S(2)}, u32[]{:S(2)}) collective-permute-start(bf16[192,2048]{1,0:T(8,128)(2,1)S(1)} %join.3.refs_0_.refs_5_), channel_id=1, source_target_pairs={{0,4},{4,0},{8,12},{12,8},{16,20},{20,16},{24,28},{28,24},{1,5},{5... | collective-permute-start | bytes 2359304 | tf_op jit(solution)/shard_map/ppermute | solution.py:15
  33.5 10.1 %collective-permute-start.18 = (bf16[384,256]{1,0:T(8,128)(2,1)S(1)}, bf16[384,256]{1,0:T(8,128)(2,1)S(1)}, u32[]{:S(2)}, u32[]{:S(2)}) collective-permute-start(bf16[384,256]{1,0:T(8,128)(2,1)S(1)} %get-tuple-element.110), channel_id=1, source_target_pairs={{0,1},{1,0},{2,3},{3,2},{4,5},{5,4},{6,7},{7,6},{8,9},{9,8},{10,11... | collective-permute-start | bytes 589832 | tf_op jit(solution)/shard_map/ppermute | solution.py:15
  35.0 11.4 %collective-permute-start.19 = (bf16[384,256]{1,0:T(8,128)(2,1)S(1)}, bf16[384,256]{1,0:T(8,128)(2,1)S(1)}, u32[]{:S(2)}, u32[]{:S(2)}) collective-permute-start(bf16[384,256]{1,0:T(8,128)(2,1)S(1)} %get-tuple-element.111), channel_id=1, source_target_pairs={{0,2},{1,3},{2,0},{3,1},{4,6},{5,7},{6,4},{7,5},{8,10},{9,11},{10,... | collective-permute-start | bytes 589832 | tf_op jit(solution)/shard_map/ppermute | solution.py:15
  35.7 10.7 %collective-permute-start.20 = (bf16[384,256]{1,0:T(8,128)(2,1)S(1)}, bf16[384,256]{1,0:T(8,128)(2,1)S(1)}, u32[]{:S(2)}, u32[]{:S(2)}) collective-permute-start(bf16[384,256]{1,0:T(8,128)(2,1)S(1)} %get-tuple-element.112), channel_id=1, source_target_pairs={{0,3},{1,2},{2,1},{3,0},{4,7},{5,6},{6,5},{7,4},{8,11},{9,10},{10,... | collective-permute-start | bytes 589832 | tf_op jit(solution)/shard_map/ppermute | solution.py:15
  38.8 2.4 %collective-permute-start.14 = (bf16[2,4,192,256]{3,2,1,0:T(8,128)(2,1)S(1)}, bf16[2,4,192,256]{3,2,1,0:T(8,128)(2,1)S(1)}, u32[]{:S(2)}, u32[]{:S(2)}) collective-permute-start(bf16[2,4,192,256]{3,2,1,0:T(8,128)(2,1)S(1)} %get-tuple-element.105), channel_id=1, source_target_pairs={{0,4},{4,0},{8,12},{12,8},{16,20},{20,16},{24,28},{28,24},{1,5},{5... | collective-permute-start | bytes 2359304 | tf_op jit(solution)/shard_map/ppermute | solution.py:15
  41.3 9.5 %collective-permute-start.15 = (bf16[384,256]{1,0:T(8,128)(2,1)S(1)}, bf16[384,256]{1,0:T(8,128)(2,1)S(1)}, u32[]{:S(2)}, u32[]{:S(2)}) collective-permute-start(bf16[384,256]{1,0:T(8,128)(2,1)S(1)} %get-tuple-element.107), channel_id=1, source_target_pairs={{0,1},{1,0},{2,3},{3,2},{4,5},{5,4},{6,7},{7,6},{8,9},{9,8},{10,11... | collective-permute-start | bytes 589832 | tf_op jit(solution)/shard_map/ppermute | solution.py:15
  42.9 16.3 %collective-permute-start.16 = (bf16[384,256]{1,0:T(8,128)(2,1)S(1)}, bf16[384,256]{1,0:T(8,128)(2,1)S(1)}, u32[]{:S(2)}, u32[]{:S(2)}) collective-permute-start(bf16[384,256]{1,0:T(8,128)(2,1)S(1)} %get-tuple-element.108), channel_id=1, source_target_pairs={{0,2},{1,3},{2,0},{3,1},{4,6},{5,7},{6,4},{7,5},{8,10},{9,11},{10,... | collective-permute-start | bytes 589832 | tf_op jit(solution)/shard_map/ppermute | solution.py:15
  43.5 15.6 %collective-permute-start.17 = (bf16[384,256]{1,0:T(8,128)(2,1)S(1)}, bf16[384,256]{1,0:T(8,128)(2,1)S(1)}, u32[]{:S(2)}, u32[]{:S(2)}) collective-permute-start(bf16[384,256]{1,0:T(8,128)(2,1)S(1)} %get-tuple-element.109), channel_id=1, source_target_pairs={{0,3},{1,2},{2,1},{3,0},{4,7},{5,6},{6,5},{7,4},{8,11},{9,10},{10,... | collective-permute-start | bytes 589832 | tf_op jit(solution)/shard_map/ppermute | solution.py:15
  46.6 5.5 %collective-permute-start.21 = (bf16[96,256]{1,0:T(8,128)(2,1)S(1)}, bf16[96,256]{1,0:T(8,128)(2,1)S(1)}, u32[]{:S(2)}, u32[]{:S(2)}) collective-permute-start(bf16[96,256]{1,0:T(8,128)(2,1)S(1)} %get-tuple-element.117), channel_id=1, source_target_pairs={{0,16},{4,20},{8,24},{12,28},{16,0},{20,4},{24,8},{28,12},{1,17},{... | collective-permute-start | bytes 147464 | tf_op jit(solution)/shard_map/ppermute | solution.py:15
  49.4 6.0 %collective-permute-start.22 = (bf16[96,256]{1,0:T(8,128)(2,1)S(1)}, bf16[96,256]{1,0:T(8,128)(2,1)S(1)}, u32[]{:S(2)}, u32[]{:S(2)}) collective-permute-start(bf16[96,256]{1,0:T(8,128)(2,1)S(1)} %get-tuple-element.118), channel_id=1, source_target_pairs={{0,24},{4,28},{8,16},{12,20},{16,8},{20,12},{24,0},{28,4},{1,25},{... | collective-permute-start | bytes 147464 | tf_op jit(solution)/shard_map/ppermute | solution.py:15
  50.8 4.6 %collective-permute-start.23 = (bf16[96,256]{1,0:T(8,128)(2,1)S(1)}, bf16[96,256]{1,0:T(8,128)(2,1)S(1)}, u32[]{:S(2)}, u32[]{:S(2)}) collective-permute-start(bf16[96,256]{1,0:T(8,128)(2,1)S(1)} %get-tuple-element.120), channel_id=1, source_target_pairs={{0,8},{4,12},{8,0},{12,4},{16,24},{20,28},{24,16},{28,20},{1,9},{5... | collective-permute-start | bytes 147464 | tf_op jit(solution)/shard_map/ppermute | solution.py:15
  55.6 5.4 %collective-permute-start.24 = (bf16[96,256]{1,0:T(8,128)(2,1)S(1)}, bf16[96,256]{1,0:T(8,128)(2,1)S(1)}, u32[]{:S(2)}, u32[]{:S(2)}) collective-permute-start(bf16[96,256]{1,0:T(8,128)(2,1)S(1)} %get-tuple-element.122), channel_id=1, source_target_pairs={{0,16},{4,20},{8,24},{12,28},{16,0},{20,4},{24,8},{28,12},{1,17},{... | collective-permute-start | bytes 147464 | tf_op jit(solution)/shard_map/ppermute | solution.py:15
  56.9 6.0 %collective-permute-start.25 = (bf16[96,256]{1,0:T(8,128)(2,1)S(1)}, bf16[96,256]{1,0:T(8,128)(2,1)S(1)}, u32[]{:S(2)}, u32[]{:S(2)}) collective-permute-start(bf16[96,256]{1,0:T(8,128)(2,1)S(1)} %get-tuple-element.123), channel_id=1, source_target_pairs={{0,24},{4,28},{8,16},{12,20},{16,8},{20,12},{24,0},{28,4},{1,25},{... | collective-permute-start | bytes 147464 | tf_op jit(solution)/shard_map/ppermute | solution.py:15
  58.2 4.6 %collective-permute-start.26 = (bf16[96,256]{1,0:T(8,128)(2,1)S(1)}, bf16[96,256]{1,0:T(8,128)(2,1)S(1)}, u32[]{:S(2)}, u32[]{:S(2)}) collective-permute-start(bf16[96,256]{1,0:T(8,128)(2,1)S(1)} %get-tuple-element.124), channel_id=1, source_target_pairs={{0,8},{4,12},{8,0},{12,4},{16,24},{20,28},{24,16},{28,20},{1,9},{5... | collective-permute-start | bytes 147464 | tf_op jit(solution)/shard_map/ppermute | solution.py:15
  63.0 3.6 %collective-permute-start.30 = (bf16[384,256]{1,0:T(8,128)(2,1)S(1)}, bf16[384,256]{1,0:T(8,128)(2,1)S(1)}, u32[]{:S(2)}, u32[]{:S(2)}) collective-permute-start(bf16[384,256]{1,0:T(8,128)(2,1)S(1)} %shard_map.96.refs_0_), channel_id=1, source_target_pairs={{0,4},{4,0},{8,12},{12,8},{16,20},{20,16},{24,28},{28,24},{1,5},{5... | collective-permute-start | bytes 589832 | tf_op jit(solution)/shard_map/ppermute | solution.py:15
  63.1 8.7 %collective-permute-start.29 = (bf16[384,256]{1,0:T(8,128)(2,1)S(1)}, bf16[384,256]{1,0:T(8,128)(2,1)S(1)}, u32[]{:S(2)}, u32[]{:S(2)}) collective-permute-start(bf16[384,256]{1,0:T(8,128)(2,1)S(1)} %shard_map.96.refs_0_), channel_id=1, source_target_pairs={{0,3},{1,2},{2,1},{3,0},{4,7},{5,6},{6,5},{7,4},{8,11},{9,10},{10,... | collective-permute-start | bytes 589832 | tf_op jit(solution)/shard_map/ppermute | solution.py:15
  64.7 10.8 %collective-permute-start.28 = (bf16[384,256]{1,0:T(8,128)(2,1)S(1)}, bf16[384,256]{1,0:T(8,128)(2,1)S(1)}, u32[]{:S(2)}, u32[]{:S(2)}) collective-permute-start(bf16[384,256]{1,0:T(8,128)(2,1)S(1)} %shard_map.96.refs_0_), channel_id=1, source_target_pairs={{0,2},{1,3},{2,0},{3,1},{4,6},{5,7},{6,4},{7,5},{8,10},{9,11},{10,... | collective-permute-start | bytes 589832 | tf_op jit(solution)/shard_map/ppermute | solution.py:15
  66.1 9.4 %collective-permute-start.27 = (bf16[384,256]{1,0:T(8,128)(2,1)S(1)}, bf16[384,256]{1,0:T(8,128)(2,1)S(1)}, u32[]{:S(2)}, u32[]{:S(2)}) collective-permute-start(bf16[384,256]{1,0:T(8,128)(2,1)S(1)} %shard_map.96.refs_0_), channel_id=1, source_target_pairs={{0,1},{1,0},{2,3},{3,2},{4,5},{5,4},{6,7},{7,6},{8,9},{9,8},{10,11... | collective-permute-start | bytes 589832 | tf_op jit(solution)/shard_map/ppermute | solution.py:15
  75.5 2.0 %collective-permute-start.31 = (bf16[384,256]{1,0:T(8,128)(2,1)S(1)}, bf16[384,256]{1,0:T(8,128)(2,1)S(1)}, u32[]{:S(2)}, u32[]{:S(2)}) collective-permute-start(bf16[384,256]{1,0:T(8,128)(2,1)S(1)} %collective-permute-done.27.refs_0_), channel_id=1, source_target_pairs={{0,4},{4,0},{8,12},{12,8},{16,20},{20,16},{24,28},{28,24},{1,5},{5... | collective-permute-start | bytes 589832 | tf_op jit(solution)/shard_map/ppermute | solution.py:15
  75.5 2.0 %collective-permute-start.32 = (bf16[384,256]{1,0:T(8,128)(2,1)S(1)}, bf16[384,256]{1,0:T(8,128)(2,1)S(1)}, u32[]{:S(2)}, u32[]{:S(2)}) collective-permute-start(bf16[384,256]{1,0:T(8,128)(2,1)S(1)} %collective-permute-done.28.refs_1_), channel_id=1, source_target_pairs={{0,4},{4,0},{8,12},{12,8},{16,20},{20,16},{24,28},{28,24},{1,5},{5... | collective-permute-start | bytes 589832 | tf_op jit(solution)/shard_map/ppermute | solution.py:15
  76.0 1.6 %collective-permute-start.33 = (bf16[384,256]{1,0:T(8,128)(2,1)S(1)}, bf16[384,256]{1,0:T(8,128)(2,1)S(1)}, u32[]{:S(2)}, u32[]{:S(2)}) collective-permute-start(bf16[384,256]{1,0:T(8,128)(2,1)S(1)} %collective-permute-done.29.refs_0_), channel_id=1, source_target_pairs={{0,4},{4,0},{8,12},{12,8},{16,20},{20,16},{24,28},{28,24},{1,5},{5... | collective-permute-start | bytes 589832 | tf_op jit(solution)/shard_map/ppermute | solution.py:15

commit v5 on v4

--- a/solution.py
+++ b/solution.py
@@ -168,7 +168,7 @@
 ANY = pl.BlockSpec(memory_space=pl.ANY)
 
 
-def call(kernel, outs, operands, out_specs=None, in_specs=None, scratch=(), aliases=None, grant=20 << 20, flops=0, name=None):
+def call(kernel, outs, operands, out_specs=None, in_specs=None, scratch=(), grant=20 << 20, flops=0, name=None):
     return pl.pallas_call(
         kernel,
         name=name,
@@ -176,7 +176,6 @@
         in_specs=in_specs or [VMEM] * len(operands),
         out_specs=out_specs or [VMEM] * len(outs),
         scratch_shapes=list(scratch),
-        input_output_aliases=aliases or {},
         compiler_params=pltpu.CompilerParams(vmem_limit_bytes=grant),
         cost_estimate=pl.CostEstimate(flops=flops, bytes_accessed=0, transcendentals=0),
     )(*operands)
@@ -383,48 +382,65 @@
     out[...] = ((total - rows) * loss_scale).astype(jnp.bfloat16)
 
 
-def backward_kernel(columns, places, first, last, *refs):
+def piece_columns(which, width, piece):
     _, core, column = place()
-    pieces, refs = refs[: len(places)], refs[len(places) :]
-    hidden_t, w2, refs = refs[0], refs[1], refs[2:]
-    if not first:
-        sum_in, refs = refs[0], refs[2:]
-    if last:
-        flat_t, slope, grad_second, grad_first, held_first, held_second, sems = refs
-    else:
-        grad_second, sum_out, held_second, sems = refs
-    piece = pieces[0].shape[1]
-    width = w2.shape[1]
-    hidden_grad = None if first else sum_in[...]
+    other, m = which
+    start = (1 - core if other else core) * (width // 2) + (column ^ m) * piece
+    return pl.ds(pl.multiple_of(start, piece), piece)
+
+
+def use_piece(ref, cols, hidden_t, w2, hidden_grad):
+    _, core, _ = place()
+    half = ref.shape[0] // 2
+    rows = jnp.concatenate(
+        [ref[pl.ds(pl.multiple_of(block * half, 16), half), :] for block in (core, 1 - core)],
+        axis=0,
+    )
+    term = dot_nt(rows, w2[:, cols])
+    hidden_grad = term if hidden_grad is None else hidden_grad + term
+    return hidden_grad, rows
+
+
+def early_kernel(places, first, *refs):
+    count = len(places)
+    pieces, (hidden_t, w2), refs = refs[:count], refs[count : count + 2], refs[count + 2 :]
+    hidden_grad = None if first else refs[0][...]
+    sum_out, *grads = refs if first else refs[1:]
+    piece, width = pieces[0].shape[1], w2.shape[1]
+    for ref, which, out in zip(pieces, places, grads):
+        cols = piece_columns(which, width, piece)
+        hidden_grad, rows = use_piece(ref, cols, hidden_t, w2, hidden_grad)
+        out[...] = dot(hidden_t[...], rows).astype(jnp.bfloat16)
+    sum_out[...] = hidden_grad
+
+
+def last_kernel(places, early, *refs):
+    count = len(places)
+    pieces, refs = refs[:count], refs[count:]
+    done, refs = refs[: len(early)], refs[len(early) :]
+    hidden_t, w2, sum_in, flat_t, slope, grad_first, grad_second, held_first, held_second, sems = refs
+    piece, width = pieces[0].shape[1], w2.shape[1]
     copies = []
 
     def leave(source, target):
         copies.append(pltpu.make_async_copy(source, target, sems.at[len(copies)]))
         copies[-1].start()
 
+    for ref, which in zip(done, early):
+        leave(ref, grad_second.at[:, piece_columns(which, width, piece)])
+    hidden_grad = sum_in[...]
     used = []
-    for ref, (other, m) in zip(pieces, places):
-        which = 1 - core if other else core
-        start = which * (width // 2) + (column ^ m) * piece
-        cols = pl.ds(pl.multiple_of(start, piece), piece)
-        half = ref.shape[0] // 2
-        rows = jnp.concatenate(
-            [ref[pl.ds(pl.multiple_of(block * half, 16), half), :] for block in (core, 1 - core)],
-            axis=0,
-        )
-        used.append((rows, cols))
-        term = dot_nt(rows, w2[:, cols])
-        hidden_grad = term if hidden_grad is None else hidden_grad + term
-    if last:
-        pre_grad = (hidden_grad * slope[...]).astype(jnp.bfloat16)
-        step = 512
-        for j in range(width // step):
-            here = slice(j * step, (j + 1) * step)
-            held_first[here, :] = dot(flat_t[here, :], pre_grad).astype(jnp.bfloat16)
-            leave(held_first.at[here, :], grad_first.at[here, :])
-    else:
-        sum_out[...] = hidden_grad
-    for i, (rows, cols) in enumerate(used):
+    for ref, which in zip(pieces, places):
+        cols = piece_columns(which, width, piece)
+        hidden_grad, rows = use_piece(ref, cols, hidden_t, w2, hidden_grad)
+        used.append((cols, rows))
+    pre_grad = (hidden_grad * slope[...]).astype(jnp.bfloat16)
+    step = 512
+    for j in range(width // step):
+        here = slice(j * step, (j + 1) * step)
+        held_first[here, :] = dot(flat_t[here, :], pre_grad).astype(jnp.bfloat16)
+        leave(held_first.at[here, :], grad_first.at[here, :])
+    for i, (cols, rows) in enumerate(used):
         held_second[i] = dot(hidden_t[...], rows).astype(jnp.bfloat16)
         leave(held_second.at[i], grad_second.at[:, cols])
     for copy in copies:
@@ -529,7 +545,7 @@
     routes = jnp.concatenate([route_t, route_s], axis=0)
     other_routes = across(routes)
     w1_t, w2_t = load(teacher_w1[0], teacher_w2[0])
-    moved = after(over_planes(sent), stay_t, stay_s, other_routes, w1_t)
+    moved = after(over_planes(sent), stay_t, other_routes, w1_t)
     mine_t, mine_s = call(
         stack_kernel, [shape((experts - 1) * capacity, feat)] * 2, moved, name="stack"
     )
@@ -557,7 +573,7 @@
     got_own = across(send)
     send, hidden_other = forward([flat_t_other], w1_t, w2_t, False, "forward_t", 0)
     got_other = across(send)
-    kept = keep(hidden_own, after(hidden_other, got_s, w1_s), w2_t, [], [])
+    kept = keep(hidden_own, after(hidden_other, got_s, w1_s, stay_s), w2_t, [], [])
     pieces_t = pair(kept, [got_own, got_other])
     sums_t = collect(*pieces_t)
 
@@ -589,7 +605,7 @@
         lambda *refs: home_kernel(experts, capacity, *refs),
         [shape(2 * capacity, piece)] * experts,
         [maps, *home],
-        flops=0 * plane_rows * width * hid,
+        flops=4 * plane_rows * width * hid,
         name="home",
     )
     teachers = [*over_planes(slots[:-1]), slots[-1]]
@@ -598,49 +614,44 @@
         [shape(plane_rows, piece)],
         [*sums_s, *teachers],
     )
-    def backward(pieces, state, last):
-        first = state is None
+    early = {}
+
+    def backward(pieces, total):
+        first = total is None
         places = tuple(pieces)
-        operands = [pieces[key] for key in places] + [hidden_t, w2_s]
-        in_specs = [VMEM] * len(operands)
-        aliases = {}
-        if not first:
-            operands += [state[1], state[0]]
-            in_specs += [VMEM, ANY]
-            aliases = {len(operands) - 1: 0}
-        outs = [shape(hid, width)]
-        scratch = [pltpu.VMEM((len(places), hid, piece), jnp.bfloat16)]
-        copies = len(places)
-        if last:
-            operands += [flat_t, slope]
-            in_specs += [VMEM, VMEM]
-            outs += [shape(width, hid)]
-            out_specs = [ANY, ANY]
-            scratch = [pltpu.VMEM((width, hid), jnp.bfloat16)] + scratch
-            copies += width // 512
-        else:
-            outs += [shape(plane_rows, hid, dtype=f32)]
-            out_specs = [ANY, VMEM]
+        total, *done = call(
+            lambda *refs: early_kernel(places, first, *refs),
+            [shape(plane_rows, hid, dtype=f32)] + [shape(hid, piece)] * len(places),
+            [*pieces.values(), hidden_t, w2_s] + ([] if first else [total]),
+            name="early",
+        )
+        early.update(zip(places, done))
+        return total
+
+    def finish(pieces, total):
+        places, kept_places = tuple(pieces), tuple(early)
         return call(
-            lambda *refs: backward_kernel(columns, places, first, last, *refs),
-            outs,
-            operands,
-            out_specs=out_specs,
-            in_specs=in_specs,
-            scratch=scratch + [pltpu.SemaphoreType.DMA((copies,))],
-            aliases=aliases,
+            lambda *refs: last_kernel(places, kept_places, *refs),
+            [shape(width, hid), shape(hid, width)],
+            [*pieces.values(), *early.values(), hidden_t, w2_s, total, flat_t, slope],
+            out_specs=[ANY, ANY],
+            scratch=[
+                pltpu.VMEM((width, hid), jnp.bfloat16),
+                pltpu.VMEM((len(places), hid, piece), jnp.bfloat16),
+                pltpu.SemaphoreType.DMA((len(places) + len(early) + width // 512,)),
+            ],
+            name="last",
         )
 
     grads = spread(upstream)
-    state = backward({(0, 0): upstream, (1, 0): across(upstream)}, None, False)
-    far = after(grads[3], state[1])
-    state = backward({(0, 3): far}, state, False)
-    near = after(grads[1:3], state[1])
-    others = [across(value) for value in (*near, far)]
-    state = backward({(0, m + 1): near[m] for m in range(2)}, state, False)
-    grad_second, grad_first = backward(
-        {(1, m + 1): value for m, value in enumerate(others)}, state, True
-    )
+    total = backward({(0, 0): upstream, (1, 0): across(upstream)}, None)
+    far = after(grads[3], total)
+    total = backward({(0, 3): far}, total)
+    near = after(grads[1:3], total)
+    other_far = across(far)
+    others = [across(value) for value in near]
+    total = backward({(0, 1): near[0], (0, 2): near[1], (1, 3): other_far}, total)
+    grad_first, grad_second = finish({(1, 1): others[0], (1, 2): others[1]}, total)
     return (grad_first[None], grad_second[None])
 
 def on_device(*arrays):

time: 80.9 us -> 79.6 us (0.984)
  Pallas kernels: 17.3 us -> 14.8 us
  starting transfers between devices: 34.6 us -> 35.5 us
  waiting for transfers between devices: 21.6 us -> 22.5 us
    pallas_call x23, Pallas kernels: 17.3 us -> 14.8 us  [call(): pl.pallas_call(kernel, name=name, out_shape=outs, in_specs=in_specs or [V...]
    ppermute x34, waiting for transfers between devices: 21.6 us -> 22.5 us  [partner(): lax.ppermute(value, axis, [(i, i ^ mask) for i in range(lax.axis_size(axi...]
    ppermute x34, starting transfers between devices: 34.6 us -> 35.5 us  [partner(): lax.ppermute(value, axis, [(i, i ^ mask) for i in range(lax.axis_size(axi...]
  transfers between devices with their start and end apart: 34 -> 34, of which waited for: 13 -> 15; matrix products, arithmetic and copies ran while one was open for 1% -> 1% of each run, Pallas kernels for 15% -> 12%
where the time goes in v5:
time: 79.6 us; the launch traced here: 79.3 us
  starting transfers between devices  35.5 us (45%)
  waiting for transfers between devices  22.5 us (28%)
  Pallas kernels  14.8 us (19%)
  local copies, waits for them, and re-layouts  4.9 us (6%)
  between operations  0.93 us (1%)
    ppermute x34, starting transfers between devices, partner(): lax.ppermute(value, axis, [(i, i ^ mask) for i in range(lax.axis_size(axi...  35.5 us
    ppermute x34, waiting for transfers between devices, partner(): lax.ppermute(value, axis, [(i, i ^ mask) for i in range(lax.axis_size(axi...  22.5 us
    pallas_call x23, Pallas kernels, call(): pl.pallas_call(kernel, name=name, out_shape=outs, in_specs=in_specs or [V...  14.8 us
    unnamed x16, local copies, waits for them, and re-layouts  4.9 us
  transfers between devices with their start and end apart: 34, of which 15 were waited for; matrix products, arithmetic and copies ran while one was open for 1% of the time, Pallas kernels for 12%

profile of v5, /device:TPU:0, one launch (start us, length us, event | category | flops | bytes accessed | tf_op | source)
XLA Modules:
  0.0 79.3 jit_solution(14184017654881228205)
XLA Ops:
  0.6 2.0 %pack.1 = (bf16[48,1024]{1,0:T(8,128)(2,1)}, bf16[48,1024]{1,0:T(8,128)(2,1)}, bf16[48,1024]{1,0:T(8,128)(2,1)}) custom-call(bf16[128,2048]{1,0:T(8,128)(2,1)} %refs_0_.5, bf16[128,2048]{1,0:T(8,128)(2,1)} %refs_1_.1, s32[1,128]{1,0:T(1,128)} %bitcast.12, s32[1,128]{1,0:T(1,128)} %bitcast.15), custom_call_target="tpu_custom_call" | custom-call | tf_op jit(solution)/shard_map/pack/pallas_call | solution.py:172
  2.6 4.1 %collective-permute-start = (bf16[48,1024]{1,0:T(8,128)(2,1)}, bf16[48,1024]{1,0:T(8,128)(2,1)S(1)}, u32[]{:S(2)}, u32[]{:S(2)}) collective-permute-start(bf16[48,1024]{1,0:T(8,128)(2,1)} %get-tuple-element.74), channel_id=1, source_target_pairs={{0,16},{4,20},{8,24},{12,28},{16,0},{20,4},{24,8},{28,12},{1,17},{... | collective-permute-start | bytes 294920 | tf_op jit(solution)/shard_map/ppermute | solution.py:15
  6.7 1.3 %collective-permute-start.1 = (bf16[48,1024]{1,0:T(8,128)(2,1)}, bf16[48,1024]{1,0:T(8,128)(2,1)S(1)}, u32[]{:S(2)}, u32[]{:S(2)}) collective-permute-start(bf16[48,1024]{1,0:T(8,128)(2,1)} %get-tuple-element.75), channel_id=1, source_target_pairs={{0,24},{4,28},{8,16},{12,20},{16,8},{20,12},{24,0},{28,4},{1,25},{... | collective-permute-start | bytes 294920 | tf_op jit(solution)/shard_map/ppermute | solution.py:15
  8.0 0.2 collective-permute-start.2
  8.3 0.7 pad_add_fusion.refs_0_
  9.0 1.0 %copy-done = bf16[128,2048]{1,0:T(8,128)(2,1)S(1)} copy-done((bf16[128,2048]{1,0:T(8,128)(2,1)S(1)}, bf16[128,2048]{1,0:T(8,128)(2,1)}, u32[]{:S(2)}) %copy-start) | copy-done | bytes 524312
  10.0 0.7 copy-done.6
  10.7 0.3 stay.3.refs_0_
  11.0 1.6 %copy-done.2 = bf16[1,2048,512]{2,1,0:T(8,128)(2,1)S(1)} copy-done((bf16[1,2048,512]{2,1,0:T(8,128)(2,1)S(1)}, bf16[1,2048,512]{2,1,0:T(8,128)(2,1)}, u32[]{:S(2)}) %copy-start.2) | copy-done | bytes 2097176
  12.6 1.6 %copy-done.3 = bf16[1,512,2048]{2,1,0:T(8,128)(2,1)S(1)} copy-done((bf16[1,512,2048]{2,1,0:T(8,128)(2,1)S(1)}, bf16[1,512,2048]{2,1,0:T(8,128)(2,1)}, u32[]{:S(2)}) %copy-start.3) | copy-done | bytes 2097176
  14.2 0.3 load.2
  14.5 0.3 collective-permute-done.refs_0_
  14.8 0.5 collective-permute-done.2.refs_2_
  15.3 2.6 %collective-permute-start.9 = (bf16[144,512]{1,0:T(8,128)(2,1)S(1)}, bf16[144,512]{1,0:T(8,128)(2,1)S(1)}, u32[]{:S(2)}, u32[]{:S(2)}) collective-permute-start(bf16[144,512]{1,0:T(8,128)(2,1)S(1)} %get-tuple-element.83.refs_1_), channel_id=1, source_target_pairs={{0,3},{1,2},{2,1},{3,0},{4,7},{5,6},{6,5},{7,4},{8,11},{9,10},{10,... | collective-permute-start | bytes 442376 | tf_op jit(solution)/shard_map/ppermute | solution.py:15
  17.9 0.5 collective-permute-start.8
  18.4 0.5 collective-permute-start.7
  18.9 0.4 maps.1.refs_0_
  19.3 2.6 %collective-permute-start.6 = (bf16[144,512]{1,0:T(8,128)(2,1)S(1)}, bf16[144,512]{1,0:T(8,128)(2,1)S(1)}, u32[]{:S(2)}, u32[]{:S(2)}) collective-permute-start(bf16[144,512]{1,0:T(8,128)(2,1)S(1)} %get-tuple-element.97.refs_1_), channel_id=1, source_target_pairs={{0,3},{1,2},{2,1},{3,0},{4,7},{5,6},{6,5},{7,4},{8,11},{9,10},{10,... | collective-permute-start | bytes 442376 | tf_op jit(solution)/shard_map/ppermute | solution.py:15
  21.8 0.5 collective-permute-start.5
  22.5 2.1 %collective-permute-start.4 = (bf16[144,512]{1,0:T(8,128)(2,1)S(1)}, bf16[144,512]{1,0:T(8,128)(2,1)S(1)}, u32[]{:S(2)}, u32[]{:S(2)}) collective-permute-start(bf16[144,512]{1,0:T(8,128)(2,1)S(1)} %get-tuple-element.97.refs_1_), channel_id=1, source_target_pairs={{0,1},{1,0},{2,3},{3,2},{4,5},{5,4},{6,7},{7,6},{8,9},{9,8},{10,11... | collective-permute-start | bytes 442376 | tf_op jit(solution)/shard_map/ppermute | solution.py:15
  24.6 2.7 %collective-permute-done.8.refs_3_ = bf16[144,512]{1,0:T(8,128)(2,1)S(1)} collective-permute-done((bf16[144,512]{1,0:T(8,128)(2,1)S(1)}, bf16[144,512]{1,0:T(8,128)(2,1)S(1)}, u32[]{:S(2)}, u32[]{:S(2)}) %collective-permute-start.8) | collective-permute-done | bytes 147488 | tf_op jit(solution)/shard_map/ppermute | solution.py:15
  27.4 0.9 %forward_t.2 = (bf16[1,4,192,256]{3,2,1,0:T(8,128)(2,1)S(1)}, bf16[192,512]{1,0:T(8,128)(2,1)S(1)}) custom-call(bf16[192,2048]{1,0:T(8,128)(2,1)S(1)} %join.2.refs_0_, bf16[2048,512]{1,0:T(8,128)(2,1)S(1)} %get-tuple-element.77.refs_1_, bf16[512,2048]{1,0:T(8,128)(2,1)S(1)} %get-tuple-element.87.refs_2_), custom_call_target="tpu_custom_call" | custom-call | flops 9663676416 | tf_op jit(solution)/shard_map/forward_t/pallas_call | solution.py:172
  28.4 0.6 collective-permute-start.11
  29.0 0.7 collective-permute-done.10.refs_0_
  29.7 0.9 %forward_t.3 = (bf16[1,4,192,256]{3,2,1,0:T(8,128)(2,1)S(1)}, bf16[192,512]{1,0:T(8,128)(2,1)S(1)}) custom-call(bf16[192,2048]{1,0:T(8,128)(2,1)S(1)} %collective-permute-done.10.refs_0_, bf16[2048,512]{1,0:T(8,128)(2,1)S(1)} %get-tuple-element.77.refs_1_, bf16[512,2048]{1,0:T(8,128)(2,1)S(1)} %get-tuple-element.87.refs_2_), custom_call_target="tpu_custom_call" | custom-call | tf_op jit(solution)/shard_map/forward_t/pallas_call | solution.py:172
  30.6 0.2 collective-permute-start.12
  30.8 0.3 stay.2.refs_0_
  31.2 0.3 load.3
  31.5 0.6 keep_t.1
  32.2 0.2 collective-permute-done.12.refs_3_
  32.7 0.2 collective-permute-start.13
  32.9 1.0 %collective-permute-start.18 = (bf16[384,256]{1,0:T(8,128)(2,1)S(1)}, bf16[384,256]{1,0:T(8,128)(2,1)S(1)}, u32[]{:S(2)}, u32[]{:S(2)}) collective-permute-start(bf16[384,256]{1,0:T(8,128)(2,1)S(1)} %get-tuple-element.113), channel_id=1, source_target_pairs={{0,1},{1,0},{2,3},{3,2},{4,5},{5,4},{6,7},{7,6},{8,9},{9,8},{10,11... | collective-permute-start | bytes 589832 | tf_op jit(solution)/shard_map/ppermute | solution.py:15
  33.9 1.9 %collective-permute-start.19 = (bf16[384,256]{1,0:T(8,128)(2,1)S(1)}, bf16[384,256]{1,0:T(8,128)(2,1)S(1)}, u32[]{:S(2)}, u32[]{:S(2)}) collective-permute-start(bf16[384,256]{1,0:T(8,128)(2,1)S(1)} %get-tuple-element.114), channel_id=1, source_target_pairs={{0,2},{1,3},{2,0},{3,1},{4,6},{5,7},{6,4},{7,5},{8,10},{9,11},{10,... | collective-permute-start | bytes 589832 | tf_op jit(solution)/shard_map/ppermute | solution.py:15
  35.8 0.6 collective-permute-start.20
  36.4 1.7 %forward_s.1 = (bf16[2,4,192,256]{3,2,1,0:T(8,128)(2,1)S(1)}, bf16[192,512]{1,0:T(8,128)(2,1)S(1)}, bf16[192,512]{1,0:T(8,128)(2,1)S(1)}, f32[192,512]{1,0:T(8,128)S(1)}, f32[192,512]{1,0:T(8,128)S(1)}) custom-call(bf16[192,2048]{1,0:T(8,128)(2,1)S(1)} %join.3.refs_0_.refs_5_, bf16[192,2048]{1,0:T(8,128)(2,1)S(1)} %collective-permute-done.13.refs_1_.refs_6_, ...), custom_call_target="tpu_custom_call" | custom-call | tf_op jit(solution)/shard_map/forward_s/pallas_call | solution.py:172
  38.2 1.4 %keep_s.1 = (bf16[4,192,256]{2,1,0:T(8,128)(2,1)S(1)}, bf16[4,192,256]{2,1,0:T(8,128)(2,1)S(1)}, bf16[2048,384]{1,0:T(8,128)(2,1)S(1)}, bf16[512,384]{1,0:T(8,128)(2,1)S(1)}, f32[384,512]{1,0:T(8,128)S(1)}) custom-call(bf16[192,512]{1,0:T(8,128)(2,1)S(1)} %get-tuple-element.102.refs_0_, bf16[192,512]{1,0:T(8,128)(2,1)S(1)} %get-tuple-element.103.refs_1_, ...), custom_call_target="tpu_custom_call" | custom-call | flops 25769803776 | tf_op jit(solution)/shard_map/keep_s/pallas_call | solution.py:172
  39.6 0.9 %collective-permute-done.14.refs_2_ = bf16[2,4,192,256]{3,2,1,0:T(8,128)(2,1)S(1)} collective-permute-done((bf16[2,4,192,256]{3,2,1,0:T(8,128)(2,1)S(1)}, bf16[2,4,192,256]{3,2,1,0:T(8,128)(2,1)S(1)}, u32[]{:S(2)}, u32[]{:S(2)}) %collective-permute-start.14) | collective-permute-done | bytes 786464 | tf_op jit(solution)/shard_map/ppermute | solution.py:15
  40.5 0.2 pair.3
  40.7 1.1 %collective-permute-start.15 = (bf16[384,256]{1,0:T(8,128)(2,1)S(1)}, bf16[384,256]{1,0:T(8,128)(2,1)S(1)}, u32[]{:S(2)}, u32[]{:S(2)}) collective-permute-start(bf16[384,256]{1,0:T(8,128)(2,1)S(1)} %get-tuple-element.110), channel_id=1, source_target_pairs={{0,1},{1,0},{2,3},{3,2},{4,5},{5,4},{6,7},{7,6},{8,9},{9,8},{10,11... | collective-permute-start | bytes 589832 | tf_op jit(solution)/shard_map/ppermute | solution.py:15
  41.7 3.3 %collective-permute-done.19.refs_2_ = bf16[384,256]{1,0:T(8,128)(2,1)S(1)} collective-permute-done((bf16[384,256]{1,0:T(8,128)(2,1)S(1)}, bf16[384,256]{1,0:T(8,128)(2,1)S(1)}, u32[]{:S(2)}, u32[]{:S(2)}) %collective-permute-start.19) | collective-permute-done | bytes 196640 | tf_op jit(solution)/shard_map/ppermute | solution.py:15
  45.0 0.2 collective-permute-done.20.refs_3_
  45.3 3.7 %collective-permute-start.21 = (bf16[96,256]{1,0:T(8,128)(2,1)S(1)}, bf16[96,256]{1,0:T(8,128)(2,1)S(1)}, u32[]{:S(2)}, u32[]{:S(2)}) collective-permute-start(bf16[96,256]{1,0:T(8,128)(2,1)S(1)} %get-tuple-element.120), channel_id=1, source_target_pairs={{0,16},{4,20},{8,24},{12,28},{16,0},{20,4},{24,8},{28,12},{1,17},{... | collective-permute-start | bytes 147464 | tf_op jit(solution)/shard_map/ppermute | solution.py:15
  49.1 0.6 collective-permute-start.22
  49.6 0.4 collective-permute-start.23
  50.0 1.4 %collective-permute-start.16 = (bf16[384,256]{1,0:T(8,128)(2,1)S(1)}, bf16[384,256]{1,0:T(8,128)(2,1)S(1)}, u32[]{:S(2)}, u32[]{:S(2)}) collective-permute-start(bf16[384,256]{1,0:T(8,128)(2,1)S(1)} %get-tuple-element.111), channel_id=1, source_target_pairs={{0,2},{1,3},{2,0},{3,1},{4,6},{5,7},{6,4},{7,5},{8,10},{9,11},{10,... | collective-permute-start | bytes 589832 | tf_op jit(solution)/shard_map/ppermute | solution.py:15
  51.4 1.6 %collective-permute-start.17 = (bf16[384,256]{1,0:T(8,128)(2,1)S(1)}, bf16[384,256]{1,0:T(8,128)(2,1)S(1)}, u32[]{:S(2)}, u32[]{:S(2)}) collective-permute-start(bf16[384,256]{1,0:T(8,128)(2,1)S(1)} %get-tuple-element.112), channel_id=1, source_target_pairs={{0,3},{1,2},{2,1},{3,0},{4,7},{5,6},{6,5},{7,4},{8,11},{9,10},{10,... | collective-permute-start | bytes 589832 | tf_op jit(solution)/shard_map/ppermute | solution.py:15
  53.0 1.9 %collective-permute-done.22.refs_2_ = bf16[96,256]{1,0:T(8,128)(2,1)S(1)} collective-permute-done((bf16[96,256]{1,0:T(8,128)(2,1)S(1)}, bf16[96,256]{1,0:T(8,128)(2,1)S(1)}, u32[]{:S(2)}, u32[]{:S(2)}) %collective-permute-start.22) | collective-permute-done | bytes 49184 | tf_op jit(solution)/shard_map/ppermute | solution.py:15
  54.9 0.2 home.1
  55.2 1.2 %collective-permute-start.24 = (bf16[96,256]{1,0:T(8,128)(2,1)S(1)}, bf16[96,256]{1,0:T(8,128)(2,1)S(1)}, u32[]{:S(2)}, u32[]{:S(2)}) collective-permute-start(bf16[96,256]{1,0:T(8,128)(2,1)S(1)} %get-tuple-element.125), channel_id=1, source_target_pairs={{0,16},{4,20},{8,24},{12,28},{16,0},{20,4},{24,8},{28,12},{1,17},{... | collective-permute-start | bytes 147464 | tf_op jit(solution)/shard_map/ppermute | solution.py:15
  56.3 1.0 %collective-permute-start.25 = (bf16[96,256]{1,0:T(8,128)(2,1)S(1)}, bf16[96,256]{1,0:T(8,128)(2,1)S(1)}, u32[]{:S(2)}, u32[]{:S(2)}) collective-permute-start(bf16[96,256]{1,0:T(8,128)(2,1)S(1)} %get-tuple-element.126), channel_id=1, source_target_pairs={{0,24},{4,28},{8,16},{12,20},{16,8},{20,12},{24,0},{28,4},{1,25},{... | collective-permute-start | bytes 147464 | tf_op jit(solution)/shard_map/ppermute | solution.py:15
  57.3 1.4 %collective-permute-start.26 = (bf16[96,256]{1,0:T(8,128)(2,1)S(1)}, bf16[96,256]{1,0:T(8,128)(2,1)S(1)}, u32[]{:S(2)}, u32[]{:S(2)}) collective-permute-start(bf16[96,256]{1,0:T(8,128)(2,1)S(1)} %get-tuple-element.127), channel_id=1, source_target_pairs={{0,8},{4,12},{8,0},{12,4},{16,24},{20,28},{24,16},{28,20},{1,9},{5... | collective-permute-start | bytes 147464 | tf_op jit(solution)/shard_map/ppermute | solution.py:15
  58.7 1.7 %collective-permute-done.16.refs_2_ = bf16[384,256]{1,0:T(8,128)(2,1)S(1)} collective-permute-done((bf16[384,256]{1,0:T(8,128)(2,1)S(1)}, bf16[384,256]{1,0:T(8,128)(2,1)S(1)}, u32[]{:S(2)}, u32[]{:S(2)}) %collective-permute-start.16) | collective-permute-done | bytes 196640 | tf_op jit(solution)/shard_map/ppermute | solution.py:15
  60.4 1.7 %collective-permute-done.25.refs_5_ = bf16[96,256]{1,0:T(8,128)(2,1)S(1)} collective-permute-done((bf16[96,256]{1,0:T(8,128)(2,1)S(1)}, bf16[96,256]{1,0:T(8,128)(2,1)S(1)}, u32[]{:S(2)}, u32[]{:S(2)}) %collective-permute-start.25) | collective-permute-done | bytes 49184 | tf_op jit(solution)/shard_map/ppermute | solution.py:15
  62.4 1.6 %collective-permute-start.29 = (bf16[384,256]{1,0:T(8,128)(2,1)S(1)}, bf16[384,256]{1,0:T(8,128)(2,1)S(1)}, u32[]{:S(2)}, u32[]{:S(2)}) collective-permute-start(bf16[384,256]{1,0:T(8,128)(2,1)S(1)} %shard_map.96.refs_0_), channel_id=1, source_target_pairs={{0,3},{1,2},{2,1},{3,0},{4,7},{5,6},{6,5},{7,4},{8,11},{9,10},{10,... | collective-permute-start | bytes 589832 | tf_op jit(solution)/shard_map/ppermute | solution.py:15
  64.1 1.3 %collective-permute-start.28 = (bf16[384,256]{1,0:T(8,128)(2,1)S(1)}, bf16[384,256]{1,0:T(8,128)(2,1)S(1)}, u32[]{:S(2)}, u32[]{:S(2)}) collective-permute-start(bf16[384,256]{1,0:T(8,128)(2,1)S(1)} %shard_map.96.refs_0_), channel_id=1, source_target_pairs={{0,2},{1,3},{2,0},{3,1},{4,6},{5,7},{6,4},{7,5},{8,10},{9,11},{10,... | collective-permute-start | bytes 589832 | tf_op jit(solution)/shard_map/ppermute | solution.py:15
  65.3 0.6 collective-permute-start.27
  66.0 0.6 early.3
  66.6 4.5 %collective-permute-done.29.refs_0_ = bf16[384,256]{1,0:T(8,128)(2,1)S(1)} collective-permute-done((bf16[384,256]{1,0:T(8,128)(2,1)S(1)}, bf16[384,256]{1,0:T(8,128)(2,1)S(1)}, u32[]{:S(2)}, u32[]{:S(2)}) %collective-permute-start.29) | collective-permute-done | bytes 196640 | tf_op jit(solution)/shard_map/ppermute | solution.py:15
  71.1 0.4 early.4
  71.5 3.3 %collective-permute-done.28.refs_1_ = bf16[384,256]{1,0:T(8,128)(2,1)S(1)} collective-permute-done((bf16[384,256]{1,0:T(8,128)(2,1)S(1)}, bf16[384,256]{1,0:T(8,128)(2,1)S(1)}, u32[]{:S(2)}, u32[]{:S(2)}) %collective-permute-start.28) | collective-permute-done | bytes 196640 | tf_op jit(solution)/shard_map/ppermute | solution.py:15
  74.9 0.5 collective-permute-start.32
  75.4 0.9 %early.5 = (f32[384,512]{1,0:T(8,128)S(1)}, bf16[512,256]{1,0:T(8,128)(2,1)S(1)}, bf16[512,256]{1,0:T(8,128)(2,1)S(1)}, bf16[512,256]{1,0:T(8,128)(2,1)S(1)}) custom-call(bf16[384,256]{1,0:T(8,128)(2,1)S(1)} %collective-permute-done.27.refs_0_, bf16[384,256]{1,0:T(8,128)(2,1)S(1)} %collective-permute-done.28.refs_1_, ...), custom_call_target="tpu_custom_call" | custom-call | tf_op jit(solution)/shard_map/early/pallas_call | solution.py:172
  76.3 0.3 collective-permute-done.32.refs_1_
  76.6 2.8 %last.1 = (bf16[2048,512]{1,0:T(8,128)(2,1)}, bf16[512,2048]{1,0:T(8,128)(2,1)}) custom-call(bf16[384,256]{1,0:T(8,128)(2,1)S(1)} %collective-permute-done.31.refs_0_, bf16[384,256]{1,0:T(8,128)(2,1)S(1)} %collective-permute-done.32.refs_1_, bf16[512,256]{1,0:T(8,128)(2,1)S(1)} %get-tuple-element.135.refs_2_, ...), custom_call_target="tpu_custom_call" | custom-call | tf_op jit(solution)/shard_map/last/pallas_call | solution.py:172
  (44 shorter events, 1.0 us)
Async XLA Ops:
  2.6 12.2 %collective-permute-start = (bf16[48,1024]{1,0:T(8,128)(2,1)}, bf16[48,1024]{1,0:T(8,128)(2,1)S(1)}, u32[]{:S(2)}, u32[]{:S(2)}) collective-permute-start(bf16[48,1024]{1,0:T(8,128)(2,1)} %get-tuple-element.74), channel_id=1, source_target_pairs={{0,16},{4,20},{8,24},{12,28},{16,0},{20,4},{24,8},{28,12},{1,17},{... | collective-permute-start | bytes 294920 | tf_op jit(solution)/shard_map/ppermute | solution.py:15
  6.7 8.1 %collective-permute-start.1 = (bf16[48,1024]{1,0:T(8,128)(2,1)}, bf16[48,1024]{1,0:T(8,128)(2,1)S(1)}, u32[]{:S(2)}, u32[]{:S(2)}) collective-permute-start(bf16[48,1024]{1,0:T(8,128)(2,1)} %get-tuple-element.75), channel_id=1, source_target_pairs={{0,24},{4,28},{8,16},{12,20},{16,8},{20,12},{24,0},{28,4},{1,25},{... | collective-permute-start | bytes 294920 | tf_op jit(solution)/shard_map/ppermute | solution.py:15
  8.0 7.3 %collective-permute-start.2 = (bf16[48,1024]{1,0:T(8,128)(2,1)}, bf16[48,1024]{1,0:T(8,128)(2,1)S(1)}, u32[]{:S(2)}, u32[]{:S(2)}) collective-permute-start(bf16[48,1024]{1,0:T(8,128)(2,1)} %get-tuple-element.76), channel_id=1, source_target_pairs={{0,8},{4,12},{8,0},{12,4},{16,24},{20,28},{24,16},{28,20},{1,9},{5... | collective-permute-start | bytes 294920 | tf_op jit(solution)/shard_map/ppermute | solution.py:15
  9.0 5.6 %collective-permute-start.3 = (s32[2,128]{1,0:T(2,128)S(1)}, s32[2,128]{1,0:T(2,128)S(1)}, u32[]{:S(2)}, u32[]{:S(2)}) collective-permute-start(s32[2,128]{1,0:T(2,128)S(1)} %pad_add_fusion.refs_0_), channel_id=1, source_target_pairs={{0,4},{4,0},{8,12},{12,8},{16,20},{20,16},{24,28},{28,24},{1,5},{5... | collective-permute-start | bytes 3080 | tf_op jit(solution)/shard_map/ppermute | solution.py:15
  9.0 1.0 %copy-start = (bf16[128,2048]{1,0:T(8,128)(2,1)S(1)}, bf16[128,2048]{1,0:T(8,128)(2,1)}, u32[]{:S(2)}) copy-start(bf16[128,2048]{1,0:T(8,128)(2,1)} %refs_0_.5) | copy-start | bytes 1572868
  10.0 0.7 copy-start.6
  11.0 1.6 %copy-start.2 = (bf16[1,2048,512]{2,1,0:T(8,128)(2,1)S(1)}, bf16[1,2048,512]{2,1,0:T(8,128)(2,1)}, u32[]{:S(2)}) copy-start(bf16[1,2048,512]{2,1,0:T(8,128)(2,1)} %param.12) | copy-start | bytes 6291460
  12.6 1.6 %copy-start.3 = (bf16[1,512,2048]{2,1,0:T(8,128)(2,1)S(1)}, bf16[1,512,2048]{2,1,0:T(8,128)(2,1)}, u32[]{:S(2)}) copy-start(bf16[1,512,2048]{2,1,0:T(8,128)(2,1)} %param.13) | copy-start | bytes 6291460
  15.3 7.1 %collective-permute-start.9 = (bf16[144,512]{1,0:T(8,128)(2,1)S(1)}, bf16[144,512]{1,0:T(8,128)(2,1)S(1)}, u32[]{:S(2)}, u32[]{:S(2)}) collective-permute-start(bf16[144,512]{1,0:T(8,128)(2,1)S(1)} %get-tuple-element.83.refs_1_), channel_id=1, source_target_pairs={{0,3},{1,2},{2,1},{3,0},{4,7},{5,6},{6,5},{7,4},{8,11},{9,10},{10,... | collective-permute-start | bytes 442376 | tf_op jit(solution)/shard_map/ppermute | solution.py:15
  17.9 9.4 %collective-permute-start.8 = (bf16[144,512]{1,0:T(8,128)(2,1)S(1)}, bf16[144,512]{1,0:T(8,128)(2,1)S(1)}, u32[]{:S(2)}, u32[]{:S(2)}) collective-permute-start(bf16[144,512]{1,0:T(8,128)(2,1)S(1)} %get-tuple-element.83.refs_1_), channel_id=1, source_target_pairs={{0,2},{1,3},{2,0},{3,1},{4,6},{5,7},{6,4},{7,5},{8,10},{9,11},{10,... | collective-permute-start | bytes 442376 | tf_op jit(solution)/shard_map/ppermute | solution.py:15
  18.4 8.9 %collective-permute-start.7 = (bf16[144,512]{1,0:T(8,128)(2,1)S(1)}, bf16[144,512]{1,0:T(8,128)(2,1)S(1)}, u32[]{:S(2)}, u32[]{:S(2)}) collective-permute-start(bf16[144,512]{1,0:T(8,128)(2,1)S(1)} %get-tuple-element.83.refs_1_), channel_id=1, source_target_pairs={{0,1},{1,0},{2,3},{3,2},{4,5},{5,4},{6,7},{7,6},{8,9},{9,8},{10,11... | collective-permute-start | bytes 442376 | tf_op jit(solution)/shard_map/ppermute | solution.py:15
  19.3 12.2 %collective-permute-start.6 = (bf16[144,512]{1,0:T(8,128)(2,1)S(1)}, bf16[144,512]{1,0:T(8,128)(2,1)S(1)}, u32[]{:S(2)}, u32[]{:S(2)}) collective-permute-start(bf16[144,512]{1,0:T(8,128)(2,1)S(1)} %get-tuple-element.97.refs_1_), channel_id=1, source_target_pairs={{0,3},{1,2},{2,1},{3,0},{4,7},{5,6},{6,5},{7,4},{8,11},{9,10},{10,... | collective-permute-start | bytes 442376 | tf_op jit(solution)/shard_map/ppermute | solution.py:15
  21.8 9.7 %collective-permute-start.5 = (bf16[144,512]{1,0:T(8,128)(2,1)S(1)}, bf16[144,512]{1,0:T(8,128)(2,1)S(1)}, u32[]{:S(2)}, u32[]{:S(2)}) collective-permute-start(bf16[144,512]{1,0:T(8,128)(2,1)S(1)} %get-tuple-element.97.refs_1_), channel_id=1, source_target_pairs={{0,2},{1,3},{2,0},{3,1},{4,6},{5,7},{6,4},{7,5},{8,10},{9,11},{10,... | collective-permute-start | bytes 442376 | tf_op jit(solution)/shard_map/ppermute | solution.py:15
  22.5 9.1 %collective-permute-start.4 = (bf16[144,512]{1,0:T(8,128)(2,1)S(1)}, bf16[144,512]{1,0:T(8,128)(2,1)S(1)}, u32[]{:S(2)}, u32[]{:S(2)}) collective-permute-start(bf16[144,512]{1,0:T(8,128)(2,1)S(1)} %get-tuple-element.97.refs_1_), channel_id=1, source_target_pairs={{0,1},{1,0},{2,3},{3,2},{4,5},{5,4},{6,7},{7,6},{8,9},{9,8},{10,11... | collective-permute-start | bytes 442376 | tf_op jit(solution)/shard_map/ppermute | solution.py:15
  27.3 2.4 %collective-permute-start.10 = (bf16[192,2048]{1,0:T(8,128)(2,1)S(1)}, bf16[192,2048]{1,0:T(8,128)(2,1)S(1)}, u32[]{:S(2)}, u32[]{:S(2)}) collective-permute-start(bf16[192,2048]{1,0:T(8,128)(2,1)S(1)} %join.2.refs_0_), channel_id=1, source_target_pairs={{0,4},{4,0},{8,12},{12,8},{16,20},{20,16},{24,28},{28,24},{1,5},{5... | collective-permute-start | bytes 2359304 | tf_op jit(solution)/shard_map/ppermute | solution.py:15
  28.4 2.5 %copy-start.1 = (bf16[128,2048]{1,0:T(8,128)(2,1)S(1)}, bf16[128,2048]{1,0:T(8,128)(2,1)}, u32[]{:S(2)}) copy-start(bf16[128,2048]{1,0:T(8,128)(2,1)} %refs_1_.1) | copy-start | bytes 1572868
  28.4 2.5 %copy-start.7 = (s32[128,1]{0,1:T(1,128)S(1)}, s32[128,1]{0,1:T(1,128)}, u32[]{:S(2)}) copy-start(s32[128,1]{0,1:T(1,128)} %param.11) | copy-start | bytes 1540
  28.4 2.8 %copy-start.4 = (bf16[1,2048,512]{2,1,0:T(8,128)(2,1)S(1)}, bf16[1,2048,512]{2,1,0:T(8,128)(2,1)}, u32[]{:S(2)}) copy-start(bf16[1,2048,512]{2,1,0:T(8,128)(2,1)} %param.14) | copy-start | bytes 6291460
  28.4 2.8 %copy-start.5 = (bf16[1,512,2048]{2,1,0:T(8,128)(2,1)S(1)}, bf16[1,512,2048]{2,1,0:T(8,128)(2,1)}, u32[]{:S(2)}) copy-start(bf16[1,512,2048]{2,1,0:T(8,128)(2,1)} %param.15) | copy-start | bytes 6291460
  28.4 3.8 %collective-permute-start.11 = (bf16[1,4,192,256]{3,2,1,0:T(8,128)(2,1)S(1)}, bf16[1,4,192,256]{3,2,1,0:T(8,128)(2,1)S(1)}, u32[]{:S(2)}, u32[]{:S(2)}) collective-permute-start(bf16[1,4,192,256]{3,2,1,0:T(8,128)(2,1)S(1)} %get-tuple-element.94), channel_id=1, source_target_pairs={{0,4},{4,0},{8,12},{12,8},{16,20},{20,16},{24,28},{28,24},{1,5},{5... | collective-permute-start | bytes 1179656 | tf_op jit(solution)/shard_map/ppermute | solution.py:15
  30.6 1.8 %collective-permute-start.12 = (bf16[1,4,192,256]{3,2,1,0:T(8,128)(2,1)S(1)}, bf16[1,4,192,256]{3,2,1,0:T(8,128)(2,1)S(1)}, u32[]{:S(2)}, u32[]{:S(2)}) collective-permute-start(bf16[1,4,192,256]{3,2,1,0:T(8,128)(2,1)S(1)} %get-tuple-element.95), channel_id=1, source_target_pairs={{0,4},{4,0},{8,12},{12,8},{16,20},{20,16},{24,28},{28,24},{1,5},{5... | collective-permute-start | bytes 1179656 | tf_op jit(solution)/shard_map/ppermute | solution.py:15
  32.7 3.7 %collective-permute-start.13 = (bf16[192,2048]{1,0:T(8,128)(2,1)S(1)}, bf16[192,2048]{1,0:T(8,128)(2,1)S(1)}, u32[]{:S(2)}, u32[]{:S(2)}) collective-permute-start(bf16[192,2048]{1,0:T(8,128)(2,1)S(1)} %join.3.refs_0_.refs_5_), channel_id=1, source_target_pairs={{0,4},{4,0},{8,12},{12,8},{16,20},{20,16},{24,28},{28,24},{1,5},{5... | collective-permute-start | bytes 2359304 | tf_op jit(solution)/shard_map/ppermute | solution.py:15
  32.9 8.8 %collective-permute-start.18 = (bf16[384,256]{1,0:T(8,128)(2,1)S(1)}, bf16[384,256]{1,0:T(8,128)(2,1)S(1)}, u32[]{:S(2)}, u32[]{:S(2)}) collective-permute-start(bf16[384,256]{1,0:T(8,128)(2,1)S(1)} %get-tuple-element.113), channel_id=1, source_target_pairs={{0,1},{1,0},{2,3},{3,2},{4,5},{5,4},{6,7},{7,6},{8,9},{9,8},{10,11... | collective-permute-start | bytes 589832 | tf_op jit(solution)/shard_map/ppermute | solution.py:15
  33.9 11.1 %collective-permute-start.19 = (bf16[384,256]{1,0:T(8,128)(2,1)S(1)}, bf16[384,256]{1,0:T(8,128)(2,1)S(1)}, u32[]{:S(2)}, u32[]{:S(2)}) collective-permute-start(bf16[384,256]{1,0:T(8,128)(2,1)S(1)} %get-tuple-element.114), channel_id=1, source_target_pairs={{0,2},{1,3},{2,0},{3,1},{4,6},{5,7},{6,4},{7,5},{8,10},{9,11},{10,... | collective-permute-start | bytes 589832 | tf_op jit(solution)/shard_map/ppermute | solution.py:15
  35.8 9.4 %collective-permute-start.20 = (bf16[384,256]{1,0:T(8,128)(2,1)S(1)}, bf16[384,256]{1,0:T(8,128)(2,1)S(1)}, u32[]{:S(2)}, u32[]{:S(2)}) collective-permute-start(bf16[384,256]{1,0:T(8,128)(2,1)S(1)} %get-tuple-element.115), channel_id=1, source_target_pairs={{0,3},{1,2},{2,1},{3,0},{4,7},{5,6},{6,5},{7,4},{8,11},{9,10},{10,... | collective-permute-start | bytes 589832 | tf_op jit(solution)/shard_map/ppermute | solution.py:15
  38.1 2.4 %collective-permute-start.14 = (bf16[2,4,192,256]{3,2,1,0:T(8,128)(2,1)S(1)}, bf16[2,4,192,256]{3,2,1,0:T(8,128)(2,1)S(1)}, u32[]{:S(2)}, u32[]{:S(2)}) collective-permute-start(bf16[2,4,192,256]{3,2,1,0:T(8,128)(2,1)S(1)} %get-tuple-element.108), channel_id=1, source_target_pairs={{0,4},{4,0},{8,12},{12,8},{16,20},{20,16},{24,28},{28,24},{1,5},{5... | collective-permute-start | bytes 2359304 | tf_op jit(solution)/shard_map/ppermute | solution.py:15
  40.7 9.0 %collective-permute-start.15 = (bf16[384,256]{1,0:T(8,128)(2,1)S(1)}, bf16[384,256]{1,0:T(8,128)(2,1)S(1)}, u32[]{:S(2)}, u32[]{:S(2)}) collective-permute-start(bf16[384,256]{1,0:T(8,128)(2,1)S(1)} %get-tuple-element.110), channel_id=1, source_target_pairs={{0,1},{1,0},{2,3},{3,2},{4,5},{5,4},{6,7},{7,6},{8,9},{9,8},{10,11... | collective-permute-start | bytes 589832 | tf_op jit(solution)/shard_map/ppermute | solution.py:15
  45.3 7.7 %collective-permute-start.21 = (bf16[96,256]{1,0:T(8,128)(2,1)S(1)}, bf16[96,256]{1,0:T(8,128)(2,1)S(1)}, u32[]{:S(2)}, u32[]{:S(2)}) collective-permute-start(bf16[96,256]{1,0:T(8,128)(2,1)S(1)} %get-tuple-element.120), channel_id=1, source_target_pairs={{0,16},{4,20},{8,24},{12,28},{16,0},{20,4},{24,8},{28,12},{1,17},{... | collective-permute-start | bytes 147464 | tf_op jit(solution)/shard_map/ppermute | solution.py:15
  49.1 5.9 %collective-permute-start.22 = (bf16[96,256]{1,0:T(8,128)(2,1)S(1)}, bf16[96,256]{1,0:T(8,128)(2,1)S(1)}, u32[]{:S(2)}, u32[]{:S(2)}) collective-permute-start(bf16[96,256]{1,0:T(8,128)(2,1)S(1)} %get-tuple-element.121), channel_id=1, source_target_pairs={{0,24},{4,28},{8,16},{12,20},{16,8},{20,12},{24,0},{28,4},{1,25},{... | collective-permute-start | bytes 147464 | tf_op jit(solution)/shard_map/ppermute | solution.py:15
  49.6 5.3 %collective-permute-start.23 = (bf16[96,256]{1,0:T(8,128)(2,1)S(1)}, bf16[96,256]{1,0:T(8,128)(2,1)S(1)}, u32[]{:S(2)}, u32[]{:S(2)}) collective-permute-start(bf16[96,256]{1,0:T(8,128)(2,1)S(1)} %get-tuple-element.123), channel_id=1, source_target_pairs={{0,8},{4,12},{8,0},{12,4},{16,24},{20,28},{24,16},{28,20},{1,9},{5... | collective-permute-start | bytes 147464 | tf_op jit(solution)/shard_map/ppermute | solution.py:15
  50.0 10.4 %collective-permute-start.16 = (bf16[384,256]{1,0:T(8,128)(2,1)S(1)}, bf16[384,256]{1,0:T(8,128)(2,1)S(1)}, u32[]{:S(2)}, u32[]{:S(2)}) collective-permute-start(bf16[384,256]{1,0:T(8,128)(2,1)S(1)} %get-tuple-element.111), channel_id=1, source_target_pairs={{0,2},{1,3},{2,0},{3,1},{4,6},{5,7},{6,4},{7,5},{8,10},{9,11},{10,... | collective-permute-start | bytes 589832 | tf_op jit(solution)/shard_map/ppermute | solution.py:15
  51.4 9.0 %collective-permute-start.17 = (bf16[384,256]{1,0:T(8,128)(2,1)S(1)}, bf16[384,256]{1,0:T(8,128)(2,1)S(1)}, u32[]{:S(2)}, u32[]{:S(2)}) collective-permute-start(bf16[384,256]{1,0:T(8,128)(2,1)S(1)} %get-tuple-element.112), channel_id=1, source_target_pairs={{0,3},{1,2},{2,1},{3,0},{4,7},{5,6},{6,5},{7,4},{8,11},{9,10},{10,... | collective-permute-start | bytes 589832 | tf_op jit(solution)/shard_map/ppermute | solution.py:15
  55.2 5.3 %collective-permute-start.24 = (bf16[96,256]{1,0:T(8,128)(2,1)S(1)}, bf16[96,256]{1,0:T(8,128)(2,1)S(1)}, u32[]{:S(2)}, u32[]{:S(2)}) collective-permute-start(bf16[96,256]{1,0:T(8,128)(2,1)S(1)} %get-tuple-element.125), channel_id=1, source_target_pairs={{0,16},{4,20},{8,24},{12,28},{16,0},{20,4},{24,8},{28,12},{1,17},{... | collective-permute-start | bytes 147464 | tf_op jit(solution)/shard_map/ppermute | solution.py:15
  56.3 5.9 %collective-permute-start.25 = (bf16[96,256]{1,0:T(8,128)(2,1)S(1)}, bf16[96,256]{1,0:T(8,128)(2,1)S(1)}, u32[]{:S(2)}, u32[]{:S(2)}) collective-permute-start(bf16[96,256]{1,0:T(8,128)(2,1)S(1)} %get-tuple-element.126), channel_id=1, source_target_pairs={{0,24},{4,28},{8,16},{12,20},{16,8},{20,12},{24,0},{28,4},{1,25},{... | collective-permute-start | bytes 147464 | tf_op jit(solution)/shard_map/ppermute | solution.py:15
  57.3 4.9 %collective-permute-start.26 = (bf16[96,256]{1,0:T(8,128)(2,1)S(1)}, bf16[96,256]{1,0:T(8,128)(2,1)S(1)}, u32[]{:S(2)}, u32[]{:S(2)}) collective-permute-start(bf16[96,256]{1,0:T(8,128)(2,1)S(1)} %get-tuple-element.127), channel_id=1, source_target_pairs={{0,8},{4,12},{8,0},{12,4},{16,24},{20,28},{24,16},{28,20},{1,9},{5... | collective-permute-start | bytes 147464 | tf_op jit(solution)/shard_map/ppermute | solution.py:15
  62.3 3.6 %collective-permute-start.30 = (bf16[384,256]{1,0:T(8,128)(2,1)S(1)}, bf16[384,256]{1,0:T(8,128)(2,1)S(1)}, u32[]{:S(2)}, u32[]{:S(2)}) collective-permute-start(bf16[384,256]{1,0:T(8,128)(2,1)S(1)} %shard_map.96.refs_0_), channel_id=1, source_target_pairs={{0,4},{4,0},{8,12},{12,8},{16,20},{20,16},{24,28},{28,24},{1,5},{5... | collective-permute-start | bytes 589832 | tf_op jit(solution)/shard_map/ppermute | solution.py:15
  62.4 8.7 %collective-permute-start.29 = (bf16[384,256]{1,0:T(8,128)(2,1)S(1)}, bf16[384,256]{1,0:T(8,128)(2,1)S(1)}, u32[]{:S(2)}, u32[]{:S(2)}) collective-permute-start(bf16[384,256]{1,0:T(8,128)(2,1)S(1)} %shard_map.96.refs_0_), channel_id=1, source_target_pairs={{0,3},{1,2},{2,1},{3,0},{4,7},{5,6},{6,5},{7,4},{8,11},{9,10},{10,... | collective-permute-start | bytes 589832 | tf_op jit(solution)/shard_map/ppermute | solution.py:15
  64.1 10.8 %collective-permute-start.28 = (bf16[384,256]{1,0:T(8,128)(2,1)S(1)}, bf16[384,256]{1,0:T(8,128)(2,1)S(1)}, u32[]{:S(2)}, u32[]{:S(2)}) collective-permute-start(bf16[384,256]{1,0:T(8,128)(2,1)S(1)} %shard_map.96.refs_0_), channel_id=1, source_target_pairs={{0,2},{1,3},{2,0},{3,1},{4,6},{5,7},{6,4},{7,5},{8,10},{9,11},{10,... | collective-permute-start | bytes 589832 | tf_op jit(solution)/shard_map/ppermute | solution.py:15
  65.3 9.5 %collective-permute-start.27 = (bf16[384,256]{1,0:T(8,128)(2,1)S(1)}, bf16[384,256]{1,0:T(8,128)(2,1)S(1)}, u32[]{:S(2)}, u32[]{:S(2)}) collective-permute-start(bf16[384,256]{1,0:T(8,128)(2,1)S(1)} %shard_map.96.refs_0_), channel_id=1, source_target_pairs={{0,1},{1,0},{2,3},{3,2},{4,5},{5,4},{6,7},{7,6},{8,9},{9,8},{10,11... | collective-permute-start | bytes 589832 | tf_op jit(solution)/shard_map/ppermute | solution.py:15
  71.1 4.2 %collective-permute-start.33 = (bf16[384,256]{1,0:T(8,128)(2,1)S(1)}, bf16[384,256]{1,0:T(8,128)(2,1)S(1)}, u32[]{:S(2)}, u32[]{:S(2)}) collective-permute-start(bf16[384,256]{1,0:T(8,128)(2,1)S(1)} %collective-permute-done.29.refs_0_), channel_id=1, source_target_pairs={{0,4},{4,0},{8,12},{12,8},{16,20},{20,16},{24,28},{28,24},{1,5},{5... | collective-permute-start | bytes 589832 | tf_op jit(solution)/shard_map/ppermute | solution.py:15
  74.8 1.4 %collective-permute-start.31 = (bf16[384,256]{1,0:T(8,128)(2,1)S(1)}, bf16[384,256]{1,0:T(8,128)(2,1)S(1)}, u32[]{:S(2)}, u32[]{:S(2)}) collective-permute-start(bf16[384,256]{1,0:T(8,128)(2,1)S(1)} %collective-permute-done.27.refs_0_), channel_id=1, source_target_pairs={{0,4},{4,0},{8,12},{12,8},{16,20},{20,16},{24,28},{28,24},{1,5},{5... | collective-permute-start | bytes 589832 | tf_op jit(solution)/shard_map/ppermute | solution.py:15
  74.9 1.7 %collective-permute-start.32 = (bf16[384,256]{1,0:T(8,128)(2,1)S(1)}, bf16[384,256]{1,0:T(8,128)(2,1)S(1)}, u32[]{:S(2)}, u32[]{:S(2)}) collective-permute-start(bf16[384,256]{1,0:T(8,128)(2,1)S(1)} %collective-permute-done.28.refs_1_), channel_id=1, source_target_pairs={{0,4},{4,0},{8,12},{12,8},{16,20},{20,16},{24,28},{28,24},{1,5},{5... | collective-permute-start | bytes 589832 | tf_op jit(solution)/shard_map/ppermute | solution.py:15

commit v6 on v5

--- a/solution.py
+++ b/solution.py
@@ -329,6 +329,7 @@
     _, core, column = place()
     half = keep_own.shape[1]
     got, (mine, *out) = refs[:-columns], refs[-columns:]
+    got = [ref for ref in got if ref.dtype != jnp.int32]
     got_own, got_other = got[0].at[0], got[-1].at[len(got) % 2]
     for m in range(columns):
         for which, keep, got in ((core, keep_own, got_other), (1 - core, keep_other, got_own)):
@@ -505,15 +506,15 @@
             lambda *refs: keep_kernel(columns, *refs),
             [shape(columns, plane_rows // 2, piece)] * 2 + outs,
             [own, other, w2, *state],
-            flops=(64 if state else 8) * plane_rows * width * hid,
+            flops=(64 if state else 0) * plane_rows * width * hid,
             name="keep_s" if state else "keep_t",
         )
 
-    def pair(kept, got):
+    def pair(kept, got, marks=()):
         return call(
             lambda *refs: pair_kernel(columns, *refs),
             [shape(plane_rows, piece, dtype=f32)] + [shape(plane_rows, piece)] * (columns - 1),
-            [*kept, *got],
+            [*kept, *marks, *got],
             name="pair",
         )
 
@@ -566,15 +567,22 @@
             name="join",
         )[0]
 
-    flat_t_own = join(stay_t, after(got_t, maps))
+    flat_t_own = join(stay_t, got_t)
     flat_t_other = across(flat_t_own)
 
     send, hidden_own = forward([flat_t_own], w1_t, w2_t, False, "forward_t", 24)
     got_own = across(send)
     send, hidden_other = forward([flat_t_other], w1_t, w2_t, False, "forward_t", 0)
     got_other = across(send)
-    kept = keep(hidden_own, after(hidden_other, got_s, w1_s, stay_s), w2_t, [], [])
-    pieces_t = pair(kept, [got_own, got_other])
+    kept = keep(hidden_own, hidden_other, w2_t, [], [])
+    (mark,) = call(
+        lambda source, out: out.__setitem__(Ellipsis, source[...]),
+        [shape(1, row_count, dtype=jnp.int32)],
+        [after(route_t, got_s, w1_s, stay_s, kept[0])],
+        flops=8 * plane_rows * width * hid,
+        name="mark",
+    )
+    pieces_t = pair(kept, [got_own, got_other], [mark])
     sums_t = collect(*pieces_t)
 
     flat_own = join(stay_s, after(got_s, pieces_t[0]))
@@ -597,7 +605,7 @@
     home = call(
         lambda *refs: total_kernel(columns, experts, *refs),
         [shape(2 * capacity, piece)] * experts,
-        after(sums_t, pieces_s[0]),
+        after(sums_t, pieces_s[0], maps),
     )
     *sent, near, own = home
     home = [*over_planes([*sent, after(near, sums_s[1])]), own]
@@ -605,7 +613,7 @@
         lambda *refs: home_kernel(experts, capacity, *refs),
         [shape(2 * capacity, piece)] * experts,
         [maps, *home],
-        flops=4 * plane_rows * width * hid,
+        flops=5 * plane_rows * width * hid,
         name="home",
     )
     teachers = [*over_planes(slots[:-1]), slots[-1]]

time: 79.6 us -> 79.3 us (level)
  starting transfers between devices: 35.5 us -> 34.7 us
    pallas_call x23 -> x24, Pallas kernels: 14.8 us -> 14.8 us  [call(): pl.pallas_call(kernel, name=name, out_shape=outs, in_specs=in_specs or [V...]
    unnamed x16 -> x18, local copies, waits for them, and re-layouts: 4.9 us -> 4.9 us
where the time goes in v6:
time: 79.3 us; the launch traced here: 79 us
  starting transfers between devices  34.7 us (44%)
  waiting for transfers between devices  23 us (29%)
  Pallas kernels  14.8 us (19%)
  local copies, waits for them, and re-layouts  4.9 us (6%)
  between operations  0.96 us (1%)
    ppermute x34, starting transfers between devices, partner(): lax.ppermute(value, axis, [(i, i ^ mask) for i in range(lax.axis_size(axi...  34.7 us
    ppermute x34, waiting for transfers between devices, partner(): lax.ppermute(value, axis, [(i, i ^ mask) for i in range(lax.axis_size(axi...  23 us
    pallas_call x24, Pallas kernels, call(): pl.pallas_call(kernel, name=name, out_shape=outs, in_specs=in_specs or [V...  14.8 us
    unnamed x18, local copies, waits for them, and re-layouts  4.9 us
  transfers between devices with their start and end apart: 34, of which 15 were waited for; matrix products, arithmetic and copies ran while one was open for 1% of the time, Pallas kernels for 12%

profile of v6, /device:TPU:0, one launch (start us, length us, event | category | flops | bytes accessed | tf_op | source)
XLA Modules:
  0.0 79.0 jit_solution(1829686711203551132)
XLA Ops:
  0.6 1.9 %pack.1 = (bf16[48,1024]{1,0:T(8,128)(2,1)}, bf16[48,1024]{1,0:T(8,128)(2,1)}, bf16[48,1024]{1,0:T(8,128)(2,1)}) custom-call(bf16[128,2048]{1,0:T(8,128)(2,1)} %refs_0_.5, bf16[128,2048]{1,0:T(8,128)(2,1)} %refs_1_.1, s32[1,128]{1,0:T(1,128)} %bitcast.15, s32[1,128]{1,0:T(1,128)} %bitcast.12), custom_call_target="tpu_custom_call" | custom-call | tf_op jit(solution)/shard_map/pack/pallas_call | solution.py:172
  2.6 4.1 %collective-permute-start = (bf16[48,1024]{1,0:T(8,128)(2,1)}, bf16[48,1024]{1,0:T(8,128)(2,1)S(1)}, u32[]{:S(2)}, u32[]{:S(2)}) collective-permute-start(bf16[48,1024]{1,0:T(8,128)(2,1)} %get-tuple-element.70), channel_id=1, source_target_pairs={{0,16},{4,20},{8,24},{12,28},{16,0},{20,4},{24,8},{28,12},{1,17},{... | collective-permute-start | bytes 294920 | tf_op jit(solution)/shard_map/ppermute | solution.py:15
  6.7 1.3 %collective-permute-start.1 = (bf16[48,1024]{1,0:T(8,128)(2,1)}, bf16[48,1024]{1,0:T(8,128)(2,1)S(1)}, u32[]{:S(2)}, u32[]{:S(2)}) collective-permute-start(bf16[48,1024]{1,0:T(8,128)(2,1)} %get-tuple-element.71), channel_id=1, source_target_pairs={{0,24},{4,28},{8,16},{12,20},{16,8},{20,12},{24,0},{28,4},{1,25},{... | collective-permute-start | bytes 294920 | tf_op jit(solution)/shard_map/ppermute | solution.py:15
  8.0 0.2 collective-permute-start.2
  8.3 0.7 pad_add_fusion.refs_0_
  9.0 1.0 %copy-done = bf16[128,2048]{1,0:T(8,128)(2,1)S(1)} copy-done((bf16[128,2048]{1,0:T(8,128)(2,1)S(1)}, bf16[128,2048]{1,0:T(8,128)(2,1)}, u32[]{:S(2)}) %copy-start) | copy-done | bytes 524312
  10.0 0.7 copy-done.7
  10.6 0.3 stay.3.refs_0_
  11.0 1.6 %copy-done.2 = bf16[1,2048,512]{2,1,0:T(8,128)(2,1)S(1)} copy-done((bf16[1,2048,512]{2,1,0:T(8,128)(2,1)S(1)}, bf16[1,2048,512]{2,1,0:T(8,128)(2,1)}, u32[]{:S(2)}) %copy-start.2) | copy-done | bytes 2097176
  12.6 1.6 %copy-done.3 = bf16[1,512,2048]{2,1,0:T(8,128)(2,1)S(1)} copy-done((bf16[1,512,2048]{2,1,0:T(8,128)(2,1)S(1)}, bf16[1,512,2048]{2,1,0:T(8,128)(2,1)}, u32[]{:S(2)}) %copy-start.3) | copy-done | bytes 2097176
  14.2 0.3 load.2
  14.5 0.3 collective-permute-done.refs_0_
  14.8 0.5 collective-permute-done.2.refs_2_
  15.3 2.6 %collective-permute-start.9 = (bf16[144,512]{1,0:T(8,128)(2,1)S(1)}, bf16[144,512]{1,0:T(8,128)(2,1)S(1)}, u32[]{:S(2)}, u32[]{:S(2)}) collective-permute-start(bf16[144,512]{1,0:T(8,128)(2,1)S(1)} %get-tuple-element.78.refs_1_), channel_id=1, source_target_pairs={{0,3},{1,2},{2,1},{3,0},{4,7},{5,6},{6,5},{7,4},{8,11},{9,10},{10,... | collective-permute-start | bytes 442376 | tf_op jit(solution)/shard_map/ppermute | solution.py:15
  17.9 0.5 collective-permute-start.8
  18.4 0.5 collective-permute-start.7
  18.9 2.5 %collective-permute-start.6 = (bf16[144,512]{1,0:T(8,128)(2,1)S(1)}, bf16[144,512]{1,0:T(8,128)(2,1)S(1)}, u32[]{:S(2)}, u32[]{:S(2)}) collective-permute-start(bf16[144,512]{1,0:T(8,128)(2,1)S(1)} %get-tuple-element.89.refs_1_), channel_id=1, source_target_pairs={{0,3},{1,2},{2,1},{3,0},{4,7},{5,6},{6,5},{7,4},{8,11},{9,10},{10,... | collective-permute-start | bytes 442376 | tf_op jit(solution)/shard_map/ppermute | solution.py:15
  21.4 0.5 collective-permute-start.5
  21.9 0.6 collective-permute-done.9.refs_4_
  22.5 2.1 %collective-permute-start.4 = (bf16[144,512]{1,0:T(8,128)(2,1)S(1)}, bf16[144,512]{1,0:T(8,128)(2,1)S(1)}, u32[]{:S(2)}, u32[]{:S(2)}) collective-permute-start(bf16[144,512]{1,0:T(8,128)(2,1)S(1)} %get-tuple-element.89.refs_1_), channel_id=1, source_target_pairs={{0,1},{1,0},{2,3},{3,2},{4,5},{5,4},{6,7},{7,6},{8,9},{9,8},{10,11... | collective-permute-start | bytes 442376 | tf_op jit(solution)/shard_map/ppermute | solution.py:15
  24.6 2.7 %collective-permute-done.8.refs_3_ = bf16[144,512]{1,0:T(8,128)(2,1)S(1)} collective-permute-done((bf16[144,512]{1,0:T(8,128)(2,1)S(1)}, bf16[144,512]{1,0:T(8,128)(2,1)S(1)}, u32[]{:S(2)}, u32[]{:S(2)}) %collective-permute-start.8) | collective-permute-done | bytes 147488 | tf_op jit(solution)/shard_map/ppermute | solution.py:15
  27.4 0.9 %forward_t.2 = (bf16[1,4,192,256]{3,2,1,0:T(8,128)(2,1)S(1)}, bf16[192,512]{1,0:T(8,128)(2,1)S(1)}) custom-call(bf16[192,2048]{1,0:T(8,128)(2,1)S(1)} %join.2.refs_0_, bf16[2048,512]{1,0:T(8,128)(2,1)S(1)} %get-tuple-element.73.refs_1_, bf16[512,2048]{1,0:T(8,128)(2,1)S(1)} %get-tuple-element.79.refs_2_), custom_call_target="tpu_custom_call" | custom-call | flops 9663676416 | tf_op jit(solution)/shard_map/forward_t/pallas_call | solution.py:172
  28.4 0.6 collective-permute-start.11
  28.9 0.7 collective-permute-done.10.refs_0_
  29.7 0.9 %forward_t.3 = (bf16[1,4,192,256]{3,2,1,0:T(8,128)(2,1)S(1)}, bf16[192,512]{1,0:T(8,128)(2,1)S(1)}) custom-call(bf16[192,2048]{1,0:T(8,128)(2,1)S(1)} %collective-permute-done.10.refs_0_, bf16[2048,512]{1,0:T(8,128)(2,1)S(1)} %get-tuple-element.73.refs_1_, bf16[512,2048]{1,0:T(8,128)(2,1)S(1)} %get-tuple-element.79.refs_2_), custom_call_target="tpu_custom_call" | custom-call | tf_op jit(solution)/shard_map/forward_t/pallas_call | solution.py:172
  30.6 0.2 collective-permute-start.12
  30.8 0.3 stay.2.refs_0_
  31.2 0.3 load.3
  31.5 0.6 keep_t.1
  32.2 0.2 collective-permute-done.12.refs_4_
  32.4 0.2 pair.2
  32.6 0.3 collective-permute-start.13
  32.9 0.6 collective-permute-start.18
  33.5 2.3 %collective-permute-start.19 = (bf16[384,256]{1,0:T(8,128)(2,1)S(1)}, bf16[384,256]{1,0:T(8,128)(2,1)S(1)}, u32[]{:S(2)}, u32[]{:S(2)}) collective-permute-start(bf16[384,256]{1,0:T(8,128)(2,1)S(1)} %get-tuple-element.106), channel_id=1, source_target_pairs={{0,2},{1,3},{2,0},{3,1},{4,6},{5,7},{6,4},{7,5},{8,10},{9,11},{10,... | collective-permute-start | bytes 589832 | tf_op jit(solution)/shard_map/ppermute | solution.py:15
  35.8 0.6 collective-permute-start.20
  36.4 1.7 %forward_s.1 = (bf16[2,4,192,256]{3,2,1,0:T(8,128)(2,1)S(1)}, bf16[192,512]{1,0:T(8,128)(2,1)S(1)}, bf16[192,512]{1,0:T(8,128)(2,1)S(1)}, f32[192,512]{1,0:T(8,128)S(1)}, f32[192,512]{1,0:T(8,128)S(1)}) custom-call(bf16[192,2048]{1,0:T(8,128)(2,1)S(1)} %join.3.refs_0_.refs_5_, bf16[192,2048]{1,0:T(8,128)(2,1)S(1)} %collective-permute-done.13.refs_1_.refs_6_, ...), custom_call_target="tpu_custom_call" | custom-call | tf_op jit(solution)/shard_map/forward_s/pallas_call | solution.py:172
  38.2 1.4 %keep_s.1 = (bf16[4,192,256]{2,1,0:T(8,128)(2,1)S(1)}, bf16[4,192,256]{2,1,0:T(8,128)(2,1)S(1)}, bf16[2048,384]{1,0:T(8,128)(2,1)S(1)}, bf16[512,384]{1,0:T(8,128)(2,1)S(1)}, f32[384,512]{1,0:T(8,128)S(1)}) custom-call(bf16[192,512]{1,0:T(8,128)(2,1)S(1)} %get-tuple-element.94.refs_0_, bf16[192,512]{1,0:T(8,128)(2,1)S(1)} %get-tuple-element.95.refs_1_, ...), custom_call_target="tpu_custom_call" | custom-call | flops 25769803776 | tf_op jit(solution)/shard_map/keep_s/pallas_call | solution.py:172
  39.6 0.9 %collective-permute-done.14.refs_2_ = bf16[2,4,192,256]{3,2,1,0:T(8,128)(2,1)S(1)} collective-permute-done((bf16[2,4,192,256]{3,2,1,0:T(8,128)(2,1)S(1)}, bf16[2,4,192,256]{3,2,1,0:T(8,128)(2,1)S(1)}, u32[]{:S(2)}, u32[]{:S(2)}) %collective-permute-start.14) | collective-permute-done | bytes 786464 | tf_op jit(solution)/shard_map/ppermute | solution.py:15
  40.7 0.9 %collective-permute-start.15 = (bf16[384,256]{1,0:T(8,128)(2,1)S(1)}, bf16[384,256]{1,0:T(8,128)(2,1)S(1)}, u32[]{:S(2)}, u32[]{:S(2)}) collective-permute-start(bf16[384,256]{1,0:T(8,128)(2,1)S(1)} %get-tuple-element.102), channel_id=1, source_target_pairs={{0,1},{1,0},{2,3},{3,2},{4,5},{5,4},{6,7},{7,6},{8,9},{9,8},{10,11... | collective-permute-start | bytes 589832 | tf_op jit(solution)/shard_map/ppermute | solution.py:15
  41.6 0.4 maps.1.refs_0_
  42.0 3.1 %collective-permute-done.19.refs_2_ = bf16[384,256]{1,0:T(8,128)(2,1)S(1)} collective-permute-done((bf16[384,256]{1,0:T(8,128)(2,1)S(1)}, bf16[384,256]{1,0:T(8,128)(2,1)S(1)}, u32[]{:S(2)}, u32[]{:S(2)}) %collective-permute-start.19) | collective-permute-done | bytes 196640 | tf_op jit(solution)/shard_map/ppermute | solution.py:15
  45.2 3.2 %collective-permute-start.21 = (bf16[96,256]{1,0:T(8,128)(2,1)S(1)}, bf16[96,256]{1,0:T(8,128)(2,1)S(1)}, u32[]{:S(2)}, u32[]{:S(2)}) collective-permute-start(bf16[96,256]{1,0:T(8,128)(2,1)S(1)} %get-tuple-element.112), channel_id=1, source_target_pairs={{0,16},{4,20},{8,24},{12,28},{16,0},{20,4},{24,8},{28,12},{1,17},{... | collective-permute-start | bytes 147464 | tf_op jit(solution)/shard_map/ppermute | solution.py:15
  48.4 0.5 collective-permute-start.22
  49.0 0.5 collective-permute-start.23
  49.5 1.3 %collective-permute-start.16 = (bf16[384,256]{1,0:T(8,128)(2,1)S(1)}, bf16[384,256]{1,0:T(8,128)(2,1)S(1)}, u32[]{:S(2)}, u32[]{:S(2)}) collective-permute-start(bf16[384,256]{1,0:T(8,128)(2,1)S(1)} %get-tuple-element.103), channel_id=1, source_target_pairs={{0,2},{1,3},{2,0},{3,1},{4,6},{5,7},{6,4},{7,5},{8,10},{9,11},{10,... | collective-permute-start | bytes 589832 | tf_op jit(solution)/shard_map/ppermute | solution.py:15
  50.8 1.6 %collective-permute-start.17 = (bf16[384,256]{1,0:T(8,128)(2,1)S(1)}, bf16[384,256]{1,0:T(8,128)(2,1)S(1)}, u32[]{:S(2)}, u32[]{:S(2)}) collective-permute-start(bf16[384,256]{1,0:T(8,128)(2,1)S(1)} %get-tuple-element.104), channel_id=1, source_target_pairs={{0,3},{1,2},{2,1},{3,0},{4,7},{5,6},{6,5},{7,4},{8,11},{9,10},{10,... | collective-permute-start | bytes 589832 | tf_op jit(solution)/shard_map/ppermute | solution.py:15
  52.4 2.0 %collective-permute-done.22.refs_2_ = bf16[96,256]{1,0:T(8,128)(2,1)S(1)} collective-permute-done((bf16[96,256]{1,0:T(8,128)(2,1)S(1)}, bf16[96,256]{1,0:T(8,128)(2,1)S(1)}, u32[]{:S(2)}, u32[]{:S(2)}) %collective-permute-start.22) | collective-permute-done | bytes 49184 | tf_op jit(solution)/shard_map/ppermute | solution.py:15
  54.3 0.2 home.1
  54.5 1.5 %collective-permute-start.24 = (bf16[96,256]{1,0:T(8,128)(2,1)S(1)}, bf16[96,256]{1,0:T(8,128)(2,1)S(1)}, u32[]{:S(2)}, u32[]{:S(2)}) collective-permute-start(bf16[96,256]{1,0:T(8,128)(2,1)S(1)} %get-tuple-element.117), channel_id=1, source_target_pairs={{0,16},{4,20},{8,24},{12,28},{16,0},{20,4},{24,8},{28,12},{1,17},{... | collective-permute-start | bytes 147464 | tf_op jit(solution)/shard_map/ppermute | solution.py:15
  56.0 0.7 collective-permute-start.25
  56.7 1.4 %collective-permute-start.26 = (bf16[96,256]{1,0:T(8,128)(2,1)S(1)}, bf16[96,256]{1,0:T(8,128)(2,1)S(1)}, u32[]{:S(2)}, u32[]{:S(2)}) collective-permute-start(bf16[96,256]{1,0:T(8,128)(2,1)S(1)} %get-tuple-element.119), channel_id=1, source_target_pairs={{0,8},{4,12},{8,0},{12,4},{16,24},{20,28},{24,16},{28,20},{1,9},{5... | collective-permute-start | bytes 147464 | tf_op jit(solution)/shard_map/ppermute | solution.py:15
  58.1 1.7 %collective-permute-done.16.refs_2_ = bf16[384,256]{1,0:T(8,128)(2,1)S(1)} collective-permute-done((bf16[384,256]{1,0:T(8,128)(2,1)S(1)}, bf16[384,256]{1,0:T(8,128)(2,1)S(1)}, u32[]{:S(2)}, u32[]{:S(2)}) %collective-permute-start.16) | collective-permute-done | bytes 196640 | tf_op jit(solution)/shard_map/ppermute | solution.py:15
  59.8 2.1 %collective-permute-done.25.refs_5_ = bf16[96,256]{1,0:T(8,128)(2,1)S(1)} collective-permute-done((bf16[96,256]{1,0:T(8,128)(2,1)S(1)}, bf16[96,256]{1,0:T(8,128)(2,1)S(1)}, u32[]{:S(2)}, u32[]{:S(2)}) %collective-permute-start.25) | collective-permute-done | bytes 49184 | tf_op jit(solution)/shard_map/ppermute | solution.py:15
  62.1 1.7 %collective-permute-start.29 = (bf16[384,256]{1,0:T(8,128)(2,1)S(1)}, bf16[384,256]{1,0:T(8,128)(2,1)S(1)}, u32[]{:S(2)}, u32[]{:S(2)}) collective-permute-start(bf16[384,256]{1,0:T(8,128)(2,1)S(1)} %shard_map.96.refs_0_), channel_id=1, source_target_pairs={{0,3},{1,2},{2,1},{3,0},{4,7},{5,6},{6,5},{7,4},{8,11},{9,10},{10,... | collective-permute-start | bytes 589832 | tf_op jit(solution)/shard_map/ppermute | solution.py:15
  63.9 0.9 %collective-permute-start.28 = (bf16[384,256]{1,0:T(8,128)(2,1)S(1)}, bf16[384,256]{1,0:T(8,128)(2,1)S(1)}, u32[]{:S(2)}, u32[]{:S(2)}) collective-permute-start(bf16[384,256]{1,0:T(8,128)(2,1)S(1)} %shard_map.96.refs_0_), channel_id=1, source_target_pairs={{0,2},{1,3},{2,0},{3,1},{4,6},{5,7},{6,4},{7,5},{8,10},{9,11},{10,... | collective-permute-start | bytes 589832 | tf_op jit(solution)/shard_map/ppermute | solution.py:15
  64.8 0.9 %collective-permute-start.27 = (bf16[384,256]{1,0:T(8,128)(2,1)S(1)}, bf16[384,256]{1,0:T(8,128)(2,1)S(1)}, u32[]{:S(2)}, u32[]{:S(2)}) collective-permute-start(bf16[384,256]{1,0:T(8,128)(2,1)S(1)} %shard_map.96.refs_0_), channel_id=1, source_target_pairs={{0,1},{1,0},{2,3},{3,2},{4,5},{5,4},{6,7},{7,6},{8,9},{9,8},{10,11... | collective-permute-start | bytes 589832 | tf_op jit(solution)/shard_map/ppermute | solution.py:15
  65.7 0.6 early.3
  66.3 4.5 %collective-permute-done.29.refs_0_ = bf16[384,256]{1,0:T(8,128)(2,1)S(1)} collective-permute-done((bf16[384,256]{1,0:T(8,128)(2,1)S(1)}, bf16[384,256]{1,0:T(8,128)(2,1)S(1)}, u32[]{:S(2)}, u32[]{:S(2)}) %collective-permute-start.29) | collective-permute-done | bytes 196640 | tf_op jit(solution)/shard_map/ppermute | solution.py:15
  70.8 0.4 early.4
  71.2 3.3 %collective-permute-done.28.refs_1_ = bf16[384,256]{1,0:T(8,128)(2,1)S(1)} collective-permute-done((bf16[384,256]{1,0:T(8,128)(2,1)S(1)}, bf16[384,256]{1,0:T(8,128)(2,1)S(1)}, u32[]{:S(2)}, u32[]{:S(2)}) %collective-permute-start.28) | collective-permute-done | bytes 196640 | tf_op jit(solution)/shard_map/ppermute | solution.py:15
  74.6 0.5 collective-permute-start.32
  75.1 0.9 %early.5 = (f32[384,512]{1,0:T(8,128)S(1)}, bf16[512,256]{1,0:T(8,128)(2,1)S(1)}, bf16[512,256]{1,0:T(8,128)(2,1)S(1)}, bf16[512,256]{1,0:T(8,128)(2,1)S(1)}) custom-call(bf16[384,256]{1,0:T(8,128)(2,1)S(1)} %collective-permute-done.27.refs_0_, bf16[384,256]{1,0:T(8,128)(2,1)S(1)} %collective-permute-done.28.refs_1_, ...), custom_call_target="tpu_custom_call" | custom-call | tf_op jit(solution)/shard_map/early/pallas_call | solution.py:172
  76.0 0.3 collective-permute-done.32.refs_1_
  76.3 2.8 %last.1 = (bf16[2048,512]{1,0:T(8,128)(2,1)}, bf16[512,2048]{1,0:T(8,128)(2,1)}) custom-call(bf16[384,256]{1,0:T(8,128)(2,1)S(1)} %collective-permute-done.31.refs_0_, bf16[384,256]{1,0:T(8,128)(2,1)S(1)} %collective-permute-done.32.refs_1_, bf16[512,256]{1,0:T(8,128)(2,1)S(1)} %get-tuple-element.127.refs_2_, ...), custom_call_target="tpu_custom_call" | custom-call | tf_op jit(solution)/shard_map/last/pallas_call | solution.py:172
  (47 shorter events, 1.0 us)
Async XLA Ops:
  2.6 12.2 %collective-permute-start = (bf16[48,1024]{1,0:T(8,128)(2,1)}, bf16[48,1024]{1,0:T(8,128)(2,1)S(1)}, u32[]{:S(2)}, u32[]{:S(2)}) collective-permute-start(bf16[48,1024]{1,0:T(8,128)(2,1)} %get-tuple-element.70), channel_id=1, source_target_pairs={{0,16},{4,20},{8,24},{12,28},{16,0},{20,4},{24,8},{28,12},{1,17},{... | collective-permute-start | bytes 294920 | tf_op jit(solution)/shard_map/ppermute | solution.py:15
  6.7 8.1 %collective-permute-start.1 = (bf16[48,1024]{1,0:T(8,128)(2,1)}, bf16[48,1024]{1,0:T(8,128)(2,1)S(1)}, u32[]{:S(2)}, u32[]{:S(2)}) collective-permute-start(bf16[48,1024]{1,0:T(8,128)(2,1)} %get-tuple-element.71), channel_id=1, source_target_pairs={{0,24},{4,28},{8,16},{12,20},{16,8},{20,12},{24,0},{28,4},{1,25},{... | collective-permute-start | bytes 294920 | tf_op jit(solution)/shard_map/ppermute | solution.py:15
  8.0 7.3 %collective-permute-start.2 = (bf16[48,1024]{1,0:T(8,128)(2,1)}, bf16[48,1024]{1,0:T(8,128)(2,1)S(1)}, u32[]{:S(2)}, u32[]{:S(2)}) collective-permute-start(bf16[48,1024]{1,0:T(8,128)(2,1)} %get-tuple-element.72), channel_id=1, source_target_pairs={{0,8},{4,12},{8,0},{12,4},{16,24},{20,28},{24,16},{28,20},{1,9},{5... | collective-permute-start | bytes 294920 | tf_op jit(solution)/shard_map/ppermute | solution.py:15
  8.9 5.6 %collective-permute-start.3 = (s32[2,128]{1,0:T(2,128)S(1)}, s32[2,128]{1,0:T(2,128)S(1)}, u32[]{:S(2)}, u32[]{:S(2)}) collective-permute-start(s32[2,128]{1,0:T(2,128)S(1)} %pad_add_fusion.refs_0_), channel_id=1, source_target_pairs={{0,4},{4,0},{8,12},{12,8},{16,20},{20,16},{24,28},{28,24},{1,5},{5... | collective-permute-start | bytes 3080 | tf_op jit(solution)/shard_map/ppermute | solution.py:15
  8.9 1.0 %copy-start = (bf16[128,2048]{1,0:T(8,128)(2,1)S(1)}, bf16[128,2048]{1,0:T(8,128)(2,1)}, u32[]{:S(2)}) copy-start(bf16[128,2048]{1,0:T(8,128)(2,1)} %refs_0_.5) | copy-start | bytes 1572868
  10.0 0.7 copy-start.7
  11.0 1.6 %copy-start.2 = (bf16[1,2048,512]{2,1,0:T(8,128)(2,1)S(1)}, bf16[1,2048,512]{2,1,0:T(8,128)(2,1)}, u32[]{:S(2)}) copy-start(bf16[1,2048,512]{2,1,0:T(8,128)(2,1)} %param.12) | copy-start | bytes 6291460
  12.6 1.6 %copy-start.3 = (bf16[1,512,2048]{2,1,0:T(8,128)(2,1)S(1)}, bf16[1,512,2048]{2,1,0:T(8,128)(2,1)}, u32[]{:S(2)}) copy-start(bf16[1,512,2048]{2,1,0:T(8,128)(2,1)} %param.13) | copy-start | bytes 6291460
  15.3 7.1 %collective-permute-start.9 = (bf16[144,512]{1,0:T(8,128)(2,1)S(1)}, bf16[144,512]{1,0:T(8,128)(2,1)S(1)}, u32[]{:S(2)}, u32[]{:S(2)}) collective-permute-start(bf16[144,512]{1,0:T(8,128)(2,1)S(1)} %get-tuple-element.78.refs_1_), channel_id=1, source_target_pairs={{0,3},{1,2},{2,1},{3,0},{4,7},{5,6},{6,5},{7,4},{8,11},{9,10},{10,... | collective-permute-start | bytes 442376 | tf_op jit(solution)/shard_map/ppermute | solution.py:15
  17.9 9.4 %collective-permute-start.8 = (bf16[144,512]{1,0:T(8,128)(2,1)S(1)}, bf16[144,512]{1,0:T(8,128)(2,1)S(1)}, u32[]{:S(2)}, u32[]{:S(2)}) collective-permute-start(bf16[144,512]{1,0:T(8,128)(2,1)S(1)} %get-tuple-element.78.refs_1_), channel_id=1, source_target_pairs={{0,2},{1,3},{2,0},{3,1},{4,6},{5,7},{6,4},{7,5},{8,10},{9,11},{10,... | collective-permute-start | bytes 442376 | tf_op jit(solution)/shard_map/ppermute | solution.py:15
  18.4 8.9 %collective-permute-start.7 = (bf16[144,512]{1,0:T(8,128)(2,1)S(1)}, bf16[144,512]{1,0:T(8,128)(2,1)S(1)}, u32[]{:S(2)}, u32[]{:S(2)}) collective-permute-start(bf16[144,512]{1,0:T(8,128)(2,1)S(1)} %get-tuple-element.78.refs_1_), channel_id=1, source_target_pairs={{0,1},{1,0},{2,3},{3,2},{4,5},{5,4},{6,7},{7,6},{8,9},{9,8},{10,11... | collective-permute-start | bytes 442376 | tf_op jit(solution)/shard_map/ppermute | solution.py:15
  18.9 13.3 %collective-permute-start.6 = (bf16[144,512]{1,0:T(8,128)(2,1)S(1)}, bf16[144,512]{1,0:T(8,128)(2,1)S(1)}, u32[]{:S(2)}, u32[]{:S(2)}) collective-permute-start(bf16[144,512]{1,0:T(8,128)(2,1)S(1)} %get-tuple-element.89.refs_1_), channel_id=1, source_target_pairs={{0,3},{1,2},{2,1},{3,0},{4,7},{5,6},{6,5},{7,4},{8,11},{9,10},{10,... | collective-permute-start | bytes 442376 | tf_op jit(solution)/shard_map/ppermute | solution.py:15
  21.4 10.8 %collective-permute-start.5 = (bf16[144,512]{1,0:T(8,128)(2,1)S(1)}, bf16[144,512]{1,0:T(8,128)(2,1)S(1)}, u32[]{:S(2)}, u32[]{:S(2)}) collective-permute-start(bf16[144,512]{1,0:T(8,128)(2,1)S(1)} %get-tuple-element.89.refs_1_), channel_id=1, source_target_pairs={{0,2},{1,3},{2,0},{3,1},{4,6},{5,7},{6,4},{7,5},{8,10},{9,11},{10,... | collective-permute-start | bytes 442376 | tf_op jit(solution)/shard_map/ppermute | solution.py:15
  22.5 9.7 %collective-permute-start.4 = (bf16[144,512]{1,0:T(8,128)(2,1)S(1)}, bf16[144,512]{1,0:T(8,128)(2,1)S(1)}, u32[]{:S(2)}, u32[]{:S(2)}) collective-permute-start(bf16[144,512]{1,0:T(8,128)(2,1)S(1)} %get-tuple-element.89.refs_1_), channel_id=1, source_target_pairs={{0,1},{1,0},{2,3},{3,2},{4,5},{5,4},{6,7},{7,6},{8,9},{9,8},{10,11... | collective-permute-start | bytes 442376 | tf_op jit(solution)/shard_map/ppermute | solution.py:15
  27.3 2.4 %collective-permute-start.10 = (bf16[192,2048]{1,0:T(8,128)(2,1)S(1)}, bf16[192,2048]{1,0:T(8,128)(2,1)S(1)}, u32[]{:S(2)}, u32[]{:S(2)}) collective-permute-start(bf16[192,2048]{1,0:T(8,128)(2,1)S(1)} %join.2.refs_0_), channel_id=1, source_target_pairs={{0,4},{4,0},{8,12},{12,8},{16,20},{20,16},{24,28},{28,24},{1,5},{5... | collective-permute-start | bytes 2359304 | tf_op jit(solution)/shard_map/ppermute | solution.py:15
  28.3 2.5 %copy-start.1 = (bf16[128,2048]{1,0:T(8,128)(2,1)S(1)}, bf16[128,2048]{1,0:T(8,128)(2,1)}, u32[]{:S(2)}) copy-start(bf16[128,2048]{1,0:T(8,128)(2,1)} %refs_1_.1) | copy-start | bytes 1572868
  28.4 2.5 %copy-start.6 = (s32[128,1]{0,1:T(1,128)S(1)}, s32[128,1]{0,1:T(1,128)}, u32[]{:S(2)}) copy-start(s32[128,1]{0,1:T(1,128)} %param.11) | copy-start | bytes 1540
  28.4 2.8 %copy-start.4 = (bf16[1,2048,512]{2,1,0:T(8,128)(2,1)S(1)}, bf16[1,2048,512]{2,1,0:T(8,128)(2,1)}, u32[]{:S(2)}) copy-start(bf16[1,2048,512]{2,1,0:T(8,128)(2,1)} %param.14) | copy-start | bytes 6291460
  28.4 2.8 %copy-start.5 = (bf16[1,512,2048]{2,1,0:T(8,128)(2,1)S(1)}, bf16[1,512,2048]{2,1,0:T(8,128)(2,1)}, u32[]{:S(2)}) copy-start(bf16[1,512,2048]{2,1,0:T(8,128)(2,1)} %param.15) | copy-start | bytes 6291460
  28.4 3.8 %collective-permute-start.11 = (bf16[1,4,192,256]{3,2,1,0:T(8,128)(2,1)S(1)}, bf16[1,4,192,256]{3,2,1,0:T(8,128)(2,1)S(1)}, u32[]{:S(2)}, u32[]{:S(2)}) collective-permute-start(bf16[1,4,192,256]{3,2,1,0:T(8,128)(2,1)S(1)} %get-tuple-element.86), channel_id=1, source_target_pairs={{0,4},{4,0},{8,12},{12,8},{16,20},{20,16},{24,28},{28,24},{1,5},{5... | collective-permute-start | bytes 1179656 | tf_op jit(solution)/shard_map/ppermute | solution.py:15
  30.6 1.8 %collective-permute-start.12 = (bf16[1,4,192,256]{3,2,1,0:T(8,128)(2,1)S(1)}, bf16[1,4,192,256]{3,2,1,0:T(8,128)(2,1)S(1)}, u32[]{:S(2)}, u32[]{:S(2)}) collective-permute-start(bf16[1,4,192,256]{3,2,1,0:T(8,128)(2,1)S(1)} %get-tuple-element.87), channel_id=1, source_target_pairs={{0,4},{4,0},{8,12},{12,8},{16,20},{20,16},{24,28},{28,24},{1,5},{5... | collective-permute-start | bytes 1179656 | tf_op jit(solution)/shard_map/ppermute | solution.py:15
  31.5 0.7 copy-start.8
  32.6 3.8 %collective-permute-start.13 = (bf16[192,2048]{1,0:T(8,128)(2,1)S(1)}, bf16[192,2048]{1,0:T(8,128)(2,1)S(1)}, u32[]{:S(2)}, u32[]{:S(2)}) collective-permute-start(bf16[192,2048]{1,0:T(8,128)(2,1)S(1)} %join.3.refs_0_.refs_5_), channel_id=1, source_target_pairs={{0,4},{4,0},{8,12},{12,8},{16,20},{20,16},{24,28},{28,24},{1,5},{5... | collective-permute-start | bytes 2359304 | tf_op jit(solution)/shard_map/ppermute | solution.py:15
  32.9 9.1 %collective-permute-start.18 = (bf16[384,256]{1,0:T(8,128)(2,1)S(1)}, bf16[384,256]{1,0:T(8,128)(2,1)S(1)}, u32[]{:S(2)}, u32[]{:S(2)}) collective-permute-start(bf16[384,256]{1,0:T(8,128)(2,1)S(1)} %get-tuple-element.105), channel_id=1, source_target_pairs={{0,1},{1,0},{2,3},{3,2},{4,5},{5,4},{6,7},{7,6},{8,9},{9,8},{10,11... | collective-permute-start | bytes 589832 | tf_op jit(solution)/shard_map/ppermute | solution.py:15
  33.5 11.6 %collective-permute-start.19 = (bf16[384,256]{1,0:T(8,128)(2,1)S(1)}, bf16[384,256]{1,0:T(8,128)(2,1)S(1)}, u32[]{:S(2)}, u32[]{:S(2)}) collective-permute-start(bf16[384,256]{1,0:T(8,128)(2,1)S(1)} %get-tuple-element.106), channel_id=1, source_target_pairs={{0,2},{1,3},{2,0},{3,1},{4,6},{5,7},{6,4},{7,5},{8,10},{9,11},{10,... | collective-permute-start | bytes 589832 | tf_op jit(solution)/shard_map/ppermute | solution.py:15
  35.8 9.4 %collective-permute-start.20 = (bf16[384,256]{1,0:T(8,128)(2,1)S(1)}, bf16[384,256]{1,0:T(8,128)(2,1)S(1)}, u32[]{:S(2)}, u32[]{:S(2)}) collective-permute-start(bf16[384,256]{1,0:T(8,128)(2,1)S(1)} %get-tuple-element.107), channel_id=1, source_target_pairs={{0,3},{1,2},{2,1},{3,0},{4,7},{5,6},{6,5},{7,4},{8,11},{9,10},{10,... | collective-permute-start | bytes 589832 | tf_op jit(solution)/shard_map/ppermute | solution.py:15
  38.1 2.4 %collective-permute-start.14 = (bf16[2,4,192,256]{3,2,1,0:T(8,128)(2,1)S(1)}, bf16[2,4,192,256]{3,2,1,0:T(8,128)(2,1)S(1)}, u32[]{:S(2)}, u32[]{:S(2)}) collective-permute-start(bf16[2,4,192,256]{3,2,1,0:T(8,128)(2,1)S(1)} %get-tuple-element.100), channel_id=1, source_target_pairs={{0,4},{4,0},{8,12},{12,8},{16,20},{20,16},{24,28},{28,24},{1,5},{5... | collective-permute-start | bytes 2359304 | tf_op jit(solution)/shard_map/ppermute | solution.py:15
  40.7 8.3 %collective-permute-start.15 = (bf16[384,256]{1,0:T(8,128)(2,1)S(1)}, bf16[384,256]{1,0:T(8,128)(2,1)S(1)}, u32[]{:S(2)}, u32[]{:S(2)}) collective-permute-start(bf16[384,256]{1,0:T(8,128)(2,1)S(1)} %get-tuple-element.102), channel_id=1, source_target_pairs={{0,1},{1,0},{2,3},{3,2},{4,5},{5,4},{6,7},{7,6},{8,9},{9,8},{10,11... | collective-permute-start | bytes 589832 | tf_op jit(solution)/shard_map/ppermute | solution.py:15
  45.2 7.1 %collective-permute-start.21 = (bf16[96,256]{1,0:T(8,128)(2,1)S(1)}, bf16[96,256]{1,0:T(8,128)(2,1)S(1)}, u32[]{:S(2)}, u32[]{:S(2)}) collective-permute-start(bf16[96,256]{1,0:T(8,128)(2,1)S(1)} %get-tuple-element.112), channel_id=1, source_target_pairs={{0,16},{4,20},{8,24},{12,28},{16,0},{20,4},{24,8},{28,12},{1,17},{... | collective-permute-start | bytes 147464 | tf_op jit(solution)/shard_map/ppermute | solution.py:15
  48.4 5.9 %collective-permute-start.22 = (bf16[96,256]{1,0:T(8,128)(2,1)S(1)}, bf16[96,256]{1,0:T(8,128)(2,1)S(1)}, u32[]{:S(2)}, u32[]{:S(2)}) collective-permute-start(bf16[96,256]{1,0:T(8,128)(2,1)S(1)} %get-tuple-element.113), channel_id=1, source_target_pairs={{0,24},{4,28},{8,16},{12,20},{16,8},{20,12},{24,0},{28,4},{1,25},{... | collective-permute-start | bytes 147464 | tf_op jit(solution)/shard_map/ppermute | solution.py:15
  49.0 5.3 %collective-permute-start.23 = (bf16[96,256]{1,0:T(8,128)(2,1)S(1)}, bf16[96,256]{1,0:T(8,128)(2,1)S(1)}, u32[]{:S(2)}, u32[]{:S(2)}) collective-permute-start(bf16[96,256]{1,0:T(8,128)(2,1)S(1)} %get-tuple-element.115), channel_id=1, source_target_pairs={{0,8},{4,12},{8,0},{12,4},{16,24},{20,28},{24,16},{28,20},{1,9},{5... | collective-permute-start | bytes 147464 | tf_op jit(solution)/shard_map/ppermute | solution.py:15
  49.5 10.3 %collective-permute-start.16 = (bf16[384,256]{1,0:T(8,128)(2,1)S(1)}, bf16[384,256]{1,0:T(8,128)(2,1)S(1)}, u32[]{:S(2)}, u32[]{:S(2)}) collective-permute-start(bf16[384,256]{1,0:T(8,128)(2,1)S(1)} %get-tuple-element.103), channel_id=1, source_target_pairs={{0,2},{1,3},{2,0},{3,1},{4,6},{5,7},{6,4},{7,5},{8,10},{9,11},{10,... | collective-permute-start | bytes 589832 | tf_op jit(solution)/shard_map/ppermute | solution.py:15
  50.8 9.0 %collective-permute-start.17 = (bf16[384,256]{1,0:T(8,128)(2,1)S(1)}, bf16[384,256]{1,0:T(8,128)(2,1)S(1)}, u32[]{:S(2)}, u32[]{:S(2)}) collective-permute-start(bf16[384,256]{1,0:T(8,128)(2,1)S(1)} %get-tuple-element.104), channel_id=1, source_target_pairs={{0,3},{1,2},{2,1},{3,0},{4,7},{5,6},{6,5},{7,4},{8,11},{9,10},{10,... | collective-permute-start | bytes 589832 | tf_op jit(solution)/shard_map/ppermute | solution.py:15
  54.5 5.3 %collective-permute-start.24 = (bf16[96,256]{1,0:T(8,128)(2,1)S(1)}, bf16[96,256]{1,0:T(8,128)(2,1)S(1)}, u32[]{:S(2)}, u32[]{:S(2)}) collective-permute-start(bf16[96,256]{1,0:T(8,128)(2,1)S(1)} %get-tuple-element.117), channel_id=1, source_target_pairs={{0,16},{4,20},{8,24},{12,28},{16,0},{20,4},{24,8},{28,12},{1,17},{... | collective-permute-start | bytes 147464 | tf_op jit(solution)/shard_map/ppermute | solution.py:15
  56.0 5.9 %collective-permute-start.25 = (bf16[96,256]{1,0:T(8,128)(2,1)S(1)}, bf16[96,256]{1,0:T(8,128)(2,1)S(1)}, u32[]{:S(2)}, u32[]{:S(2)}) collective-permute-start(bf16[96,256]{1,0:T(8,128)(2,1)S(1)} %get-tuple-element.118), channel_id=1, source_target_pairs={{0,24},{4,28},{8,16},{12,20},{16,8},{20,12},{24,0},{28,4},{1,25},{... | collective-permute-start | bytes 147464 | tf_op jit(solution)/shard_map/ppermute | solution.py:15
  56.7 5.2 %collective-permute-start.26 = (bf16[96,256]{1,0:T(8,128)(2,1)S(1)}, bf16[96,256]{1,0:T(8,128)(2,1)S(1)}, u32[]{:S(2)}, u32[]{:S(2)}) collective-permute-start(bf16[96,256]{1,0:T(8,128)(2,1)S(1)} %get-tuple-element.119), channel_id=1, source_target_pairs={{0,8},{4,12},{8,0},{12,4},{16,24},{20,28},{24,16},{28,20},{1,9},{5... | collective-permute-start | bytes 147464 | tf_op jit(solution)/shard_map/ppermute | solution.py:15
  62.0 3.6 %collective-permute-start.30 = (bf16[384,256]{1,0:T(8,128)(2,1)S(1)}, bf16[384,256]{1,0:T(8,128)(2,1)S(1)}, u32[]{:S(2)}, u32[]{:S(2)}) collective-permute-start(bf16[384,256]{1,0:T(8,128)(2,1)S(1)} %shard_map.96.refs_0_), channel_id=1, source_target_pairs={{0,4},{4,0},{8,12},{12,8},{16,20},{20,16},{24,28},{28,24},{1,5},{5... | collective-permute-start | bytes 589832 | tf_op jit(solution)/shard_map/ppermute | solution.py:15
  62.1 8.7 %collective-permute-start.29 = (bf16[384,256]{1,0:T(8,128)(2,1)S(1)}, bf16[384,256]{1,0:T(8,128)(2,1)S(1)}, u32[]{:S(2)}, u32[]{:S(2)}) collective-permute-start(bf16[384,256]{1,0:T(8,128)(2,1)S(1)} %shard_map.96.refs_0_), channel_id=1, source_target_pairs={{0,3},{1,2},{2,1},{3,0},{4,7},{5,6},{6,5},{7,4},{8,11},{9,10},{10,... | collective-permute-start | bytes 589832 | tf_op jit(solution)/shard_map/ppermute | solution.py:15
  63.9 10.7 %collective-permute-start.28 = (bf16[384,256]{1,0:T(8,128)(2,1)S(1)}, bf16[384,256]{1,0:T(8,128)(2,1)S(1)}, u32[]{:S(2)}, u32[]{:S(2)}) collective-permute-start(bf16[384,256]{1,0:T(8,128)(2,1)S(1)} %shard_map.96.refs_0_), channel_id=1, source_target_pairs={{0,2},{1,3},{2,0},{3,1},{4,6},{5,7},{6,4},{7,5},{8,10},{9,11},{10,... | collective-permute-start | bytes 589832 | tf_op jit(solution)/shard_map/ppermute | solution.py:15
  64.8 9.8 %collective-permute-start.27 = (bf16[384,256]{1,0:T(8,128)(2,1)S(1)}, bf16[384,256]{1,0:T(8,128)(2,1)S(1)}, u32[]{:S(2)}, u32[]{:S(2)}) collective-permute-start(bf16[384,256]{1,0:T(8,128)(2,1)S(1)} %shard_map.96.refs_0_), channel_id=1, source_target_pairs={{0,1},{1,0},{2,3},{3,2},{4,5},{5,4},{6,7},{7,6},{8,9},{9,8},{10,11... | collective-permute-start | bytes 589832 | tf_op jit(solution)/shard_map/ppermute | solution.py:15
  70.8 4.2 %collective-permute-start.33 = (bf16[384,256]{1,0:T(8,128)(2,1)S(1)}, bf16[384,256]{1,0:T(8,128)(2,1)S(1)}, u32[]{:S(2)}, u32[]{:S(2)}) collective-permute-start(bf16[384,256]{1,0:T(8,128)(2,1)S(1)} %collective-permute-done.29.refs_0_), channel_id=1, source_target_pairs={{0,4},{4,0},{8,12},{12,8},{16,20},{20,16},{24,28},{28,24},{1,5},{5... | collective-permute-start | bytes 589832 | tf_op jit(solution)/shard_map/ppermute | solution.py:15
  74.5 1.4 %collective-permute-start.31 = (bf16[384,256]{1,0:T(8,128)(2,1)S(1)}, bf16[384,256]{1,0:T(8,128)(2,1)S(1)}, u32[]{:S(2)}, u32[]{:S(2)}) collective-permute-start(bf16[384,256]{1,0:T(8,128)(2,1)S(1)} %collective-permute-done.27.refs_0_), channel_id=1, source_target_pairs={{0,4},{4,0},{8,12},{12,8},{16,20},{20,16},{24,28},{28,24},{1,5},{5... | collective-permute-start | bytes 589832 | tf_op jit(solution)/shard_map/ppermute | solution.py:15
  74.6 1.7 %collective-permute-start.32 = (bf16[384,256]{1,0:T(8,128)(2,1)S(1)}, bf16[384,256]{1,0:T(8,128)(2,1)S(1)}, u32[]{:S(2)}, u32[]{:S(2)}) collective-permute-start(bf16[384,256]{1,0:T(8,128)(2,1)S(1)} %collective-permute-done.28.refs_1_), channel_id=1, source_target_pairs={{0,4},{4,0},{8,12},{12,8},{16,20},{20,16},{24,28},{28,24},{1,5},{5... | collective-permute-start | bytes 589832 | tf_op jit(solution)/shard_map/ppermute | solution.py:15

commit v7 on v6

--- a/solution.py
+++ b/solution.py
@@ -214,7 +214,7 @@
 def pack_kernel(experts, capacity, feat, *refs):
     plane, _, column = place()
     values, routes, refs = refs[:2], refs[2:4], refs[4:]
-    moved, refs = refs[: experts - 1], refs[experts - 1 :]
+    moved, refs = refs[: 2 * (experts - 1)], refs[2 * (experts - 1) :]
     slices, blocks, sems = refs[:2], refs[2:4], refs[4]
     cols = pl.ds(pl.multiple_of(column * feat, feat), feat)
     copies = [
@@ -232,8 +232,8 @@
         copies[2 + i].wait()
     for i in range(2):
         sent = dot(places[i][capacity:], slices[i][...]).astype(jnp.bfloat16)
-        for out, s in zip(moved, plane_order(experts)):
-            out[:, i * feat : (i + 1) * feat] = sent[(s - 1) * capacity : s * capacity]
+        for out, s in zip(moved[i * (experts - 1) :], plane_order(experts)[:-1]):
+            out[...] = sent[(s - 1) * capacity : s * capacity]
 
 
 def stay_kernel(experts, capacity, values, route, stay):
@@ -263,13 +263,10 @@
 
 
 def stack_kernel(*refs):
-    moved, out = refs[:-2], refs[-2:]
-    capacity, both = moved[0].shape
+    moved, out = refs[:-1], refs[-1]
+    capacity = moved[0].shape[0]
     for ref, s in zip(moved, plane_order(len(moved) + 1)):
-        for i in range(2):
-            out[i][(s - 1) * capacity : s * capacity, :] = ref[
-                :, i * (both // 2) : (i + 1) * (both // 2)
-            ]
+        out[(s - 1) * capacity : s * capacity, :] = ref[...]
 
 
 def join_kernel(columns, stay, *refs):
@@ -533,7 +530,7 @@
 
     sent = call(
         lambda *refs: pack_kernel(experts, capacity, feat, *refs),
-        [shape(capacity, 2 * feat)] * (experts - 1),
+        [shape(capacity, feat)] * (2 * (experts - 1)),
         [teacher_in, student_in, route_t, route_s],
         in_specs=[ANY] * 4,
         grant=(253 << 20) // 4,
@@ -545,11 +542,20 @@
     stay_t, stay_s = stay(teacher_in, route_t), stay(student_in, route_s)
     routes = jnp.concatenate([route_t, route_s], axis=0)
     other_routes = across(routes)
-    w1_t, w2_t = load(teacher_w1[0], teacher_w2[0])
-    moved = after(over_planes(sent), stay_t, other_routes, w1_t)
-    mine_t, mine_s = call(
-        stack_kernel, [shape((experts - 1) * capacity, feat)] * 2, moved, name="stack"
-    )
+    def stack(moved, units=0):
+        return call(
+            stack_kernel,
+            [shape((experts - 1) * capacity, feat)],
+            moved,
+            flops=units * plane_rows * width * hid,
+            name="stack",
+        )[0]
+
+    sent_t, sent_s = sent[: experts - 1], sent[experts - 1 :]
+    moved_t = after(over_planes(sent_t), stay_t)
+    moved_s = over_planes(sent_s)
+    mine_t, mine_s = stack(moved_t, 0), stack(moved_s, 8)
+    w1_t, w2_t = load(*after((teacher_w1[0], teacher_w2[0]), mine_s))
     got_t, got_s = spread(mine_t), spread(mine_s)
     w1_s, w2_s = load(student_w1[0], student_w2[0])
     (maps,) = call(
@@ -567,7 +573,7 @@
             name="join",
         )[0]
 
-    flat_t_own = join(stay_t, got_t)
+    flat_t_own = join(stay_t, after(got_t, w1_t))
     flat_t_other = across(flat_t_own)
 
     send, hidden_own = forward([flat_t_own], w1_t, w2_t, False, "forward_t", 24)
@@ -613,7 +619,7 @@
         lambda *refs: home_kernel(experts, capacity, *refs),
         [shape(2 * capacity, piece)] * experts,
         [maps, *home],
-        flops=5 * plane_rows * width * hid,
+        flops=4 * plane_rows * width * hid,
         name="home",
     )
     teachers = [*over_planes(slots[:-1]), slots[-1]]

time: 79.3 us -> 78.5 us (0.990)
  starting transfers between devices: 34.7 us -> 38.6 us
  local copies, waits for them, and re-layouts: 4.9 us -> 1.74 us
  waiting for transfers between devices: 23 us -> 22.2 us
    ppermute x34 -> x37, starting transfers between devices: 34.7 us -> 38.6 us  [partner(): lax.ppermute(value, axis, [(i, i ^ mask) for i in range(lax.axis_size(axi...]
    unnamed x18, local copies, waits for them, and re-layouts: 4.9 us -> 1.74 us
    ppermute x34 -> x37, waiting for transfers between devices: 23 us -> 22.2 us  [partner(): lax.ppermute(value, axis, [(i, i ^ mask) for i in range(lax.axis_size(axi...]
    pallas_call x24 -> x25, Pallas kernels: 14.8 us -> 14.7 us  [call(): pl.pallas_call(kernel, name=name, out_shape=outs, in_specs=in_specs or [V...]
  transfers between devices with their start and end apart: 34 -> 37, of which waited for: 15 -> 15; matrix products, arithmetic and copies ran while one was open for 1% -> 0% of each run, Pallas kernels for 12% -> 12%
where the time goes in v7:
time: 78.5 us; the launch traced here: 78.3 us
  starting transfers between devices  38.6 us (49%)
  waiting for transfers between devices  22.2 us (28%)
  Pallas kernels  14.7 us (19%)
  local copies, waits for them, and re-layouts  1.74 us (2%)
  between operations  0.99 us (1%)
    ppermute x37, starting transfers between devices, partner(): lax.ppermute(value, axis, [(i, i ^ mask) for i in range(lax.axis_size(axi...  38.6 us
    ppermute x37, waiting for transfers between devices, partner(): lax.ppermute(value, axis, [(i, i ^ mask) for i in range(lax.axis_size(axi...  22.2 us
    pallas_call x25, Pallas kernels, call(): pl.pallas_call(kernel, name=name, out_shape=outs, in_specs=in_specs or [V...  14.7 us
    unnamed x18, local copies, waits for them, and re-layouts  1.74 us
  transfers between devices with their start and end apart: 37, of which 15 were waited for; matrix products, arithmetic and copies ran while one was open for 0% of the time, Pallas kernels for 12%

profile of v7, /device:TPU:0, one launch (start us, length us, event | category | flops | bytes accessed | tf_op | source)
XLA Modules:
  0.0 78.3 jit_solution(17627992364336264927)
XLA Ops:
  0.6 1.9 %pack.1 = (bf16[48,512]{1,0:T(8,128)(2,1)}, bf16[48,512]{1,0:T(8,128)(2,1)}, bf16[48,512]{1,0:T(8,128)(2,1)}, bf16[48,512]{1,0:T(8,128)(2,1)}, bf16[48,512]{1,0:T(8,128)(2,1)}, /*index=5*/bf16[48,512]{1,0:T(8,128)(2,1)}) custom-call(bf16[128,2048]{1,0:T(8,128)(2,1)} %refs_0_.5, bf16[128,2048]{1,0:T(8,128)(2,1)} %refs_1_.1, s32[1,128]{1,0:T(1,128)} %bitcast.15, ...), custom_call_target="tpu_custom_call" | custom-call | tf_op jit(solution)/shard_map/pack/pallas_call | solution.py:172
  2.5 4.1 %collective-permute-start.6 = (bf16[48,512]{1,0:T(8,128)(2,1)}, bf16[48,512]{1,0:T(8,128)(2,1)S(1)}, u32[]{:S(2)}, u32[]{:S(2)}) collective-permute-start(bf16[48,512]{1,0:T(8,128)(2,1)} %get-tuple-element.80), channel_id=1, source_target_pairs={{0,16},{4,20},{8,24},{12,28},{16,0},{20,4},{24,8},{28,12},{1,17},{... | collective-permute-start | bytes 147464 | tf_op jit(solution)/shard_map/ppermute | solution.py:15
  6.6 1.3 %collective-permute-start.7 = (bf16[48,512]{1,0:T(8,128)(2,1)}, bf16[48,512]{1,0:T(8,128)(2,1)S(1)}, u32[]{:S(2)}, u32[]{:S(2)}) collective-permute-start(bf16[48,512]{1,0:T(8,128)(2,1)} %get-tuple-element.81), channel_id=1, source_target_pairs={{0,24},{4,28},{8,16},{12,20},{16,8},{20,12},{24,0},{28,4},{1,25},{... | collective-permute-start | bytes 147464 | tf_op jit(solution)/shard_map/ppermute | solution.py:15
  8.0 0.2 collective-permute-start.8
  8.2 2.8 %collective-permute-start = (bf16[48,512]{1,0:T(8,128)(2,1)}, bf16[48,512]{1,0:T(8,128)(2,1)S(1)}, u32[]{:S(2)}, u32[]{:S(2)}) collective-permute-start(bf16[48,512]{1,0:T(8,128)(2,1)} %get-tuple-element.77), channel_id=1, source_target_pairs={{0,16},{4,20},{8,24},{12,28},{16,0},{20,4},{24,8},{28,12},{1,17},{... | collective-permute-start | bytes 147464 | tf_op jit(solution)/shard_map/ppermute | solution.py:15
  11.0 1.3 %collective-permute-start.1 = (bf16[48,512]{1,0:T(8,128)(2,1)}, bf16[48,512]{1,0:T(8,128)(2,1)S(1)}, u32[]{:S(2)}, u32[]{:S(2)}) collective-permute-start(bf16[48,512]{1,0:T(8,128)(2,1)} %get-tuple-element.78), channel_id=1, source_target_pairs={{0,24},{4,28},{8,16},{12,20},{16,8},{20,12},{24,0},{28,4},{1,25},{... | collective-permute-start | bytes 147464 | tf_op jit(solution)/shard_map/ppermute | solution.py:15
  12.4 1.0 %copy-done = bf16[128,2048]{1,0:T(8,128)(2,1)S(1)} copy-done((bf16[128,2048]{1,0:T(8,128)(2,1)S(1)}, bf16[128,2048]{1,0:T(8,128)(2,1)}, u32[]{:S(2)}) %copy-start) | copy-done | bytes 524312
  13.4 0.7 copy-done.7
  14.1 0.3 stay.3.refs_0_
  14.5 2.5 %collective-permute-start.11 = (bf16[144,512]{1,0:T(8,128)(2,1)S(1)}, bf16[144,512]{1,0:T(8,128)(2,1)S(1)}, u32[]{:S(2)}, u32[]{:S(2)}) collective-permute-start(bf16[144,512]{1,0:T(8,128)(2,1)S(1)} %stack.3.refs_1_), channel_id=1, source_target_pairs={{0,3},{1,2},{2,1},{3,0},{4,7},{5,6},{6,5},{7,4},{8,11},{9,10},{10,... | collective-permute-start | bytes 442376 | tf_op jit(solution)/shard_map/ppermute | solution.py:15
  17.0 0.5 collective-permute-start.10
  17.5 0.5 collective-permute-start.9
  18.1 2.5 %collective-permute-start.5 = (bf16[144,512]{1,0:T(8,128)(2,1)S(1)}, bf16[144,512]{1,0:T(8,128)(2,1)S(1)}, u32[]{:S(2)}, u32[]{:S(2)}) collective-permute-start(bf16[144,512]{1,0:T(8,128)(2,1)S(1)} %stack.2.refs_1_), channel_id=1, source_target_pairs={{0,3},{1,2},{2,1},{3,0},{4,7},{5,6},{6,5},{7,4},{8,11},{9,10},{10,... | collective-permute-start | bytes 442376 | tf_op jit(solution)/shard_map/ppermute | solution.py:15
  20.6 0.5 collective-permute-start.4
  21.1 0.3 load.2
  21.4 0.9 %collective-permute-done.11.refs_4_ = bf16[144,512]{1,0:T(8,128)(2,1)S(1)} collective-permute-done((bf16[144,512]{1,0:T(8,128)(2,1)S(1)}, bf16[144,512]{1,0:T(8,128)(2,1)S(1)}, u32[]{:S(2)}, u32[]{:S(2)}) %collective-permute-start.11) | collective-permute-done | bytes 147488 | tf_op jit(solution)/shard_map/ppermute | solution.py:15
  22.3 1.6 %collective-permute-start.3 = (bf16[144,512]{1,0:T(8,128)(2,1)S(1)}, bf16[144,512]{1,0:T(8,128)(2,1)S(1)}, u32[]{:S(2)}, u32[]{:S(2)}) collective-permute-start(bf16[144,512]{1,0:T(8,128)(2,1)S(1)} %stack.2.refs_1_), channel_id=1, source_target_pairs={{0,1},{1,0},{2,3},{3,2},{4,5},{5,4},{6,7},{7,6},{8,9},{9,8},{10,11... | collective-permute-start | bytes 442376 | tf_op jit(solution)/shard_map/ppermute | solution.py:15
  23.9 3.0 %collective-permute-done.10.refs_3_ = bf16[144,512]{1,0:T(8,128)(2,1)S(1)} collective-permute-done((bf16[144,512]{1,0:T(8,128)(2,1)S(1)}, bf16[144,512]{1,0:T(8,128)(2,1)S(1)}, u32[]{:S(2)}, u32[]{:S(2)}) %collective-permute-start.10) | collective-permute-done | bytes 147488 | tf_op jit(solution)/shard_map/ppermute | solution.py:15
  27.0 0.9 %forward_t.2 = (bf16[1,4,192,256]{3,2,1,0:T(8,128)(2,1)S(1)}, bf16[192,512]{1,0:T(8,128)(2,1)S(1)}) custom-call(bf16[192,2048]{1,0:T(8,128)(2,1)S(1)} %join.2.refs_0_, bf16[2048,512]{1,0:T(8,128)(2,1)S(1)} %get-tuple-element.88.refs_1_, bf16[512,2048]{1,0:T(8,128)(2,1)S(1)} %get-tuple-element.93.refs_2_), custom_call_target="tpu_custom_call" | custom-call | flops 9663676416 | tf_op jit(solution)/shard_map/forward_t/pallas_call | solution.py:172
  28.0 0.6 collective-permute-start.13
  28.5 0.7 collective-permute-done.12.refs_0_
  29.3 0.9 %forward_t.3 = (bf16[1,4,192,256]{3,2,1,0:T(8,128)(2,1)S(1)}, bf16[192,512]{1,0:T(8,128)(2,1)S(1)}) custom-call(bf16[192,2048]{1,0:T(8,128)(2,1)S(1)} %collective-permute-done.12.refs_0_, bf16[2048,512]{1,0:T(8,128)(2,1)S(1)} %get-tuple-element.88.refs_1_, bf16[512,2048]{1,0:T(8,128)(2,1)S(1)} %get-tuple-element.93.refs_2_), custom_call_target="tpu_custom_call" | custom-call | tf_op jit(solution)/shard_map/forward_t/pallas_call | solution.py:172
  30.2 0.2 collective-permute-start.14
  30.4 0.3 stay.2.refs_0_
  30.8 0.3 load.3
  31.1 0.6 keep_t.1
  31.8 0.2 collective-permute-done.14.refs_4_
  32.0 0.2 pair.2
  32.2 0.3 collective-permute-start.15
  32.5 0.7 collective-permute-start.21
  33.2 0.5 collective-permute-start.22
  33.7 2.3 %collective-permute-start.23 = (bf16[384,256]{1,0:T(8,128)(2,1)S(1)}, bf16[384,256]{1,0:T(8,128)(2,1)S(1)}, u32[]{:S(2)}, u32[]{:S(2)}) collective-permute-start(bf16[384,256]{1,0:T(8,128)(2,1)S(1)} %get-tuple-element.121), channel_id=1, source_target_pairs={{0,3},{1,2},{2,1},{3,0},{4,7},{5,6},{6,5},{7,4},{8,11},{9,10},{10,... | collective-permute-start | bytes 589832 | tf_op jit(solution)/shard_map/ppermute | solution.py:15
  36.0 1.7 %forward_s.1 = (bf16[2,4,192,256]{3,2,1,0:T(8,128)(2,1)S(1)}, bf16[192,512]{1,0:T(8,128)(2,1)S(1)}, bf16[192,512]{1,0:T(8,128)(2,1)S(1)}, f32[192,512]{1,0:T(8,128)S(1)}, f32[192,512]{1,0:T(8,128)S(1)}) custom-call(bf16[192,2048]{1,0:T(8,128)(2,1)S(1)} %join.3.refs_0_.refs_5_, bf16[192,2048]{1,0:T(8,128)(2,1)S(1)} %collective-permute-done.15.refs_1_.refs_6_, ...), custom_call_target="tpu_custom_call" | custom-call | tf_op jit(solution)/shard_map/forward_s/pallas_call | solution.py:172
  37.8 1.4 %keep_s.1 = (bf16[4,192,256]{2,1,0:T(8,128)(2,1)S(1)}, bf16[4,192,256]{2,1,0:T(8,128)(2,1)S(1)}, bf16[2048,384]{1,0:T(8,128)(2,1)S(1)}, bf16[512,384]{1,0:T(8,128)(2,1)S(1)}, f32[384,512]{1,0:T(8,128)S(1)}) custom-call(bf16[192,512]{1,0:T(8,128)(2,1)S(1)} %get-tuple-element.108.refs_0_, bf16[192,512]{1,0:T(8,128)(2,1)S(1)} %get-tuple-element.109.refs_1_, ...), custom_call_target="tpu_custom_call" | custom-call | flops 25769803776 | tf_op jit(solution)/shard_map/keep_s/pallas_call | solution.py:172
  39.2 0.9 %collective-permute-done.16.refs_2_ = bf16[2,4,192,256]{3,2,1,0:T(8,128)(2,1)S(1)} collective-permute-done((bf16[2,4,192,256]{3,2,1,0:T(8,128)(2,1)S(1)}, bf16[2,4,192,256]{3,2,1,0:T(8,128)(2,1)S(1)}, u32[]{:S(2)}, u32[]{:S(2)}) %collective-permute-start.16) | collective-permute-done | bytes 786464 | tf_op jit(solution)/shard_map/ppermute | solution.py:15
  40.2 0.7 collective-permute-start.17
  41.0 1.1 %collective-permute-done.20.refs_1_ = s32[2,128]{1,0:T(2,128)S(1)} collective-permute-done((s32[2,128]{1,0:T(2,128)S(1)}, s32[2,128]{1,0:T(2,128)S(1)}, u32[]{:S(2)}, u32[]{:S(2)}) %collective-permute-start.20) | collective-permute-done | bytes 1056 | tf_op jit(solution)/shard_map/ppermute | solution.py:15
  42.1 0.4 maps.1.refs_0_
  42.5 1.4 %collective-permute-done.22.refs_2_ = bf16[384,256]{1,0:T(8,128)(2,1)S(1)} collective-permute-done((bf16[384,256]{1,0:T(8,128)(2,1)S(1)}, bf16[384,256]{1,0:T(8,128)(2,1)S(1)}, u32[]{:S(2)}, u32[]{:S(2)}) %collective-permute-start.22) | collective-permute-done | bytes 196640 | tf_op jit(solution)/shard_map/ppermute | solution.py:15
  43.9 0.7 collective-permute-done.23.refs_3_
  44.6 2.8 %collective-permute-start.24 = (bf16[96,256]{1,0:T(8,128)(2,1)S(1)}, bf16[96,256]{1,0:T(8,128)(2,1)S(1)}, u32[]{:S(2)}, u32[]{:S(2)}) collective-permute-start(bf16[96,256]{1,0:T(8,128)(2,1)S(1)} %get-tuple-element.126), channel_id=1, source_target_pairs={{0,16},{4,20},{8,24},{12,28},{16,0},{20,4},{24,8},{28,12},{1,17},{... | collective-permute-start | bytes 147464 | tf_op jit(solution)/shard_map/ppermute | solution.py:15
  47.5 1.6 %collective-permute-start.25 = (bf16[96,256]{1,0:T(8,128)(2,1)S(1)}, bf16[96,256]{1,0:T(8,128)(2,1)S(1)}, u32[]{:S(2)}, u32[]{:S(2)}) collective-permute-start(bf16[96,256]{1,0:T(8,128)(2,1)S(1)} %get-tuple-element.127), channel_id=1, source_target_pairs={{0,24},{4,28},{8,16},{12,20},{16,8},{20,12},{24,0},{28,4},{1,25},{... | collective-permute-start | bytes 147464 | tf_op jit(solution)/shard_map/ppermute | solution.py:15
  49.1 0.7 collective-permute-start.26
  49.8 1.0 %collective-permute-start.18 = (bf16[384,256]{1,0:T(8,128)(2,1)S(1)}, bf16[384,256]{1,0:T(8,128)(2,1)S(1)}, u32[]{:S(2)}, u32[]{:S(2)}) collective-permute-start(bf16[384,256]{1,0:T(8,128)(2,1)S(1)} %get-tuple-element.117), channel_id=1, source_target_pairs={{0,2},{1,3},{2,0},{3,1},{4,6},{5,7},{6,4},{7,5},{8,10},{9,11},{10,... | collective-permute-start | bytes 589832 | tf_op jit(solution)/shard_map/ppermute | solution.py:15
  50.8 1.4 %collective-permute-start.19 = (bf16[384,256]{1,0:T(8,128)(2,1)S(1)}, bf16[384,256]{1,0:T(8,128)(2,1)S(1)}, u32[]{:S(2)}, u32[]{:S(2)}) collective-permute-start(bf16[384,256]{1,0:T(8,128)(2,1)S(1)} %get-tuple-element.118), channel_id=1, source_target_pairs={{0,3},{1,2},{2,1},{3,0},{4,7},{5,6},{6,5},{7,4},{8,11},{9,10},{10,... | collective-permute-start | bytes 589832 | tf_op jit(solution)/shard_map/ppermute | solution.py:15
  52.2 1.3 %collective-permute-done.25.refs_2_ = bf16[96,256]{1,0:T(8,128)(2,1)S(1)} collective-permute-done((bf16[96,256]{1,0:T(8,128)(2,1)S(1)}, bf16[96,256]{1,0:T(8,128)(2,1)S(1)}, u32[]{:S(2)}, u32[]{:S(2)}) %collective-permute-start.25) | collective-permute-done | bytes 49184 | tf_op jit(solution)/shard_map/ppermute | solution.py:15
  53.5 0.3 collective-permute-done.26.refs_3_
  53.7 0.2 home.1
  53.9 1.2 %collective-permute-start.27 = (bf16[96,256]{1,0:T(8,128)(2,1)S(1)}, bf16[96,256]{1,0:T(8,128)(2,1)S(1)}, u32[]{:S(2)}, u32[]{:S(2)}) collective-permute-start(bf16[96,256]{1,0:T(8,128)(2,1)S(1)} %get-tuple-element.131), channel_id=1, source_target_pairs={{0,16},{4,20},{8,24},{12,28},{16,0},{20,4},{24,8},{28,12},{1,17},{... | collective-permute-start | bytes 147464 | tf_op jit(solution)/shard_map/ppermute | solution.py:15
  55.1 1.4 %collective-permute-start.28 = (bf16[96,256]{1,0:T(8,128)(2,1)S(1)}, bf16[96,256]{1,0:T(8,128)(2,1)S(1)}, u32[]{:S(2)}, u32[]{:S(2)}) collective-permute-start(bf16[96,256]{1,0:T(8,128)(2,1)S(1)} %get-tuple-element.132), channel_id=1, source_target_pairs={{0,24},{4,28},{8,16},{12,20},{16,8},{20,12},{24,0},{28,4},{1,25},{... | collective-permute-start | bytes 147464 | tf_op jit(solution)/shard_map/ppermute | solution.py:15
  56.5 1.0 %collective-permute-start.29 = (bf16[96,256]{1,0:T(8,128)(2,1)S(1)}, bf16[96,256]{1,0:T(8,128)(2,1)S(1)}, u32[]{:S(2)}, u32[]{:S(2)}) collective-permute-start(bf16[96,256]{1,0:T(8,128)(2,1)S(1)} %get-tuple-element.133), channel_id=1, source_target_pairs={{0,8},{4,12},{8,0},{12,4},{16,24},{20,28},{24,16},{28,20},{1,9},{5... | collective-permute-start | bytes 147464 | tf_op jit(solution)/shard_map/ppermute | solution.py:15
  57.5 2.6 %collective-permute-done.18.refs_2_ = bf16[384,256]{1,0:T(8,128)(2,1)S(1)} collective-permute-done((bf16[384,256]{1,0:T(8,128)(2,1)S(1)}, bf16[384,256]{1,0:T(8,128)(2,1)S(1)}, u32[]{:S(2)}, u32[]{:S(2)}) %collective-permute-start.18) | collective-permute-done | bytes 196640 | tf_op jit(solution)/shard_map/ppermute | solution.py:15
  60.0 1.0 %collective-permute-done.28.refs_5_ = bf16[96,256]{1,0:T(8,128)(2,1)S(1)} collective-permute-done((bf16[96,256]{1,0:T(8,128)(2,1)S(1)}, bf16[96,256]{1,0:T(8,128)(2,1)S(1)}, u32[]{:S(2)}, u32[]{:S(2)}) %collective-permute-start.28) | collective-permute-done | bytes 49184 | tf_op jit(solution)/shard_map/ppermute | solution.py:15
  61.3 1.3 %collective-permute-start.32 = (bf16[384,256]{1,0:T(8,128)(2,1)S(1)}, bf16[384,256]{1,0:T(8,128)(2,1)S(1)}, u32[]{:S(2)}, u32[]{:S(2)}) collective-permute-start(bf16[384,256]{1,0:T(8,128)(2,1)S(1)} %shard_map.96.refs_0_), channel_id=1, source_target_pairs={{0,3},{1,2},{2,1},{3,0},{4,7},{5,6},{6,5},{7,4},{8,11},{9,10},{10,... | collective-permute-start | bytes 589832 | tf_op jit(solution)/shard_map/ppermute | solution.py:15
  62.7 1.1 %collective-permute-start.31 = (bf16[384,256]{1,0:T(8,128)(2,1)S(1)}, bf16[384,256]{1,0:T(8,128)(2,1)S(1)}, u32[]{:S(2)}, u32[]{:S(2)}) collective-permute-start(bf16[384,256]{1,0:T(8,128)(2,1)S(1)} %shard_map.96.refs_0_), channel_id=1, source_target_pairs={{0,2},{1,3},{2,0},{3,1},{4,6},{5,7},{6,4},{7,5},{8,10},{9,11},{10,... | collective-permute-start | bytes 589832 | tf_op jit(solution)/shard_map/ppermute | solution.py:15
  63.8 1.1 %collective-permute-start.30 = (bf16[384,256]{1,0:T(8,128)(2,1)S(1)}, bf16[384,256]{1,0:T(8,128)(2,1)S(1)}, u32[]{:S(2)}, u32[]{:S(2)}) collective-permute-start(bf16[384,256]{1,0:T(8,128)(2,1)S(1)} %shard_map.96.refs_0_), channel_id=1, source_target_pairs={{0,1},{1,0},{2,3},{3,2},{4,5},{5,4},{6,7},{7,6},{8,9},{9,8},{10,11... | collective-permute-start | bytes 589832 | tf_op jit(solution)/shard_map/ppermute | solution.py:15
  64.9 0.6 early.3
  65.5 4.5 %collective-permute-done.32.refs_0_ = bf16[384,256]{1,0:T(8,128)(2,1)S(1)} collective-permute-done((bf16[384,256]{1,0:T(8,128)(2,1)S(1)}, bf16[384,256]{1,0:T(8,128)(2,1)S(1)}, u32[]{:S(2)}, u32[]{:S(2)}) %collective-permute-start.32) | collective-permute-done | bytes 196640 | tf_op jit(solution)/shard_map/ppermute | solution.py:15
  70.0 0.4 early.4
  70.5 3.3 %collective-permute-done.31.refs_1_ = bf16[384,256]{1,0:T(8,128)(2,1)S(1)} collective-permute-done((bf16[384,256]{1,0:T(8,128)(2,1)S(1)}, bf16[384,256]{1,0:T(8,128)(2,1)S(1)}, u32[]{:S(2)}, u32[]{:S(2)}) %collective-permute-start.31) | collective-permute-done | bytes 196640 | tf_op jit(solution)/shard_map/ppermute | solution.py:15
  73.8 0.5 collective-permute-start.35
  74.3 0.9 %early.5 = (f32[384,512]{1,0:T(8,128)S(1)}, bf16[512,256]{1,0:T(8,128)(2,1)S(1)}, bf16[512,256]{1,0:T(8,128)(2,1)S(1)}, bf16[512,256]{1,0:T(8,128)(2,1)S(1)}) custom-call(bf16[384,256]{1,0:T(8,128)(2,1)S(1)} %collective-permute-done.30.refs_0_, bf16[384,256]{1,0:T(8,128)(2,1)S(1)} %collective-permute-done.31.refs_1_, ...), custom_call_target="tpu_custom_call" | custom-call | tf_op jit(solution)/shard_map/early/pallas_call | solution.py:172
  75.2 0.3 collective-permute-done.35.refs_1_
  75.5 2.8 %last.1 = (bf16[2048,512]{1,0:T(8,128)(2,1)}, bf16[512,2048]{1,0:T(8,128)(2,1)}) custom-call(bf16[384,256]{1,0:T(8,128)(2,1)S(1)} %collective-permute-done.34.refs_0_, bf16[384,256]{1,0:T(8,128)(2,1)S(1)} %collective-permute-done.35.refs_1_, bf16[512,256]{1,0:T(8,128)(2,1)S(1)} %get-tuple-element.141.refs_2_, ...), custom_call_target="tpu_custom_call" | custom-call | tf_op jit(solution)/shard_map/last/pallas_call | solution.py:172
  (54 shorter events, 1.0 us)
Async XLA Ops:
  2.5 9.8 %collective-permute-start.6 = (bf16[48,512]{1,0:T(8,128)(2,1)}, bf16[48,512]{1,0:T(8,128)(2,1)S(1)}, u32[]{:S(2)}, u32[]{:S(2)}) collective-permute-start(bf16[48,512]{1,0:T(8,128)(2,1)} %get-tuple-element.80), channel_id=1, source_target_pairs={{0,16},{4,20},{8,24},{12,28},{16,0},{20,4},{24,8},{28,12},{1,17},{... | collective-permute-start | bytes 147464 | tf_op jit(solution)/shard_map/ppermute | solution.py:15
  6.6 7.8 %collective-permute-start.7 = (bf16[48,512]{1,0:T(8,128)(2,1)}, bf16[48,512]{1,0:T(8,128)(2,1)S(1)}, u32[]{:S(2)}, u32[]{:S(2)}) collective-permute-start(bf16[48,512]{1,0:T(8,128)(2,1)} %get-tuple-element.81), channel_id=1, source_target_pairs={{0,24},{4,28},{8,16},{12,20},{16,8},{20,12},{24,0},{28,4},{1,25},{... | collective-permute-start | bytes 147464 | tf_op jit(solution)/shard_map/ppermute | solution.py:15
  8.0 6.5 %collective-permute-start.8 = (bf16[48,512]{1,0:T(8,128)(2,1)}, bf16[48,512]{1,0:T(8,128)(2,1)S(1)}, u32[]{:S(2)}, u32[]{:S(2)}) collective-permute-start(bf16[48,512]{1,0:T(8,128)(2,1)} %get-tuple-element.82), channel_id=1, source_target_pairs={{0,8},{4,12},{8,0},{12,4},{16,24},{20,28},{24,16},{28,20},{1,9},{5... | collective-permute-start | bytes 147464 | tf_op jit(solution)/shard_map/ppermute | solution.py:15
  8.2 9.3 %collective-permute-start = (bf16[48,512]{1,0:T(8,128)(2,1)}, bf16[48,512]{1,0:T(8,128)(2,1)S(1)}, u32[]{:S(2)}, u32[]{:S(2)}) collective-permute-start(bf16[48,512]{1,0:T(8,128)(2,1)} %get-tuple-element.77), channel_id=1, source_target_pairs={{0,16},{4,20},{8,24},{12,28},{16,0},{20,4},{24,8},{28,12},{1,17},{... | collective-permute-start | bytes 147464 | tf_op jit(solution)/shard_map/ppermute | solution.py:15
  11.0 7.0 %collective-permute-start.1 = (bf16[48,512]{1,0:T(8,128)(2,1)}, bf16[48,512]{1,0:T(8,128)(2,1)S(1)}, u32[]{:S(2)}, u32[]{:S(2)}) collective-permute-start(bf16[48,512]{1,0:T(8,128)(2,1)} %get-tuple-element.78), channel_id=1, source_target_pairs={{0,24},{4,28},{8,16},{12,20},{16,8},{20,12},{24,0},{28,4},{1,25},{... | collective-permute-start | bytes 147464 | tf_op jit(solution)/shard_map/ppermute | solution.py:15
  12.4 5.7 %collective-permute-start.2 = (bf16[48,512]{1,0:T(8,128)(2,1)}, bf16[48,512]{1,0:T(8,128)(2,1)S(1)}, u32[]{:S(2)}, u32[]{:S(2)}) collective-permute-start(bf16[48,512]{1,0:T(8,128)(2,1)} %get-tuple-element.79), channel_id=1, source_target_pairs={{0,8},{4,12},{8,0},{12,4},{16,24},{20,28},{24,16},{28,20},{1,9},{5... | collective-permute-start | bytes 147464 | tf_op jit(solution)/shard_map/ppermute | solution.py:15
  12.4 1.0 %copy-start = (bf16[128,2048]{1,0:T(8,128)(2,1)S(1)}, bf16[128,2048]{1,0:T(8,128)(2,1)}, u32[]{:S(2)}) copy-start(bf16[128,2048]{1,0:T(8,128)(2,1)} %refs_0_.5) | copy-start | bytes 1572868
  13.4 0.7 copy-start.7
  14.5 6.6 %copy-start.2 = (bf16[1,2048,512]{2,1,0:T(8,128)(2,1)S(1)}, bf16[1,2048,512]{2,1,0:T(8,128)(2,1)}, u32[]{:S(2)}) copy-start(bf16[1,2048,512]{2,1,0:T(8,128)(2,1)} %param.12) | copy-start | bytes 6291460
  14.5 6.6 %copy-start.3 = (bf16[1,512,2048]{2,1,0:T(8,128)(2,1)S(1)}, bf16[1,512,2048]{2,1,0:T(8,128)(2,1)}, u32[]{:S(2)}) copy-start(bf16[1,512,2048]{2,1,0:T(8,128)(2,1)} %param.13) | copy-start | bytes 6291460
  14.5 7.8 %collective-permute-start.11 = (bf16[144,512]{1,0:T(8,128)(2,1)S(1)}, bf16[144,512]{1,0:T(8,128)(2,1)S(1)}, u32[]{:S(2)}, u32[]{:S(2)}) collective-permute-start(bf16[144,512]{1,0:T(8,128)(2,1)S(1)} %stack.3.refs_1_), channel_id=1, source_target_pairs={{0,3},{1,2},{2,1},{3,0},{4,7},{5,6},{6,5},{7,4},{8,11},{9,10},{10,... | collective-permute-start | bytes 442376 | tf_op jit(solution)/shard_map/ppermute | solution.py:15
  17.0 9.8 %collective-permute-start.10 = (bf16[144,512]{1,0:T(8,128)(2,1)S(1)}, bf16[144,512]{1,0:T(8,128)(2,1)S(1)}, u32[]{:S(2)}, u32[]{:S(2)}) collective-permute-start(bf16[144,512]{1,0:T(8,128)(2,1)S(1)} %stack.3.refs_1_), channel_id=1, source_target_pairs={{0,2},{1,3},{2,0},{3,1},{4,6},{5,7},{6,4},{7,5},{8,10},{9,11},{10,... | collective-permute-start | bytes 442376 | tf_op jit(solution)/shard_map/ppermute | solution.py:15
  17.5 9.3 %collective-permute-start.9 = (bf16[144,512]{1,0:T(8,128)(2,1)S(1)}, bf16[144,512]{1,0:T(8,128)(2,1)S(1)}, u32[]{:S(2)}, u32[]{:S(2)}) collective-permute-start(bf16[144,512]{1,0:T(8,128)(2,1)S(1)} %stack.3.refs_1_), channel_id=1, source_target_pairs={{0,1},{1,0},{2,3},{3,2},{4,5},{5,4},{6,7},{7,6},{8,9},{9,8},{10,11... | collective-permute-start | bytes 442376 | tf_op jit(solution)/shard_map/ppermute | solution.py:15
  18.1 13.6 %collective-permute-start.5 = (bf16[144,512]{1,0:T(8,128)(2,1)S(1)}, bf16[144,512]{1,0:T(8,128)(2,1)S(1)}, u32[]{:S(2)}, u32[]{:S(2)}) collective-permute-start(bf16[144,512]{1,0:T(8,128)(2,1)S(1)} %stack.2.refs_1_), channel_id=1, source_target_pairs={{0,3},{1,2},{2,1},{3,0},{4,7},{5,6},{6,5},{7,4},{8,11},{9,10},{10,... | collective-permute-start | bytes 442376 | tf_op jit(solution)/shard_map/ppermute | solution.py:15
  20.6 11.1 %collective-permute-start.4 = (bf16[144,512]{1,0:T(8,128)(2,1)S(1)}, bf16[144,512]{1,0:T(8,128)(2,1)S(1)}, u32[]{:S(2)}, u32[]{:S(2)}) collective-permute-start(bf16[144,512]{1,0:T(8,128)(2,1)S(1)} %stack.2.refs_1_), channel_id=1, source_target_pairs={{0,2},{1,3},{2,0},{3,1},{4,6},{5,7},{6,4},{7,5},{8,10},{9,11},{10,... | collective-permute-start | bytes 442376 | tf_op jit(solution)/shard_map/ppermute | solution.py:15
  22.3 9.5 %collective-permute-start.3 = (bf16[144,512]{1,0:T(8,128)(2,1)S(1)}, bf16[144,512]{1,0:T(8,128)(2,1)S(1)}, u32[]{:S(2)}, u32[]{:S(2)}) collective-permute-start(bf16[144,512]{1,0:T(8,128)(2,1)S(1)} %stack.2.refs_1_), channel_id=1, source_target_pairs={{0,1},{1,0},{2,3},{3,2},{4,5},{5,4},{6,7},{7,6},{8,9},{9,8},{10,11... | collective-permute-start | bytes 442376 | tf_op jit(solution)/shard_map/ppermute | solution.py:15
  26.9 2.4 %collective-permute-start.12 = (bf16[192,2048]{1,0:T(8,128)(2,1)S(1)}, bf16[192,2048]{1,0:T(8,128)(2,1)S(1)}, u32[]{:S(2)}, u32[]{:S(2)}) collective-permute-start(bf16[192,2048]{1,0:T(8,128)(2,1)S(1)} %join.2.refs_0_), channel_id=1, source_target_pairs={{0,4},{4,0},{8,12},{12,8},{16,20},{20,16},{24,28},{28,24},{1,5},{5... | collective-permute-start | bytes 2359304 | tf_op jit(solution)/shard_map/ppermute | solution.py:15
  27.9 2.5 %copy-start.1 = (bf16[128,2048]{1,0:T(8,128)(2,1)S(1)}, bf16[128,2048]{1,0:T(8,128)(2,1)}, u32[]{:S(2)}) copy-start(bf16[128,2048]{1,0:T(8,128)(2,1)} %refs_1_.1) | copy-start | bytes 1572868
  27.9 2.5 %copy-start.6 = (s32[128,1]{0,1:T(1,128)S(1)}, s32[128,1]{0,1:T(1,128)}, u32[]{:S(2)}) copy-start(s32[128,1]{0,1:T(1,128)} %param.11) | copy-start | bytes 1540
  28.0 2.8 %copy-start.4 = (bf16[1,2048,512]{2,1,0:T(8,128)(2,1)S(1)}, bf16[1,2048,512]{2,1,0:T(8,128)(2,1)}, u32[]{:S(2)}) copy-start(bf16[1,2048,512]{2,1,0:T(8,128)(2,1)} %param.14) | copy-start | bytes 6291460
  28.0 2.8 %copy-start.5 = (bf16[1,512,2048]{2,1,0:T(8,128)(2,1)S(1)}, bf16[1,512,2048]{2,1,0:T(8,128)(2,1)}, u32[]{:S(2)}) copy-start(bf16[1,512,2048]{2,1,0:T(8,128)(2,1)} %param.15) | copy-start | bytes 6291460
  28.0 3.8 %collective-permute-start.13 = (bf16[1,4,192,256]{3,2,1,0:T(8,128)(2,1)S(1)}, bf16[1,4,192,256]{3,2,1,0:T(8,128)(2,1)S(1)}, u32[]{:S(2)}, u32[]{:S(2)}) collective-permute-start(bf16[1,4,192,256]{3,2,1,0:T(8,128)(2,1)S(1)} %get-tuple-element.100), channel_id=1, source_target_pairs={{0,4},{4,0},{8,12},{12,8},{16,20},{20,16},{24,28},{28,24},{1,5},{5... | collective-permute-start | bytes 1179656 | tf_op jit(solution)/shard_map/ppermute | solution.py:15
  30.2 1.8 %collective-permute-start.14 = (bf16[1,4,192,256]{3,2,1,0:T(8,128)(2,1)S(1)}, bf16[1,4,192,256]{3,2,1,0:T(8,128)(2,1)S(1)}, u32[]{:S(2)}, u32[]{:S(2)}) collective-permute-start(bf16[1,4,192,256]{3,2,1,0:T(8,128)(2,1)S(1)} %get-tuple-element.101), channel_id=1, source_target_pairs={{0,4},{4,0},{8,12},{12,8},{16,20},{20,16},{24,28},{28,24},{1,5},{5... | collective-permute-start | bytes 1179656 | tf_op jit(solution)/shard_map/ppermute | solution.py:15
  31.1 0.7 copy-start.8
  32.2 3.8 %collective-permute-start.15 = (bf16[192,2048]{1,0:T(8,128)(2,1)S(1)}, bf16[192,2048]{1,0:T(8,128)(2,1)S(1)}, u32[]{:S(2)}, u32[]{:S(2)}) collective-permute-start(bf16[192,2048]{1,0:T(8,128)(2,1)S(1)} %join.3.refs_0_.refs_5_), channel_id=1, source_target_pairs={{0,4},{4,0},{8,12},{12,8},{16,20},{20,16},{24,28},{28,24},{1,5},{5... | collective-permute-start | bytes 2359304 | tf_op jit(solution)/shard_map/ppermute | solution.py:15
  32.5 10.0 %collective-permute-start.21 = (bf16[384,256]{1,0:T(8,128)(2,1)S(1)}, bf16[384,256]{1,0:T(8,128)(2,1)S(1)}, u32[]{:S(2)}, u32[]{:S(2)}) collective-permute-start(bf16[384,256]{1,0:T(8,128)(2,1)S(1)} %get-tuple-element.119), channel_id=1, source_target_pairs={{0,1},{1,0},{2,3},{3,2},{4,5},{5,4},{6,7},{7,6},{8,9},{9,8},{10,11... | collective-permute-start | bytes 589832 | tf_op jit(solution)/shard_map/ppermute | solution.py:15
  33.2 10.7 %collective-permute-start.22 = (bf16[384,256]{1,0:T(8,128)(2,1)S(1)}, bf16[384,256]{1,0:T(8,128)(2,1)S(1)}, u32[]{:S(2)}, u32[]{:S(2)}) collective-permute-start(bf16[384,256]{1,0:T(8,128)(2,1)S(1)} %get-tuple-element.120), channel_id=1, source_target_pairs={{0,2},{1,3},{2,0},{3,1},{4,6},{5,7},{6,4},{7,5},{8,10},{9,11},{10,... | collective-permute-start | bytes 589832 | tf_op jit(solution)/shard_map/ppermute | solution.py:15
  33.7 10.9 %collective-permute-start.23 = (bf16[384,256]{1,0:T(8,128)(2,1)S(1)}, bf16[384,256]{1,0:T(8,128)(2,1)S(1)}, u32[]{:S(2)}, u32[]{:S(2)}) collective-permute-start(bf16[384,256]{1,0:T(8,128)(2,1)S(1)} %get-tuple-element.121), channel_id=1, source_target_pairs={{0,3},{1,2},{2,1},{3,0},{4,7},{5,6},{6,5},{7,4},{8,11},{9,10},{10,... | collective-permute-start | bytes 589832 | tf_op jit(solution)/shard_map/ppermute | solution.py:15
  37.7 2.4 %collective-permute-start.16 = (bf16[2,4,192,256]{3,2,1,0:T(8,128)(2,1)S(1)}, bf16[2,4,192,256]{3,2,1,0:T(8,128)(2,1)S(1)}, u32[]{:S(2)}, u32[]{:S(2)}) collective-permute-start(bf16[2,4,192,256]{3,2,1,0:T(8,128)(2,1)S(1)} %get-tuple-element.114), channel_id=1, source_target_pairs={{0,4},{4,0},{8,12},{12,8},{16,20},{20,16},{24,28},{28,24},{1,5},{5... | collective-permute-start | bytes 2359304 | tf_op jit(solution)/shard_map/ppermute | solution.py:15
  40.2 8.9 %collective-permute-start.17 = (bf16[384,256]{1,0:T(8,128)(2,1)S(1)}, bf16[384,256]{1,0:T(8,128)(2,1)S(1)}, u32[]{:S(2)}, u32[]{:S(2)}) collective-permute-start(bf16[384,256]{1,0:T(8,128)(2,1)S(1)} %get-tuple-element.116), channel_id=1, source_target_pairs={{0,1},{1,0},{2,3},{3,2},{4,5},{5,4},{6,7},{7,6},{8,9},{9,8},{10,11... | collective-permute-start | bytes 589832 | tf_op jit(solution)/shard_map/ppermute | solution.py:15
  41.0 1.1 %collective-permute-start.20 = (s32[2,128]{1,0:T(2,128)S(1)}, s32[2,128]{1,0:T(2,128)S(1)}, u32[]{:S(2)}, u32[]{:S(2)}) collective-permute-start(s32[2,128]{1,0:T(2,128)S(1)} %pad_add_fusion.refs_0_), channel_id=1, source_target_pairs={{0,4},{4,0},{8,12},{12,8},{16,20},{20,16},{24,28},{28,24},{1,5},{5... | collective-permute-start | bytes 3080 | tf_op jit(solution)/shard_map/ppermute | solution.py:15
  44.6 7.5 %collective-permute-start.24 = (bf16[96,256]{1,0:T(8,128)(2,1)S(1)}, bf16[96,256]{1,0:T(8,128)(2,1)S(1)}, u32[]{:S(2)}, u32[]{:S(2)}) collective-permute-start(bf16[96,256]{1,0:T(8,128)(2,1)S(1)} %get-tuple-element.126), channel_id=1, source_target_pairs={{0,16},{4,20},{8,24},{12,28},{16,0},{20,4},{24,8},{28,12},{1,17},{... | collective-permute-start | bytes 147464 | tf_op jit(solution)/shard_map/ppermute | solution.py:15
  47.5 6.0 %collective-permute-start.25 = (bf16[96,256]{1,0:T(8,128)(2,1)S(1)}, bf16[96,256]{1,0:T(8,128)(2,1)S(1)}, u32[]{:S(2)}, u32[]{:S(2)}) collective-permute-start(bf16[96,256]{1,0:T(8,128)(2,1)S(1)} %get-tuple-element.127), channel_id=1, source_target_pairs={{0,24},{4,28},{8,16},{12,20},{16,8},{20,12},{24,0},{28,4},{1,25},{... | collective-permute-start | bytes 147464 | tf_op jit(solution)/shard_map/ppermute | solution.py:15
  49.1 4.6 %collective-permute-start.26 = (bf16[96,256]{1,0:T(8,128)(2,1)S(1)}, bf16[96,256]{1,0:T(8,128)(2,1)S(1)}, u32[]{:S(2)}, u32[]{:S(2)}) collective-permute-start(bf16[96,256]{1,0:T(8,128)(2,1)S(1)} %get-tuple-element.129), channel_id=1, source_target_pairs={{0,8},{4,12},{8,0},{12,4},{16,24},{20,28},{24,16},{28,20},{1,9},{5... | collective-permute-start | bytes 147464 | tf_op jit(solution)/shard_map/ppermute | solution.py:15
  49.8 10.2 %collective-permute-start.18 = (bf16[384,256]{1,0:T(8,128)(2,1)S(1)}, bf16[384,256]{1,0:T(8,128)(2,1)S(1)}, u32[]{:S(2)}, u32[]{:S(2)}) collective-permute-start(bf16[384,256]{1,0:T(8,128)(2,1)S(1)} %get-tuple-element.117), channel_id=1, source_target_pairs={{0,2},{1,3},{2,0},{3,1},{4,6},{5,7},{6,4},{7,5},{8,10},{9,11},{10,... | collective-permute-start | bytes 589832 | tf_op jit(solution)/shard_map/ppermute | solution.py:15
  50.8 9.3 %collective-permute-start.19 = (bf16[384,256]{1,0:T(8,128)(2,1)S(1)}, bf16[384,256]{1,0:T(8,128)(2,1)S(1)}, u32[]{:S(2)}, u32[]{:S(2)}) collective-permute-start(bf16[384,256]{1,0:T(8,128)(2,1)S(1)} %get-tuple-element.118), channel_id=1, source_target_pairs={{0,3},{1,2},{2,1},{3,0},{4,7},{5,6},{6,5},{7,4},{8,11},{9,10},{10,... | collective-permute-start | bytes 589832 | tf_op jit(solution)/shard_map/ppermute | solution.py:15
  53.9 6.1 %collective-permute-start.27 = (bf16[96,256]{1,0:T(8,128)(2,1)S(1)}, bf16[96,256]{1,0:T(8,128)(2,1)S(1)}, u32[]{:S(2)}, u32[]{:S(2)}) collective-permute-start(bf16[96,256]{1,0:T(8,128)(2,1)S(1)} %get-tuple-element.131), channel_id=1, source_target_pairs={{0,16},{4,20},{8,24},{12,28},{16,0},{20,4},{24,8},{28,12},{1,17},{... | collective-permute-start | bytes 147464 | tf_op jit(solution)/shard_map/ppermute | solution.py:15
  55.1 6.0 %collective-permute-start.28 = (bf16[96,256]{1,0:T(8,128)(2,1)S(1)}, bf16[96,256]{1,0:T(8,128)(2,1)S(1)}, u32[]{:S(2)}, u32[]{:S(2)}) collective-permute-start(bf16[96,256]{1,0:T(8,128)(2,1)S(1)} %get-tuple-element.132), channel_id=1, source_target_pairs={{0,24},{4,28},{8,16},{12,20},{16,8},{20,12},{24,0},{28,4},{1,25},{... | collective-permute-start | bytes 147464 | tf_op jit(solution)/shard_map/ppermute | solution.py:15
  56.5 4.6 %collective-permute-start.29 = (bf16[96,256]{1,0:T(8,128)(2,1)S(1)}, bf16[96,256]{1,0:T(8,128)(2,1)S(1)}, u32[]{:S(2)}, u32[]{:S(2)}) collective-permute-start(bf16[96,256]{1,0:T(8,128)(2,1)S(1)} %get-tuple-element.133), channel_id=1, source_target_pairs={{0,8},{4,12},{8,0},{12,4},{16,24},{20,28},{24,16},{28,20},{1,9},{5... | collective-permute-start | bytes 147464 | tf_op jit(solution)/shard_map/ppermute | solution.py:15
  61.3 3.6 %collective-permute-start.33 = (bf16[384,256]{1,0:T(8,128)(2,1)S(1)}, bf16[384,256]{1,0:T(8,128)(2,1)S(1)}, u32[]{:S(2)}, u32[]{:S(2)}) collective-permute-start(bf16[384,256]{1,0:T(8,128)(2,1)S(1)} %shard_map.96.refs_0_), channel_id=1, source_target_pairs={{0,4},{4,0},{8,12},{12,8},{16,20},{20,16},{24,28},{28,24},{1,5},{5... | collective-permute-start | bytes 589832 | tf_op jit(solution)/shard_map/ppermute | solution.py:15
  61.3 8.7 %collective-permute-start.32 = (bf16[384,256]{1,0:T(8,128)(2,1)S(1)}, bf16[384,256]{1,0:T(8,128)(2,1)S(1)}, u32[]{:S(2)}, u32[]{:S(2)}) collective-permute-start(bf16[384,256]{1,0:T(8,128)(2,1)S(1)} %shard_map.96.refs_0_), channel_id=1, source_target_pairs={{0,3},{1,2},{2,1},{3,0},{4,7},{5,6},{6,5},{7,4},{8,11},{9,10},{10,... | collective-permute-start | bytes 589832 | tf_op jit(solution)/shard_map/ppermute | solution.py:15
  62.7 11.1 %collective-permute-start.31 = (bf16[384,256]{1,0:T(8,128)(2,1)S(1)}, bf16[384,256]{1,0:T(8,128)(2,1)S(1)}, u32[]{:S(2)}, u32[]{:S(2)}) collective-permute-start(bf16[384,256]{1,0:T(8,128)(2,1)S(1)} %shard_map.96.refs_0_), channel_id=1, source_target_pairs={{0,2},{1,3},{2,0},{3,1},{4,6},{5,7},{6,4},{7,5},{8,10},{9,11},{10,... | collective-permute-start | bytes 589832 | tf_op jit(solution)/shard_map/ppermute | solution.py:15
  63.8 10.0 %collective-permute-start.30 = (bf16[384,256]{1,0:T(8,128)(2,1)S(1)}, bf16[384,256]{1,0:T(8,128)(2,1)S(1)}, u32[]{:S(2)}, u32[]{:S(2)}) collective-permute-start(bf16[384,256]{1,0:T(8,128)(2,1)S(1)} %shard_map.96.refs_0_), channel_id=1, source_target_pairs={{0,1},{1,0},{2,3},{3,2},{4,5},{5,4},{6,7},{7,6},{8,9},{9,8},{10,11... | collective-permute-start | bytes 589832 | tf_op jit(solution)/shard_map/ppermute | solution.py:15
  70.0 4.2 %collective-permute-start.36 = (bf16[384,256]{1,0:T(8,128)(2,1)S(1)}, bf16[384,256]{1,0:T(8,128)(2,1)S(1)}, u32[]{:S(2)}, u32[]{:S(2)}) collective-permute-start(bf16[384,256]{1,0:T(8,128)(2,1)S(1)} %collective-permute-done.32.refs_0_), channel_id=1, source_target_pairs={{0,4},{4,0},{8,12},{12,8},{16,20},{20,16},{24,28},{28,24},{1,5},{5... | collective-permute-start | bytes 589832 | tf_op jit(solution)/shard_map/ppermute | solution.py:15
  73.8 1.4 %collective-permute-start.34 = (bf16[384,256]{1,0:T(8,128)(2,1)S(1)}, bf16[384,256]{1,0:T(8,128)(2,1)S(1)}, u32[]{:S(2)}, u32[]{:S(2)}) collective-permute-start(bf16[384,256]{1,0:T(8,128)(2,1)S(1)} %collective-permute-done.30.refs_0_), channel_id=1, source_target_pairs={{0,4},{4,0},{8,12},{12,8},{16,20},{20,16},{24,28},{28,24},{1,5},{5... | collective-permute-start | bytes 589832 | tf_op jit(solution)/shard_map/ppermute | solution.py:15
  73.8 1.7 %collective-permute-start.35 = (bf16[384,256]{1,0:T(8,128)(2,1)S(1)}, bf16[384,256]{1,0:T(8,128)(2,1)S(1)}, u32[]{:S(2)}, u32[]{:S(2)}) collective-permute-start(bf16[384,256]{1,0:T(8,128)(2,1)S(1)} %collective-permute-done.31.refs_1_), channel_id=1, source_target_pairs={{0,4},{4,0},{8,12},{12,8},{16,20},{20,16},{24,28},{28,24},{1,5},{5... | collective-permute-start | bytes 589832 | tf_op jit(solution)/shard_map/ppermute | solution.py:15

commit v8 on v7

--- a/solution.py
+++ b/solution.py
@@ -539,7 +539,7 @@
         + [pltpu.VMEM((1, row_count), jnp.int32)] * 2
         + [pltpu.SemaphoreType.DMA((4,))],
     )
-    stay_t, stay_s = stay(teacher_in, route_t), stay(student_in, route_s)
+    stay_s = stay(student_in, route_s)
     routes = jnp.concatenate([route_t, route_s], axis=0)
     other_routes = across(routes)
     def stack(moved, units=0):
@@ -552,10 +552,11 @@
         )[0]
 
     sent_t, sent_s = sent[: experts - 1], sent[experts - 1 :]
-    moved_t = after(over_planes(sent_t), stay_t)
+    moved_t = over_planes(sent_t)
     moved_s = over_planes(sent_s)
     mine_t, mine_s = stack(moved_t, 0), stack(moved_s, 8)
     w1_t, w2_t = load(*after((teacher_w1[0], teacher_w2[0]), mine_s))
+    stay_t = stay(after(teacher_in, mine_s), route_t)
     got_t, got_s = spread(mine_t), spread(mine_s)
     w1_s, w2_s = load(student_w1[0], student_w2[0])
     (maps,) = call(

time: 78.5 us -> 76.9 us (0.980)
  local copies, waits for them, and re-layouts: 1.74 us -> 0.05 us
  waiting for transfers between devices: 22.2 us -> 23.7 us
  starting transfers between devices: 38.6 us -> 37.3 us
    unnamed x18 -> x16, local copies, waits for them, and re-layouts: 1.74 us -> 0.05 us
    ppermute x37, waiting for transfers between devices: 22.2 us -> 23.7 us  [partner(): lax.ppermute(value, axis, [(i, i ^ mask) for i in range(lax.axis_size(axi...]
    ppermute x37, starting transfers between devices: 38.6 us -> 37.3 us  [partner(): lax.ppermute(value, axis, [(i, i ^ mask) for i in range(lax.axis_size(axi...]
  transfers between devices with their start and end apart: 37 -> 37, of which waited for: 15 -> 16; matrix products, arithmetic and copies ran while one was open for 0% -> 0% of each run, Pallas kernels for 12% -> 13%
where the time goes in v8:
time: 76.9 us; the launch traced here: 76.8 us
  starting transfers between devices  37.3 us (49%)
  waiting for transfers between devices  23.7 us (31%)
  Pallas kernels  14.8 us (19%)
  between operations  0.96 us (1%)
    ppermute x37, starting transfers between devices, partner(): lax.ppermute(value, axis, [(i, i ^ mask) for i in range(lax.axis_size(axi...  37.3 us
    ppermute x37, waiting for transfers between devices, partner(): lax.ppermute(value, axis, [(i, i ^ mask) for i in range(lax.axis_size(axi...  23.7 us
    pallas_call x25, Pallas kernels, call(): pl.pallas_call(kernel, name=name, out_shape=outs, in_specs=in_specs or [V...  14.8 us
  transfers between devices with their start and end apart: 37, of which 16 were waited for; matrix products, arithmetic and copies ran while one was open for 0% of the time, Pallas kernels for 13%

profile of v8, /device:TPU:0, one launch (start us, length us, event | category | flops | bytes accessed | tf_op | source)
XLA Modules:
  0.0 76.8 jit_solution(17652440663415921078)
XLA Ops:
  0.6 1.9 %pack.1 = (bf16[48,512]{1,0:T(8,128)(2,1)}, bf16[48,512]{1,0:T(8,128)(2,1)}, bf16[48,512]{1,0:T(8,128)(2,1)}, bf16[48,512]{1,0:T(8,128)(2,1)}, bf16[48,512]{1,0:T(8,128)(2,1)}, /*index=5*/bf16[48,512]{1,0:T(8,128)(2,1)}) custom-call(bf16[128,2048]{1,0:T(8,128)(2,1)} %refs_0_.4, bf16[128,2048]{1,0:T(8,128)(2,1)} %refs_1_.1, s32[1,128]{1,0:T(1,128)} %bitcast.15, ...), custom_call_target="tpu_custom_call" | custom-call | tf_op jit(solution)/shard_map/pack/pallas_call | solution.py:172
  2.5 4.1 %collective-permute-start.6 = (bf16[48,512]{1,0:T(8,128)(2,1)}, bf16[48,512]{1,0:T(8,128)(2,1)S(1)}, u32[]{:S(2)}, u32[]{:S(2)}) collective-permute-start(bf16[48,512]{1,0:T(8,128)(2,1)} %get-tuple-element.79), channel_id=1, source_target_pairs={{0,16},{4,20},{8,24},{12,28},{16,0},{20,4},{24,8},{28,12},{1,17},{... | collective-permute-start | bytes 147464 | tf_op jit(solution)/shard_map/ppermute | solution.py:15
  6.6 1.3 %collective-permute-start.7 = (bf16[48,512]{1,0:T(8,128)(2,1)}, bf16[48,512]{1,0:T(8,128)(2,1)S(1)}, u32[]{:S(2)}, u32[]{:S(2)}) collective-permute-start(bf16[48,512]{1,0:T(8,128)(2,1)} %get-tuple-element.80), channel_id=1, source_target_pairs={{0,24},{4,28},{8,16},{12,20},{16,8},{20,12},{24,0},{28,4},{1,25},{... | collective-permute-start | bytes 147464 | tf_op jit(solution)/shard_map/ppermute | solution.py:15
  8.0 0.2 collective-permute-start.8
  8.2 2.8 %collective-permute-start = (bf16[48,512]{1,0:T(8,128)(2,1)}, bf16[48,512]{1,0:T(8,128)(2,1)S(1)}, u32[]{:S(2)}, u32[]{:S(2)}) collective-permute-start(bf16[48,512]{1,0:T(8,128)(2,1)} %get-tuple-element.75), channel_id=1, source_target_pairs={{0,16},{4,20},{8,24},{12,28},{16,0},{20,4},{24,8},{28,12},{1,17},{... | collective-permute-start | bytes 147464 | tf_op jit(solution)/shard_map/ppermute | solution.py:15
  11.0 1.3 %collective-permute-start.1 = (bf16[48,512]{1,0:T(8,128)(2,1)}, bf16[48,512]{1,0:T(8,128)(2,1)S(1)}, u32[]{:S(2)}, u32[]{:S(2)}) collective-permute-start(bf16[48,512]{1,0:T(8,128)(2,1)} %get-tuple-element.76), channel_id=1, source_target_pairs={{0,24},{4,28},{8,16},{12,20},{16,8},{20,12},{24,0},{28,4},{1,25},{... | collective-permute-start | bytes 147464 | tf_op jit(solution)/shard_map/ppermute | solution.py:15
  12.4 0.9 %collective-permute-done.7.refs_1_ = bf16[48,512]{1,0:T(8,128)(2,1)S(1)} collective-permute-done((bf16[48,512]{1,0:T(8,128)(2,1)}, bf16[48,512]{1,0:T(8,128)(2,1)S(1)}, u32[]{:S(2)}, u32[]{:S(2)}) %collective-permute-start.7) | collective-permute-done | bytes 49184 | tf_op jit(solution)/shard_map/ppermute | solution.py:15
  13.4 2.5 %collective-permute-start.11 = (bf16[144,512]{1,0:T(8,128)(2,1)S(1)}, bf16[144,512]{1,0:T(8,128)(2,1)S(1)}, u32[]{:S(2)}, u32[]{:S(2)}) collective-permute-start(bf16[144,512]{1,0:T(8,128)(2,1)S(1)} %stack.3.refs_1_), channel_id=1, source_target_pairs={{0,3},{1,2},{2,1},{3,0},{4,7},{5,6},{6,5},{7,4},{8,11},{9,10},{10,... | collective-permute-start | bytes 442376 | tf_op jit(solution)/shard_map/ppermute | solution.py:15
  15.9 0.5 collective-permute-start.10
  16.4 0.6 collective-permute-start.9
  17.0 0.2 collective-permute-done.1.refs_1_
  17.2 2.5 %collective-permute-start.5 = (bf16[144,512]{1,0:T(8,128)(2,1)S(1)}, bf16[144,512]{1,0:T(8,128)(2,1)S(1)}, u32[]{:S(2)}, u32[]{:S(2)}) collective-permute-start(bf16[144,512]{1,0:T(8,128)(2,1)S(1)} %stack.2.refs_1_), channel_id=1, source_target_pairs={{0,3},{1,2},{2,1},{3,0},{4,7},{5,6},{6,5},{7,4},{8,11},{9,10},{10,... | collective-permute-start | bytes 442376 | tf_op jit(solution)/shard_map/ppermute | solution.py:15
  19.8 0.5 collective-permute-start.4
  20.3 0.3 stay.3.refs_0_
  20.6 0.3 load.2
  20.9 0.1 collective-permute-done.11.refs_4_
  21.1 0.9 %collective-permute-start.3 = (bf16[144,512]{1,0:T(8,128)(2,1)S(1)}, bf16[144,512]{1,0:T(8,128)(2,1)S(1)}, u32[]{:S(2)}, u32[]{:S(2)}) collective-permute-start(bf16[144,512]{1,0:T(8,128)(2,1)S(1)} %stack.2.refs_1_), channel_id=1, source_target_pairs={{0,1},{1,0},{2,3},{3,2},{4,5},{5,4},{6,7},{7,6},{8,9},{9,8},{10,11... | collective-permute-start | bytes 442376 | tf_op jit(solution)/shard_map/ppermute | solution.py:15
  21.9 3.5 %collective-permute-done.10.refs_3_ = bf16[144,512]{1,0:T(8,128)(2,1)S(1)} collective-permute-done((bf16[144,512]{1,0:T(8,128)(2,1)S(1)}, bf16[144,512]{1,0:T(8,128)(2,1)S(1)}, u32[]{:S(2)}, u32[]{:S(2)}) %collective-permute-start.10) | collective-permute-done | bytes 147488 | tf_op jit(solution)/shard_map/ppermute | solution.py:15
  25.6 0.9 %forward_t.2 = (bf16[1,4,192,256]{3,2,1,0:T(8,128)(2,1)S(1)}, bf16[192,512]{1,0:T(8,128)(2,1)S(1)}) custom-call(bf16[192,2048]{1,0:T(8,128)(2,1)S(1)} %join.2.refs_0_, bf16[2048,512]{1,0:T(8,128)(2,1)S(1)} %get-tuple-element.84.refs_1_, bf16[512,2048]{1,0:T(8,128)(2,1)S(1)} %get-tuple-element.89.refs_2_), custom_call_target="tpu_custom_call" | custom-call | flops 9663676416 | tf_op jit(solution)/shard_map/forward_t/pallas_call | solution.py:172
  26.6 0.6 collective-permute-start.13
  27.2 0.7 collective-permute-done.12.refs_0_
  27.9 0.9 %forward_t.3 = (bf16[1,4,192,256]{3,2,1,0:T(8,128)(2,1)S(1)}, bf16[192,512]{1,0:T(8,128)(2,1)S(1)}) custom-call(bf16[192,2048]{1,0:T(8,128)(2,1)S(1)} %collective-permute-done.12.refs_0_, bf16[2048,512]{1,0:T(8,128)(2,1)S(1)} %get-tuple-element.84.refs_1_, bf16[512,2048]{1,0:T(8,128)(2,1)S(1)} %get-tuple-element.89.refs_2_), custom_call_target="tpu_custom_call" | custom-call | tf_op jit(solution)/shard_map/forward_t/pallas_call | solution.py:172
  28.8 0.2 collective-permute-start.14
  29.0 0.3 stay.2.refs_0_
  29.4 0.3 load.3
  29.7 0.6 keep_t.1
  30.4 0.2 collective-permute-done.14.refs_4_
  30.6 0.2 pair.2
  30.9 0.2 collective-permute-start.15
  31.1 0.9 %collective-permute-start.21 = (bf16[384,256]{1,0:T(8,128)(2,1)S(1)}, bf16[384,256]{1,0:T(8,128)(2,1)S(1)}, u32[]{:S(2)}, u32[]{:S(2)}) collective-permute-start(bf16[384,256]{1,0:T(8,128)(2,1)S(1)} %get-tuple-element.115), channel_id=1, source_target_pairs={{0,1},{1,0},{2,3},{3,2},{4,5},{5,4},{6,7},{7,6},{8,9},{9,8},{10,11... | collective-permute-start | bytes 589832 | tf_op jit(solution)/shard_map/ppermute | solution.py:15
  32.0 2.5 %collective-permute-start.23 = (bf16[384,256]{1,0:T(8,128)(2,1)S(1)}, bf16[384,256]{1,0:T(8,128)(2,1)S(1)}, u32[]{:S(2)}, u32[]{:S(2)}) collective-permute-start(bf16[384,256]{1,0:T(8,128)(2,1)S(1)} %get-tuple-element.117), channel_id=1, source_target_pairs={{0,3},{1,2},{2,1},{3,0},{4,7},{5,6},{6,5},{7,4},{8,11},{9,10},{10,... | collective-permute-start | bytes 589832 | tf_op jit(solution)/shard_map/ppermute | solution.py:15
  34.6 1.7 %forward_s.1 = (bf16[2,4,192,256]{3,2,1,0:T(8,128)(2,1)S(1)}, bf16[192,512]{1,0:T(8,128)(2,1)S(1)}, bf16[192,512]{1,0:T(8,128)(2,1)S(1)}, f32[192,512]{1,0:T(8,128)S(1)}, f32[192,512]{1,0:T(8,128)S(1)}) custom-call(bf16[192,2048]{1,0:T(8,128)(2,1)S(1)} %join.3.refs_0_.refs_5_, bf16[192,2048]{1,0:T(8,128)(2,1)S(1)} %collective-permute-done.15.refs_1_.refs_6_, ...), custom_call_target="tpu_custom_call" | custom-call | tf_op jit(solution)/shard_map/forward_s/pallas_call | solution.py:172
  36.4 1.4 %keep_s.1 = (bf16[4,192,256]{2,1,0:T(8,128)(2,1)S(1)}, bf16[4,192,256]{2,1,0:T(8,128)(2,1)S(1)}, bf16[2048,384]{1,0:T(8,128)(2,1)S(1)}, bf16[512,384]{1,0:T(8,128)(2,1)S(1)}, f32[384,512]{1,0:T(8,128)S(1)}) custom-call(bf16[192,512]{1,0:T(8,128)(2,1)S(1)} %get-tuple-element.104.refs_0_, bf16[192,512]{1,0:T(8,128)(2,1)S(1)} %get-tuple-element.105.refs_1_, ...), custom_call_target="tpu_custom_call" | custom-call | flops 25769803776 | tf_op jit(solution)/shard_map/keep_s/pallas_call | solution.py:172
  37.8 0.9 %collective-permute-done.16.refs_2_ = bf16[2,4,192,256]{3,2,1,0:T(8,128)(2,1)S(1)} collective-permute-done((bf16[2,4,192,256]{3,2,1,0:T(8,128)(2,1)S(1)}, bf16[2,4,192,256]{3,2,1,0:T(8,128)(2,1)S(1)}, u32[]{:S(2)}, u32[]{:S(2)}) %collective-permute-start.16) | collective-permute-done | bytes 786464 | tf_op jit(solution)/shard_map/ppermute | solution.py:15
  38.7 0.2 pair.3
  38.8 1.0 %collective-permute-start.17 = (bf16[384,256]{1,0:T(8,128)(2,1)S(1)}, bf16[384,256]{1,0:T(8,128)(2,1)S(1)}, u32[]{:S(2)}, u32[]{:S(2)}) collective-permute-start(bf16[384,256]{1,0:T(8,128)(2,1)S(1)} %get-tuple-element.112), channel_id=1, source_target_pairs={{0,1},{1,0},{2,3},{3,2},{4,5},{5,4},{6,7},{7,6},{8,9},{9,8},{10,11... | collective-permute-start | bytes 589832 | tf_op jit(solution)/shard_map/ppermute | solution.py:15
  39.8 1.1 %collective-permute-done.20.refs_1_ = s32[2,128]{1,0:T(2,128)S(1)} collective-permute-done((s32[2,128]{1,0:T(2,128)S(1)}, s32[2,128]{1,0:T(2,128)S(1)}, u32[]{:S(2)}, u32[]{:S(2)}) %collective-permute-start.20) | collective-permute-done | bytes 1056 | tf_op jit(solution)/shard_map/ppermute | solution.py:15
  40.9 0.4 maps.1.refs_0_
  41.3 1.4 %collective-permute-done.22.refs_2_ = bf16[384,256]{1,0:T(8,128)(2,1)S(1)} collective-permute-done((bf16[384,256]{1,0:T(8,128)(2,1)S(1)}, bf16[384,256]{1,0:T(8,128)(2,1)S(1)}, u32[]{:S(2)}, u32[]{:S(2)}) %collective-permute-start.22) | collective-permute-done | bytes 196640 | tf_op jit(solution)/shard_map/ppermute | solution.py:15
  42.7 0.7 collective-permute-done.23.refs_3_
  43.5 3.0 %collective-permute-start.24 = (bf16[96,256]{1,0:T(8,128)(2,1)S(1)}, bf16[96,256]{1,0:T(8,128)(2,1)S(1)}, u32[]{:S(2)}, u32[]{:S(2)}) collective-permute-start(bf16[96,256]{1,0:T(8,128)(2,1)S(1)} %get-tuple-element.122), channel_id=1, source_target_pairs={{0,16},{4,20},{8,24},{12,28},{16,0},{20,4},{24,8},{28,12},{1,17},{... | collective-permute-start | bytes 147464 | tf_op jit(solution)/shard_map/ppermute | solution.py:15
  46.5 0.5 collective-permute-start.25
  47.0 0.9 %collective-permute-start.26 = (bf16[96,256]{1,0:T(8,128)(2,1)S(1)}, bf16[96,256]{1,0:T(8,128)(2,1)S(1)}, u32[]{:S(2)}, u32[]{:S(2)}) collective-permute-start(bf16[96,256]{1,0:T(8,128)(2,1)S(1)} %get-tuple-element.125), channel_id=1, source_target_pairs={{0,8},{4,12},{8,0},{12,4},{16,24},{20,28},{24,16},{28,20},{1,9},{5... | collective-permute-start | bytes 147464 | tf_op jit(solution)/shard_map/ppermute | solution.py:15
  47.9 0.8 %collective-permute-start.18 = (bf16[384,256]{1,0:T(8,128)(2,1)S(1)}, bf16[384,256]{1,0:T(8,128)(2,1)S(1)}, u32[]{:S(2)}, u32[]{:S(2)}) collective-permute-start(bf16[384,256]{1,0:T(8,128)(2,1)S(1)} %get-tuple-element.113), channel_id=1, source_target_pairs={{0,2},{1,3},{2,0},{3,1},{4,6},{5,7},{6,4},{7,5},{8,10},{9,11},{10,... | collective-permute-start | bytes 589832 | tf_op jit(solution)/shard_map/ppermute | solution.py:15
  48.7 1.4 %collective-permute-start.19 = (bf16[384,256]{1,0:T(8,128)(2,1)S(1)}, bf16[384,256]{1,0:T(8,128)(2,1)S(1)}, u32[]{:S(2)}, u32[]{:S(2)}) collective-permute-start(bf16[384,256]{1,0:T(8,128)(2,1)S(1)} %get-tuple-element.114), channel_id=1, source_target_pairs={{0,3},{1,2},{2,1},{3,0},{4,7},{5,6},{6,5},{7,4},{8,11},{9,10},{10,... | collective-permute-start | bytes 589832 | tf_op jit(solution)/shard_map/ppermute | solution.py:15
  50.1 2.3 %collective-permute-done.25.refs_2_ = bf16[96,256]{1,0:T(8,128)(2,1)S(1)} collective-permute-done((bf16[96,256]{1,0:T(8,128)(2,1)S(1)}, bf16[96,256]{1,0:T(8,128)(2,1)S(1)}, u32[]{:S(2)}, u32[]{:S(2)}) %collective-permute-start.25) | collective-permute-done | bytes 49184 | tf_op jit(solution)/shard_map/ppermute | solution.py:15
  52.4 0.2 home.1
  52.6 1.1 %collective-permute-start.27 = (bf16[96,256]{1,0:T(8,128)(2,1)S(1)}, bf16[96,256]{1,0:T(8,128)(2,1)S(1)}, u32[]{:S(2)}, u32[]{:S(2)}) collective-permute-start(bf16[96,256]{1,0:T(8,128)(2,1)S(1)} %get-tuple-element.127), channel_id=1, source_target_pairs={{0,16},{4,20},{8,24},{12,28},{16,0},{20,4},{24,8},{28,12},{1,17},{... | collective-permute-start | bytes 147464 | tf_op jit(solution)/shard_map/ppermute | solution.py:15
  53.8 1.0 %collective-permute-start.28 = (bf16[96,256]{1,0:T(8,128)(2,1)S(1)}, bf16[96,256]{1,0:T(8,128)(2,1)S(1)}, u32[]{:S(2)}, u32[]{:S(2)}) collective-permute-start(bf16[96,256]{1,0:T(8,128)(2,1)S(1)} %get-tuple-element.128), channel_id=1, source_target_pairs={{0,24},{4,28},{8,16},{12,20},{16,8},{20,12},{24,0},{28,4},{1,25},{... | collective-permute-start | bytes 147464 | tf_op jit(solution)/shard_map/ppermute | solution.py:15
  54.8 1.4 %collective-permute-start.29 = (bf16[96,256]{1,0:T(8,128)(2,1)S(1)}, bf16[96,256]{1,0:T(8,128)(2,1)S(1)}, u32[]{:S(2)}, u32[]{:S(2)}) collective-permute-start(bf16[96,256]{1,0:T(8,128)(2,1)S(1)} %get-tuple-element.129), channel_id=1, source_target_pairs={{0,8},{4,12},{8,0},{12,4},{16,24},{20,28},{24,16},{28,20},{1,9},{5... | collective-permute-start | bytes 147464 | tf_op jit(solution)/shard_map/ppermute | solution.py:15
  56.2 2.0 %collective-permute-done.18.refs_2_ = bf16[384,256]{1,0:T(8,128)(2,1)S(1)} collective-permute-done((bf16[384,256]{1,0:T(8,128)(2,1)S(1)}, bf16[384,256]{1,0:T(8,128)(2,1)S(1)}, u32[]{:S(2)}, u32[]{:S(2)}) %collective-permute-start.18) | collective-permute-done | bytes 196640 | tf_op jit(solution)/shard_map/ppermute | solution.py:15
  58.2 1.5 %collective-permute-done.28.refs_5_ = bf16[96,256]{1,0:T(8,128)(2,1)S(1)} collective-permute-done((bf16[96,256]{1,0:T(8,128)(2,1)S(1)}, bf16[96,256]{1,0:T(8,128)(2,1)S(1)}, u32[]{:S(2)}, u32[]{:S(2)}) %collective-permute-start.28) | collective-permute-done | bytes 49184 | tf_op jit(solution)/shard_map/ppermute | solution.py:15
  59.7 0.1 shard_map.96.refs_0_
  59.9 1.5 %collective-permute-start.32 = (bf16[384,256]{1,0:T(8,128)(2,1)S(1)}, bf16[384,256]{1,0:T(8,128)(2,1)S(1)}, u32[]{:S(2)}, u32[]{:S(2)}) collective-permute-start(bf16[384,256]{1,0:T(8,128)(2,1)S(1)} %shard_map.96.refs_0_), channel_id=1, source_target_pairs={{0,3},{1,2},{2,1},{3,0},{4,7},{5,6},{6,5},{7,4},{8,11},{9,10},{10,... | collective-permute-start | bytes 589832 | tf_op jit(solution)/shard_map/ppermute | solution.py:15
  61.4 1.2 %collective-permute-start.31 = (bf16[384,256]{1,0:T(8,128)(2,1)S(1)}, bf16[384,256]{1,0:T(8,128)(2,1)S(1)}, u32[]{:S(2)}, u32[]{:S(2)}) collective-permute-start(bf16[384,256]{1,0:T(8,128)(2,1)S(1)} %shard_map.96.refs_0_), channel_id=1, source_target_pairs={{0,2},{1,3},{2,0},{3,1},{4,6},{5,7},{6,4},{7,5},{8,10},{9,11},{10,... | collective-permute-start | bytes 589832 | tf_op jit(solution)/shard_map/ppermute | solution.py:15
  62.5 0.9 %collective-permute-start.30 = (bf16[384,256]{1,0:T(8,128)(2,1)S(1)}, bf16[384,256]{1,0:T(8,128)(2,1)S(1)}, u32[]{:S(2)}, u32[]{:S(2)}) collective-permute-start(bf16[384,256]{1,0:T(8,128)(2,1)S(1)} %shard_map.96.refs_0_), channel_id=1, source_target_pairs={{0,1},{1,0},{2,3},{3,2},{4,5},{5,4},{6,7},{7,6},{8,9},{9,8},{10,11... | collective-permute-start | bytes 589832 | tf_op jit(solution)/shard_map/ppermute | solution.py:15
  63.4 0.6 early.3
  64.1 4.5 %collective-permute-done.32.refs_0_ = bf16[384,256]{1,0:T(8,128)(2,1)S(1)} collective-permute-done((bf16[384,256]{1,0:T(8,128)(2,1)S(1)}, bf16[384,256]{1,0:T(8,128)(2,1)S(1)}, u32[]{:S(2)}, u32[]{:S(2)}) %collective-permute-start.32) | collective-permute-done | bytes 196640 | tf_op jit(solution)/shard_map/ppermute | solution.py:15
  68.6 0.4 early.4
  69.0 3.3 %collective-permute-done.31.refs_1_ = bf16[384,256]{1,0:T(8,128)(2,1)S(1)} collective-permute-done((bf16[384,256]{1,0:T(8,128)(2,1)S(1)}, bf16[384,256]{1,0:T(8,128)(2,1)S(1)}, u32[]{:S(2)}, u32[]{:S(2)}) %collective-permute-start.31) | collective-permute-done | bytes 196640 | tf_op jit(solution)/shard_map/ppermute | solution.py:15
  72.3 0.5 collective-permute-start.35
  72.8 0.9 %early.5 = (f32[384,512]{1,0:T(8,128)S(1)}, bf16[512,256]{1,0:T(8,128)(2,1)S(1)}, bf16[512,256]{1,0:T(8,128)(2,1)S(1)}, bf16[512,256]{1,0:T(8,128)(2,1)S(1)}) custom-call(bf16[384,256]{1,0:T(8,128)(2,1)S(1)} %collective-permute-done.30.refs_0_, bf16[384,256]{1,0:T(8,128)(2,1)S(1)} %collective-permute-done.31.refs_1_, ...), custom_call_target="tpu_custom_call" | custom-call | tf_op jit(solution)/shard_map/early/pallas_call | solution.py:172
  73.7 0.3 collective-permute-done.35.refs_1_
  74.0 2.8 %last.1 = (bf16[2048,512]{1,0:T(8,128)(2,1)}, bf16[512,2048]{1,0:T(8,128)(2,1)}) custom-call(bf16[384,256]{1,0:T(8,128)(2,1)S(1)} %collective-permute-done.34.refs_0_, bf16[384,256]{1,0:T(8,128)(2,1)S(1)} %collective-permute-done.35.refs_1_, bf16[512,256]{1,0:T(8,128)(2,1)S(1)} %get-tuple-element.137.refs_2_, ...), custom_call_target="tpu_custom_call" | custom-call | tf_op jit(solution)/shard_map/last/pallas_call | solution.py:172
  (52 shorter events, 0.7 us)
Async XLA Ops:
  2.5 9.8 %collective-permute-start.6 = (bf16[48,512]{1,0:T(8,128)(2,1)}, bf16[48,512]{1,0:T(8,128)(2,1)S(1)}, u32[]{:S(2)}, u32[]{:S(2)}) collective-permute-start(bf16[48,512]{1,0:T(8,128)(2,1)} %get-tuple-element.79), channel_id=1, source_target_pairs={{0,16},{4,20},{8,24},{12,28},{16,0},{20,4},{24,8},{28,12},{1,17},{... | collective-permute-start | bytes 147464 | tf_op jit(solution)/shard_map/ppermute | solution.py:15
  6.6 6.7 %collective-permute-start.7 = (bf16[48,512]{1,0:T(8,128)(2,1)}, bf16[48,512]{1,0:T(8,128)(2,1)S(1)}, u32[]{:S(2)}, u32[]{:S(2)}) collective-permute-start(bf16[48,512]{1,0:T(8,128)(2,1)} %get-tuple-element.80), channel_id=1, source_target_pairs={{0,24},{4,28},{8,16},{12,20},{16,8},{20,12},{24,0},{28,4},{1,25},{... | collective-permute-start | bytes 147464 | tf_op jit(solution)/shard_map/ppermute | solution.py:15
  8.0 5.3 %collective-permute-start.8 = (bf16[48,512]{1,0:T(8,128)(2,1)}, bf16[48,512]{1,0:T(8,128)(2,1)S(1)}, u32[]{:S(2)}, u32[]{:S(2)}) collective-permute-start(bf16[48,512]{1,0:T(8,128)(2,1)} %get-tuple-element.81), channel_id=1, source_target_pairs={{0,8},{4,12},{8,0},{12,4},{16,24},{20,28},{24,16},{28,20},{1,9},{5... | collective-permute-start | bytes 147464 | tf_op jit(solution)/shard_map/ppermute | solution.py:15
  8.2 8.2 %collective-permute-start = (bf16[48,512]{1,0:T(8,128)(2,1)}, bf16[48,512]{1,0:T(8,128)(2,1)S(1)}, u32[]{:S(2)}, u32[]{:S(2)}) collective-permute-start(bf16[48,512]{1,0:T(8,128)(2,1)} %get-tuple-element.75), channel_id=1, source_target_pairs={{0,16},{4,20},{8,24},{12,28},{16,0},{20,4},{24,8},{28,12},{1,17},{... | collective-permute-start | bytes 147464 | tf_op jit(solution)/shard_map/ppermute | solution.py:15
  11.0 6.2 %collective-permute-start.1 = (bf16[48,512]{1,0:T(8,128)(2,1)}, bf16[48,512]{1,0:T(8,128)(2,1)S(1)}, u32[]{:S(2)}, u32[]{:S(2)}) collective-permute-start(bf16[48,512]{1,0:T(8,128)(2,1)} %get-tuple-element.76), channel_id=1, source_target_pairs={{0,24},{4,28},{8,16},{12,20},{16,8},{20,12},{24,0},{28,4},{1,25},{... | collective-permute-start | bytes 147464 | tf_op jit(solution)/shard_map/ppermute | solution.py:15
  12.4 4.8 %collective-permute-start.2 = (bf16[48,512]{1,0:T(8,128)(2,1)}, bf16[48,512]{1,0:T(8,128)(2,1)S(1)}, u32[]{:S(2)}, u32[]{:S(2)}) collective-permute-start(bf16[48,512]{1,0:T(8,128)(2,1)} %get-tuple-element.77), channel_id=1, source_target_pairs={{0,8},{4,12},{8,0},{12,4},{16,24},{20,28},{24,16},{28,20},{1,9},{5... | collective-permute-start | bytes 147464 | tf_op jit(solution)/shard_map/ppermute | solution.py:15
  13.4 6.9 %copy-start = (bf16[128,2048]{1,0:T(8,128)(2,1)S(1)}, bf16[128,2048]{1,0:T(8,128)(2,1)}, u32[]{:S(2)}) copy-start(bf16[128,2048]{1,0:T(8,128)(2,1)} %refs_0_.4) | copy-start | bytes 1572868
  13.4 6.9 %copy-start.7 = (s32[128,1]{0,1:T(1,128)S(1)}, s32[128,1]{0,1:T(1,128)}, u32[]{:S(2)}) copy-start(s32[128,1]{0,1:T(1,128)} %param.10) | copy-start | bytes 1540
  13.4 7.7 %collective-permute-start.11 = (bf16[144,512]{1,0:T(8,128)(2,1)S(1)}, bf16[144,512]{1,0:T(8,128)(2,1)S(1)}, u32[]{:S(2)}, u32[]{:S(2)}) collective-permute-start(bf16[144,512]{1,0:T(8,128)(2,1)S(1)} %stack.3.refs_1_), channel_id=1, source_target_pairs={{0,3},{1,2},{2,1},{3,0},{4,7},{5,6},{6,5},{7,4},{8,11},{9,10},{10,... | collective-permute-start | bytes 442376 | tf_op jit(solution)/shard_map/ppermute | solution.py:15
  15.9 9.6 %collective-permute-start.10 = (bf16[144,512]{1,0:T(8,128)(2,1)S(1)}, bf16[144,512]{1,0:T(8,128)(2,1)S(1)}, u32[]{:S(2)}, u32[]{:S(2)}) collective-permute-start(bf16[144,512]{1,0:T(8,128)(2,1)S(1)} %stack.3.refs_1_), channel_id=1, source_target_pairs={{0,2},{1,3},{2,0},{3,1},{4,6},{5,7},{6,4},{7,5},{8,10},{9,11},{10,... | collective-permute-start | bytes 442376 | tf_op jit(solution)/shard_map/ppermute | solution.py:15
  16.4 9.1 %collective-permute-start.9 = (bf16[144,512]{1,0:T(8,128)(2,1)S(1)}, bf16[144,512]{1,0:T(8,128)(2,1)S(1)}, u32[]{:S(2)}, u32[]{:S(2)}) collective-permute-start(bf16[144,512]{1,0:T(8,128)(2,1)S(1)} %stack.3.refs_1_), channel_id=1, source_target_pairs={{0,1},{1,0},{2,3},{3,2},{4,5},{5,4},{6,7},{7,6},{8,9},{9,8},{10,11... | collective-permute-start | bytes 442376 | tf_op jit(solution)/shard_map/ppermute | solution.py:15
  17.2 3.4 %copy-start.2 = (bf16[1,2048,512]{2,1,0:T(8,128)(2,1)S(1)}, bf16[1,2048,512]{2,1,0:T(8,128)(2,1)}, u32[]{:S(2)}) copy-start(bf16[1,2048,512]{2,1,0:T(8,128)(2,1)} %param.12) | copy-start | bytes 6291460
  17.2 3.4 %copy-start.3 = (bf16[1,512,2048]{2,1,0:T(8,128)(2,1)S(1)}, bf16[1,512,2048]{2,1,0:T(8,128)(2,1)}, u32[]{:S(2)}) copy-start(bf16[1,512,2048]{2,1,0:T(8,128)(2,1)} %param.13) | copy-start | bytes 6291460
  17.2 13.1 %collective-permute-start.5 = (bf16[144,512]{1,0:T(8,128)(2,1)S(1)}, bf16[144,512]{1,0:T(8,128)(2,1)S(1)}, u32[]{:S(2)}, u32[]{:S(2)}) collective-permute-start(bf16[144,512]{1,0:T(8,128)(2,1)S(1)} %stack.2.refs_1_), channel_id=1, source_target_pairs={{0,3},{1,2},{2,1},{3,0},{4,7},{5,6},{6,5},{7,4},{8,11},{9,10},{10,... | collective-permute-start | bytes 442376 | tf_op jit(solution)/shard_map/ppermute | solution.py:15
  19.8 10.6 %collective-permute-start.4 = (bf16[144,512]{1,0:T(8,128)(2,1)S(1)}, bf16[144,512]{1,0:T(8,128)(2,1)S(1)}, u32[]{:S(2)}, u32[]{:S(2)}) collective-permute-start(bf16[144,512]{1,0:T(8,128)(2,1)S(1)} %stack.2.refs_1_), channel_id=1, source_target_pairs={{0,2},{1,3},{2,0},{3,1},{4,6},{5,7},{6,4},{7,5},{8,10},{9,11},{10,... | collective-permute-start | bytes 442376 | tf_op jit(solution)/shard_map/ppermute | solution.py:15
  21.1 9.3 %collective-permute-start.3 = (bf16[144,512]{1,0:T(8,128)(2,1)S(1)}, bf16[144,512]{1,0:T(8,128)(2,1)S(1)}, u32[]{:S(2)}, u32[]{:S(2)}) collective-permute-start(bf16[144,512]{1,0:T(8,128)(2,1)S(1)} %stack.2.refs_1_), channel_id=1, source_target_pairs={{0,1},{1,0},{2,3},{3,2},{4,5},{5,4},{6,7},{7,6},{8,9},{9,8},{10,11... | collective-permute-start | bytes 442376 | tf_op jit(solution)/shard_map/ppermute | solution.py:15
  25.5 2.4 %collective-permute-start.12 = (bf16[192,2048]{1,0:T(8,128)(2,1)S(1)}, bf16[192,2048]{1,0:T(8,128)(2,1)S(1)}, u32[]{:S(2)}, u32[]{:S(2)}) collective-permute-start(bf16[192,2048]{1,0:T(8,128)(2,1)S(1)} %join.2.refs_0_), channel_id=1, source_target_pairs={{0,4},{4,0},{8,12},{12,8},{16,20},{20,16},{24,28},{28,24},{1,5},{5... | collective-permute-start | bytes 2359304 | tf_op jit(solution)/shard_map/ppermute | solution.py:15
  26.5 2.5 %copy-start.1 = (bf16[128,2048]{1,0:T(8,128)(2,1)S(1)}, bf16[128,2048]{1,0:T(8,128)(2,1)}, u32[]{:S(2)}) copy-start(bf16[128,2048]{1,0:T(8,128)(2,1)} %refs_1_.1) | copy-start | bytes 1572868
  26.6 2.5 %copy-start.6 = (s32[128,1]{0,1:T(1,128)S(1)}, s32[128,1]{0,1:T(1,128)}, u32[]{:S(2)}) copy-start(s32[128,1]{0,1:T(1,128)} %param.11) | copy-start | bytes 1540
  26.6 2.8 %copy-start.4 = (bf16[1,2048,512]{2,1,0:T(8,128)(2,1)S(1)}, bf16[1,2048,512]{2,1,0:T(8,128)(2,1)}, u32[]{:S(2)}) copy-start(bf16[1,2048,512]{2,1,0:T(8,128)(2,1)} %param.14) | copy-start | bytes 6291460
  26.6 2.8 %copy-start.5 = (bf16[1,512,2048]{2,1,0:T(8,128)(2,1)S(1)}, bf16[1,512,2048]{2,1,0:T(8,128)(2,1)}, u32[]{:S(2)}) copy-start(bf16[1,512,2048]{2,1,0:T(8,128)(2,1)} %param.15) | copy-start | bytes 6291460
  26.6 3.8 %collective-permute-start.13 = (bf16[1,4,192,256]{3,2,1,0:T(8,128)(2,1)S(1)}, bf16[1,4,192,256]{3,2,1,0:T(8,128)(2,1)S(1)}, u32[]{:S(2)}, u32[]{:S(2)}) collective-permute-start(bf16[1,4,192,256]{3,2,1,0:T(8,128)(2,1)S(1)} %get-tuple-element.96), channel_id=1, source_target_pairs={{0,4},{4,0},{8,12},{12,8},{16,20},{20,16},{24,28},{28,24},{1,5},{5... | collective-permute-start | bytes 1179656 | tf_op jit(solution)/shard_map/ppermute | solution.py:15
  28.8 1.8 %collective-permute-start.14 = (bf16[1,4,192,256]{3,2,1,0:T(8,128)(2,1)S(1)}, bf16[1,4,192,256]{3,2,1,0:T(8,128)(2,1)S(1)}, u32[]{:S(2)}, u32[]{:S(2)}) collective-permute-start(bf16[1,4,192,256]{3,2,1,0:T(8,128)(2,1)S(1)} %get-tuple-element.97), channel_id=1, source_target_pairs={{0,4},{4,0},{8,12},{12,8},{16,20},{20,16},{24,28},{28,24},{1,5},{5... | collective-permute-start | bytes 1179656 | tf_op jit(solution)/shard_map/ppermute | solution.py:15
  30.9 3.7 %collective-permute-start.15 = (bf16[192,2048]{1,0:T(8,128)(2,1)S(1)}, bf16[192,2048]{1,0:T(8,128)(2,1)S(1)}, u32[]{:S(2)}, u32[]{:S(2)}) collective-permute-start(bf16[192,2048]{1,0:T(8,128)(2,1)S(1)} %join.3.refs_0_.refs_5_), channel_id=1, source_target_pairs={{0,4},{4,0},{8,12},{12,8},{16,20},{20,16},{24,28},{28,24},{1,5},{5... | collective-permute-start | bytes 2359304 | tf_op jit(solution)/shard_map/ppermute | solution.py:15
  31.1 10.2 %collective-permute-start.21 = (bf16[384,256]{1,0:T(8,128)(2,1)S(1)}, bf16[384,256]{1,0:T(8,128)(2,1)S(1)}, u32[]{:S(2)}, u32[]{:S(2)}) collective-permute-start(bf16[384,256]{1,0:T(8,128)(2,1)S(1)} %get-tuple-element.115), channel_id=1, source_target_pairs={{0,1},{1,0},{2,3},{3,2},{4,5},{5,4},{6,7},{7,6},{8,9},{9,8},{10,11... | collective-permute-start | bytes 589832 | tf_op jit(solution)/shard_map/ppermute | solution.py:15
  32.0 10.7 %collective-permute-start.22 = (bf16[384,256]{1,0:T(8,128)(2,1)S(1)}, bf16[384,256]{1,0:T(8,128)(2,1)S(1)}, u32[]{:S(2)}, u32[]{:S(2)}) collective-permute-start(bf16[384,256]{1,0:T(8,128)(2,1)S(1)} %get-tuple-element.116), channel_id=1, source_target_pairs={{0,2},{1,3},{2,0},{3,1},{4,6},{5,7},{6,4},{7,5},{8,10},{9,11},{10,... | collective-permute-start | bytes 589832 | tf_op jit(solution)/shard_map/ppermute | solution.py:15
  32.0 11.4 %collective-permute-start.23 = (bf16[384,256]{1,0:T(8,128)(2,1)S(1)}, bf16[384,256]{1,0:T(8,128)(2,1)S(1)}, u32[]{:S(2)}, u32[]{:S(2)}) collective-permute-start(bf16[384,256]{1,0:T(8,128)(2,1)S(1)} %get-tuple-element.117), channel_id=1, source_target_pairs={{0,3},{1,2},{2,1},{3,0},{4,7},{5,6},{6,5},{7,4},{8,11},{9,10},{10,... | collective-permute-start | bytes 589832 | tf_op jit(solution)/shard_map/ppermute | solution.py:15
  36.3 2.4 %collective-permute-start.16 = (bf16[2,4,192,256]{3,2,1,0:T(8,128)(2,1)S(1)}, bf16[2,4,192,256]{3,2,1,0:T(8,128)(2,1)S(1)}, u32[]{:S(2)}, u32[]{:S(2)}) collective-permute-start(bf16[2,4,192,256]{3,2,1,0:T(8,128)(2,1)S(1)} %get-tuple-element.110), channel_id=1, source_target_pairs={{0,4},{4,0},{8,12},{12,8},{16,20},{20,16},{24,28},{28,24},{1,5},{5... | collective-permute-start | bytes 2359304 | tf_op jit(solution)/shard_map/ppermute | solution.py:15
  38.8 8.2 %collective-permute-start.17 = (bf16[384,256]{1,0:T(8,128)(2,1)S(1)}, bf16[384,256]{1,0:T(8,128)(2,1)S(1)}, u32[]{:S(2)}, u32[]{:S(2)}) collective-permute-start(bf16[384,256]{1,0:T(8,128)(2,1)S(1)} %get-tuple-element.112), channel_id=1, source_target_pairs={{0,1},{1,0},{2,3},{3,2},{4,5},{5,4},{6,7},{7,6},{8,9},{9,8},{10,11... | collective-permute-start | bytes 589832 | tf_op jit(solution)/shard_map/ppermute | solution.py:15
  39.8 1.1 %collective-permute-start.20 = (s32[2,128]{1,0:T(2,128)S(1)}, s32[2,128]{1,0:T(2,128)S(1)}, u32[]{:S(2)}, u32[]{:S(2)}) collective-permute-start(s32[2,128]{1,0:T(2,128)S(1)} %pad_add_fusion.refs_0_), channel_id=1, source_target_pairs={{0,4},{4,0},{8,12},{12,8},{16,20},{20,16},{24,28},{28,24},{1,5},{5... | collective-permute-start | bytes 3080 | tf_op jit(solution)/shard_map/ppermute | solution.py:15
  43.5 6.6 %collective-permute-start.24 = (bf16[96,256]{1,0:T(8,128)(2,1)S(1)}, bf16[96,256]{1,0:T(8,128)(2,1)S(1)}, u32[]{:S(2)}, u32[]{:S(2)}) collective-permute-start(bf16[96,256]{1,0:T(8,128)(2,1)S(1)} %get-tuple-element.122), channel_id=1, source_target_pairs={{0,16},{4,20},{8,24},{12,28},{16,0},{20,4},{24,8},{28,12},{1,17},{... | collective-permute-start | bytes 147464 | tf_op jit(solution)/shard_map/ppermute | solution.py:15
  46.5 5.9 %collective-permute-start.25 = (bf16[96,256]{1,0:T(8,128)(2,1)S(1)}, bf16[96,256]{1,0:T(8,128)(2,1)S(1)}, u32[]{:S(2)}, u32[]{:S(2)}) collective-permute-start(bf16[96,256]{1,0:T(8,128)(2,1)S(1)} %get-tuple-element.123), channel_id=1, source_target_pairs={{0,24},{4,28},{8,16},{12,20},{16,8},{20,12},{24,0},{28,4},{1,25},{... | collective-permute-start | bytes 147464 | tf_op jit(solution)/shard_map/ppermute | solution.py:15
  47.0 5.4 %collective-permute-start.26 = (bf16[96,256]{1,0:T(8,128)(2,1)S(1)}, bf16[96,256]{1,0:T(8,128)(2,1)S(1)}, u32[]{:S(2)}, u32[]{:S(2)}) collective-permute-start(bf16[96,256]{1,0:T(8,128)(2,1)S(1)} %get-tuple-element.125), channel_id=1, source_target_pairs={{0,8},{4,12},{8,0},{12,4},{16,24},{20,28},{24,16},{28,20},{1,9},{5... | collective-permute-start | bytes 147464 | tf_op jit(solution)/shard_map/ppermute | solution.py:15
  47.9 10.3 %collective-permute-start.18 = (bf16[384,256]{1,0:T(8,128)(2,1)S(1)}, bf16[384,256]{1,0:T(8,128)(2,1)S(1)}, u32[]{:S(2)}, u32[]{:S(2)}) collective-permute-start(bf16[384,256]{1,0:T(8,128)(2,1)S(1)} %get-tuple-element.113), channel_id=1, source_target_pairs={{0,2},{1,3},{2,0},{3,1},{4,6},{5,7},{6,4},{7,5},{8,10},{9,11},{10,... | collective-permute-start | bytes 589832 | tf_op jit(solution)/shard_map/ppermute | solution.py:15
  48.7 9.5 %collective-permute-start.19 = (bf16[384,256]{1,0:T(8,128)(2,1)S(1)}, bf16[384,256]{1,0:T(8,128)(2,1)S(1)}, u32[]{:S(2)}, u32[]{:S(2)}) collective-permute-start(bf16[384,256]{1,0:T(8,128)(2,1)S(1)} %get-tuple-element.114), channel_id=1, source_target_pairs={{0,3},{1,2},{2,1},{3,0},{4,7},{5,6},{6,5},{7,4},{8,11},{9,10},{10,... | collective-permute-start | bytes 589832 | tf_op jit(solution)/shard_map/ppermute | solution.py:15
  52.6 5.6 %collective-permute-start.27 = (bf16[96,256]{1,0:T(8,128)(2,1)S(1)}, bf16[96,256]{1,0:T(8,128)(2,1)S(1)}, u32[]{:S(2)}, u32[]{:S(2)}) collective-permute-start(bf16[96,256]{1,0:T(8,128)(2,1)S(1)} %get-tuple-element.127), channel_id=1, source_target_pairs={{0,16},{4,20},{8,24},{12,28},{16,0},{20,4},{24,8},{28,12},{1,17},{... | collective-permute-start | bytes 147464 | tf_op jit(solution)/shard_map/ppermute | solution.py:15
  53.8 5.9 %collective-permute-start.28 = (bf16[96,256]{1,0:T(8,128)(2,1)S(1)}, bf16[96,256]{1,0:T(8,128)(2,1)S(1)}, u32[]{:S(2)}, u32[]{:S(2)}) collective-permute-start(bf16[96,256]{1,0:T(8,128)(2,1)S(1)} %get-tuple-element.128), channel_id=1, source_target_pairs={{0,24},{4,28},{8,16},{12,20},{16,8},{20,12},{24,0},{28,4},{1,25},{... | collective-permute-start | bytes 147464 | tf_op jit(solution)/shard_map/ppermute | solution.py:15
  54.8 4.9 %collective-permute-start.29 = (bf16[96,256]{1,0:T(8,128)(2,1)S(1)}, bf16[96,256]{1,0:T(8,128)(2,1)S(1)}, u32[]{:S(2)}, u32[]{:S(2)}) collective-permute-start(bf16[96,256]{1,0:T(8,128)(2,1)S(1)} %get-tuple-element.129), channel_id=1, source_target_pairs={{0,8},{4,12},{8,0},{12,4},{16,24},{20,28},{24,16},{28,20},{1,9},{5... | collective-permute-start | bytes 147464 | tf_op jit(solution)/shard_map/ppermute | solution.py:15
  59.8 3.6 %collective-permute-start.33 = (bf16[384,256]{1,0:T(8,128)(2,1)S(1)}, bf16[384,256]{1,0:T(8,128)(2,1)S(1)}, u32[]{:S(2)}, u32[]{:S(2)}) collective-permute-start(bf16[384,256]{1,0:T(8,128)(2,1)S(1)} %shard_map.96.refs_0_), channel_id=1, source_target_pairs={{0,4},{4,0},{8,12},{12,8},{16,20},{20,16},{24,28},{28,24},{1,5},{5... | collective-permute-start | bytes 589832 | tf_op jit(solution)/shard_map/ppermute | solution.py:15
  59.9 8.7 %collective-permute-start.32 = (bf16[384,256]{1,0:T(8,128)(2,1)S(1)}, bf16[384,256]{1,0:T(8,128)(2,1)S(1)}, u32[]{:S(2)}, u32[]{:S(2)}) collective-permute-start(bf16[384,256]{1,0:T(8,128)(2,1)S(1)} %shard_map.96.refs_0_), channel_id=1, source_target_pairs={{0,3},{1,2},{2,1},{3,0},{4,7},{5,6},{6,5},{7,4},{8,11},{9,10},{10,... | collective-permute-start | bytes 589832 | tf_op jit(solution)/shard_map/ppermute | solution.py:15
  61.4 10.9 %collective-permute-start.31 = (bf16[384,256]{1,0:T(8,128)(2,1)S(1)}, bf16[384,256]{1,0:T(8,128)(2,1)S(1)}, u32[]{:S(2)}, u32[]{:S(2)}) collective-permute-start(bf16[384,256]{1,0:T(8,128)(2,1)S(1)} %shard_map.96.refs_0_), channel_id=1, source_target_pairs={{0,2},{1,3},{2,0},{3,1},{4,6},{5,7},{6,4},{7,5},{8,10},{9,11},{10,... | collective-permute-start | bytes 589832 | tf_op jit(solution)/shard_map/ppermute | solution.py:15
  62.5 9.8 %collective-permute-start.30 = (bf16[384,256]{1,0:T(8,128)(2,1)S(1)}, bf16[384,256]{1,0:T(8,128)(2,1)S(1)}, u32[]{:S(2)}, u32[]{:S(2)}) collective-permute-start(bf16[384,256]{1,0:T(8,128)(2,1)S(1)} %shard_map.96.refs_0_), channel_id=1, source_target_pairs={{0,1},{1,0},{2,3},{3,2},{4,5},{5,4},{6,7},{7,6},{8,9},{9,8},{10,11... | collective-permute-start | bytes 589832 | tf_op jit(solution)/shard_map/ppermute | solution.py:15
  68.6 4.2 %collective-permute-start.36 = (bf16[384,256]{1,0:T(8,128)(2,1)S(1)}, bf16[384,256]{1,0:T(8,128)(2,1)S(1)}, u32[]{:S(2)}, u32[]{:S(2)}) collective-permute-start(bf16[384,256]{1,0:T(8,128)(2,1)S(1)} %collective-permute-done.32.refs_0_), channel_id=1, source_target_pairs={{0,4},{4,0},{8,12},{12,8},{16,20},{20,16},{24,28},{28,24},{1,5},{5... | collective-permute-start | bytes 589832 | tf_op jit(solution)/shard_map/ppermute | solution.py:15
  72.3 1.4 %collective-permute-start.34 = (bf16[384,256]{1,0:T(8,128)(2,1)S(1)}, bf16[384,256]{1,0:T(8,128)(2,1)S(1)}, u32[]{:S(2)}, u32[]{:S(2)}) collective-permute-start(bf16[384,256]{1,0:T(8,128)(2,1)S(1)} %collective-permute-done.30.refs_0_), channel_id=1, source_target_pairs={{0,4},{4,0},{8,12},{12,8},{16,20},{20,16},{24,28},{28,24},{1,5},{5... | collective-permute-start | bytes 589832 | tf_op jit(solution)/shard_map/ppermute | solution.py:15
  72.3 1.7 %collective-permute-start.35 = (bf16[384,256]{1,0:T(8,128)(2,1)S(1)}, bf16[384,256]{1,0:T(8,128)(2,1)S(1)}, u32[]{:S(2)}, u32[]{:S(2)}) collective-permute-start(bf16[384,256]{1,0:T(8,128)(2,1)S(1)} %collective-permute-done.31.refs_1_), channel_id=1, source_target_pairs={{0,4},{4,0},{8,12},{12,8},{16,20},{20,16},{24,28},{28,24},{1,5},{5... | collective-permute-start | bytes 589832 | tf_op jit(solution)/shard_map/ppermute | solution.py:15

commit v9 on v8

--- a/solution.py
+++ b/solution.py
@@ -155,8 +155,8 @@
     return (grad_first[None], grad_second[None])
 
 
-def plane_order(experts):
-    return (*range(2, experts), 1, 0)
+def plane_order(experts, near_first=False):
+    return (*range(1, experts), 0) if near_first else (*range(2, experts), 1, 0)
 
 
 def place():
@@ -232,7 +232,7 @@
         copies[2 + i].wait()
     for i in range(2):
         sent = dot(places[i][capacity:], slices[i][...]).astype(jnp.bfloat16)
-        for out, s in zip(moved[i * (experts - 1) :], plane_order(experts)[:-1]):
+        for out, s in zip(moved[i * (experts - 1) :], plane_order(experts, i)[:-1]):
             out[...] = sent[(s - 1) * capacity : s * capacity]
 
 
@@ -262,10 +262,10 @@
         copy.wait()
 
 
-def stack_kernel(*refs):
+def stack_kernel(near_first, *refs):
     moved, out = refs[:-1], refs[-1]
     capacity = moved[0].shape[0]
-    for ref, s in zip(moved, plane_order(len(moved) + 1)):
+    for ref, s in zip(moved, plane_order(len(moved) + 1, near_first)):
         out[(s - 1) * capacity : s * capacity, :] = ref[...]
 
 
@@ -333,7 +333,7 @@
             rows = pl.ds(pl.multiple_of(which * half, 16), half)
             both = keep[column ^ m].astype(jnp.float32) + got[column ^ m].astype(jnp.float32)
             if m:
-                out[m - 1][rows, :] = both.astype(jnp.bfloat16)
+                out[-m][rows, :] = both.astype(jnp.bfloat16)
             else:
                 mine[rows, :] = both
 
@@ -466,9 +466,9 @@
     def after(value, *others):
         return lax.optimization_barrier((value, others))[0]
 
-    def over_planes(sent):
+    def over_planes(sent, near_first=False):
         return [
-            partner(value, "dp", s << 1) for value, s in zip(sent, plane_order(experts))
+            partner(value, "dp", s << 1) for value, s in zip(sent, plane_order(experts, near_first))
         ]
 
     def spread(mine):
@@ -516,7 +516,9 @@
         )
 
     def collect(mine, *out):
-        return [mine] + [partner(value, "expert", m + 1) for m, value in enumerate(out)]
+        return [mine] + [
+            partner(value, "expert", columns - 1 - i) for i, value in enumerate(out)
+        ]
 
     route_t = teacher_route.reshape(1, row_count)
     route_s = student_route.reshape(1, row_count)
@@ -542,9 +544,9 @@
     stay_s = stay(student_in, route_s)
     routes = jnp.concatenate([route_t, route_s], axis=0)
     other_routes = across(routes)
-    def stack(moved, units=0):
-        return call(
-            stack_kernel,
+    def stack(moved, near_first, units=0):
+        return call(
+            lambda *refs: stack_kernel(near_first, *refs),
             [shape((experts - 1) * capacity, feat)],
             moved,
             flops=units * plane_rows * width * hid,
@@ -553,8 +555,8 @@
 
     sent_t, sent_s = sent[: experts - 1], sent[experts - 1 :]
     moved_t = over_planes(sent_t)
-    moved_s = over_planes(sent_s)
-    mine_t, mine_s = stack(moved_t, 0), stack(moved_s, 8)
+    moved_s = over_planes(sent_s, True)
+    mine_t, mine_s = stack(moved_t, False, 0), stack(moved_s, True, 8)
     w1_t, w2_t = load(*after((teacher_w1[0], teacher_w2[0]), mine_s))
     stay_t = stay(after(teacher_in, mine_s), route_t)
     got_t, got_s = spread(mine_t), spread(mine_s)

time: 76.9 us -> 77 us (level)
  starting transfers between devices: 37.3 us -> 38.7 us
  waiting for transfers between devices: 23.7 us -> 22.4 us
    ppermute x37, starting transfers between devices: 37.3 us -> 38.7 us  [partner(): lax.ppermute(value, axis, [(i, i ^ mask) for i in range(lax.axis_size(axi...]
    ppermute x37, waiting for transfers between devices: 23.7 us -> 22.4 us  [partner(): lax.ppermute(value, axis, [(i, i ^ mask) for i in range(lax.axis_size(axi...]
  transfers between devices with their start and end apart: 37 -> 37, of which waited for: 16 -> 18; matrix products, arithmetic and copies ran while one was open for 0% -> 0% of each run, Pallas kernels for 13% -> 13%
where the time goes in v9:
time: 77 us; the launch traced here: 76.9 us
  starting transfers between devices  38.7 us (50%)
  waiting for transfers between devices  22.4 us (29%)
  Pallas kernels  14.8 us (19%)
  between operations  0.98 us (1%)
    ppermute x37, starting transfers between devices, partner(): lax.ppermute(value, axis, [(i, i ^ mask) for i in range(lax.axis_size(axi...  38.7 us
    ppermute x37, waiting for transfers between devices, partner(): lax.ppermute(value, axis, [(i, i ^ mask) for i in range(lax.axis_size(axi...  22.4 us
    pallas_call x25, Pallas kernels, call(): pl.pallas_call(kernel, name=name, out_shape=outs, in_specs=in_specs or [V...  14.8 us
  transfers between devices with their start and end apart: 37, of which 18 were waited for; matrix products, arithmetic and copies ran while one was open for 0% of the time, Pallas kernels for 13%

profile of v9, /device:TPU:0, one launch (start us, length us, event | category | flops | bytes accessed | tf_op | source)
XLA Modules:
  0.0 76.9 jit_solution(17065601826293624033)
XLA Ops:
  0.6 1.9 %pack.1 = (bf16[48,512]{1,0:T(8,128)(2,1)}, bf16[48,512]{1,0:T(8,128)(2,1)}, bf16[48,512]{1,0:T(8,128)(2,1)}, bf16[48,512]{1,0:T(8,128)(2,1)}, bf16[48,512]{1,0:T(8,128)(2,1)}, /*index=5*/bf16[48,512]{1,0:T(8,128)(2,1)}) custom-call(bf16[128,2048]{1,0:T(8,128)(2,1)} %refs_0_.4, bf16[128,2048]{1,0:T(8,128)(2,1)} %refs_1_.1, s32[1,128]{1,0:T(1,128)} %bitcast.15, ...), custom_call_target="tpu_custom_call" | custom-call | tf_op jit(solution)/shard_map/pack/pallas_call | solution.py:172
  2.5 4.1 %collective-permute-start.6 = (bf16[48,512]{1,0:T(8,128)(2,1)}, bf16[48,512]{1,0:T(8,128)(2,1)S(1)}, u32[]{:S(2)}, u32[]{:S(2)}) collective-permute-start(bf16[48,512]{1,0:T(8,128)(2,1)} %get-tuple-element.79), channel_id=1, source_target_pairs={{0,16},{4,20},{8,24},{12,28},{16,0},{20,4},{24,8},{28,12},{1,17},{... | collective-permute-start | bytes 147464 | tf_op jit(solution)/shard_map/ppermute | solution.py:15
  6.6 1.3 %collective-permute-start.7 = (bf16[48,512]{1,0:T(8,128)(2,1)}, bf16[48,512]{1,0:T(8,128)(2,1)S(1)}, u32[]{:S(2)}, u32[]{:S(2)}) collective-permute-start(bf16[48,512]{1,0:T(8,128)(2,1)} %get-tuple-element.80), channel_id=1, source_target_pairs={{0,24},{4,28},{8,16},{12,20},{16,8},{20,12},{24,0},{28,4},{1,25},{... | collective-permute-start | bytes 147464 | tf_op jit(solution)/shard_map/ppermute | solution.py:15
  8.0 0.2 collective-permute-start.8
  8.2 1.8 %collective-permute-start = (bf16[48,512]{1,0:T(8,128)(2,1)}, bf16[48,512]{1,0:T(8,128)(2,1)S(1)}, u32[]{:S(2)}, u32[]{:S(2)}) collective-permute-start(bf16[48,512]{1,0:T(8,128)(2,1)} %get-tuple-element.75), channel_id=1, source_target_pairs={{0,8},{4,12},{8,0},{12,4},{16,24},{20,28},{24,16},{28,20},{1,9},{5... | collective-permute-start | bytes 147464 | tf_op jit(solution)/shard_map/ppermute | solution.py:15
  10.0 1.7 %collective-permute-start.1 = (bf16[48,512]{1,0:T(8,128)(2,1)}, bf16[48,512]{1,0:T(8,128)(2,1)S(1)}, u32[]{:S(2)}, u32[]{:S(2)}) collective-permute-start(bf16[48,512]{1,0:T(8,128)(2,1)} %get-tuple-element.76), channel_id=1, source_target_pairs={{0,16},{4,20},{8,24},{12,28},{16,0},{20,4},{24,8},{28,12},{1,17},{... | collective-permute-start | bytes 147464 | tf_op jit(solution)/shard_map/ppermute | solution.py:15
  11.7 3.1 %collective-permute-start.2 = (bf16[48,512]{1,0:T(8,128)(2,1)}, bf16[48,512]{1,0:T(8,128)(2,1)S(1)}, u32[]{:S(2)}, u32[]{:S(2)}) collective-permute-start(bf16[48,512]{1,0:T(8,128)(2,1)} %get-tuple-element.77), channel_id=1, source_target_pairs={{0,24},{4,28},{8,16},{12,20},{16,8},{20,12},{24,0},{28,4},{1,25},{... | collective-permute-start | bytes 147464 | tf_op jit(solution)/shard_map/ppermute | solution.py:15
  14.8 2.5 %collective-permute-start.11 = (bf16[144,512]{1,0:T(8,128)(2,1)S(1)}, bf16[144,512]{1,0:T(8,128)(2,1)S(1)}, u32[]{:S(2)}, u32[]{:S(2)}) collective-permute-start(bf16[144,512]{1,0:T(8,128)(2,1)S(1)} %stack.3.refs_1_), channel_id=1, source_target_pairs={{0,3},{1,2},{2,1},{3,0},{4,7},{5,6},{6,5},{7,4},{8,11},{9,10},{10,... | collective-permute-start | bytes 442376 | tf_op jit(solution)/shard_map/ppermute | solution.py:15
  17.3 0.5 collective-permute-start.10
  17.9 0.5 collective-permute-start.9
  18.4 2.5 %collective-permute-start.5 = (bf16[144,512]{1,0:T(8,128)(2,1)S(1)}, bf16[144,512]{1,0:T(8,128)(2,1)S(1)}, u32[]{:S(2)}, u32[]{:S(2)}) collective-permute-start(bf16[144,512]{1,0:T(8,128)(2,1)S(1)} %stack.2.refs_1_), channel_id=1, source_target_pairs={{0,3},{1,2},{2,1},{3,0},{4,7},{5,6},{6,5},{7,4},{8,11},{9,10},{10,... | collective-permute-start | bytes 442376 | tf_op jit(solution)/shard_map/ppermute | solution.py:15
  20.9 0.5 collective-permute-start.4
  21.5 0.3 stay.3.refs_0_
  21.8 0.3 load.2
  22.1 0.5 collective-permute-done.11.refs_4_
  22.6 1.5 %collective-permute-start.3 = (bf16[144,512]{1,0:T(8,128)(2,1)S(1)}, bf16[144,512]{1,0:T(8,128)(2,1)S(1)}, u32[]{:S(2)}, u32[]{:S(2)}) collective-permute-start(bf16[144,512]{1,0:T(8,128)(2,1)S(1)} %stack.2.refs_1_), channel_id=1, source_target_pairs={{0,1},{1,0},{2,3},{3,2},{4,5},{5,4},{6,7},{7,6},{8,9},{9,8},{10,11... | collective-permute-start | bytes 442376 | tf_op jit(solution)/shard_map/ppermute | solution.py:15
  24.1 1.6 %collective-permute-done.10.refs_3_ = bf16[144,512]{1,0:T(8,128)(2,1)S(1)} collective-permute-done((bf16[144,512]{1,0:T(8,128)(2,1)S(1)}, bf16[144,512]{1,0:T(8,128)(2,1)S(1)}, u32[]{:S(2)}, u32[]{:S(2)}) %collective-permute-start.10) | collective-permute-done | bytes 147488 | tf_op jit(solution)/shard_map/ppermute | solution.py:15
  25.9 0.9 %forward_t.2 = (bf16[1,4,192,256]{3,2,1,0:T(8,128)(2,1)S(1)}, bf16[192,512]{1,0:T(8,128)(2,1)S(1)}) custom-call(bf16[192,2048]{1,0:T(8,128)(2,1)S(1)} %join.2.refs_0_, bf16[2048,512]{1,0:T(8,128)(2,1)S(1)} %get-tuple-element.84.refs_1_, bf16[512,2048]{1,0:T(8,128)(2,1)S(1)} %get-tuple-element.89.refs_2_), custom_call_target="tpu_custom_call" | custom-call | flops 9663676416 | tf_op jit(solution)/shard_map/forward_t/pallas_call | solution.py:172
  26.9 0.6 collective-permute-start.13
  27.5 0.7 collective-permute-done.12.refs_0_
  28.2 0.9 %forward_t.3 = (bf16[1,4,192,256]{3,2,1,0:T(8,128)(2,1)S(1)}, bf16[192,512]{1,0:T(8,128)(2,1)S(1)}) custom-call(bf16[192,2048]{1,0:T(8,128)(2,1)S(1)} %collective-permute-done.12.refs_0_, bf16[2048,512]{1,0:T(8,128)(2,1)S(1)} %get-tuple-element.84.refs_1_, bf16[512,2048]{1,0:T(8,128)(2,1)S(1)} %get-tuple-element.89.refs_2_), custom_call_target="tpu_custom_call" | custom-call | tf_op jit(solution)/shard_map/forward_t/pallas_call | solution.py:172
  29.1 0.2 collective-permute-start.14
  29.3 0.3 stay.2.refs_0_
  29.7 0.3 load.3
  30.0 0.6 keep_t.1
  30.7 0.2 collective-permute-done.14.refs_4_
  31.2 0.2 collective-permute-start.15
  31.4 1.7 %collective-permute-start.21 = (bf16[384,256]{1,0:T(8,128)(2,1)S(1)}, bf16[384,256]{1,0:T(8,128)(2,1)S(1)}, u32[]{:S(2)}, u32[]{:S(2)}) collective-permute-start(bf16[384,256]{1,0:T(8,128)(2,1)S(1)} %get-tuple-element.115), channel_id=1, source_target_pairs={{0,3},{1,2},{2,1},{3,0},{4,7},{5,6},{6,5},{7,4},{8,11},{9,10},{10,... | collective-permute-start | bytes 589832 | tf_op jit(solution)/shard_map/ppermute | solution.py:15
  33.1 1.3 %collective-permute-start.22 = (bf16[384,256]{1,0:T(8,128)(2,1)S(1)}, bf16[384,256]{1,0:T(8,128)(2,1)S(1)}, u32[]{:S(2)}, u32[]{:S(2)}) collective-permute-start(bf16[384,256]{1,0:T(8,128)(2,1)S(1)} %get-tuple-element.116), channel_id=1, source_target_pairs={{0,2},{1,3},{2,0},{3,1},{4,6},{5,7},{6,4},{7,5},{8,10},{9,11},{10,... | collective-permute-start | bytes 589832 | tf_op jit(solution)/shard_map/ppermute | solution.py:15
  34.4 0.5 collective-permute-start.23
  34.9 1.7 %forward_s.1 = (bf16[2,4,192,256]{3,2,1,0:T(8,128)(2,1)S(1)}, bf16[192,512]{1,0:T(8,128)(2,1)S(1)}, bf16[192,512]{1,0:T(8,128)(2,1)S(1)}, f32[192,512]{1,0:T(8,128)S(1)}, f32[192,512]{1,0:T(8,128)S(1)}) custom-call(bf16[192,2048]{1,0:T(8,128)(2,1)S(1)} %join.3.refs_0_.refs_5_, bf16[192,2048]{1,0:T(8,128)(2,1)S(1)} %collective-permute-done.15.refs_1_.refs_6_, ...), custom_call_target="tpu_custom_call" | custom-call | tf_op jit(solution)/shard_map/forward_s/pallas_call | solution.py:172
  36.7 1.4 %keep_s.1 = (bf16[4,192,256]{2,1,0:T(8,128)(2,1)S(1)}, bf16[4,192,256]{2,1,0:T(8,128)(2,1)S(1)}, bf16[2048,384]{1,0:T(8,128)(2,1)S(1)}, bf16[512,384]{1,0:T(8,128)(2,1)S(1)}, f32[384,512]{1,0:T(8,128)S(1)}) custom-call(bf16[192,512]{1,0:T(8,128)(2,1)S(1)} %get-tuple-element.104.refs_0_, bf16[192,512]{1,0:T(8,128)(2,1)S(1)} %get-tuple-element.105.refs_1_, ...), custom_call_target="tpu_custom_call" | custom-call | flops 25769803776 | tf_op jit(solution)/shard_map/keep_s/pallas_call | solution.py:172
  38.1 0.9 %collective-permute-done.16.refs_2_ = bf16[2,4,192,256]{3,2,1,0:T(8,128)(2,1)S(1)} collective-permute-done((bf16[2,4,192,256]{3,2,1,0:T(8,128)(2,1)S(1)}, bf16[2,4,192,256]{3,2,1,0:T(8,128)(2,1)S(1)}, u32[]{:S(2)}, u32[]{:S(2)}) %collective-permute-start.16) | collective-permute-done | bytes 786464 | tf_op jit(solution)/shard_map/ppermute | solution.py:15
  39.0 0.2 pair.3
  39.2 1.7 %collective-permute-start.17 = (bf16[384,256]{1,0:T(8,128)(2,1)S(1)}, bf16[384,256]{1,0:T(8,128)(2,1)S(1)}, u32[]{:S(2)}, u32[]{:S(2)}) collective-permute-start(bf16[384,256]{1,0:T(8,128)(2,1)S(1)} %get-tuple-element.112), channel_id=1, source_target_pairs={{0,3},{1,2},{2,1},{3,0},{4,7},{5,6},{6,5},{7,4},{8,11},{9,10},{10,... | collective-permute-start | bytes 589832 | tf_op jit(solution)/shard_map/ppermute | solution.py:15
  40.9 1.1 %collective-permute-done.20.refs_1_ = s32[2,128]{1,0:T(2,128)S(1)} collective-permute-done((s32[2,128]{1,0:T(2,128)S(1)}, s32[2,128]{1,0:T(2,128)S(1)}, u32[]{:S(2)}, u32[]{:S(2)}) %collective-permute-start.20) | collective-permute-done | bytes 1056 | tf_op jit(solution)/shard_map/ppermute | solution.py:15
  42.0 0.4 maps.1.refs_0_
  42.4 1.8 %collective-permute-done.22.refs_2_ = bf16[384,256]{1,0:T(8,128)(2,1)S(1)} collective-permute-done((bf16[384,256]{1,0:T(8,128)(2,1)S(1)}, bf16[384,256]{1,0:T(8,128)(2,1)S(1)}, u32[]{:S(2)}, u32[]{:S(2)}) %collective-permute-start.22) | collective-permute-done | bytes 196640 | tf_op jit(solution)/shard_map/ppermute | solution.py:15
  44.3 1.0 %collective-permute-start.24 = (bf16[96,256]{1,0:T(8,128)(2,1)S(1)}, bf16[96,256]{1,0:T(8,128)(2,1)S(1)}, u32[]{:S(2)}, u32[]{:S(2)}) collective-permute-start(bf16[96,256]{1,0:T(8,128)(2,1)S(1)} %get-tuple-element.122), channel_id=1, source_target_pairs={{0,16},{4,20},{8,24},{12,28},{16,0},{20,4},{24,8},{28,12},{1,17},{... | collective-permute-start | bytes 147464 | tf_op jit(solution)/shard_map/ppermute | solution.py:15
  45.4 1.1 %collective-permute-start.25 = (bf16[96,256]{1,0:T(8,128)(2,1)S(1)}, bf16[96,256]{1,0:T(8,128)(2,1)S(1)}, u32[]{:S(2)}, u32[]{:S(2)}) collective-permute-start(bf16[96,256]{1,0:T(8,128)(2,1)S(1)} %get-tuple-element.123), channel_id=1, source_target_pairs={{0,24},{4,28},{8,16},{12,20},{16,8},{20,12},{24,0},{28,4},{1,25},{... | collective-permute-start | bytes 147464 | tf_op jit(solution)/shard_map/ppermute | solution.py:15
  46.4 1.5 %collective-permute-done.17.refs_1_ = bf16[384,256]{1,0:T(8,128)(2,1)S(1)} collective-permute-done((bf16[384,256]{1,0:T(8,128)(2,1)S(1)}, bf16[384,256]{1,0:T(8,128)(2,1)S(1)}, u32[]{:S(2)}, u32[]{:S(2)}) %collective-permute-start.17) | collective-permute-done | bytes 196640 | tf_op jit(solution)/shard_map/ppermute | solution.py:15
  47.9 0.5 collective-permute-start.26
  48.4 1.0 %collective-permute-start.18 = (bf16[384,256]{1,0:T(8,128)(2,1)S(1)}, bf16[384,256]{1,0:T(8,128)(2,1)S(1)}, u32[]{:S(2)}, u32[]{:S(2)}) collective-permute-start(bf16[384,256]{1,0:T(8,128)(2,1)S(1)} %get-tuple-element.113), channel_id=1, source_target_pairs={{0,2},{1,3},{2,0},{3,1},{4,6},{5,7},{6,4},{7,5},{8,10},{9,11},{10,... | collective-permute-start | bytes 589832 | tf_op jit(solution)/shard_map/ppermute | solution.py:15
  49.4 0.8 %collective-permute-start.19 = (bf16[384,256]{1,0:T(8,128)(2,1)S(1)}, bf16[384,256]{1,0:T(8,128)(2,1)S(1)}, u32[]{:S(2)}, u32[]{:S(2)}) collective-permute-start(bf16[384,256]{1,0:T(8,128)(2,1)S(1)} %get-tuple-element.114), channel_id=1, source_target_pairs={{0,1},{1,0},{2,3},{3,2},{4,5},{5,4},{6,7},{7,6},{8,9},{9,8},{10,11... | collective-permute-start | bytes 589832 | tf_op jit(solution)/shard_map/ppermute | solution.py:15
  50.2 0.2 collective-permute-done.24.refs_1_
  50.4 1.3 %collective-permute-done.25.refs_2_ = bf16[96,256]{1,0:T(8,128)(2,1)S(1)} collective-permute-done((bf16[96,256]{1,0:T(8,128)(2,1)S(1)}, bf16[96,256]{1,0:T(8,128)(2,1)S(1)}, u32[]{:S(2)}, u32[]{:S(2)}) %collective-permute-start.25) | collective-permute-done | bytes 49184 | tf_op jit(solution)/shard_map/ppermute | solution.py:15
  51.7 0.4 collective-permute-done.26.refs_3_
  52.1 0.2 home.1
  52.3 1.3 %collective-permute-start.27 = (bf16[96,256]{1,0:T(8,128)(2,1)S(1)}, bf16[96,256]{1,0:T(8,128)(2,1)S(1)}, u32[]{:S(2)}, u32[]{:S(2)}) collective-permute-start(bf16[96,256]{1,0:T(8,128)(2,1)S(1)} %get-tuple-element.127), channel_id=1, source_target_pairs={{0,16},{4,20},{8,24},{12,28},{16,0},{20,4},{24,8},{28,12},{1,17},{... | collective-permute-start | bytes 147464 | tf_op jit(solution)/shard_map/ppermute | solution.py:15
  53.6 1.5 %collective-permute-start.28 = (bf16[96,256]{1,0:T(8,128)(2,1)S(1)}, bf16[96,256]{1,0:T(8,128)(2,1)S(1)}, u32[]{:S(2)}, u32[]{:S(2)}) collective-permute-start(bf16[96,256]{1,0:T(8,128)(2,1)S(1)} %get-tuple-element.128), channel_id=1, source_target_pairs={{0,24},{4,28},{8,16},{12,20},{16,8},{20,12},{24,0},{28,4},{1,25},{... | collective-permute-start | bytes 147464 | tf_op jit(solution)/shard_map/ppermute | solution.py:15
  55.1 0.8 collective-permute-start.29
  55.9 2.3 %collective-permute-done.27.refs_4_ = bf16[96,256]{1,0:T(8,128)(2,1)S(1)} collective-permute-done((bf16[96,256]{1,0:T(8,128)(2,1)S(1)}, bf16[96,256]{1,0:T(8,128)(2,1)S(1)}, u32[]{:S(2)}, u32[]{:S(2)}) %collective-permute-start.27) | collective-permute-done | bytes 49184 | tf_op jit(solution)/shard_map/ppermute | solution.py:15
  58.1 1.5 %collective-permute-done.28.refs_5_ = bf16[96,256]{1,0:T(8,128)(2,1)S(1)} collective-permute-done((bf16[96,256]{1,0:T(8,128)(2,1)S(1)}, bf16[96,256]{1,0:T(8,128)(2,1)S(1)}, u32[]{:S(2)}, u32[]{:S(2)}) %collective-permute-start.28) | collective-permute-done | bytes 49184 | tf_op jit(solution)/shard_map/ppermute | solution.py:15
  59.9 1.3 %collective-permute-start.32 = (bf16[384,256]{1,0:T(8,128)(2,1)S(1)}, bf16[384,256]{1,0:T(8,128)(2,1)S(1)}, u32[]{:S(2)}, u32[]{:S(2)}) collective-permute-start(bf16[384,256]{1,0:T(8,128)(2,1)S(1)} %shard_map.96.refs_0_), channel_id=1, source_target_pairs={{0,3},{1,2},{2,1},{3,0},{4,7},{5,6},{6,5},{7,4},{8,11},{9,10},{10,... | collective-permute-start | bytes 589832 | tf_op jit(solution)/shard_map/ppermute | solution.py:15
  61.2 1.3 %collective-permute-start.31 = (bf16[384,256]{1,0:T(8,128)(2,1)S(1)}, bf16[384,256]{1,0:T(8,128)(2,1)S(1)}, u32[]{:S(2)}, u32[]{:S(2)}) collective-permute-start(bf16[384,256]{1,0:T(8,128)(2,1)S(1)} %shard_map.96.refs_0_), channel_id=1, source_target_pairs={{0,2},{1,3},{2,0},{3,1},{4,6},{5,7},{6,4},{7,5},{8,10},{9,11},{10,... | collective-permute-start | bytes 589832 | tf_op jit(solution)/shard_map/ppermute | solution.py:15
  62.5 1.0 %collective-permute-start.30 = (bf16[384,256]{1,0:T(8,128)(2,1)S(1)}, bf16[384,256]{1,0:T(8,128)(2,1)S(1)}, u32[]{:S(2)}, u32[]{:S(2)}) collective-permute-start(bf16[384,256]{1,0:T(8,128)(2,1)S(1)} %shard_map.96.refs_0_), channel_id=1, source_target_pairs={{0,1},{1,0},{2,3},{3,2},{4,5},{5,4},{6,7},{7,6},{8,9},{9,8},{10,11... | collective-permute-start | bytes 589832 | tf_op jit(solution)/shard_map/ppermute | solution.py:15
  63.5 0.6 early.3
  64.1 4.5 %collective-permute-done.32.refs_0_ = bf16[384,256]{1,0:T(8,128)(2,1)S(1)} collective-permute-done((bf16[384,256]{1,0:T(8,128)(2,1)S(1)}, bf16[384,256]{1,0:T(8,128)(2,1)S(1)}, u32[]{:S(2)}, u32[]{:S(2)}) %collective-permute-start.32) | collective-permute-done | bytes 196640 | tf_op jit(solution)/shard_map/ppermute | solution.py:15
  68.6 0.4 early.4
  69.1 3.3 %collective-permute-done.31.refs_1_ = bf16[384,256]{1,0:T(8,128)(2,1)S(1)} collective-permute-done((bf16[384,256]{1,0:T(8,128)(2,1)S(1)}, bf16[384,256]{1,0:T(8,128)(2,1)S(1)}, u32[]{:S(2)}, u32[]{:S(2)}) %collective-permute-start.31) | collective-permute-done | bytes 196640 | tf_op jit(solution)/shard_map/ppermute | solution.py:15
  72.4 0.5 collective-permute-start.35
  72.9 0.9 %early.5 = (f32[384,512]{1,0:T(8,128)S(1)}, bf16[512,256]{1,0:T(8,128)(2,1)S(1)}, bf16[512,256]{1,0:T(8,128)(2,1)S(1)}, bf16[512,256]{1,0:T(8,128)(2,1)S(1)}) custom-call(bf16[384,256]{1,0:T(8,128)(2,1)S(1)} %collective-permute-done.30.refs_0_, bf16[384,256]{1,0:T(8,128)(2,1)S(1)} %collective-permute-done.31.refs_1_, ...), custom_call_target="tpu_custom_call" | custom-call | tf_op jit(solution)/shard_map/early/pallas_call | solution.py:172
  73.8 0.3 collective-permute-done.35.refs_1_
  74.1 2.8 %last.1 = (bf16[2048,512]{1,0:T(8,128)(2,1)}, bf16[512,2048]{1,0:T(8,128)(2,1)}) custom-call(bf16[384,256]{1,0:T(8,128)(2,1)S(1)} %collective-permute-done.34.refs_0_, bf16[384,256]{1,0:T(8,128)(2,1)S(1)} %collective-permute-done.35.refs_1_, bf16[512,256]{1,0:T(8,128)(2,1)S(1)} %get-tuple-element.137.refs_2_, ...), custom_call_target="tpu_custom_call" | custom-call | tf_op jit(solution)/shard_map/last/pallas_call | solution.py:172
  (52 shorter events, 1.1 us)
Async XLA Ops:
  2.5 9.2 %collective-permute-start.6 = (bf16[48,512]{1,0:T(8,128)(2,1)}, bf16[48,512]{1,0:T(8,128)(2,1)S(1)}, u32[]{:S(2)}, u32[]{:S(2)}) collective-permute-start(bf16[48,512]{1,0:T(8,128)(2,1)} %get-tuple-element.79), channel_id=1, source_target_pairs={{0,16},{4,20},{8,24},{12,28},{16,0},{20,4},{24,8},{28,12},{1,17},{... | collective-permute-start | bytes 147464 | tf_op jit(solution)/shard_map/ppermute | solution.py:15
  6.6 8.2 %collective-permute-start.7 = (bf16[48,512]{1,0:T(8,128)(2,1)}, bf16[48,512]{1,0:T(8,128)(2,1)S(1)}, u32[]{:S(2)}, u32[]{:S(2)}) collective-permute-start(bf16[48,512]{1,0:T(8,128)(2,1)} %get-tuple-element.80), channel_id=1, source_target_pairs={{0,24},{4,28},{8,16},{12,20},{16,8},{20,12},{24,0},{28,4},{1,25},{... | collective-permute-start | bytes 147464 | tf_op jit(solution)/shard_map/ppermute | solution.py:15
  8.0 6.8 %collective-permute-start.8 = (bf16[48,512]{1,0:T(8,128)(2,1)}, bf16[48,512]{1,0:T(8,128)(2,1)S(1)}, u32[]{:S(2)}, u32[]{:S(2)}) collective-permute-start(bf16[48,512]{1,0:T(8,128)(2,1)} %get-tuple-element.81), channel_id=1, source_target_pairs={{0,8},{4,12},{8,0},{12,4},{16,24},{20,28},{24,16},{28,20},{1,9},{5... | collective-permute-start | bytes 147464 | tf_op jit(solution)/shard_map/ppermute | solution.py:15
  8.2 9.6 %collective-permute-start = (bf16[48,512]{1,0:T(8,128)(2,1)}, bf16[48,512]{1,0:T(8,128)(2,1)S(1)}, u32[]{:S(2)}, u32[]{:S(2)}) collective-permute-start(bf16[48,512]{1,0:T(8,128)(2,1)} %get-tuple-element.75), channel_id=1, source_target_pairs={{0,8},{4,12},{8,0},{12,4},{16,24},{20,28},{24,16},{28,20},{1,9},{5... | collective-permute-start | bytes 147464 | tf_op jit(solution)/shard_map/ppermute | solution.py:15
  10.0 8.4 %collective-permute-start.1 = (bf16[48,512]{1,0:T(8,128)(2,1)}, bf16[48,512]{1,0:T(8,128)(2,1)S(1)}, u32[]{:S(2)}, u32[]{:S(2)}) collective-permute-start(bf16[48,512]{1,0:T(8,128)(2,1)} %get-tuple-element.76), channel_id=1, source_target_pairs={{0,16},{4,20},{8,24},{12,28},{16,0},{20,4},{24,8},{28,12},{1,17},{... | collective-permute-start | bytes 147464 | tf_op jit(solution)/shard_map/ppermute | solution.py:15
  11.7 6.7 %collective-permute-start.2 = (bf16[48,512]{1,0:T(8,128)(2,1)}, bf16[48,512]{1,0:T(8,128)(2,1)S(1)}, u32[]{:S(2)}, u32[]{:S(2)}) collective-permute-start(bf16[48,512]{1,0:T(8,128)(2,1)} %get-tuple-element.77), channel_id=1, source_target_pairs={{0,24},{4,28},{8,16},{12,20},{16,8},{20,12},{24,0},{28,4},{1,25},{... | collective-permute-start | bytes 147464 | tf_op jit(solution)/shard_map/ppermute | solution.py:15
  14.8 6.6 %copy-start = (bf16[128,2048]{1,0:T(8,128)(2,1)S(1)}, bf16[128,2048]{1,0:T(8,128)(2,1)}, u32[]{:S(2)}) copy-start(bf16[128,2048]{1,0:T(8,128)(2,1)} %refs_0_.4) | copy-start | bytes 1572868
  14.8 6.6 %copy-start.7 = (s32[128,1]{0,1:T(1,128)S(1)}, s32[128,1]{0,1:T(1,128)}, u32[]{:S(2)}) copy-start(s32[128,1]{0,1:T(1,128)} %param.10) | copy-start | bytes 1540
  14.8 7.8 %collective-permute-start.11 = (bf16[144,512]{1,0:T(8,128)(2,1)S(1)}, bf16[144,512]{1,0:T(8,128)(2,1)S(1)}, u32[]{:S(2)}, u32[]{:S(2)}) collective-permute-start(bf16[144,512]{1,0:T(8,128)(2,1)S(1)} %stack.3.refs_1_), channel_id=1, source_target_pairs={{0,3},{1,2},{2,1},{3,0},{4,7},{5,6},{6,5},{7,4},{8,11},{9,10},{10,... | collective-permute-start | bytes 442376 | tf_op jit(solution)/shard_map/ppermute | solution.py:15
  17.3 8.4 %collective-permute-start.10 = (bf16[144,512]{1,0:T(8,128)(2,1)S(1)}, bf16[144,512]{1,0:T(8,128)(2,1)S(1)}, u32[]{:S(2)}, u32[]{:S(2)}) collective-permute-start(bf16[144,512]{1,0:T(8,128)(2,1)S(1)} %stack.3.refs_1_), channel_id=1, source_target_pairs={{0,2},{1,3},{2,0},{3,1},{4,6},{5,7},{6,4},{7,5},{8,10},{9,11},{10,... | collective-permute-start | bytes 442376 | tf_op jit(solution)/shard_map/ppermute | solution.py:15
  17.9 7.9 %collective-permute-start.9 = (bf16[144,512]{1,0:T(8,128)(2,1)S(1)}, bf16[144,512]{1,0:T(8,128)(2,1)S(1)}, u32[]{:S(2)}, u32[]{:S(2)}) collective-permute-start(bf16[144,512]{1,0:T(8,128)(2,1)S(1)} %stack.3.refs_1_), channel_id=1, source_target_pairs={{0,1},{1,0},{2,3},{3,2},{4,5},{5,4},{6,7},{7,6},{8,9},{9,8},{10,11... | collective-permute-start | bytes 442376 | tf_op jit(solution)/shard_map/ppermute | solution.py:15
  18.4 3.4 %copy-start.2 = (bf16[1,2048,512]{2,1,0:T(8,128)(2,1)S(1)}, bf16[1,2048,512]{2,1,0:T(8,128)(2,1)}, u32[]{:S(2)}) copy-start(bf16[1,2048,512]{2,1,0:T(8,128)(2,1)} %param.12) | copy-start | bytes 6291460
  18.4 3.4 %copy-start.3 = (bf16[1,512,2048]{2,1,0:T(8,128)(2,1)S(1)}, bf16[1,512,2048]{2,1,0:T(8,128)(2,1)}, u32[]{:S(2)}) copy-start(bf16[1,512,2048]{2,1,0:T(8,128)(2,1)} %param.13) | copy-start | bytes 6291460
  18.4 12.2 %collective-permute-start.5 = (bf16[144,512]{1,0:T(8,128)(2,1)S(1)}, bf16[144,512]{1,0:T(8,128)(2,1)S(1)}, u32[]{:S(2)}, u32[]{:S(2)}) collective-permute-start(bf16[144,512]{1,0:T(8,128)(2,1)S(1)} %stack.2.refs_1_), channel_id=1, source_target_pairs={{0,3},{1,2},{2,1},{3,0},{4,7},{5,6},{6,5},{7,4},{8,11},{9,10},{10,... | collective-permute-start | bytes 442376 | tf_op jit(solution)/shard_map/ppermute | solution.py:15
  20.9 9.7 %collective-permute-start.4 = (bf16[144,512]{1,0:T(8,128)(2,1)S(1)}, bf16[144,512]{1,0:T(8,128)(2,1)S(1)}, u32[]{:S(2)}, u32[]{:S(2)}) collective-permute-start(bf16[144,512]{1,0:T(8,128)(2,1)S(1)} %stack.2.refs_1_), channel_id=1, source_target_pairs={{0,2},{1,3},{2,0},{3,1},{4,6},{5,7},{6,4},{7,5},{8,10},{9,11},{10,... | collective-permute-start | bytes 442376 | tf_op jit(solution)/shard_map/ppermute | solution.py:15
  22.6 8.1 %collective-permute-start.3 = (bf16[144,512]{1,0:T(8,128)(2,1)S(1)}, bf16[144,512]{1,0:T(8,128)(2,1)S(1)}, u32[]{:S(2)}, u32[]{:S(2)}) collective-permute-start(bf16[144,512]{1,0:T(8,128)(2,1)S(1)} %stack.2.refs_1_), channel_id=1, source_target_pairs={{0,1},{1,0},{2,3},{3,2},{4,5},{5,4},{6,7},{7,6},{8,9},{9,8},{10,11... | collective-permute-start | bytes 442376 | tf_op jit(solution)/shard_map/ppermute | solution.py:15
  25.8 2.4 %collective-permute-start.12 = (bf16[192,2048]{1,0:T(8,128)(2,1)S(1)}, bf16[192,2048]{1,0:T(8,128)(2,1)S(1)}, u32[]{:S(2)}, u32[]{:S(2)}) collective-permute-start(bf16[192,2048]{1,0:T(8,128)(2,1)S(1)} %join.2.refs_0_), channel_id=1, source_target_pairs={{0,4},{4,0},{8,12},{12,8},{16,20},{20,16},{24,28},{28,24},{1,5},{5... | collective-permute-start | bytes 2359304 | tf_op jit(solution)/shard_map/ppermute | solution.py:15
  26.9 2.5 %copy-start.1 = (bf16[128,2048]{1,0:T(8,128)(2,1)S(1)}, bf16[128,2048]{1,0:T(8,128)(2,1)}, u32[]{:S(2)}) copy-start(bf16[128,2048]{1,0:T(8,128)(2,1)} %refs_1_.1) | copy-start | bytes 1572868
  26.9 2.5 %copy-start.6 = (s32[128,1]{0,1:T(1,128)S(1)}, s32[128,1]{0,1:T(1,128)}, u32[]{:S(2)}) copy-start(s32[128,1]{0,1:T(1,128)} %param.11) | copy-start | bytes 1540
  26.9 2.8 %copy-start.4 = (bf16[1,2048,512]{2,1,0:T(8,128)(2,1)S(1)}, bf16[1,2048,512]{2,1,0:T(8,128)(2,1)}, u32[]{:S(2)}) copy-start(bf16[1,2048,512]{2,1,0:T(8,128)(2,1)} %param.14) | copy-start | bytes 6291460
  26.9 2.8 %copy-start.5 = (bf16[1,512,2048]{2,1,0:T(8,128)(2,1)S(1)}, bf16[1,512,2048]{2,1,0:T(8,128)(2,1)}, u32[]{:S(2)}) copy-start(bf16[1,512,2048]{2,1,0:T(8,128)(2,1)} %param.15) | copy-start | bytes 6291460
  26.9 3.8 %collective-permute-start.13 = (bf16[1,4,192,256]{3,2,1,0:T(8,128)(2,1)S(1)}, bf16[1,4,192,256]{3,2,1,0:T(8,128)(2,1)S(1)}, u32[]{:S(2)}, u32[]{:S(2)}) collective-permute-start(bf16[1,4,192,256]{3,2,1,0:T(8,128)(2,1)S(1)} %get-tuple-element.96), channel_id=1, source_target_pairs={{0,4},{4,0},{8,12},{12,8},{16,20},{20,16},{24,28},{28,24},{1,5},{5... | collective-permute-start | bytes 1179656 | tf_op jit(solution)/shard_map/ppermute | solution.py:15
  29.1 1.8 %collective-permute-start.14 = (bf16[1,4,192,256]{3,2,1,0:T(8,128)(2,1)S(1)}, bf16[1,4,192,256]{3,2,1,0:T(8,128)(2,1)S(1)}, u32[]{:S(2)}, u32[]{:S(2)}) collective-permute-start(bf16[1,4,192,256]{3,2,1,0:T(8,128)(2,1)S(1)} %get-tuple-element.97), channel_id=1, source_target_pairs={{0,4},{4,0},{8,12},{12,8},{16,20},{20,16},{24,28},{28,24},{1,5},{5... | collective-permute-start | bytes 1179656 | tf_op jit(solution)/shard_map/ppermute | solution.py:15
  31.2 3.7 %collective-permute-start.15 = (bf16[192,2048]{1,0:T(8,128)(2,1)S(1)}, bf16[192,2048]{1,0:T(8,128)(2,1)S(1)}, u32[]{:S(2)}, u32[]{:S(2)}) collective-permute-start(bf16[192,2048]{1,0:T(8,128)(2,1)S(1)} %join.3.refs_0_.refs_5_), channel_id=1, source_target_pairs={{0,4},{4,0},{8,12},{12,8},{16,20},{20,16},{24,28},{28,24},{1,5},{5... | collective-permute-start | bytes 2359304 | tf_op jit(solution)/shard_map/ppermute | solution.py:15
  31.4 11.0 %collective-permute-start.21 = (bf16[384,256]{1,0:T(8,128)(2,1)S(1)}, bf16[384,256]{1,0:T(8,128)(2,1)S(1)}, u32[]{:S(2)}, u32[]{:S(2)}) collective-permute-start(bf16[384,256]{1,0:T(8,128)(2,1)S(1)} %get-tuple-element.115), channel_id=1, source_target_pairs={{0,3},{1,2},{2,1},{3,0},{4,7},{5,6},{6,5},{7,4},{8,11},{9,10},{10,... | collective-permute-start | bytes 589832 | tf_op jit(solution)/shard_map/ppermute | solution.py:15
  33.1 11.1 %collective-permute-start.22 = (bf16[384,256]{1,0:T(8,128)(2,1)S(1)}, bf16[384,256]{1,0:T(8,128)(2,1)S(1)}, u32[]{:S(2)}, u32[]{:S(2)}) collective-permute-start(bf16[384,256]{1,0:T(8,128)(2,1)S(1)} %get-tuple-element.116), channel_id=1, source_target_pairs={{0,2},{1,3},{2,0},{3,1},{4,6},{5,7},{6,4},{7,5},{8,10},{9,11},{10,... | collective-permute-start | bytes 589832 | tf_op jit(solution)/shard_map/ppermute | solution.py:15
  34.4 9.9 %collective-permute-start.23 = (bf16[384,256]{1,0:T(8,128)(2,1)S(1)}, bf16[384,256]{1,0:T(8,128)(2,1)S(1)}, u32[]{:S(2)}, u32[]{:S(2)}) collective-permute-start(bf16[384,256]{1,0:T(8,128)(2,1)S(1)} %get-tuple-element.117), channel_id=1, source_target_pairs={{0,1},{1,0},{2,3},{3,2},{4,5},{5,4},{6,7},{7,6},{8,9},{9,8},{10,11... | collective-permute-start | bytes 589832 | tf_op jit(solution)/shard_map/ppermute | solution.py:15
  36.6 2.4 %collective-permute-start.16 = (bf16[2,4,192,256]{3,2,1,0:T(8,128)(2,1)S(1)}, bf16[2,4,192,256]{3,2,1,0:T(8,128)(2,1)S(1)}, u32[]{:S(2)}, u32[]{:S(2)}) collective-permute-start(bf16[2,4,192,256]{3,2,1,0:T(8,128)(2,1)S(1)} %get-tuple-element.110), channel_id=1, source_target_pairs={{0,4},{4,0},{8,12},{12,8},{16,20},{20,16},{24,28},{28,24},{1,5},{5... | collective-permute-start | bytes 2359304 | tf_op jit(solution)/shard_map/ppermute | solution.py:15
  39.2 8.8 %collective-permute-start.17 = (bf16[384,256]{1,0:T(8,128)(2,1)S(1)}, bf16[384,256]{1,0:T(8,128)(2,1)S(1)}, u32[]{:S(2)}, u32[]{:S(2)}) collective-permute-start(bf16[384,256]{1,0:T(8,128)(2,1)S(1)} %get-tuple-element.112), channel_id=1, source_target_pairs={{0,3},{1,2},{2,1},{3,0},{4,7},{5,6},{6,5},{7,4},{8,11},{9,10},{10,... | collective-permute-start | bytes 589832 | tf_op jit(solution)/shard_map/ppermute | solution.py:15
  40.9 1.1 %collective-permute-start.20 = (s32[2,128]{1,0:T(2,128)S(1)}, s32[2,128]{1,0:T(2,128)S(1)}, u32[]{:S(2)}, u32[]{:S(2)}) collective-permute-start(s32[2,128]{1,0:T(2,128)S(1)} %pad_add_fusion.refs_0_), channel_id=1, source_target_pairs={{0,4},{4,0},{8,12},{12,8},{16,20},{20,16},{24,28},{28,24},{1,5},{5... | collective-permute-start | bytes 3080 | tf_op jit(solution)/shard_map/ppermute | solution.py:15
  44.3 6.0 %collective-permute-start.24 = (bf16[96,256]{1,0:T(8,128)(2,1)S(1)}, bf16[96,256]{1,0:T(8,128)(2,1)S(1)}, u32[]{:S(2)}, u32[]{:S(2)}) collective-permute-start(bf16[96,256]{1,0:T(8,128)(2,1)S(1)} %get-tuple-element.122), channel_id=1, source_target_pairs={{0,16},{4,20},{8,24},{12,28},{16,0},{20,4},{24,8},{28,12},{1,17},{... | collective-permute-start | bytes 147464 | tf_op jit(solution)/shard_map/ppermute | solution.py:15
  45.4 6.3 %collective-permute-start.25 = (bf16[96,256]{1,0:T(8,128)(2,1)S(1)}, bf16[96,256]{1,0:T(8,128)(2,1)S(1)}, u32[]{:S(2)}, u32[]{:S(2)}) collective-permute-start(bf16[96,256]{1,0:T(8,128)(2,1)S(1)} %get-tuple-element.123), channel_id=1, source_target_pairs={{0,24},{4,28},{8,16},{12,20},{16,8},{20,12},{24,0},{28,4},{1,25},{... | collective-permute-start | bytes 147464 | tf_op jit(solution)/shard_map/ppermute | solution.py:15
  47.9 4.2 %collective-permute-start.26 = (bf16[96,256]{1,0:T(8,128)(2,1)S(1)}, bf16[96,256]{1,0:T(8,128)(2,1)S(1)}, u32[]{:S(2)}, u32[]{:S(2)}) collective-permute-start(bf16[96,256]{1,0:T(8,128)(2,1)S(1)} %get-tuple-element.125), channel_id=1, source_target_pairs={{0,8},{4,12},{8,0},{12,4},{16,24},{20,28},{24,16},{28,20},{1,9},{5... | collective-permute-start | bytes 147464 | tf_op jit(solution)/shard_map/ppermute | solution.py:15
  48.4 7.5 %collective-permute-start.18 = (bf16[384,256]{1,0:T(8,128)(2,1)S(1)}, bf16[384,256]{1,0:T(8,128)(2,1)S(1)}, u32[]{:S(2)}, u32[]{:S(2)}) collective-permute-start(bf16[384,256]{1,0:T(8,128)(2,1)S(1)} %get-tuple-element.113), channel_id=1, source_target_pairs={{0,2},{1,3},{2,0},{3,1},{4,6},{5,7},{6,4},{7,5},{8,10},{9,11},{10,... | collective-permute-start | bytes 589832 | tf_op jit(solution)/shard_map/ppermute | solution.py:15
  49.4 6.5 %collective-permute-start.19 = (bf16[384,256]{1,0:T(8,128)(2,1)S(1)}, bf16[384,256]{1,0:T(8,128)(2,1)S(1)}, u32[]{:S(2)}, u32[]{:S(2)}) collective-permute-start(bf16[384,256]{1,0:T(8,128)(2,1)S(1)} %get-tuple-element.114), channel_id=1, source_target_pairs={{0,1},{1,0},{2,3},{3,2},{4,5},{5,4},{6,7},{7,6},{8,9},{9,8},{10,11... | collective-permute-start | bytes 589832 | tf_op jit(solution)/shard_map/ppermute | solution.py:15
  52.3 5.8 %collective-permute-start.27 = (bf16[96,256]{1,0:T(8,128)(2,1)S(1)}, bf16[96,256]{1,0:T(8,128)(2,1)S(1)}, u32[]{:S(2)}, u32[]{:S(2)}) collective-permute-start(bf16[96,256]{1,0:T(8,128)(2,1)S(1)} %get-tuple-element.127), channel_id=1, source_target_pairs={{0,16},{4,20},{8,24},{12,28},{16,0},{20,4},{24,8},{28,12},{1,17},{... | collective-permute-start | bytes 147464 | tf_op jit(solution)/shard_map/ppermute | solution.py:15
  53.6 6.0 %collective-permute-start.28 = (bf16[96,256]{1,0:T(8,128)(2,1)S(1)}, bf16[96,256]{1,0:T(8,128)(2,1)S(1)}, u32[]{:S(2)}, u32[]{:S(2)}) collective-permute-start(bf16[96,256]{1,0:T(8,128)(2,1)S(1)} %get-tuple-element.128), channel_id=1, source_target_pairs={{0,24},{4,28},{8,16},{12,20},{16,8},{20,12},{24,0},{28,4},{1,25},{... | collective-permute-start | bytes 147464 | tf_op jit(solution)/shard_map/ppermute | solution.py:15
  55.1 4.6 %collective-permute-start.29 = (bf16[96,256]{1,0:T(8,128)(2,1)S(1)}, bf16[96,256]{1,0:T(8,128)(2,1)S(1)}, u32[]{:S(2)}, u32[]{:S(2)}) collective-permute-start(bf16[96,256]{1,0:T(8,128)(2,1)S(1)} %get-tuple-element.129), channel_id=1, source_target_pairs={{0,8},{4,12},{8,0},{12,4},{16,24},{20,28},{24,16},{28,20},{1,9},{5... | collective-permute-start | bytes 147464 | tf_op jit(solution)/shard_map/ppermute | solution.py:15
  59.8 3.6 %collective-permute-start.33 = (bf16[384,256]{1,0:T(8,128)(2,1)S(1)}, bf16[384,256]{1,0:T(8,128)(2,1)S(1)}, u32[]{:S(2)}, u32[]{:S(2)}) collective-permute-start(bf16[384,256]{1,0:T(8,128)(2,1)S(1)} %shard_map.96.refs_0_), channel_id=1, source_target_pairs={{0,4},{4,0},{8,12},{12,8},{16,20},{20,16},{24,28},{28,24},{1,5},{5... | collective-permute-start | bytes 589832 | tf_op jit(solution)/shard_map/ppermute | solution.py:15
  59.9 8.7 %collective-permute-start.32 = (bf16[384,256]{1,0:T(8,128)(2,1)S(1)}, bf16[384,256]{1,0:T(8,128)(2,1)S(1)}, u32[]{:S(2)}, u32[]{:S(2)}) collective-permute-start(bf16[384,256]{1,0:T(8,128)(2,1)S(1)} %shard_map.96.refs_0_), channel_id=1, source_target_pairs={{0,3},{1,2},{2,1},{3,0},{4,7},{5,6},{6,5},{7,4},{8,11},{9,10},{10,... | collective-permute-start | bytes 589832 | tf_op jit(solution)/shard_map/ppermute | solution.py:15
  61.2 11.1 %collective-permute-start.31 = (bf16[384,256]{1,0:T(8,128)(2,1)S(1)}, bf16[384,256]{1,0:T(8,128)(2,1)S(1)}, u32[]{:S(2)}, u32[]{:S(2)}) collective-permute-start(bf16[384,256]{1,0:T(8,128)(2,1)S(1)} %shard_map.96.refs_0_), channel_id=1, source_target_pairs={{0,2},{1,3},{2,0},{3,1},{4,6},{5,7},{6,4},{7,5},{8,10},{9,11},{10,... | collective-permute-start | bytes 589832 | tf_op jit(solution)/shard_map/ppermute | solution.py:15
  62.5 9.9 %collective-permute-start.30 = (bf16[384,256]{1,0:T(8,128)(2,1)S(1)}, bf16[384,256]{1,0:T(8,128)(2,1)S(1)}, u32[]{:S(2)}, u32[]{:S(2)}) collective-permute-start(bf16[384,256]{1,0:T(8,128)(2,1)S(1)} %shard_map.96.refs_0_), channel_id=1, source_target_pairs={{0,1},{1,0},{2,3},{3,2},{4,5},{5,4},{6,7},{7,6},{8,9},{9,8},{10,11... | collective-permute-start | bytes 589832 | tf_op jit(solution)/shard_map/ppermute | solution.py:15
  68.6 4.2 %collective-permute-start.36 = (bf16[384,256]{1,0:T(8,128)(2,1)S(1)}, bf16[384,256]{1,0:T(8,128)(2,1)S(1)}, u32[]{:S(2)}, u32[]{:S(2)}) collective-permute-start(bf16[384,256]{1,0:T(8,128)(2,1)S(1)} %collective-permute-done.32.refs_0_), channel_id=1, source_target_pairs={{0,4},{4,0},{8,12},{12,8},{16,20},{20,16},{24,28},{28,24},{1,5},{5... | collective-permute-start | bytes 589832 | tf_op jit(solution)/shard_map/ppermute | solution.py:15
  72.4 1.4 %collective-permute-start.34 = (bf16[384,256]{1,0:T(8,128)(2,1)S(1)}, bf16[384,256]{1,0:T(8,128)(2,1)S(1)}, u32[]{:S(2)}, u32[]{:S(2)}) collective-permute-start(bf16[384,256]{1,0:T(8,128)(2,1)S(1)} %collective-permute-done.30.refs_0_), channel_id=1, source_target_pairs={{0,4},{4,0},{8,12},{12,8},{16,20},{20,16},{24,28},{28,24},{1,5},{5... | collective-permute-start | bytes 589832 | tf_op jit(solution)/shard_map/ppermute | solution.py:15
  72.4 1.7 %collective-permute-start.35 = (bf16[384,256]{1,0:T(8,128)(2,1)S(1)}, bf16[384,256]{1,0:T(8,128)(2,1)S(1)}, u32[]{:S(2)}, u32[]{:S(2)}) collective-permute-start(bf16[384,256]{1,0:T(8,128)(2,1)S(1)} %collective-permute-done.31.refs_1_), channel_id=1, source_target_pairs={{0,4},{4,0},{8,12},{12,8},{16,20},{20,16},{24,28},{28,24},{1,5},{5... | collective-permute-start | bytes 589832 | tf_op jit(solution)/shard_map/ppermute | solution.py:15

commit v10 on v9

--- a/solution.py
+++ b/solution.py
@@ -277,7 +277,7 @@
     flat[:capacity, :] = stay[...]
     for m in range(columns):
         cols = pl.ds(pl.multiple_of((column ^ m) * feat, feat), feat)
-        flat[capacity:, cols] = parts[m][...]
+        flat[capacity:, cols] = parts[-m if m else 0][...]
 
 
 def part_pieces(hidden, w2, which, columns, out):
@@ -560,6 +560,7 @@
     w1_t, w2_t = load(*after((teacher_w1[0], teacher_w2[0]), mine_s))
     stay_t = stay(after(teacher_in, mine_s), route_t)
     got_t, got_s = spread(mine_t), spread(mine_s)
+    got_t, got_s = (got[:1] + got[:0:-1] for got in (got_t, got_s))
     w1_s, w2_s = load(student_w1[0], student_w2[0])
     (maps,) = call(
         lambda *refs: map_kernel(experts, capacity, *refs),

time: 77 us -> 76.6 us (level)
  transfers between devices with their start and end apart: 37 -> 37, of which waited for: 18 -> 17; matrix products, arithmetic and copies ran while one was open for 0% -> 0% of each run, Pallas kernels for 13% -> 13%
where the time goes in v10:
time: 76.6 us; the launch traced here: 76.5 us
  starting transfers between devices  38.1 us (50%)
  waiting for transfers between devices  22.5 us (29%)
  Pallas kernels  14.8 us (19%)
  between operations  0.99 us (1%)
    ppermute x37, starting transfers between devices, partner(): lax.ppermute(value, axis, [(i, i ^ mask) for i in range(lax.axis_size(axi...  38.1 us
    ppermute x37, waiting for transfers between devices, partner(): lax.ppermute(value, axis, [(i, i ^ mask) for i in range(lax.axis_size(axi...  22.5 us
    pallas_call x25, Pallas kernels, call(): pl.pallas_call(kernel, name=name, out_shape=outs, in_specs=in_specs or [V...  14.8 us
  transfers between devices with their start and end apart: 37, of which 17 were waited for; matrix products, arithmetic and copies ran while one was open for 0% of the time, Pallas kernels for 13%

profile of v10, /device:TPU:0, one launch (start us, length us, event | category | flops | bytes accessed | tf_op | source)
XLA Modules:
  0.0 76.5 jit_solution(3975592241085783916)
XLA Ops:
  0.6 1.9 %pack.1 = (bf16[48,512]{1,0:T(8,128)(2,1)}, bf16[48,512]{1,0:T(8,128)(2,1)}, bf16[48,512]{1,0:T(8,128)(2,1)}, bf16[48,512]{1,0:T(8,128)(2,1)}, bf16[48,512]{1,0:T(8,128)(2,1)}, /*index=5*/bf16[48,512]{1,0:T(8,128)(2,1)}) custom-call(bf16[128,2048]{1,0:T(8,128)(2,1)} %refs_0_.4, bf16[128,2048]{1,0:T(8,128)(2,1)} %refs_1_.1, s32[1,128]{1,0:T(1,128)} %bitcast.15, ...), custom_call_target="tpu_custom_call" | custom-call | tf_op jit(solution)/shard_map/pack/pallas_call | solution.py:172
  2.5 4.1 %collective-permute-start.6 = (bf16[48,512]{1,0:T(8,128)(2,1)}, bf16[48,512]{1,0:T(8,128)(2,1)S(1)}, u32[]{:S(2)}, u32[]{:S(2)}) collective-permute-start(bf16[48,512]{1,0:T(8,128)(2,1)} %get-tuple-element.79), channel_id=1, source_target_pairs={{0,16},{4,20},{8,24},{12,28},{16,0},{20,4},{24,8},{28,12},{1,17},{... | collective-permute-start | bytes 147464 | tf_op jit(solution)/shard_map/ppermute | solution.py:15
  6.6 1.3 %collective-permute-start.7 = (bf16[48,512]{1,0:T(8,128)(2,1)}, bf16[48,512]{1,0:T(8,128)(2,1)S(1)}, u32[]{:S(2)}, u32[]{:S(2)}) collective-permute-start(bf16[48,512]{1,0:T(8,128)(2,1)} %get-tuple-element.80), channel_id=1, source_target_pairs={{0,24},{4,28},{8,16},{12,20},{16,8},{20,12},{24,0},{28,4},{1,25},{... | collective-permute-start | bytes 147464 | tf_op jit(solution)/shard_map/ppermute | solution.py:15
  8.0 0.2 collective-permute-start.8
  8.2 1.8 %collective-permute-start = (bf16[48,512]{1,0:T(8,128)(2,1)}, bf16[48,512]{1,0:T(8,128)(2,1)S(1)}, u32[]{:S(2)}, u32[]{:S(2)}) collective-permute-start(bf16[48,512]{1,0:T(8,128)(2,1)} %get-tuple-element.75), channel_id=1, source_target_pairs={{0,8},{4,12},{8,0},{12,4},{16,24},{20,28},{24,16},{28,20},{1,9},{5... | collective-permute-start | bytes 147464 | tf_op jit(solution)/shard_map/ppermute | solution.py:15
  10.0 1.7 %collective-permute-start.1 = (bf16[48,512]{1,0:T(8,128)(2,1)}, bf16[48,512]{1,0:T(8,128)(2,1)S(1)}, u32[]{:S(2)}, u32[]{:S(2)}) collective-permute-start(bf16[48,512]{1,0:T(8,128)(2,1)} %get-tuple-element.76), channel_id=1, source_target_pairs={{0,16},{4,20},{8,24},{12,28},{16,0},{20,4},{24,8},{28,12},{1,17},{... | collective-permute-start | bytes 147464 | tf_op jit(solution)/shard_map/ppermute | solution.py:15
  11.7 3.1 %collective-permute-start.2 = (bf16[48,512]{1,0:T(8,128)(2,1)}, bf16[48,512]{1,0:T(8,128)(2,1)S(1)}, u32[]{:S(2)}, u32[]{:S(2)}) collective-permute-start(bf16[48,512]{1,0:T(8,128)(2,1)} %get-tuple-element.77), channel_id=1, source_target_pairs={{0,24},{4,28},{8,16},{12,20},{16,8},{20,12},{24,0},{28,4},{1,25},{... | collective-permute-start | bytes 147464 | tf_op jit(solution)/shard_map/ppermute | solution.py:15
  14.8 1.6 %collective-permute-start.11 = (bf16[144,512]{1,0:T(8,128)(2,1)S(1)}, bf16[144,512]{1,0:T(8,128)(2,1)S(1)}, u32[]{:S(2)}, u32[]{:S(2)}) collective-permute-start(bf16[144,512]{1,0:T(8,128)(2,1)S(1)} %stack.3.refs_1_), channel_id=1, source_target_pairs={{0,1},{1,0},{2,3},{3,2},{4,5},{5,4},{6,7},{7,6},{8,9},{9,8},{10,11... | collective-permute-start | bytes 442376 | tf_op jit(solution)/shard_map/ppermute | solution.py:15
  16.4 1.5 %collective-permute-start.10 = (bf16[144,512]{1,0:T(8,128)(2,1)S(1)}, bf16[144,512]{1,0:T(8,128)(2,1)S(1)}, u32[]{:S(2)}, u32[]{:S(2)}) collective-permute-start(bf16[144,512]{1,0:T(8,128)(2,1)S(1)} %stack.3.refs_1_), channel_id=1, source_target_pairs={{0,2},{1,3},{2,0},{3,1},{4,6},{5,7},{6,4},{7,5},{8,10},{9,11},{10,... | collective-permute-start | bytes 442376 | tf_op jit(solution)/shard_map/ppermute | solution.py:15
  17.9 0.5 collective-permute-start.9
  18.4 1.6 %collective-permute-start.5 = (bf16[144,512]{1,0:T(8,128)(2,1)S(1)}, bf16[144,512]{1,0:T(8,128)(2,1)S(1)}, u32[]{:S(2)}, u32[]{:S(2)}) collective-permute-start(bf16[144,512]{1,0:T(8,128)(2,1)S(1)} %stack.2.refs_1_), channel_id=1, source_target_pairs={{0,1},{1,0},{2,3},{3,2},{4,5},{5,4},{6,7},{7,6},{8,9},{9,8},{10,11... | collective-permute-start | bytes 442376 | tf_op jit(solution)/shard_map/ppermute | solution.py:15
  20.0 1.5 %collective-permute-start.4 = (bf16[144,512]{1,0:T(8,128)(2,1)S(1)}, bf16[144,512]{1,0:T(8,128)(2,1)S(1)}, u32[]{:S(2)}, u32[]{:S(2)}) collective-permute-start(bf16[144,512]{1,0:T(8,128)(2,1)S(1)} %stack.2.refs_1_), channel_id=1, source_target_pairs={{0,2},{1,3},{2,0},{3,1},{4,6},{5,7},{6,4},{7,5},{8,10},{9,11},{10,... | collective-permute-start | bytes 442376 | tf_op jit(solution)/shard_map/ppermute | solution.py:15
  21.5 0.3 stay.3.refs_0_
  21.9 0.3 load.2
  22.2 1.9 %collective-permute-start.3 = (bf16[144,512]{1,0:T(8,128)(2,1)S(1)}, bf16[144,512]{1,0:T(8,128)(2,1)S(1)}, u32[]{:S(2)}, u32[]{:S(2)}) collective-permute-start(bf16[144,512]{1,0:T(8,128)(2,1)S(1)} %stack.2.refs_1_), channel_id=1, source_target_pairs={{0,3},{1,2},{2,1},{3,0},{4,7},{5,6},{6,5},{7,4},{8,11},{9,10},{10,... | collective-permute-start | bytes 442376 | tf_op jit(solution)/shard_map/ppermute | solution.py:15
  24.1 1.9 %collective-permute-done.10.refs_3_ = bf16[144,512]{1,0:T(8,128)(2,1)S(1)} collective-permute-done((bf16[144,512]{1,0:T(8,128)(2,1)S(1)}, bf16[144,512]{1,0:T(8,128)(2,1)S(1)}, u32[]{:S(2)}, u32[]{:S(2)}) %collective-permute-start.10) | collective-permute-done | bytes 147488 | tf_op jit(solution)/shard_map/ppermute | solution.py:15
  26.1 0.9 %forward_t.2 = (bf16[1,4,192,256]{3,2,1,0:T(8,128)(2,1)S(1)}, bf16[192,512]{1,0:T(8,128)(2,1)S(1)}) custom-call(bf16[192,2048]{1,0:T(8,128)(2,1)S(1)} %join.2.refs_0_, bf16[2048,512]{1,0:T(8,128)(2,1)S(1)} %get-tuple-element.84.refs_1_, bf16[512,2048]{1,0:T(8,128)(2,1)S(1)} %get-tuple-element.89.refs_2_), custom_call_target="tpu_custom_call" | custom-call | flops 9663676416 | tf_op jit(solution)/shard_map/forward_t/pallas_call | solution.py:172
  27.1 0.6 collective-permute-start.13
  27.7 0.7 collective-permute-done.12.refs_0_
  28.4 0.9 %forward_t.3 = (bf16[1,4,192,256]{3,2,1,0:T(8,128)(2,1)S(1)}, bf16[192,512]{1,0:T(8,128)(2,1)S(1)}) custom-call(bf16[192,2048]{1,0:T(8,128)(2,1)S(1)} %collective-permute-done.12.refs_0_, bf16[2048,512]{1,0:T(8,128)(2,1)S(1)} %get-tuple-element.84.refs_1_, bf16[512,2048]{1,0:T(8,128)(2,1)S(1)} %get-tuple-element.89.refs_2_), custom_call_target="tpu_custom_call" | custom-call | tf_op jit(solution)/shard_map/forward_t/pallas_call | solution.py:172
  29.4 0.2 collective-permute-start.14
  29.6 0.3 stay.2.refs_0_
  29.9 0.3 load.3
  30.3 0.6 keep_t.1
  30.9 0.2 collective-permute-done.14.refs_4_
  31.2 0.2 pair.2
  31.4 0.2 collective-permute-start.15
  31.6 1.4 %collective-permute-start.21 = (bf16[384,256]{1,0:T(8,128)(2,1)S(1)}, bf16[384,256]{1,0:T(8,128)(2,1)S(1)}, u32[]{:S(2)}, u32[]{:S(2)}) collective-permute-start(bf16[384,256]{1,0:T(8,128)(2,1)S(1)} %get-tuple-element.115), channel_id=1, source_target_pairs={{0,3},{1,2},{2,1},{3,0},{4,7},{5,6},{6,5},{7,4},{8,11},{9,10},{10,... | collective-permute-start | bytes 589832 | tf_op jit(solution)/shard_map/ppermute | solution.py:15
  33.0 1.4 %collective-permute-start.22 = (bf16[384,256]{1,0:T(8,128)(2,1)S(1)}, bf16[384,256]{1,0:T(8,128)(2,1)S(1)}, u32[]{:S(2)}, u32[]{:S(2)}) collective-permute-start(bf16[384,256]{1,0:T(8,128)(2,1)S(1)} %get-tuple-element.116), channel_id=1, source_target_pairs={{0,2},{1,3},{2,0},{3,1},{4,6},{5,7},{6,4},{7,5},{8,10},{9,11},{10,... | collective-permute-start | bytes 589832 | tf_op jit(solution)/shard_map/ppermute | solution.py:15
  34.4 0.7 collective-permute-start.23
  35.1 1.7 %forward_s.1 = (bf16[2,4,192,256]{3,2,1,0:T(8,128)(2,1)S(1)}, bf16[192,512]{1,0:T(8,128)(2,1)S(1)}, bf16[192,512]{1,0:T(8,128)(2,1)S(1)}, f32[192,512]{1,0:T(8,128)S(1)}, f32[192,512]{1,0:T(8,128)S(1)}) custom-call(bf16[192,2048]{1,0:T(8,128)(2,1)S(1)} %join.3.refs_0_.refs_5_, bf16[192,2048]{1,0:T(8,128)(2,1)S(1)} %collective-permute-done.15.refs_1_.refs_6_, ...), custom_call_target="tpu_custom_call" | custom-call | tf_op jit(solution)/shard_map/forward_s/pallas_call | solution.py:172
  36.9 1.4 %keep_s.1 = (bf16[4,192,256]{2,1,0:T(8,128)(2,1)S(1)}, bf16[4,192,256]{2,1,0:T(8,128)(2,1)S(1)}, bf16[2048,384]{1,0:T(8,128)(2,1)S(1)}, bf16[512,384]{1,0:T(8,128)(2,1)S(1)}, f32[384,512]{1,0:T(8,128)S(1)}) custom-call(bf16[192,512]{1,0:T(8,128)(2,1)S(1)} %get-tuple-element.104.refs_0_, bf16[192,512]{1,0:T(8,128)(2,1)S(1)} %get-tuple-element.105.refs_1_, ...), custom_call_target="tpu_custom_call" | custom-call | flops 25769803776 | tf_op jit(solution)/shard_map/keep_s/pallas_call | solution.py:172
  38.3 0.9 %collective-permute-done.16.refs_2_ = bf16[2,4,192,256]{3,2,1,0:T(8,128)(2,1)S(1)} collective-permute-done((bf16[2,4,192,256]{3,2,1,0:T(8,128)(2,1)S(1)}, bf16[2,4,192,256]{3,2,1,0:T(8,128)(2,1)S(1)}, u32[]{:S(2)}, u32[]{:S(2)}) %collective-permute-start.16) | collective-permute-done | bytes 786464 | tf_op jit(solution)/shard_map/ppermute | solution.py:15
  39.2 0.2 pair.3
  39.4 1.4 %collective-permute-start.17 = (bf16[384,256]{1,0:T(8,128)(2,1)S(1)}, bf16[384,256]{1,0:T(8,128)(2,1)S(1)}, u32[]{:S(2)}, u32[]{:S(2)}) collective-permute-start(bf16[384,256]{1,0:T(8,128)(2,1)S(1)} %get-tuple-element.112), channel_id=1, source_target_pairs={{0,3},{1,2},{2,1},{3,0},{4,7},{5,6},{6,5},{7,4},{8,11},{9,10},{10,... | collective-permute-start | bytes 589832 | tf_op jit(solution)/shard_map/ppermute | solution.py:15
  40.8 1.1 %collective-permute-done.20.refs_1_ = s32[2,128]{1,0:T(2,128)S(1)} collective-permute-done((s32[2,128]{1,0:T(2,128)S(1)}, s32[2,128]{1,0:T(2,128)S(1)}, u32[]{:S(2)}, u32[]{:S(2)}) %collective-permute-start.20) | collective-permute-done | bytes 1056 | tf_op jit(solution)/shard_map/ppermute | solution.py:15
  42.0 0.4 maps.1.refs_0_
  42.4 2.1 %collective-permute-done.22.refs_2_ = bf16[384,256]{1,0:T(8,128)(2,1)S(1)} collective-permute-done((bf16[384,256]{1,0:T(8,128)(2,1)S(1)}, bf16[384,256]{1,0:T(8,128)(2,1)S(1)}, u32[]{:S(2)}, u32[]{:S(2)}) %collective-permute-start.22) | collective-permute-done | bytes 196640 | tf_op jit(solution)/shard_map/ppermute | solution.py:15
  44.7 0.2 collective-permute-start.24
  44.9 1.5 %collective-permute-start.25 = (bf16[96,256]{1,0:T(8,128)(2,1)S(1)}, bf16[96,256]{1,0:T(8,128)(2,1)S(1)}, u32[]{:S(2)}, u32[]{:S(2)}) collective-permute-start(bf16[96,256]{1,0:T(8,128)(2,1)S(1)} %get-tuple-element.123), channel_id=1, source_target_pairs={{0,24},{4,28},{8,16},{12,20},{16,8},{20,12},{24,0},{28,4},{1,25},{... | collective-permute-start | bytes 147464 | tf_op jit(solution)/shard_map/ppermute | solution.py:15
  46.4 1.8 %collective-permute-done.17.refs_1_ = bf16[384,256]{1,0:T(8,128)(2,1)S(1)} collective-permute-done((bf16[384,256]{1,0:T(8,128)(2,1)S(1)}, bf16[384,256]{1,0:T(8,128)(2,1)S(1)}, u32[]{:S(2)}, u32[]{:S(2)}) %collective-permute-start.17) | collective-permute-done | bytes 196640 | tf_op jit(solution)/shard_map/ppermute | solution.py:15
  48.2 1.5 %collective-permute-start.18 = (bf16[384,256]{1,0:T(8,128)(2,1)S(1)}, bf16[384,256]{1,0:T(8,128)(2,1)S(1)}, u32[]{:S(2)}, u32[]{:S(2)}) collective-permute-start(bf16[384,256]{1,0:T(8,128)(2,1)S(1)} %get-tuple-element.113), channel_id=1, source_target_pairs={{0,2},{1,3},{2,0},{3,1},{4,6},{5,7},{6,4},{7,5},{8,10},{9,11},{10,... | collective-permute-start | bytes 589832 | tf_op jit(solution)/shard_map/ppermute | solution.py:15
  49.7 0.4 collective-permute-start.19
  50.1 0.8 collective-permute-done.24.refs_1_
  50.8 0.3 collective-permute-done.25.refs_2_
  51.2 1.1 %collective-permute-done.26.refs_3_ = bf16[96,256]{1,0:T(8,128)(2,1)S(1)} collective-permute-done((bf16[96,256]{1,0:T(8,128)(2,1)S(1)}, bf16[96,256]{1,0:T(8,128)(2,1)S(1)}, u32[]{:S(2)}, u32[]{:S(2)}) %collective-permute-start.26) | collective-permute-done | bytes 49184 | tf_op jit(solution)/shard_map/ppermute | solution.py:15
  52.2 0.2 home.1
  52.4 0.4 collective-permute-start.27
  52.8 2.1 %collective-permute-start.28 = (bf16[96,256]{1,0:T(8,128)(2,1)S(1)}, bf16[96,256]{1,0:T(8,128)(2,1)S(1)}, u32[]{:S(2)}, u32[]{:S(2)}) collective-permute-start(bf16[96,256]{1,0:T(8,128)(2,1)S(1)} %get-tuple-element.128), channel_id=1, source_target_pairs={{0,24},{4,28},{8,16},{12,20},{16,8},{20,12},{24,0},{28,4},{1,25},{... | collective-permute-start | bytes 147464 | tf_op jit(solution)/shard_map/ppermute | solution.py:15
  54.9 1.1 %collective-permute-start.29 = (bf16[96,256]{1,0:T(8,128)(2,1)S(1)}, bf16[96,256]{1,0:T(8,128)(2,1)S(1)}, u32[]{:S(2)}, u32[]{:S(2)}) collective-permute-start(bf16[96,256]{1,0:T(8,128)(2,1)S(1)} %get-tuple-element.129), channel_id=1, source_target_pairs={{0,8},{4,12},{8,0},{12,4},{16,24},{20,28},{24,16},{28,20},{1,9},{5... | collective-permute-start | bytes 147464 | tf_op jit(solution)/shard_map/ppermute | solution.py:15
  56.0 2.1 %collective-permute-done.27.refs_4_ = bf16[96,256]{1,0:T(8,128)(2,1)S(1)} collective-permute-done((bf16[96,256]{1,0:T(8,128)(2,1)S(1)}, bf16[96,256]{1,0:T(8,128)(2,1)S(1)}, u32[]{:S(2)}, u32[]{:S(2)}) %collective-permute-start.27) | collective-permute-done | bytes 49184 | tf_op jit(solution)/shard_map/ppermute | solution.py:15
  58.1 0.8 collective-permute-done.28.refs_5_
  58.8 0.5 collective-permute-done.29.refs_6_
  59.5 1.5 %collective-permute-start.32 = (bf16[384,256]{1,0:T(8,128)(2,1)S(1)}, bf16[384,256]{1,0:T(8,128)(2,1)S(1)}, u32[]{:S(2)}, u32[]{:S(2)}) collective-permute-start(bf16[384,256]{1,0:T(8,128)(2,1)S(1)} %shard_map.96.refs_0_), channel_id=1, source_target_pairs={{0,3},{1,2},{2,1},{3,0},{4,7},{5,6},{6,5},{7,4},{8,11},{9,10},{10,... | collective-permute-start | bytes 589832 | tf_op jit(solution)/shard_map/ppermute | solution.py:15
  61.1 1.5 %collective-permute-start.31 = (bf16[384,256]{1,0:T(8,128)(2,1)S(1)}, bf16[384,256]{1,0:T(8,128)(2,1)S(1)}, u32[]{:S(2)}, u32[]{:S(2)}) collective-permute-start(bf16[384,256]{1,0:T(8,128)(2,1)S(1)} %shard_map.96.refs_0_), channel_id=1, source_target_pairs={{0,2},{1,3},{2,0},{3,1},{4,6},{5,7},{6,4},{7,5},{8,10},{9,11},{10,... | collective-permute-start | bytes 589832 | tf_op jit(solution)/shard_map/ppermute | solution.py:15
  62.6 0.5 collective-permute-start.30
  63.1 0.6 early.3
  63.7 4.5 %collective-permute-done.32.refs_0_ = bf16[384,256]{1,0:T(8,128)(2,1)S(1)} collective-permute-done((bf16[384,256]{1,0:T(8,128)(2,1)S(1)}, bf16[384,256]{1,0:T(8,128)(2,1)S(1)}, u32[]{:S(2)}, u32[]{:S(2)}) %collective-permute-start.32) | collective-permute-done | bytes 196640 | tf_op jit(solution)/shard_map/ppermute | solution.py:15
  68.2 0.4 early.4
  68.7 3.3 %collective-permute-done.31.refs_1_ = bf16[384,256]{1,0:T(8,128)(2,1)S(1)} collective-permute-done((bf16[384,256]{1,0:T(8,128)(2,1)S(1)}, bf16[384,256]{1,0:T(8,128)(2,1)S(1)}, u32[]{:S(2)}, u32[]{:S(2)}) %collective-permute-start.31) | collective-permute-done | bytes 196640 | tf_op jit(solution)/shard_map/ppermute | solution.py:15
  72.0 0.5 collective-permute-start.35
  72.5 0.9 %early.5 = (f32[384,512]{1,0:T(8,128)S(1)}, bf16[512,256]{1,0:T(8,128)(2,1)S(1)}, bf16[512,256]{1,0:T(8,128)(2,1)S(1)}, bf16[512,256]{1,0:T(8,128)(2,1)S(1)}) custom-call(bf16[384,256]{1,0:T(8,128)(2,1)S(1)} %collective-permute-done.30.refs_0_, bf16[384,256]{1,0:T(8,128)(2,1)S(1)} %collective-permute-done.31.refs_1_, ...), custom_call_target="tpu_custom_call" | custom-call | tf_op jit(solution)/shard_map/early/pallas_call | solution.py:172
  73.4 0.3 collective-permute-done.35.refs_1_
  73.7 2.8 %last.1 = (bf16[2048,512]{1,0:T(8,128)(2,1)}, bf16[512,2048]{1,0:T(8,128)(2,1)}) custom-call(bf16[384,256]{1,0:T(8,128)(2,1)S(1)} %collective-permute-done.34.refs_0_, bf16[384,256]{1,0:T(8,128)(2,1)S(1)} %collective-permute-done.35.refs_1_, bf16[512,256]{1,0:T(8,128)(2,1)S(1)} %get-tuple-element.137.refs_2_, ...), custom_call_target="tpu_custom_call" | custom-call | tf_op jit(solution)/shard_map/last/pallas_call | solution.py:172
  (52 shorter events, 1.0 us)
Async XLA Ops:
  2.5 9.2 %collective-permute-start.6 = (bf16[48,512]{1,0:T(8,128)(2,1)}, bf16[48,512]{1,0:T(8,128)(2,1)S(1)}, u32[]{:S(2)}, u32[]{:S(2)}) collective-permute-start(bf16[48,512]{1,0:T(8,128)(2,1)} %get-tuple-element.79), channel_id=1, source_target_pairs={{0,16},{4,20},{8,24},{12,28},{16,0},{20,4},{24,8},{28,12},{1,17},{... | collective-permute-start | bytes 147464 | tf_op jit(solution)/shard_map/ppermute | solution.py:15
  6.6 8.2 %collective-permute-start.7 = (bf16[48,512]{1,0:T(8,128)(2,1)}, bf16[48,512]{1,0:T(8,128)(2,1)S(1)}, u32[]{:S(2)}, u32[]{:S(2)}) collective-permute-start(bf16[48,512]{1,0:T(8,128)(2,1)} %get-tuple-element.80), channel_id=1, source_target_pairs={{0,24},{4,28},{8,16},{12,20},{16,8},{20,12},{24,0},{28,4},{1,25},{... | collective-permute-start | bytes 147464 | tf_op jit(solution)/shard_map/ppermute | solution.py:15
  8.0 6.8 %collective-permute-start.8 = (bf16[48,512]{1,0:T(8,128)(2,1)}, bf16[48,512]{1,0:T(8,128)(2,1)S(1)}, u32[]{:S(2)}, u32[]{:S(2)}) collective-permute-start(bf16[48,512]{1,0:T(8,128)(2,1)} %get-tuple-element.81), channel_id=1, source_target_pairs={{0,8},{4,12},{8,0},{12,4},{16,24},{20,28},{24,16},{28,20},{1,9},{5... | collective-permute-start | bytes 147464 | tf_op jit(solution)/shard_map/ppermute | solution.py:15
  8.2 9.7 %collective-permute-start = (bf16[48,512]{1,0:T(8,128)(2,1)}, bf16[48,512]{1,0:T(8,128)(2,1)S(1)}, u32[]{:S(2)}, u32[]{:S(2)}) collective-permute-start(bf16[48,512]{1,0:T(8,128)(2,1)} %get-tuple-element.75), channel_id=1, source_target_pairs={{0,8},{4,12},{8,0},{12,4},{16,24},{20,28},{24,16},{28,20},{1,9},{5... | collective-permute-start | bytes 147464 | tf_op jit(solution)/shard_map/ppermute | solution.py:15
  10.0 8.4 %collective-permute-start.1 = (bf16[48,512]{1,0:T(8,128)(2,1)}, bf16[48,512]{1,0:T(8,128)(2,1)S(1)}, u32[]{:S(2)}, u32[]{:S(2)}) collective-permute-start(bf16[48,512]{1,0:T(8,128)(2,1)} %get-tuple-element.76), channel_id=1, source_target_pairs={{0,16},{4,20},{8,24},{12,28},{16,0},{20,4},{24,8},{28,12},{1,17},{... | collective-permute-start | bytes 147464 | tf_op jit(solution)/shard_map/ppermute | solution.py:15
  11.7 6.7 %collective-permute-start.2 = (bf16[48,512]{1,0:T(8,128)(2,1)}, bf16[48,512]{1,0:T(8,128)(2,1)S(1)}, u32[]{:S(2)}, u32[]{:S(2)}) collective-permute-start(bf16[48,512]{1,0:T(8,128)(2,1)} %get-tuple-element.77), channel_id=1, source_target_pairs={{0,24},{4,28},{8,16},{12,20},{16,8},{20,12},{24,0},{28,4},{1,25},{... | collective-permute-start | bytes 147464 | tf_op jit(solution)/shard_map/ppermute | solution.py:15
  14.8 6.7 %copy-start = (bf16[128,2048]{1,0:T(8,128)(2,1)S(1)}, bf16[128,2048]{1,0:T(8,128)(2,1)}, u32[]{:S(2)}) copy-start(bf16[128,2048]{1,0:T(8,128)(2,1)} %refs_0_.4) | copy-start | bytes 1572868
  14.8 6.7 %copy-start.7 = (s32[128,1]{0,1:T(1,128)S(1)}, s32[128,1]{0,1:T(1,128)}, u32[]{:S(2)}) copy-start(s32[128,1]{0,1:T(1,128)} %param.10) | copy-start | bytes 1540
  14.8 7.4 %collective-permute-start.11 = (bf16[144,512]{1,0:T(8,128)(2,1)S(1)}, bf16[144,512]{1,0:T(8,128)(2,1)S(1)}, u32[]{:S(2)}, u32[]{:S(2)}) collective-permute-start(bf16[144,512]{1,0:T(8,128)(2,1)S(1)} %stack.3.refs_1_), channel_id=1, source_target_pairs={{0,1},{1,0},{2,3},{3,2},{4,5},{5,4},{6,7},{7,6},{8,9},{9,8},{10,11... | collective-permute-start | bytes 442376 | tf_op jit(solution)/shard_map/ppermute | solution.py:15
  16.4 9.6 %collective-permute-start.10 = (bf16[144,512]{1,0:T(8,128)(2,1)S(1)}, bf16[144,512]{1,0:T(8,128)(2,1)S(1)}, u32[]{:S(2)}, u32[]{:S(2)}) collective-permute-start(bf16[144,512]{1,0:T(8,128)(2,1)S(1)} %stack.3.refs_1_), channel_id=1, source_target_pairs={{0,2},{1,3},{2,0},{3,1},{4,6},{5,7},{6,4},{7,5},{8,10},{9,11},{10,... | collective-permute-start | bytes 442376 | tf_op jit(solution)/shard_map/ppermute | solution.py:15
  17.9 8.1 %collective-permute-start.9 = (bf16[144,512]{1,0:T(8,128)(2,1)S(1)}, bf16[144,512]{1,0:T(8,128)(2,1)S(1)}, u32[]{:S(2)}, u32[]{:S(2)}) collective-permute-start(bf16[144,512]{1,0:T(8,128)(2,1)S(1)} %stack.3.refs_1_), channel_id=1, source_target_pairs={{0,3},{1,2},{2,1},{3,0},{4,7},{5,6},{6,5},{7,4},{8,11},{9,10},{10,... | collective-permute-start | bytes 442376 | tf_op jit(solution)/shard_map/ppermute | solution.py:15
  18.4 3.5 %copy-start.2 = (bf16[1,2048,512]{2,1,0:T(8,128)(2,1)S(1)}, bf16[1,2048,512]{2,1,0:T(8,128)(2,1)}, u32[]{:S(2)}) copy-start(bf16[1,2048,512]{2,1,0:T(8,128)(2,1)} %param.12) | copy-start | bytes 6291460
  18.4 3.5 %copy-start.3 = (bf16[1,512,2048]{2,1,0:T(8,128)(2,1)S(1)}, bf16[1,512,2048]{2,1,0:T(8,128)(2,1)}, u32[]{:S(2)}) copy-start(bf16[1,512,2048]{2,1,0:T(8,128)(2,1)} %param.13) | copy-start | bytes 6291460
  18.4 12.4 %collective-permute-start.5 = (bf16[144,512]{1,0:T(8,128)(2,1)S(1)}, bf16[144,512]{1,0:T(8,128)(2,1)S(1)}, u32[]{:S(2)}, u32[]{:S(2)}) collective-permute-start(bf16[144,512]{1,0:T(8,128)(2,1)S(1)} %stack.2.refs_1_), channel_id=1, source_target_pairs={{0,1},{1,0},{2,3},{3,2},{4,5},{5,4},{6,7},{7,6},{8,9},{9,8},{10,11... | collective-permute-start | bytes 442376 | tf_op jit(solution)/shard_map/ppermute | solution.py:15
  20.0 10.9 %collective-permute-start.4 = (bf16[144,512]{1,0:T(8,128)(2,1)S(1)}, bf16[144,512]{1,0:T(8,128)(2,1)S(1)}, u32[]{:S(2)}, u32[]{:S(2)}) collective-permute-start(bf16[144,512]{1,0:T(8,128)(2,1)S(1)} %stack.2.refs_1_), channel_id=1, source_target_pairs={{0,2},{1,3},{2,0},{3,1},{4,6},{5,7},{6,4},{7,5},{8,10},{9,11},{10,... | collective-permute-start | bytes 442376 | tf_op jit(solution)/shard_map/ppermute | solution.py:15
  22.2 8.7 %collective-permute-start.3 = (bf16[144,512]{1,0:T(8,128)(2,1)S(1)}, bf16[144,512]{1,0:T(8,128)(2,1)S(1)}, u32[]{:S(2)}, u32[]{:S(2)}) collective-permute-start(bf16[144,512]{1,0:T(8,128)(2,1)S(1)} %stack.2.refs_1_), channel_id=1, source_target_pairs={{0,3},{1,2},{2,1},{3,0},{4,7},{5,6},{6,5},{7,4},{8,11},{9,10},{10,... | collective-permute-start | bytes 442376 | tf_op jit(solution)/shard_map/ppermute | solution.py:15
  26.1 2.4 %collective-permute-start.12 = (bf16[192,2048]{1,0:T(8,128)(2,1)S(1)}, bf16[192,2048]{1,0:T(8,128)(2,1)S(1)}, u32[]{:S(2)}, u32[]{:S(2)}) collective-permute-start(bf16[192,2048]{1,0:T(8,128)(2,1)S(1)} %join.2.refs_0_), channel_id=1, source_target_pairs={{0,4},{4,0},{8,12},{12,8},{16,20},{20,16},{24,28},{28,24},{1,5},{5... | collective-permute-start | bytes 2359304 | tf_op jit(solution)/shard_map/ppermute | solution.py:15
  27.1 2.5 %copy-start.1 = (bf16[128,2048]{1,0:T(8,128)(2,1)S(1)}, bf16[128,2048]{1,0:T(8,128)(2,1)}, u32[]{:S(2)}) copy-start(bf16[128,2048]{1,0:T(8,128)(2,1)} %refs_1_.1) | copy-start | bytes 1572868
  27.1 2.5 %copy-start.6 = (s32[128,1]{0,1:T(1,128)S(1)}, s32[128,1]{0,1:T(1,128)}, u32[]{:S(2)}) copy-start(s32[128,1]{0,1:T(1,128)} %param.11) | copy-start | bytes 1540
  27.1 2.8 %copy-start.4 = (bf16[1,2048,512]{2,1,0:T(8,128)(2,1)S(1)}, bf16[1,2048,512]{2,1,0:T(8,128)(2,1)}, u32[]{:S(2)}) copy-start(bf16[1,2048,512]{2,1,0:T(8,128)(2,1)} %param.14) | copy-start | bytes 6291460
  27.1 2.8 %copy-start.5 = (bf16[1,512,2048]{2,1,0:T(8,128)(2,1)S(1)}, bf16[1,512,2048]{2,1,0:T(8,128)(2,1)}, u32[]{:S(2)}) copy-start(bf16[1,512,2048]{2,1,0:T(8,128)(2,1)} %param.15) | copy-start | bytes 6291460
  27.1 3.8 %collective-permute-start.13 = (bf16[1,4,192,256]{3,2,1,0:T(8,128)(2,1)S(1)}, bf16[1,4,192,256]{3,2,1,0:T(8,128)(2,1)S(1)}, u32[]{:S(2)}, u32[]{:S(2)}) collective-permute-start(bf16[1,4,192,256]{3,2,1,0:T(8,128)(2,1)S(1)} %get-tuple-element.96), channel_id=1, source_target_pairs={{0,4},{4,0},{8,12},{12,8},{16,20},{20,16},{24,28},{28,24},{1,5},{5... | collective-permute-start | bytes 1179656 | tf_op jit(solution)/shard_map/ppermute | solution.py:15
  29.4 1.8 %collective-permute-start.14 = (bf16[1,4,192,256]{3,2,1,0:T(8,128)(2,1)S(1)}, bf16[1,4,192,256]{3,2,1,0:T(8,128)(2,1)S(1)}, u32[]{:S(2)}, u32[]{:S(2)}) collective-permute-start(bf16[1,4,192,256]{3,2,1,0:T(8,128)(2,1)S(1)} %get-tuple-element.97), channel_id=1, source_target_pairs={{0,4},{4,0},{8,12},{12,8},{16,20},{20,16},{24,28},{28,24},{1,5},{5... | collective-permute-start | bytes 1179656 | tf_op jit(solution)/shard_map/ppermute | solution.py:15
  31.4 3.7 %collective-permute-start.15 = (bf16[192,2048]{1,0:T(8,128)(2,1)S(1)}, bf16[192,2048]{1,0:T(8,128)(2,1)S(1)}, u32[]{:S(2)}, u32[]{:S(2)}) collective-permute-start(bf16[192,2048]{1,0:T(8,128)(2,1)S(1)} %join.3.refs_0_.refs_5_), channel_id=1, source_target_pairs={{0,4},{4,0},{8,12},{12,8},{16,20},{20,16},{24,28},{28,24},{1,5},{5... | collective-permute-start | bytes 2359304 | tf_op jit(solution)/shard_map/ppermute | solution.py:15
  31.6 10.7 %collective-permute-start.21 = (bf16[384,256]{1,0:T(8,128)(2,1)S(1)}, bf16[384,256]{1,0:T(8,128)(2,1)S(1)}, u32[]{:S(2)}, u32[]{:S(2)}) collective-permute-start(bf16[384,256]{1,0:T(8,128)(2,1)S(1)} %get-tuple-element.115), channel_id=1, source_target_pairs={{0,3},{1,2},{2,1},{3,0},{4,7},{5,6},{6,5},{7,4},{8,11},{9,10},{10,... | collective-permute-start | bytes 589832 | tf_op jit(solution)/shard_map/ppermute | solution.py:15
  33.0 11.4 %collective-permute-start.22 = (bf16[384,256]{1,0:T(8,128)(2,1)S(1)}, bf16[384,256]{1,0:T(8,128)(2,1)S(1)}, u32[]{:S(2)}, u32[]{:S(2)}) collective-permute-start(bf16[384,256]{1,0:T(8,128)(2,1)S(1)} %get-tuple-element.116), channel_id=1, source_target_pairs={{0,2},{1,3},{2,0},{3,1},{4,6},{5,7},{6,4},{7,5},{8,10},{9,11},{10,... | collective-permute-start | bytes 589832 | tf_op jit(solution)/shard_map/ppermute | solution.py:15
  34.4 10.2 %collective-permute-start.23 = (bf16[384,256]{1,0:T(8,128)(2,1)S(1)}, bf16[384,256]{1,0:T(8,128)(2,1)S(1)}, u32[]{:S(2)}, u32[]{:S(2)}) collective-permute-start(bf16[384,256]{1,0:T(8,128)(2,1)S(1)} %get-tuple-element.117), channel_id=1, source_target_pairs={{0,1},{1,0},{2,3},{3,2},{4,5},{5,4},{6,7},{7,6},{8,9},{9,8},{10,11... | collective-permute-start | bytes 589832 | tf_op jit(solution)/shard_map/ppermute | solution.py:15
  36.9 2.4 %collective-permute-start.16 = (bf16[2,4,192,256]{3,2,1,0:T(8,128)(2,1)S(1)}, bf16[2,4,192,256]{3,2,1,0:T(8,128)(2,1)S(1)}, u32[]{:S(2)}, u32[]{:S(2)}) collective-permute-start(bf16[2,4,192,256]{3,2,1,0:T(8,128)(2,1)S(1)} %get-tuple-element.110), channel_id=1, source_target_pairs={{0,4},{4,0},{8,12},{12,8},{16,20},{20,16},{24,28},{28,24},{1,5},{5... | collective-permute-start | bytes 2359304 | tf_op jit(solution)/shard_map/ppermute | solution.py:15
  39.4 8.8 %collective-permute-start.17 = (bf16[384,256]{1,0:T(8,128)(2,1)S(1)}, bf16[384,256]{1,0:T(8,128)(2,1)S(1)}, u32[]{:S(2)}, u32[]{:S(2)}) collective-permute-start(bf16[384,256]{1,0:T(8,128)(2,1)S(1)} %get-tuple-element.112), channel_id=1, source_target_pairs={{0,3},{1,2},{2,1},{3,0},{4,7},{5,6},{6,5},{7,4},{8,11},{9,10},{10,... | collective-permute-start | bytes 589832 | tf_op jit(solution)/shard_map/ppermute | solution.py:15
  40.8 1.1 %collective-permute-start.20 = (s32[2,128]{1,0:T(2,128)S(1)}, s32[2,128]{1,0:T(2,128)S(1)}, u32[]{:S(2)}, u32[]{:S(2)}) collective-permute-start(s32[2,128]{1,0:T(2,128)S(1)} %pad_add_fusion.refs_0_), channel_id=1, source_target_pairs={{0,4},{4,0},{8,12},{12,8},{16,20},{20,16},{24,28},{28,24},{1,5},{5... | collective-permute-start | bytes 3080 | tf_op jit(solution)/shard_map/ppermute | solution.py:15
  44.7 6.2 %collective-permute-start.24 = (bf16[96,256]{1,0:T(8,128)(2,1)S(1)}, bf16[96,256]{1,0:T(8,128)(2,1)S(1)}, u32[]{:S(2)}, u32[]{:S(2)}) collective-permute-start(bf16[96,256]{1,0:T(8,128)(2,1)S(1)} %get-tuple-element.122), channel_id=1, source_target_pairs={{0,16},{4,20},{8,24},{12,28},{16,0},{20,4},{24,8},{28,12},{1,17},{... | collective-permute-start | bytes 147464 | tf_op jit(solution)/shard_map/ppermute | solution.py:15
  44.9 6.3 %collective-permute-start.25 = (bf16[96,256]{1,0:T(8,128)(2,1)S(1)}, bf16[96,256]{1,0:T(8,128)(2,1)S(1)}, u32[]{:S(2)}, u32[]{:S(2)}) collective-permute-start(bf16[96,256]{1,0:T(8,128)(2,1)S(1)} %get-tuple-element.123), channel_id=1, source_target_pairs={{0,24},{4,28},{8,16},{12,20},{16,8},{20,12},{24,0},{28,4},{1,25},{... | collective-permute-start | bytes 147464 | tf_op jit(solution)/shard_map/ppermute | solution.py:15
  48.2 4.1 %collective-permute-start.26 = (bf16[96,256]{1,0:T(8,128)(2,1)S(1)}, bf16[96,256]{1,0:T(8,128)(2,1)S(1)}, u32[]{:S(2)}, u32[]{:S(2)}) collective-permute-start(bf16[96,256]{1,0:T(8,128)(2,1)S(1)} %get-tuple-element.125), channel_id=1, source_target_pairs={{0,8},{4,12},{8,0},{12,4},{16,24},{20,28},{24,16},{28,20},{1,9},{5... | collective-permute-start | bytes 147464 | tf_op jit(solution)/shard_map/ppermute | solution.py:15
  48.2 7.8 %collective-permute-start.18 = (bf16[384,256]{1,0:T(8,128)(2,1)S(1)}, bf16[384,256]{1,0:T(8,128)(2,1)S(1)}, u32[]{:S(2)}, u32[]{:S(2)}) collective-permute-start(bf16[384,256]{1,0:T(8,128)(2,1)S(1)} %get-tuple-element.113), channel_id=1, source_target_pairs={{0,2},{1,3},{2,0},{3,1},{4,6},{5,7},{6,4},{7,5},{8,10},{9,11},{10,... | collective-permute-start | bytes 589832 | tf_op jit(solution)/shard_map/ppermute | solution.py:15
  49.7 6.3 %collective-permute-start.19 = (bf16[384,256]{1,0:T(8,128)(2,1)S(1)}, bf16[384,256]{1,0:T(8,128)(2,1)S(1)}, u32[]{:S(2)}, u32[]{:S(2)}) collective-permute-start(bf16[384,256]{1,0:T(8,128)(2,1)S(1)} %get-tuple-element.114), channel_id=1, source_target_pairs={{0,1},{1,0},{2,3},{3,2},{4,5},{5,4},{6,7},{7,6},{8,9},{9,8},{10,11... | collective-permute-start | bytes 589832 | tf_op jit(solution)/shard_map/ppermute | solution.py:15
  52.4 5.6 %collective-permute-start.27 = (bf16[96,256]{1,0:T(8,128)(2,1)S(1)}, bf16[96,256]{1,0:T(8,128)(2,1)S(1)}, u32[]{:S(2)}, u32[]{:S(2)}) collective-permute-start(bf16[96,256]{1,0:T(8,128)(2,1)S(1)} %get-tuple-element.127), channel_id=1, source_target_pairs={{0,16},{4,20},{8,24},{12,28},{16,0},{20,4},{24,8},{28,12},{1,17},{... | collective-permute-start | bytes 147464 | tf_op jit(solution)/shard_map/ppermute | solution.py:15
  52.8 6.0 %collective-permute-start.28 = (bf16[96,256]{1,0:T(8,128)(2,1)S(1)}, bf16[96,256]{1,0:T(8,128)(2,1)S(1)}, u32[]{:S(2)}, u32[]{:S(2)}) collective-permute-start(bf16[96,256]{1,0:T(8,128)(2,1)S(1)} %get-tuple-element.128), channel_id=1, source_target_pairs={{0,24},{4,28},{8,16},{12,20},{16,8},{20,12},{24,0},{28,4},{1,25},{... | collective-permute-start | bytes 147464 | tf_op jit(solution)/shard_map/ppermute | solution.py:15
  54.9 4.4 %collective-permute-start.29 = (bf16[96,256]{1,0:T(8,128)(2,1)S(1)}, bf16[96,256]{1,0:T(8,128)(2,1)S(1)}, u32[]{:S(2)}, u32[]{:S(2)}) collective-permute-start(bf16[96,256]{1,0:T(8,128)(2,1)S(1)} %get-tuple-element.129), channel_id=1, source_target_pairs={{0,8},{4,12},{8,0},{12,4},{16,24},{20,28},{24,16},{28,20},{1,9},{5... | collective-permute-start | bytes 147464 | tf_op jit(solution)/shard_map/ppermute | solution.py:15
  59.4 3.6 %collective-permute-start.33 = (bf16[384,256]{1,0:T(8,128)(2,1)S(1)}, bf16[384,256]{1,0:T(8,128)(2,1)S(1)}, u32[]{:S(2)}, u32[]{:S(2)}) collective-permute-start(bf16[384,256]{1,0:T(8,128)(2,1)S(1)} %shard_map.96.refs_0_), channel_id=1, source_target_pairs={{0,4},{4,0},{8,12},{12,8},{16,20},{20,16},{24,28},{28,24},{1,5},{5... | collective-permute-start | bytes 589832 | tf_op jit(solution)/shard_map/ppermute | solution.py:15
  59.5 8.7 %collective-permute-start.32 = (bf16[384,256]{1,0:T(8,128)(2,1)S(1)}, bf16[384,256]{1,0:T(8,128)(2,1)S(1)}, u32[]{:S(2)}, u32[]{:S(2)}) collective-permute-start(bf16[384,256]{1,0:T(8,128)(2,1)S(1)} %shard_map.96.refs_0_), channel_id=1, source_target_pairs={{0,3},{1,2},{2,1},{3,0},{4,7},{5,6},{6,5},{7,4},{8,11},{9,10},{10,... | collective-permute-start | bytes 589832 | tf_op jit(solution)/shard_map/ppermute | solution.py:15
  61.1 10.9 %collective-permute-start.31 = (bf16[384,256]{1,0:T(8,128)(2,1)S(1)}, bf16[384,256]{1,0:T(8,128)(2,1)S(1)}, u32[]{:S(2)}, u32[]{:S(2)}) collective-permute-start(bf16[384,256]{1,0:T(8,128)(2,1)S(1)} %shard_map.96.refs_0_), channel_id=1, source_target_pairs={{0,2},{1,3},{2,0},{3,1},{4,6},{5,7},{6,4},{7,5},{8,10},{9,11},{10,... | collective-permute-start | bytes 589832 | tf_op jit(solution)/shard_map/ppermute | solution.py:15
  62.6 9.4 %collective-permute-start.30 = (bf16[384,256]{1,0:T(8,128)(2,1)S(1)}, bf16[384,256]{1,0:T(8,128)(2,1)S(1)}, u32[]{:S(2)}, u32[]{:S(2)}) collective-permute-start(bf16[384,256]{1,0:T(8,128)(2,1)S(1)} %shard_map.96.refs_0_), channel_id=1, source_target_pairs={{0,1},{1,0},{2,3},{3,2},{4,5},{5,4},{6,7},{7,6},{8,9},{9,8},{10,11... | collective-permute-start | bytes 589832 | tf_op jit(solution)/shard_map/ppermute | solution.py:15
  68.2 4.2 %collective-permute-start.36 = (bf16[384,256]{1,0:T(8,128)(2,1)S(1)}, bf16[384,256]{1,0:T(8,128)(2,1)S(1)}, u32[]{:S(2)}, u32[]{:S(2)}) collective-permute-start(bf16[384,256]{1,0:T(8,128)(2,1)S(1)} %collective-permute-done.32.refs_0_), channel_id=1, source_target_pairs={{0,4},{4,0},{8,12},{12,8},{16,20},{20,16},{24,28},{28,24},{1,5},{5... | collective-permute-start | bytes 589832 | tf_op jit(solution)/shard_map/ppermute | solution.py:15
  72.0 1.4 %collective-permute-start.34 = (bf16[384,256]{1,0:T(8,128)(2,1)S(1)}, bf16[384,256]{1,0:T(8,128)(2,1)S(1)}, u32[]{:S(2)}, u32[]{:S(2)}) collective-permute-start(bf16[384,256]{1,0:T(8,128)(2,1)S(1)} %collective-permute-done.30.refs_0_), channel_id=1, source_target_pairs={{0,4},{4,0},{8,12},{12,8},{16,20},{20,16},{24,28},{28,24},{1,5},{5... | collective-permute-start | bytes 589832 | tf_op jit(solution)/shard_map/ppermute | solution.py:15
  72.0 1.7 %collective-permute-start.35 = (bf16[384,256]{1,0:T(8,128)(2,1)S(1)}, bf16[384,256]{1,0:T(8,128)(2,1)S(1)}, u32[]{:S(2)}, u32[]{:S(2)}) collective-permute-start(bf16[384,256]{1,0:T(8,128)(2,1)S(1)} %collective-permute-done.31.refs_1_), channel_id=1, source_target_pairs={{0,4},{4,0},{8,12},{12,8},{16,20},{20,16},{24,28},{28,24},{1,5},{5... | collective-permute-start | bytes 589832 | tf_op jit(solution)/shard_map/ppermute | solution.py:15

commit v11 on v10

--- a/solution.py
+++ b/solution.py
@@ -617,8 +617,7 @@
         [shape(2 * capacity, piece)] * experts,
         after(sums_t, pieces_s[0], maps),
     )
-    *sent, near, own = home
-    home = [*over_planes([*sent, after(near, sums_s[1])]), own]
+    home = [*over_planes(home[:-1]), home[-1]]
     slots = call(
         lambda *refs: home_kernel(experts, capacity, *refs),
         [shape(2 * capacity, piece)] * experts,
@@ -626,7 +625,8 @@
         flops=4 * plane_rows * width * hid,
         name="home",
     )
-    teachers = [*over_planes(slots[:-1]), slots[-1]]
+    *sent, near, own = slots
+    teachers = [*over_planes([*sent, after(near, sums_s[1])]), own]
     (upstream,) = call(
         lambda *refs: upstream_kernel(columns, experts, loss_scale, *refs),
         [shape(plane_rows, piece)],

time: 76.6 us -> 80.2 us (1.047)
  waiting for transfers between devices: 22.5 us -> 24.3 us
  starting transfers between devices: 38.1 us -> 39.9 us
    ppermute x37, starting transfers between devices: 38.1 us -> 39.9 us  [partner(): lax.ppermute(value, axis, [(i, i ^ mask) for i in range(lax.axis_size(axi...]
    ppermute x37, waiting for transfers between devices: 22.5 us -> 24.3 us  [partner(): lax.ppermute(value, axis, [(i, i ^ mask) for i in range(lax.axis_size(axi...]
  transfers between devices with their start and end apart: 37 -> 37, of which waited for: 17 -> 18; matrix products, arithmetic and copies ran while one was open for 0% -> 0% of each run, Pallas kernels for 13% -> 12%
where the time goes in v11:
time: 80.2 us; the launch traced here: 80 us
  starting transfers between devices  39.9 us (50%)
  waiting for transfers between devices  24.3 us (30%)
  Pallas kernels  14.8 us (18%)
  between operations  0.98 us (1%)
    ppermute x37, starting transfers between devices, partner(): lax.ppermute(value, axis, [(i, i ^ mask) for i in range(lax.axis_size(axi...  39.9 us
    ppermute x37, waiting for transfers between devices, partner(): lax.ppermute(value, axis, [(i, i ^ mask) for i in range(lax.axis_size(axi...  24.3 us
    pallas_call x25, Pallas kernels, call(): pl.pallas_call(kernel, name=name, out_shape=outs, in_specs=in_specs or [V...  14.8 us
  transfers between devices with their start and end apart: 37, of which 18 were waited for; matrix products, arithmetic and copies ran while one was open for 0% of the time, Pallas kernels for 12%

profile of v11, /device:TPU:0, one launch (start us, length us, event | category | flops | bytes accessed | tf_op | source)
XLA Modules:
  0.0 80.0 jit_solution(7253533308540489306)
XLA Ops:
  0.6 1.9 %pack.1 = (bf16[48,512]{1,0:T(8,128)(2,1)}, bf16[48,512]{1,0:T(8,128)(2,1)}, bf16[48,512]{1,0:T(8,128)(2,1)}, bf16[48,512]{1,0:T(8,128)(2,1)}, bf16[48,512]{1,0:T(8,128)(2,1)}, /*index=5*/bf16[48,512]{1,0:T(8,128)(2,1)}) custom-call(bf16[128,2048]{1,0:T(8,128)(2,1)} %refs_0_.4, bf16[128,2048]{1,0:T(8,128)(2,1)} %refs_1_.1, s32[1,128]{1,0:T(1,128)} %bitcast.15, ...), custom_call_target="tpu_custom_call" | custom-call | tf_op jit(solution)/shard_map/pack/pallas_call | solution.py:172
  2.5 4.1 %collective-permute-start.6 = (bf16[48,512]{1,0:T(8,128)(2,1)}, bf16[48,512]{1,0:T(8,128)(2,1)S(1)}, u32[]{:S(2)}, u32[]{:S(2)}) collective-permute-start(bf16[48,512]{1,0:T(8,128)(2,1)} %get-tuple-element.79), channel_id=1, source_target_pairs={{0,16},{4,20},{8,24},{12,28},{16,0},{20,4},{24,8},{28,12},{1,17},{... | collective-permute-start | bytes 147464 | tf_op jit(solution)/shard_map/ppermute | solution.py:15
  6.6 1.3 %collective-permute-start.7 = (bf16[48,512]{1,0:T(8,128)(2,1)}, bf16[48,512]{1,0:T(8,128)(2,1)S(1)}, u32[]{:S(2)}, u32[]{:S(2)}) collective-permute-start(bf16[48,512]{1,0:T(8,128)(2,1)} %get-tuple-element.80), channel_id=1, source_target_pairs={{0,24},{4,28},{8,16},{12,20},{16,8},{20,12},{24,0},{28,4},{1,25},{... | collective-permute-start | bytes 147464 | tf_op jit(solution)/shard_map/ppermute | solution.py:15
  8.0 0.2 collective-permute-start.8
  8.2 1.8 %collective-permute-start = (bf16[48,512]{1,0:T(8,128)(2,1)}, bf16[48,512]{1,0:T(8,128)(2,1)S(1)}, u32[]{:S(2)}, u32[]{:S(2)}) collective-permute-start(bf16[48,512]{1,0:T(8,128)(2,1)} %get-tuple-element.75), channel_id=1, source_target_pairs={{0,8},{4,12},{8,0},{12,4},{16,24},{20,28},{24,16},{28,20},{1,9},{5... | collective-permute-start | bytes 147464 | tf_op jit(solution)/shard_map/ppermute | solution.py:15
  10.0 1.7 %collective-permute-start.1 = (bf16[48,512]{1,0:T(8,128)(2,1)}, bf16[48,512]{1,0:T(8,128)(2,1)S(1)}, u32[]{:S(2)}, u32[]{:S(2)}) collective-permute-start(bf16[48,512]{1,0:T(8,128)(2,1)} %get-tuple-element.76), channel_id=1, source_target_pairs={{0,16},{4,20},{8,24},{12,28},{16,0},{20,4},{24,8},{28,12},{1,17},{... | collective-permute-start | bytes 147464 | tf_op jit(solution)/shard_map/ppermute | solution.py:15
  11.7 3.1 %collective-permute-start.2 = (bf16[48,512]{1,0:T(8,128)(2,1)}, bf16[48,512]{1,0:T(8,128)(2,1)S(1)}, u32[]{:S(2)}, u32[]{:S(2)}) collective-permute-start(bf16[48,512]{1,0:T(8,128)(2,1)} %get-tuple-element.77), channel_id=1, source_target_pairs={{0,24},{4,28},{8,16},{12,20},{16,8},{20,12},{24,0},{28,4},{1,25},{... | collective-permute-start | bytes 147464 | tf_op jit(solution)/shard_map/ppermute | solution.py:15
  14.8 1.6 %collective-permute-start.11 = (bf16[144,512]{1,0:T(8,128)(2,1)S(1)}, bf16[144,512]{1,0:T(8,128)(2,1)S(1)}, u32[]{:S(2)}, u32[]{:S(2)}) collective-permute-start(bf16[144,512]{1,0:T(8,128)(2,1)S(1)} %stack.3.refs_1_), channel_id=1, source_target_pairs={{0,1},{1,0},{2,3},{3,2},{4,5},{5,4},{6,7},{7,6},{8,9},{9,8},{10,11... | collective-permute-start | bytes 442376 | tf_op jit(solution)/shard_map/ppermute | solution.py:15
  16.4 1.5 %collective-permute-start.10 = (bf16[144,512]{1,0:T(8,128)(2,1)S(1)}, bf16[144,512]{1,0:T(8,128)(2,1)S(1)}, u32[]{:S(2)}, u32[]{:S(2)}) collective-permute-start(bf16[144,512]{1,0:T(8,128)(2,1)S(1)} %stack.3.refs_1_), channel_id=1, source_target_pairs={{0,2},{1,3},{2,0},{3,1},{4,6},{5,7},{6,4},{7,5},{8,10},{9,11},{10,... | collective-permute-start | bytes 442376 | tf_op jit(solution)/shard_map/ppermute | solution.py:15
  17.9 0.5 collective-permute-start.9
  18.4 1.6 %collective-permute-start.5 = (bf16[144,512]{1,0:T(8,128)(2,1)S(1)}, bf16[144,512]{1,0:T(8,128)(2,1)S(1)}, u32[]{:S(2)}, u32[]{:S(2)}) collective-permute-start(bf16[144,512]{1,0:T(8,128)(2,1)S(1)} %stack.2.refs_1_), channel_id=1, source_target_pairs={{0,1},{1,0},{2,3},{3,2},{4,5},{5,4},{6,7},{7,6},{8,9},{9,8},{10,11... | collective-permute-start | bytes 442376 | tf_op jit(solution)/shard_map/ppermute | solution.py:15
  20.0 1.5 %collective-permute-start.4 = (bf16[144,512]{1,0:T(8,128)(2,1)S(1)}, bf16[144,512]{1,0:T(8,128)(2,1)S(1)}, u32[]{:S(2)}, u32[]{:S(2)}) collective-permute-start(bf16[144,512]{1,0:T(8,128)(2,1)S(1)} %stack.2.refs_1_), channel_id=1, source_target_pairs={{0,2},{1,3},{2,0},{3,1},{4,6},{5,7},{6,4},{7,5},{8,10},{9,11},{10,... | collective-permute-start | bytes 442376 | tf_op jit(solution)/shard_map/ppermute | solution.py:15
  21.5 0.3 stay.3.refs_0_
  21.9 0.3 load.2
  22.2 1.9 %collective-permute-start.3 = (bf16[144,512]{1,0:T(8,128)(2,1)S(1)}, bf16[144,512]{1,0:T(8,128)(2,1)S(1)}, u32[]{:S(2)}, u32[]{:S(2)}) collective-permute-start(bf16[144,512]{1,0:T(8,128)(2,1)S(1)} %stack.2.refs_1_), channel_id=1, source_target_pairs={{0,3},{1,2},{2,1},{3,0},{4,7},{5,6},{6,5},{7,4},{8,11},{9,10},{10,... | collective-permute-start | bytes 442376 | tf_op jit(solution)/shard_map/ppermute | solution.py:15
  24.1 1.9 %collective-permute-done.10.refs_3_ = bf16[144,512]{1,0:T(8,128)(2,1)S(1)} collective-permute-done((bf16[144,512]{1,0:T(8,128)(2,1)S(1)}, bf16[144,512]{1,0:T(8,128)(2,1)S(1)}, u32[]{:S(2)}, u32[]{:S(2)}) %collective-permute-start.10) | collective-permute-done | bytes 147488 | tf_op jit(solution)/shard_map/ppermute | solution.py:15
  26.1 0.9 %forward_t.2 = (bf16[1,4,192,256]{3,2,1,0:T(8,128)(2,1)S(1)}, bf16[192,512]{1,0:T(8,128)(2,1)S(1)}) custom-call(bf16[192,2048]{1,0:T(8,128)(2,1)S(1)} %join.2.refs_0_, bf16[2048,512]{1,0:T(8,128)(2,1)S(1)} %get-tuple-element.84.refs_1_, bf16[512,2048]{1,0:T(8,128)(2,1)S(1)} %get-tuple-element.89.refs_2_), custom_call_target="tpu_custom_call" | custom-call | flops 9663676416 | tf_op jit(solution)/shard_map/forward_t/pallas_call | solution.py:172
  27.1 0.6 collective-permute-start.13
  27.7 0.7 collective-permute-done.12.refs_0_
  28.4 0.9 %forward_t.3 = (bf16[1,4,192,256]{3,2,1,0:T(8,128)(2,1)S(1)}, bf16[192,512]{1,0:T(8,128)(2,1)S(1)}) custom-call(bf16[192,2048]{1,0:T(8,128)(2,1)S(1)} %collective-permute-done.12.refs_0_, bf16[2048,512]{1,0:T(8,128)(2,1)S(1)} %get-tuple-element.84.refs_1_, bf16[512,2048]{1,0:T(8,128)(2,1)S(1)} %get-tuple-element.89.refs_2_), custom_call_target="tpu_custom_call" | custom-call | tf_op jit(solution)/shard_map/forward_t/pallas_call | solution.py:172
  29.4 0.2 collective-permute-start.14
  29.6 0.3 stay.2.refs_0_
  29.9 0.3 load.3
  30.3 0.6 keep_t.1
  30.9 0.2 collective-permute-done.14.refs_4_
  31.2 0.2 pair.2
  31.4 0.2 collective-permute-start.15
  31.6 0.3 collective-permute-start.20
  32.0 1.8 %collective-permute-done.20.refs_1_ = s32[2,128]{1,0:T(2,128)S(1)} collective-permute-done((s32[2,128]{1,0:T(2,128)S(1)}, s32[2,128]{1,0:T(2,128)S(1)}, u32[]{:S(2)}, u32[]{:S(2)}) %collective-permute-start.20) | collective-permute-done | bytes 1056 | tf_op jit(solution)/shard_map/ppermute | solution.py:15
  33.8 0.4 maps.1.refs_0_
  34.1 1.4 %collective-permute-start.21 = (bf16[384,256]{1,0:T(8,128)(2,1)S(1)}, bf16[384,256]{1,0:T(8,128)(2,1)S(1)}, u32[]{:S(2)}, u32[]{:S(2)}) collective-permute-start(bf16[384,256]{1,0:T(8,128)(2,1)S(1)} %get-tuple-element.115), channel_id=1, source_target_pairs={{0,3},{1,2},{2,1},{3,0},{4,7},{5,6},{6,5},{7,4},{8,11},{9,10},{10,... | collective-permute-start | bytes 589832 | tf_op jit(solution)/shard_map/ppermute | solution.py:15
  35.6 1.4 %collective-permute-start.22 = (bf16[384,256]{1,0:T(8,128)(2,1)S(1)}, bf16[384,256]{1,0:T(8,128)(2,1)S(1)}, u32[]{:S(2)}, u32[]{:S(2)}) collective-permute-start(bf16[384,256]{1,0:T(8,128)(2,1)S(1)} %get-tuple-element.116), channel_id=1, source_target_pairs={{0,2},{1,3},{2,0},{3,1},{4,6},{5,7},{6,4},{7,5},{8,10},{9,11},{10,... | collective-permute-start | bytes 589832 | tf_op jit(solution)/shard_map/ppermute | solution.py:15
  37.0 0.7 collective-permute-start.23
  37.7 1.7 %forward_s.1 = (bf16[2,4,192,256]{3,2,1,0:T(8,128)(2,1)S(1)}, bf16[192,512]{1,0:T(8,128)(2,1)S(1)}, bf16[192,512]{1,0:T(8,128)(2,1)S(1)}, f32[192,512]{1,0:T(8,128)S(1)}, f32[192,512]{1,0:T(8,128)S(1)}) custom-call(bf16[192,2048]{1,0:T(8,128)(2,1)S(1)} %join.3.refs_0_.refs_5_, bf16[192,2048]{1,0:T(8,128)(2,1)S(1)} %collective-permute-done.15.refs_1_.refs_6_, ...), custom_call_target="tpu_custom_call" | custom-call | tf_op jit(solution)/shard_map/forward_s/pallas_call | solution.py:172
  39.5 1.4 %keep_s.1 = (bf16[4,192,256]{2,1,0:T(8,128)(2,1)S(1)}, bf16[4,192,256]{2,1,0:T(8,128)(2,1)S(1)}, bf16[2048,384]{1,0:T(8,128)(2,1)S(1)}, bf16[512,384]{1,0:T(8,128)(2,1)S(1)}, f32[384,512]{1,0:T(8,128)S(1)}) custom-call(bf16[192,512]{1,0:T(8,128)(2,1)S(1)} %get-tuple-element.104.refs_0_, bf16[192,512]{1,0:T(8,128)(2,1)S(1)} %get-tuple-element.105.refs_1_, ...), custom_call_target="tpu_custom_call" | custom-call | flops 25769803776 | tf_op jit(solution)/shard_map/keep_s/pallas_call | solution.py:172
  40.9 0.9 %collective-permute-done.16.refs_2_ = bf16[2,4,192,256]{3,2,1,0:T(8,128)(2,1)S(1)} collective-permute-done((bf16[2,4,192,256]{3,2,1,0:T(8,128)(2,1)S(1)}, bf16[2,4,192,256]{3,2,1,0:T(8,128)(2,1)S(1)}, u32[]{:S(2)}, u32[]{:S(2)}) %collective-permute-start.16) | collective-permute-done | bytes 786464 | tf_op jit(solution)/shard_map/ppermute | solution.py:15
  42.0 0.9 %collective-permute-done.21.refs_1_ = bf16[384,256]{1,0:T(8,128)(2,1)S(1)} collective-permute-done((bf16[384,256]{1,0:T(8,128)(2,1)S(1)}, bf16[384,256]{1,0:T(8,128)(2,1)S(1)}, u32[]{:S(2)}, u32[]{:S(2)}) %collective-permute-start.21) | collective-permute-done | bytes 196640 | tf_op jit(solution)/shard_map/ppermute | solution.py:15
  42.9 3.4 %collective-permute-done.22.refs_2_ = bf16[384,256]{1,0:T(8,128)(2,1)S(1)} collective-permute-done((bf16[384,256]{1,0:T(8,128)(2,1)S(1)}, bf16[384,256]{1,0:T(8,128)(2,1)S(1)}, u32[]{:S(2)}, u32[]{:S(2)}) %collective-permute-start.22) | collective-permute-done | bytes 196640 | tf_op jit(solution)/shard_map/ppermute | solution.py:15
  46.5 0.2 collective-permute-start.24
  46.7 1.4 %collective-permute-start.25 = (bf16[96,256]{1,0:T(8,128)(2,1)S(1)}, bf16[96,256]{1,0:T(8,128)(2,1)S(1)}, u32[]{:S(2)}, u32[]{:S(2)}) collective-permute-start(bf16[96,256]{1,0:T(8,128)(2,1)S(1)} %get-tuple-element.123), channel_id=1, source_target_pairs={{0,24},{4,28},{8,16},{12,20},{16,8},{20,12},{24,0},{28,4},{1,25},{... | collective-permute-start | bytes 147464 | tf_op jit(solution)/shard_map/ppermute | solution.py:15
  48.2 1.9 %collective-permute-start.26 = (bf16[96,256]{1,0:T(8,128)(2,1)S(1)}, bf16[96,256]{1,0:T(8,128)(2,1)S(1)}, u32[]{:S(2)}, u32[]{:S(2)}) collective-permute-start(bf16[96,256]{1,0:T(8,128)(2,1)S(1)} %get-tuple-element.124), channel_id=1, source_target_pairs={{0,8},{4,12},{8,0},{12,4},{16,24},{20,28},{24,16},{28,20},{1,9},{5... | collective-permute-start | bytes 147464 | tf_op jit(solution)/shard_map/ppermute | solution.py:15
  50.1 1.3 %collective-permute-start.17 = (bf16[384,256]{1,0:T(8,128)(2,1)S(1)}, bf16[384,256]{1,0:T(8,128)(2,1)S(1)}, u32[]{:S(2)}, u32[]{:S(2)}) collective-permute-start(bf16[384,256]{1,0:T(8,128)(2,1)S(1)} %get-tuple-element.112), channel_id=1, source_target_pairs={{0,3},{1,2},{2,1},{3,0},{4,7},{5,6},{6,5},{7,4},{8,11},{9,10},{10,... | collective-permute-start | bytes 589832 | tf_op jit(solution)/shard_map/ppermute | solution.py:15
  51.3 1.4 %collective-permute-start.18 = (bf16[384,256]{1,0:T(8,128)(2,1)S(1)}, bf16[384,256]{1,0:T(8,128)(2,1)S(1)}, u32[]{:S(2)}, u32[]{:S(2)}) collective-permute-start(bf16[384,256]{1,0:T(8,128)(2,1)S(1)} %get-tuple-element.113), channel_id=1, source_target_pairs={{0,2},{1,3},{2,0},{3,1},{4,6},{5,7},{6,4},{7,5},{8,10},{9,11},{10,... | collective-permute-start | bytes 589832 | tf_op jit(solution)/shard_map/ppermute | solution.py:15
  52.7 0.2 collective-permute-done.24.refs_1_
  53.0 0.6 collective-permute-start.19
  53.6 0.2 home.1
  53.8 1.1 %collective-permute-start.27 = (bf16[96,256]{1,0:T(8,128)(2,1)S(1)}, bf16[96,256]{1,0:T(8,128)(2,1)S(1)}, u32[]{:S(2)}, u32[]{:S(2)}) collective-permute-start(bf16[96,256]{1,0:T(8,128)(2,1)S(1)} %get-tuple-element.126), channel_id=1, source_target_pairs={{0,16},{4,20},{8,24},{12,28},{16,0},{20,4},{24,8},{28,12},{1,17},{... | collective-permute-start | bytes 147464 | tf_op jit(solution)/shard_map/ppermute | solution.py:15
  54.9 1.9 %collective-permute-start.28 = (bf16[96,256]{1,0:T(8,128)(2,1)S(1)}, bf16[96,256]{1,0:T(8,128)(2,1)S(1)}, u32[]{:S(2)}, u32[]{:S(2)}) collective-permute-start(bf16[96,256]{1,0:T(8,128)(2,1)S(1)} %get-tuple-element.127), channel_id=1, source_target_pairs={{0,24},{4,28},{8,16},{12,20},{16,8},{20,12},{24,0},{28,4},{1,25},{... | collective-permute-start | bytes 147464 | tf_op jit(solution)/shard_map/ppermute | solution.py:15
  56.8 2.0 %collective-permute-done.17.refs_1_ = bf16[384,256]{1,0:T(8,128)(2,1)S(1)} collective-permute-done((bf16[384,256]{1,0:T(8,128)(2,1)S(1)}, bf16[384,256]{1,0:T(8,128)(2,1)S(1)}, u32[]{:S(2)}, u32[]{:S(2)}) %collective-permute-start.17) | collective-permute-done | bytes 196640 | tf_op jit(solution)/shard_map/ppermute | solution.py:15
  58.8 0.2 collective-permute-start.29
  59.0 0.9 %collective-permute-done.27.refs_4_ = bf16[96,256]{1,0:T(8,128)(2,1)S(1)} collective-permute-done((bf16[96,256]{1,0:T(8,128)(2,1)S(1)}, bf16[96,256]{1,0:T(8,128)(2,1)S(1)}, u32[]{:S(2)}, u32[]{:S(2)}) %collective-permute-start.27) | collective-permute-done | bytes 49184 | tf_op jit(solution)/shard_map/ppermute | solution.py:15
  59.9 1.0 %collective-permute-done.28.refs_5_ = bf16[96,256]{1,0:T(8,128)(2,1)S(1)} collective-permute-done((bf16[96,256]{1,0:T(8,128)(2,1)S(1)}, bf16[96,256]{1,0:T(8,128)(2,1)S(1)}, u32[]{:S(2)}, u32[]{:S(2)}) %collective-permute-start.28) | collective-permute-done | bytes 49184 | tf_op jit(solution)/shard_map/ppermute | solution.py:15
  61.2 1.8 %collective-permute-done.29.refs_6_ = bf16[96,256]{1,0:T(8,128)(2,1)S(1)} collective-permute-done((bf16[96,256]{1,0:T(8,128)(2,1)S(1)}, bf16[96,256]{1,0:T(8,128)(2,1)S(1)}, u32[]{:S(2)}, u32[]{:S(2)}) %collective-permute-start.29) | collective-permute-done | bytes 49184 | tf_op jit(solution)/shard_map/ppermute | solution.py:15
  63.1 1.4 %collective-permute-start.32 = (bf16[384,256]{1,0:T(8,128)(2,1)S(1)}, bf16[384,256]{1,0:T(8,128)(2,1)S(1)}, u32[]{:S(2)}, u32[]{:S(2)}) collective-permute-start(bf16[384,256]{1,0:T(8,128)(2,1)S(1)} %shard_map.96.refs_0_), channel_id=1, source_target_pairs={{0,3},{1,2},{2,1},{3,0},{4,7},{5,6},{6,5},{7,4},{8,11},{9,10},{10,... | collective-permute-start | bytes 589832 | tf_op jit(solution)/shard_map/ppermute | solution.py:15
  64.5 1.4 %collective-permute-start.31 = (bf16[384,256]{1,0:T(8,128)(2,1)S(1)}, bf16[384,256]{1,0:T(8,128)(2,1)S(1)}, u32[]{:S(2)}, u32[]{:S(2)}) collective-permute-start(bf16[384,256]{1,0:T(8,128)(2,1)S(1)} %shard_map.96.refs_0_), channel_id=1, source_target_pairs={{0,2},{1,3},{2,0},{3,1},{4,6},{5,7},{6,4},{7,5},{8,10},{9,11},{10,... | collective-permute-start | bytes 589832 | tf_op jit(solution)/shard_map/ppermute | solution.py:15
  65.9 0.8 collective-permute-start.30
  66.7 0.6 early.3
  67.3 4.5 %collective-permute-done.32.refs_0_ = bf16[384,256]{1,0:T(8,128)(2,1)S(1)} collective-permute-done((bf16[384,256]{1,0:T(8,128)(2,1)S(1)}, bf16[384,256]{1,0:T(8,128)(2,1)S(1)}, u32[]{:S(2)}, u32[]{:S(2)}) %collective-permute-start.32) | collective-permute-done | bytes 196640 | tf_op jit(solution)/shard_map/ppermute | solution.py:15
  71.8 0.4 early.4
  72.2 3.3 %collective-permute-done.31.refs_1_ = bf16[384,256]{1,0:T(8,128)(2,1)S(1)} collective-permute-done((bf16[384,256]{1,0:T(8,128)(2,1)S(1)}, bf16[384,256]{1,0:T(8,128)(2,1)S(1)}, u32[]{:S(2)}, u32[]{:S(2)}) %collective-permute-start.31) | collective-permute-done | bytes 196640 | tf_op jit(solution)/shard_map/ppermute | solution.py:15
  75.6 0.5 collective-permute-start.35
  76.1 0.9 %early.5 = (f32[384,512]{1,0:T(8,128)S(1)}, bf16[512,256]{1,0:T(8,128)(2,1)S(1)}, bf16[512,256]{1,0:T(8,128)(2,1)S(1)}, bf16[512,256]{1,0:T(8,128)(2,1)S(1)}) custom-call(bf16[384,256]{1,0:T(8,128)(2,1)S(1)} %collective-permute-done.30.refs_0_, bf16[384,256]{1,0:T(8,128)(2,1)S(1)} %collective-permute-done.31.refs_1_, ...), custom_call_target="tpu_custom_call" | custom-call | tf_op jit(solution)/shard_map/early/pallas_call | solution.py:172
  77.0 0.3 collective-permute-done.35.refs_1_
  77.3 2.8 %last.1 = (bf16[2048,512]{1,0:T(8,128)(2,1)}, bf16[512,2048]{1,0:T(8,128)(2,1)}) custom-call(bf16[384,256]{1,0:T(8,128)(2,1)S(1)} %collective-permute-done.34.refs_0_, bf16[384,256]{1,0:T(8,128)(2,1)S(1)} %collective-permute-done.35.refs_1_, bf16[512,256]{1,0:T(8,128)(2,1)S(1)} %get-tuple-element.137.refs_2_, ...), custom_call_target="tpu_custom_call" | custom-call | tf_op jit(solution)/shard_map/last/pallas_call | solution.py:172
  (52 shorter events, 1.3 us)
Async XLA Ops:
  2.5 9.2 %collective-permute-start.6 = (bf16[48,512]{1,0:T(8,128)(2,1)}, bf16[48,512]{1,0:T(8,128)(2,1)S(1)}, u32[]{:S(2)}, u32[]{:S(2)}) collective-permute-start(bf16[48,512]{1,0:T(8,128)(2,1)} %get-tuple-element.79), channel_id=1, source_target_pairs={{0,16},{4,20},{8,24},{12,28},{16,0},{20,4},{24,8},{28,12},{1,17},{... | collective-permute-start | bytes 147464 | tf_op jit(solution)/shard_map/ppermute | solution.py:15
  6.6 8.2 %collective-permute-start.7 = (bf16[48,512]{1,0:T(8,128)(2,1)}, bf16[48,512]{1,0:T(8,128)(2,1)S(1)}, u32[]{:S(2)}, u32[]{:S(2)}) collective-permute-start(bf16[48,512]{1,0:T(8,128)(2,1)} %get-tuple-element.80), channel_id=1, source_target_pairs={{0,24},{4,28},{8,16},{12,20},{16,8},{20,12},{24,0},{28,4},{1,25},{... | collective-permute-start | bytes 147464 | tf_op jit(solution)/shard_map/ppermute | solution.py:15
  8.0 6.8 %collective-permute-start.8 = (bf16[48,512]{1,0:T(8,128)(2,1)}, bf16[48,512]{1,0:T(8,128)(2,1)S(1)}, u32[]{:S(2)}, u32[]{:S(2)}) collective-permute-start(bf16[48,512]{1,0:T(8,128)(2,1)} %get-tuple-element.81), channel_id=1, source_target_pairs={{0,8},{4,12},{8,0},{12,4},{16,24},{20,28},{24,16},{28,20},{1,9},{5... | collective-permute-start | bytes 147464 | tf_op jit(solution)/shard_map/ppermute | solution.py:15
  8.2 9.7 %collective-permute-start = (bf16[48,512]{1,0:T(8,128)(2,1)}, bf16[48,512]{1,0:T(8,128)(2,1)S(1)}, u32[]{:S(2)}, u32[]{:S(2)}) collective-permute-start(bf16[48,512]{1,0:T(8,128)(2,1)} %get-tuple-element.75), channel_id=1, source_target_pairs={{0,8},{4,12},{8,0},{12,4},{16,24},{20,28},{24,16},{28,20},{1,9},{5... | collective-permute-start | bytes 147464 | tf_op jit(solution)/shard_map/ppermute | solution.py:15
  10.0 8.4 %collective-permute-start.1 = (bf16[48,512]{1,0:T(8,128)(2,1)}, bf16[48,512]{1,0:T(8,128)(2,1)S(1)}, u32[]{:S(2)}, u32[]{:S(2)}) collective-permute-start(bf16[48,512]{1,0:T(8,128)(2,1)} %get-tuple-element.76), channel_id=1, source_target_pairs={{0,16},{4,20},{8,24},{12,28},{16,0},{20,4},{24,8},{28,12},{1,17},{... | collective-permute-start | bytes 147464 | tf_op jit(solution)/shard_map/ppermute | solution.py:15
  11.7 6.7 %collective-permute-start.2 = (bf16[48,512]{1,0:T(8,128)(2,1)}, bf16[48,512]{1,0:T(8,128)(2,1)S(1)}, u32[]{:S(2)}, u32[]{:S(2)}) collective-permute-start(bf16[48,512]{1,0:T(8,128)(2,1)} %get-tuple-element.77), channel_id=1, source_target_pairs={{0,24},{4,28},{8,16},{12,20},{16,8},{20,12},{24,0},{28,4},{1,25},{... | collective-permute-start | bytes 147464 | tf_op jit(solution)/shard_map/ppermute | solution.py:15
  14.8 6.7 %copy-start = (bf16[128,2048]{1,0:T(8,128)(2,1)S(1)}, bf16[128,2048]{1,0:T(8,128)(2,1)}, u32[]{:S(2)}) copy-start(bf16[128,2048]{1,0:T(8,128)(2,1)} %refs_0_.4) | copy-start | bytes 1572868
  14.8 6.7 %copy-start.7 = (s32[128,1]{0,1:T(1,128)S(1)}, s32[128,1]{0,1:T(1,128)}, u32[]{:S(2)}) copy-start(s32[128,1]{0,1:T(1,128)} %param.10) | copy-start | bytes 1540
  14.8 7.4 %collective-permute-start.11 = (bf16[144,512]{1,0:T(8,128)(2,1)S(1)}, bf16[144,512]{1,0:T(8,128)(2,1)S(1)}, u32[]{:S(2)}, u32[]{:S(2)}) collective-permute-start(bf16[144,512]{1,0:T(8,128)(2,1)S(1)} %stack.3.refs_1_), channel_id=1, source_target_pairs={{0,1},{1,0},{2,3},{3,2},{4,5},{5,4},{6,7},{7,6},{8,9},{9,8},{10,11... | collective-permute-start | bytes 442376 | tf_op jit(solution)/shard_map/ppermute | solution.py:15
  16.4 9.6 %collective-permute-start.10 = (bf16[144,512]{1,0:T(8,128)(2,1)S(1)}, bf16[144,512]{1,0:T(8,128)(2,1)S(1)}, u32[]{:S(2)}, u32[]{:S(2)}) collective-permute-start(bf16[144,512]{1,0:T(8,128)(2,1)S(1)} %stack.3.refs_1_), channel_id=1, source_target_pairs={{0,2},{1,3},{2,0},{3,1},{4,6},{5,7},{6,4},{7,5},{8,10},{9,11},{10,... | collective-permute-start | bytes 442376 | tf_op jit(solution)/shard_map/ppermute | solution.py:15
  17.9 8.1 %collective-permute-start.9 = (bf16[144,512]{1,0:T(8,128)(2,1)S(1)}, bf16[144,512]{1,0:T(8,128)(2,1)S(1)}, u32[]{:S(2)}, u32[]{:S(2)}) collective-permute-start(bf16[144,512]{1,0:T(8,128)(2,1)S(1)} %stack.3.refs_1_), channel_id=1, source_target_pairs={{0,3},{1,2},{2,1},{3,0},{4,7},{5,6},{6,5},{7,4},{8,11},{9,10},{10,... | collective-permute-start | bytes 442376 | tf_op jit(solution)/shard_map/ppermute | solution.py:15
  18.4 3.5 %copy-start.2 = (bf16[1,2048,512]{2,1,0:T(8,128)(2,1)S(1)}, bf16[1,2048,512]{2,1,0:T(8,128)(2,1)}, u32[]{:S(2)}) copy-start(bf16[1,2048,512]{2,1,0:T(8,128)(2,1)} %param.12) | copy-start | bytes 6291460
  18.4 3.5 %copy-start.3 = (bf16[1,512,2048]{2,1,0:T(8,128)(2,1)S(1)}, bf16[1,512,2048]{2,1,0:T(8,128)(2,1)}, u32[]{:S(2)}) copy-start(bf16[1,512,2048]{2,1,0:T(8,128)(2,1)} %param.13) | copy-start | bytes 6291460
  18.4 12.4 %collective-permute-start.5 = (bf16[144,512]{1,0:T(8,128)(2,1)S(1)}, bf16[144,512]{1,0:T(8,128)(2,1)S(1)}, u32[]{:S(2)}, u32[]{:S(2)}) collective-permute-start(bf16[144,512]{1,0:T(8,128)(2,1)S(1)} %stack.2.refs_1_), channel_id=1, source_target_pairs={{0,1},{1,0},{2,3},{3,2},{4,5},{5,4},{6,7},{7,6},{8,9},{9,8},{10,11... | collective-permute-start | bytes 442376 | tf_op jit(solution)/shard_map/ppermute | solution.py:15
  20.0 10.9 %collective-permute-start.4 = (bf16[144,512]{1,0:T(8,128)(2,1)S(1)}, bf16[144,512]{1,0:T(8,128)(2,1)S(1)}, u32[]{:S(2)}, u32[]{:S(2)}) collective-permute-start(bf16[144,512]{1,0:T(8,128)(2,1)S(1)} %stack.2.refs_1_), channel_id=1, source_target_pairs={{0,2},{1,3},{2,0},{3,1},{4,6},{5,7},{6,4},{7,5},{8,10},{9,11},{10,... | collective-permute-start | bytes 442376 | tf_op jit(solution)/shard_map/ppermute | solution.py:15
  22.2 8.7 %collective-permute-start.3 = (bf16[144,512]{1,0:T(8,128)(2,1)S(1)}, bf16[144,512]{1,0:T(8,128)(2,1)S(1)}, u32[]{:S(2)}, u32[]{:S(2)}) collective-permute-start(bf16[144,512]{1,0:T(8,128)(2,1)S(1)} %stack.2.refs_1_), channel_id=1, source_target_pairs={{0,3},{1,2},{2,1},{3,0},{4,7},{5,6},{6,5},{7,4},{8,11},{9,10},{10,... | collective-permute-start | bytes 442376 | tf_op jit(solution)/shard_map/ppermute | solution.py:15
  26.1 2.4 %collective-permute-start.12 = (bf16[192,2048]{1,0:T(8,128)(2,1)S(1)}, bf16[192,2048]{1,0:T(8,128)(2,1)S(1)}, u32[]{:S(2)}, u32[]{:S(2)}) collective-permute-start(bf16[192,2048]{1,0:T(8,128)(2,1)S(1)} %join.2.refs_0_), channel_id=1, source_target_pairs={{0,4},{4,0},{8,12},{12,8},{16,20},{20,16},{24,28},{28,24},{1,5},{5... | collective-permute-start | bytes 2359304 | tf_op jit(solution)/shard_map/ppermute | solution.py:15
  27.1 2.5 %copy-start.1 = (bf16[128,2048]{1,0:T(8,128)(2,1)S(1)}, bf16[128,2048]{1,0:T(8,128)(2,1)}, u32[]{:S(2)}) copy-start(bf16[128,2048]{1,0:T(8,128)(2,1)} %refs_1_.1) | copy-start | bytes 1572868
  27.1 2.5 %copy-start.6 = (s32[128,1]{0,1:T(1,128)S(1)}, s32[128,1]{0,1:T(1,128)}, u32[]{:S(2)}) copy-start(s32[128,1]{0,1:T(1,128)} %param.11) | copy-start | bytes 1540
  27.1 2.8 %copy-start.4 = (bf16[1,2048,512]{2,1,0:T(8,128)(2,1)S(1)}, bf16[1,2048,512]{2,1,0:T(8,128)(2,1)}, u32[]{:S(2)}) copy-start(bf16[1,2048,512]{2,1,0:T(8,128)(2,1)} %param.14) | copy-start | bytes 6291460
  27.1 2.8 %copy-start.5 = (bf16[1,512,2048]{2,1,0:T(8,128)(2,1)S(1)}, bf16[1,512,2048]{2,1,0:T(8,128)(2,1)}, u32[]{:S(2)}) copy-start(bf16[1,512,2048]{2,1,0:T(8,128)(2,1)} %param.15) | copy-start | bytes 6291460
  27.1 3.8 %collective-permute-start.13 = (bf16[1,4,192,256]{3,2,1,0:T(8,128)(2,1)S(1)}, bf16[1,4,192,256]{3,2,1,0:T(8,128)(2,1)S(1)}, u32[]{:S(2)}, u32[]{:S(2)}) collective-permute-start(bf16[1,4,192,256]{3,2,1,0:T(8,128)(2,1)S(1)} %get-tuple-element.96), channel_id=1, source_target_pairs={{0,4},{4,0},{8,12},{12,8},{16,20},{20,16},{24,28},{28,24},{1,5},{5... | collective-permute-start | bytes 1179656 | tf_op jit(solution)/shard_map/ppermute | solution.py:15
  29.4 1.8 %collective-permute-start.14 = (bf16[1,4,192,256]{3,2,1,0:T(8,128)(2,1)S(1)}, bf16[1,4,192,256]{3,2,1,0:T(8,128)(2,1)S(1)}, u32[]{:S(2)}, u32[]{:S(2)}) collective-permute-start(bf16[1,4,192,256]{3,2,1,0:T(8,128)(2,1)S(1)} %get-tuple-element.97), channel_id=1, source_target_pairs={{0,4},{4,0},{8,12},{12,8},{16,20},{20,16},{24,28},{28,24},{1,5},{5... | collective-permute-start | bytes 1179656 | tf_op jit(solution)/shard_map/ppermute | solution.py:15
  31.4 6.3 %collective-permute-start.15 = (bf16[192,2048]{1,0:T(8,128)(2,1)S(1)}, bf16[192,2048]{1,0:T(8,128)(2,1)S(1)}, u32[]{:S(2)}, u32[]{:S(2)}) collective-permute-start(bf16[192,2048]{1,0:T(8,128)(2,1)S(1)} %join.3.refs_0_.refs_5_), channel_id=1, source_target_pairs={{0,4},{4,0},{8,12},{12,8},{16,20},{20,16},{24,28},{28,24},{1,5},{5... | collective-permute-start | bytes 2359304 | tf_op jit(solution)/shard_map/ppermute | solution.py:15
  31.6 2.1 %collective-permute-start.20 = (s32[2,128]{1,0:T(2,128)S(1)}, s32[2,128]{1,0:T(2,128)S(1)}, u32[]{:S(2)}, u32[]{:S(2)}) collective-permute-start(s32[2,128]{1,0:T(2,128)S(1)} %pad_add_fusion.refs_0_), channel_id=1, source_target_pairs={{0,4},{4,0},{8,12},{12,8},{16,20},{20,16},{24,28},{28,24},{1,5},{5... | collective-permute-start | bytes 3080 | tf_op jit(solution)/shard_map/ppermute | solution.py:15
  34.1 8.8 %collective-permute-start.21 = (bf16[384,256]{1,0:T(8,128)(2,1)S(1)}, bf16[384,256]{1,0:T(8,128)(2,1)S(1)}, u32[]{:S(2)}, u32[]{:S(2)}) collective-permute-start(bf16[384,256]{1,0:T(8,128)(2,1)S(1)} %get-tuple-element.115), channel_id=1, source_target_pairs={{0,3},{1,2},{2,1},{3,0},{4,7},{5,6},{6,5},{7,4},{8,11},{9,10},{10,... | collective-permute-start | bytes 589832 | tf_op jit(solution)/shard_map/ppermute | solution.py:15
  35.6 10.7 %collective-permute-start.22 = (bf16[384,256]{1,0:T(8,128)(2,1)S(1)}, bf16[384,256]{1,0:T(8,128)(2,1)S(1)}, u32[]{:S(2)}, u32[]{:S(2)}) collective-permute-start(bf16[384,256]{1,0:T(8,128)(2,1)S(1)} %get-tuple-element.116), channel_id=1, source_target_pairs={{0,2},{1,3},{2,0},{3,1},{4,6},{5,7},{6,4},{7,5},{8,10},{9,11},{10,... | collective-permute-start | bytes 589832 | tf_op jit(solution)/shard_map/ppermute | solution.py:15
  37.0 9.4 %collective-permute-start.23 = (bf16[384,256]{1,0:T(8,128)(2,1)S(1)}, bf16[384,256]{1,0:T(8,128)(2,1)S(1)}, u32[]{:S(2)}, u32[]{:S(2)}) collective-permute-start(bf16[384,256]{1,0:T(8,128)(2,1)S(1)} %get-tuple-element.117), channel_id=1, source_target_pairs={{0,1},{1,0},{2,3},{3,2},{4,5},{5,4},{6,7},{7,6},{8,9},{9,8},{10,11... | collective-permute-start | bytes 589832 | tf_op jit(solution)/shard_map/ppermute | solution.py:15
  39.4 2.4 %collective-permute-start.16 = (bf16[2,4,192,256]{3,2,1,0:T(8,128)(2,1)S(1)}, bf16[2,4,192,256]{3,2,1,0:T(8,128)(2,1)S(1)}, u32[]{:S(2)}, u32[]{:S(2)}) collective-permute-start(bf16[2,4,192,256]{3,2,1,0:T(8,128)(2,1)S(1)} %get-tuple-element.110), channel_id=1, source_target_pairs={{0,4},{4,0},{8,12},{12,8},{16,20},{20,16},{24,28},{28,24},{1,5},{5... | collective-permute-start | bytes 2359304 | tf_op jit(solution)/shard_map/ppermute | solution.py:15
  46.5 6.5 %collective-permute-start.24 = (bf16[96,256]{1,0:T(8,128)(2,1)S(1)}, bf16[96,256]{1,0:T(8,128)(2,1)S(1)}, u32[]{:S(2)}, u32[]{:S(2)}) collective-permute-start(bf16[96,256]{1,0:T(8,128)(2,1)S(1)} %get-tuple-element.122), channel_id=1, source_target_pairs={{0,16},{4,20},{8,24},{12,28},{16,0},{20,4},{24,8},{28,12},{1,17},{... | collective-permute-start | bytes 147464 | tf_op jit(solution)/shard_map/ppermute | solution.py:15
  46.7 6.8 %collective-permute-start.25 = (bf16[96,256]{1,0:T(8,128)(2,1)S(1)}, bf16[96,256]{1,0:T(8,128)(2,1)S(1)}, u32[]{:S(2)}, u32[]{:S(2)}) collective-permute-start(bf16[96,256]{1,0:T(8,128)(2,1)S(1)} %get-tuple-element.123), channel_id=1, source_target_pairs={{0,24},{4,28},{8,16},{12,20},{16,8},{20,12},{24,0},{28,4},{1,25},{... | collective-permute-start | bytes 147464 | tf_op jit(solution)/shard_map/ppermute | solution.py:15
  48.2 5.4 %collective-permute-start.26 = (bf16[96,256]{1,0:T(8,128)(2,1)S(1)}, bf16[96,256]{1,0:T(8,128)(2,1)S(1)}, u32[]{:S(2)}, u32[]{:S(2)}) collective-permute-start(bf16[96,256]{1,0:T(8,128)(2,1)S(1)} %get-tuple-element.124), channel_id=1, source_target_pairs={{0,8},{4,12},{8,0},{12,4},{16,24},{20,28},{24,16},{28,20},{1,9},{5... | collective-permute-start | bytes 147464 | tf_op jit(solution)/shard_map/ppermute | solution.py:15
  50.1 8.8 %collective-permute-start.17 = (bf16[384,256]{1,0:T(8,128)(2,1)S(1)}, bf16[384,256]{1,0:T(8,128)(2,1)S(1)}, u32[]{:S(2)}, u32[]{:S(2)}) collective-permute-start(bf16[384,256]{1,0:T(8,128)(2,1)S(1)} %get-tuple-element.112), channel_id=1, source_target_pairs={{0,3},{1,2},{2,1},{3,0},{4,7},{5,6},{6,5},{7,4},{8,11},{9,10},{10,... | collective-permute-start | bytes 589832 | tf_op jit(solution)/shard_map/ppermute | solution.py:15
  51.3 9.7 %collective-permute-start.18 = (bf16[384,256]{1,0:T(8,128)(2,1)S(1)}, bf16[384,256]{1,0:T(8,128)(2,1)S(1)}, u32[]{:S(2)}, u32[]{:S(2)}) collective-permute-start(bf16[384,256]{1,0:T(8,128)(2,1)S(1)} %get-tuple-element.113), channel_id=1, source_target_pairs={{0,2},{1,3},{2,0},{3,1},{4,6},{5,7},{6,4},{7,5},{8,10},{9,11},{10,... | collective-permute-start | bytes 589832 | tf_op jit(solution)/shard_map/ppermute | solution.py:15
  53.0 8.2 %collective-permute-start.19 = (bf16[384,256]{1,0:T(8,128)(2,1)S(1)}, bf16[384,256]{1,0:T(8,128)(2,1)S(1)}, u32[]{:S(2)}, u32[]{:S(2)}) collective-permute-start(bf16[384,256]{1,0:T(8,128)(2,1)S(1)} %get-tuple-element.114), channel_id=1, source_target_pairs={{0,1},{1,0},{2,3},{3,2},{4,5},{5,4},{6,7},{7,6},{8,9},{9,8},{10,11... | collective-permute-start | bytes 589832 | tf_op jit(solution)/shard_map/ppermute | solution.py:15
  53.8 6.1 %collective-permute-start.27 = (bf16[96,256]{1,0:T(8,128)(2,1)S(1)}, bf16[96,256]{1,0:T(8,128)(2,1)S(1)}, u32[]{:S(2)}, u32[]{:S(2)}) collective-permute-start(bf16[96,256]{1,0:T(8,128)(2,1)S(1)} %get-tuple-element.126), channel_id=1, source_target_pairs={{0,16},{4,20},{8,24},{12,28},{16,0},{20,4},{24,8},{28,12},{1,17},{... | collective-permute-start | bytes 147464 | tf_op jit(solution)/shard_map/ppermute | solution.py:15
  54.9 6.0 %collective-permute-start.28 = (bf16[96,256]{1,0:T(8,128)(2,1)S(1)}, bf16[96,256]{1,0:T(8,128)(2,1)S(1)}, u32[]{:S(2)}, u32[]{:S(2)}) collective-permute-start(bf16[96,256]{1,0:T(8,128)(2,1)S(1)} %get-tuple-element.127), channel_id=1, source_target_pairs={{0,24},{4,28},{8,16},{12,20},{16,8},{20,12},{24,0},{28,4},{1,25},{... | collective-permute-start | bytes 147464 | tf_op jit(solution)/shard_map/ppermute | solution.py:15
  58.8 4.1 %collective-permute-start.29 = (bf16[96,256]{1,0:T(8,128)(2,1)S(1)}, bf16[96,256]{1,0:T(8,128)(2,1)S(1)}, u32[]{:S(2)}, u32[]{:S(2)}) collective-permute-start(bf16[96,256]{1,0:T(8,128)(2,1)S(1)} %get-tuple-element.129), channel_id=1, source_target_pairs={{0,8},{4,12},{8,0},{12,4},{16,24},{20,28},{24,16},{28,20},{1,9},{5... | collective-permute-start | bytes 147464 | tf_op jit(solution)/shard_map/ppermute | solution.py:15
  63.0 3.6 %collective-permute-start.33 = (bf16[384,256]{1,0:T(8,128)(2,1)S(1)}, bf16[384,256]{1,0:T(8,128)(2,1)S(1)}, u32[]{:S(2)}, u32[]{:S(2)}) collective-permute-start(bf16[384,256]{1,0:T(8,128)(2,1)S(1)} %shard_map.96.refs_0_), channel_id=1, source_target_pairs={{0,4},{4,0},{8,12},{12,8},{16,20},{20,16},{24,28},{28,24},{1,5},{5... | collective-permute-start | bytes 589832 | tf_op jit(solution)/shard_map/ppermute | solution.py:15
  63.1 8.7 %collective-permute-start.32 = (bf16[384,256]{1,0:T(8,128)(2,1)S(1)}, bf16[384,256]{1,0:T(8,128)(2,1)S(1)}, u32[]{:S(2)}, u32[]{:S(2)}) collective-permute-start(bf16[384,256]{1,0:T(8,128)(2,1)S(1)} %shard_map.96.refs_0_), channel_id=1, source_target_pairs={{0,3},{1,2},{2,1},{3,0},{4,7},{5,6},{6,5},{7,4},{8,11},{9,10},{10,... | collective-permute-start | bytes 589832 | tf_op jit(solution)/shard_map/ppermute | solution.py:15
  64.5 11.1 %collective-permute-start.31 = (bf16[384,256]{1,0:T(8,128)(2,1)S(1)}, bf16[384,256]{1,0:T(8,128)(2,1)S(1)}, u32[]{:S(2)}, u32[]{:S(2)}) collective-permute-start(bf16[384,256]{1,0:T(8,128)(2,1)S(1)} %shard_map.96.refs_0_), channel_id=1, source_target_pairs={{0,2},{1,3},{2,0},{3,1},{4,6},{5,7},{6,4},{7,5},{8,10},{9,11},{10,... | collective-permute-start | bytes 589832 | tf_op jit(solution)/shard_map/ppermute | solution.py:15
  65.9 9.7 %collective-permute-start.30 = (bf16[384,256]{1,0:T(8,128)(2,1)S(1)}, bf16[384,256]{1,0:T(8,128)(2,1)S(1)}, u32[]{:S(2)}, u32[]{:S(2)}) collective-permute-start(bf16[384,256]{1,0:T(8,128)(2,1)S(1)} %shard_map.96.refs_0_), channel_id=1, source_target_pairs={{0,1},{1,0},{2,3},{3,2},{4,5},{5,4},{6,7},{7,6},{8,9},{9,8},{10,11... | collective-permute-start | bytes 589832 | tf_op jit(solution)/shard_map/ppermute | solution.py:15
  71.8 4.2 %collective-permute-start.36 = (bf16[384,256]{1,0:T(8,128)(2,1)S(1)}, bf16[384,256]{1,0:T(8,128)(2,1)S(1)}, u32[]{:S(2)}, u32[]{:S(2)}) collective-permute-start(bf16[384,256]{1,0:T(8,128)(2,1)S(1)} %collective-permute-done.32.refs_0_), channel_id=1, source_target_pairs={{0,4},{4,0},{8,12},{12,8},{16,20},{20,16},{24,28},{28,24},{1,5},{5... | collective-permute-start | bytes 589832 | tf_op jit(solution)/shard_map/ppermute | solution.py:15
  75.5 1.4 %collective-permute-start.34 = (bf16[384,256]{1,0:T(8,128)(2,1)S(1)}, bf16[384,256]{1,0:T(8,128)(2,1)S(1)}, u32[]{:S(2)}, u32[]{:S(2)}) collective-permute-start(bf16[384,256]{1,0:T(8,128)(2,1)S(1)} %collective-permute-done.30.refs_0_), channel_id=1, source_target_pairs={{0,4},{4,0},{8,12},{12,8},{16,20},{20,16},{24,28},{28,24},{1,5},{5... | collective-permute-start | bytes 589832 | tf_op jit(solution)/shard_map/ppermute | solution.py:15
  75.6 1.7 %collective-permute-start.35 = (bf16[384,256]{1,0:T(8,128)(2,1)S(1)}, bf16[384,256]{1,0:T(8,128)(2,1)S(1)}, u32[]{:S(2)}, u32[]{:S(2)}) collective-permute-start(bf16[384,256]{1,0:T(8,128)(2,1)S(1)} %collective-permute-done.31.refs_1_), channel_id=1, source_target_pairs={{0,4},{4,0},{8,12},{12,8},{16,20},{20,16},{24,28},{28,24},{1,5},{5... | collective-permute-start | bytes 589832 | tf_op jit(solution)/shard_map/ppermute | solution.py:15
